TPU v7x, 32 devices: a whole 2x2x4 slice. The times are simulated.
32 devices in a mesh: dp: 2 (over core), seq: 4 (over z), head: 4 (over y, x).
Axes of the slice: x: 2, y: 2, z: 4, core: 2. Of those that a mesh axis runs over, the one named last changes fastest.
Arguments:
- tokens: float32 [2, 2048, 1536], P('dp', 'seq'), may hold values from -6 to 6
- cotangent: float32 [2, 2048, 1536], P('dp', 'seq'), may hold values from -6 to 6
- pre_gain: float32 [2, 1536], replicated, may hold values from 0.5 to 1.5
- gate_weight: float32 [2, 1536, 3072], P(None, None, 'head'), may hold values from -0.15625 to 0.15625
- inner_weight: float32 [2, 1536, 3072], P(None, None, 'head'), may hold values from -0.15625 to 0.15625
- state_weight: float32 [2, 1536, 256], P(None, None, 'head'), may hold values from -0.15625 to 0.15625
- step_weight: float32 [2, 1536, 48], P(None, None, 'head'), may hold values from -0.15625 to 0.15625
- filter_inner: float32 [2, 4, 3072], P(None, None, 'head'), may hold values from -3 to 3
- filter_inner_bias: float32 [2, 3072], P(None, 'head'), may hold values from -3 to 3
- filter_state: float32 [2, 4, 256], P(None, None, 'head'), may hold values from -3 to 3
- filter_state_bias: float32 [2, 256], P(None, 'head'), may hold values from -3 to 3
- step_bias: float32 [2, 48], P(None, 'head'), may hold values from -4.5 to -3.5
- log_rate: float32 [2, 48], P(None, 'head'), may hold values from -9 to 1, as said below
- skip_gain: float32 [2, 48], P(None, 'head'), may hold values from 0.5 to 1.5
- norm_gain: float32 [2, 3072], P(None, 'head'), may hold values from 0.5 to 1.5
- out_weight: float32 [2, 1536, 3072], P(None, None, 'head'), may hold values from -0.109375 to 0.109375
Outputs:
- mixed: float32 [2, 2048, 1536], P('dp', 'seq')
- token_grad: float32 [2, 2048, 1536], P('dp', 'seq')
- grad_pre_gain: float32 [2, 1536], replicated
- grad_gate_weight: float32 [2, 1536, 3072], P(None, 'seq', 'head')
- grad_inner_weight: float32 [2, 1536, 3072], P(None, 'seq', 'head')
- grad_state_weight: float32 [2, 1536, 256], P(None, 'seq', 'head')
- grad_step_weight: float32 [2, 1536, 48], P(None, 'seq', 'head')
- grad_filter_inner: float32 [2, 4, 3072], P(None, None, 'head')
- grad_filter_inner_bias: float32 [2, 3072], P(None, 'head')
- grad_filter_state: float32 [2, 4, 256], P(None, None, 'head')
- grad_filter_state_bias: float32 [2, 256], P(None, 'head')
- grad_step_bias: float32 [2, 48], P(None, 'head')
- grad_log_rate: float32 [2, 48], P(None, 'head')
- grad_skip_gain: float32 [2, 48], P(None, 'head')
- grad_norm_gain: float32 [2, 3072], P(None, 'head')
- grad_out_weight: float32 [2, 1536, 3072], P(None, 'seq', 'head')
Inputs may be any that keep to these rules, and one draw needn't show every extreme that they name: log_rate holds logarithms of the heads' decay rates.
All inputs are finite; a program needn't handle non-finite values.
Results may differ from a plain program's by a relative error of at most 0.0003.
Values sent between devices are 32-bit elements; how exact they have to be, the bound alone decides.
No kernel may reach another device: no remote copies, remote signals or barrier semaphores. Data moves between devices by JAX's collectives and lax.ppermute only.
A program may use at most 384 MiB of HBM per device.

v0:
```python
import jax
import jax.numpy as jnp
from jax import lax
from jax.sharding import PartitionSpec as P

INNER = 3072
GROUP = 256


epsilon = 1e-05
highest = lax.Precision.HIGHEST


def passed_along(value, axis, steps):
    count = lax.axis_size(axis)
    leading, last = (max(0, -steps), min(count, count - steps))
    return lax.ppermute(value, axis, [(source, source + steps) for source in range(leading, last)])


def prefix(part, axis, combine, identity, reverse):
    count = lax.axis_size(axis)
    place = lax.axis_index(axis)
    ahead = count - 1 - place if reverse else place
    gathered = jax.tree.map(lambda a: lax.all_gather(a, axis), part)
    state = jax.tree.map(lambda a, e: jnp.zeros_like(a) + jnp.asarray(e, a.dtype), part, identity)

    def one(step, state):
        source = count - 1 - step if reverse else step
        return combine(
            state, jax.tree.map(lambda a: lax.dynamic_index_in_dim(a, source, 0, False), gathered)
        )

    return lax.fori_loop(0, ahead, one, state)


def matmul(left, right):
    return jnp.dot(left, right, precision=highest)


def project_out(values, weight):
    return lax.dot_general(values, weight, (((1,), (1,)), ((), ())), precision=highest)


def pre_norm(current, gain):
    return (
        current
        * lax.rsqrt(jnp.mean(current * current, axis=-1, keepdims=True) + epsilon)
        * gain[None, :]
    )


def project(normed, gate_weight, inner_weight, state_weight, step_weight):
    return (
        matmul(normed, gate_weight),
        matmul(normed, inner_weight),
        matmul(normed, state_weight),
        matmul(normed, step_weight),
    )


def causal_filter(signal, border, weight, bias):
    length = signal.shape[0]
    padded = jnp.concatenate([border, signal], axis=0)
    total = bias[None, :] + weight[0][None, :] * padded[0:length]
    for offset in range(1, weight.shape[0]):
        total = total + weight[offset][None, :] * padded[offset : offset + length]
    return jax.nn.silu(total)


def filters(
    inner_pre,
    state_pre,
    inner_border,
    state_border,
    filter_inner,
    filter_inner_bias,
    filter_state,
    filter_state_bias,
):
    return (
        causal_filter(inner_pre, inner_border, filter_inner, filter_inner_bias),
        causal_filter(state_pre, state_border, filter_state, filter_state_bias),
    )


def block_step(carry, block):
    state, offset = carry
    values, steps, rates, inputs_b, outputs_c = block
    within = jnp.cumsum(rates, axis=0)
    across = within.T
    length = rates.shape[0]
    lower = jnp.arange(length)[:, None] >= jnp.arange(length)[None, :]
    spread = jnp.where(lower[None], across[:, :, None] - across[:, None, :], 0.0)
    decay = jnp.where(lower[None], jnp.exp(spread), 0.0)
    intersection = matmul(outputs_c, inputs_b.T)
    mixing = decay * intersection[None] * steps.T[:, None, :]
    local = jnp.einsum("hij,jhp->ihp", mixing, values, precision=highest)
    carried = jnp.exp(within)[:, :, None] * jnp.einsum(
        "in,hpn->ihp", outputs_c, state, precision=highest
    )
    final = within[-1]
    weights = jnp.exp(final[None, :] - within) * steps
    fresh = jnp.einsum("jhp,jn->hpn", weights[:, :, None] * values, inputs_b, precision=highest)
    new_state = jnp.exp(final)[:, None, None] * state + fresh
    return ((new_state, offset + final), (local + carried, offset[None, :] + within))


def scan_local(inner_conv, state_full, step_raw, step_bias, log_rate, skip_gain):
    length = inner_conv.shape[0]
    heads = step_raw.shape[1]
    width = state_full.shape[1] // 2
    values = inner_conv.reshape(length, heads, -1)
    steps = jax.nn.softplus(step_raw + step_bias[None, :])
    rates = -jnp.exp(log_rate)[None, :] * steps
    blocks = length // GROUP

    def split(array):
        return array.reshape((blocks, GROUP) + array.shape[1:])

    start = (
        jnp.zeros((heads, values.shape[2], width), jnp.float32),
        jnp.zeros((heads,), jnp.float32),
    )
    (state, total), (output, within) = lax.scan(
        block_step,
        start,
        (
            split(values),
            split(steps),
            split(rates),
            split(state_full[:, :width]),
            split(state_full[:, width:]),
        ),
    )
    output = output.reshape(values.shape) + skip_gain[None, :, None] * values
    return (output, within.reshape(length, heads), state, jnp.exp(total))


def add_carried(output, within, state_full, incoming):
    width = state_full.shape[1] // 2
    return output + jnp.exp(within)[:, :, None] * jnp.einsum(
        "tn,hpn->thp", state_full[:, width:], incoming, precision=highest
    )


def gate_squares(mixer, gate):
    gated = mixer.reshape(gate.shape) * jax.nn.silu(gate)
    return (gated, jnp.sum(gated * gated, axis=-1))


def normed_out(gated, squares, norm_gain, out_weight):
    scale = lax.rsqrt(squares / INNER + epsilon)
    return project_out(gated * scale[:, None] * norm_gain[None, :], out_weight)


def chain(earlier, later):
    return (earlier[0] * later[0], later[0][:, None, None] * earlier[1] + later[1])


def body(
    tokens,
    cotangent,
    pre_gain,
    gate_weight,
    inner_weight,
    state_weight,
    step_weight,
    filter_inner,
    filter_inner_bias,
    filter_state,
    filter_state_bias,
    step_bias,
    log_rate,
    skip_gain,
    norm_gain,
    out_weight,
):
    current = tokens[0]
    kernel = filter_inner.shape[1]
    layers = pre_gain.shape[0]
    saved = []
    for layer in range(layers):
        normed, norm_back = jax.vjp(pre_norm, current, pre_gain[layer])
        (gate, inner_pre, state_pre, step_raw), project_back = jax.vjp(
            project,
            normed,
            gate_weight[layer],
            inner_weight[layer],
            state_weight[layer],
            step_weight[layer],
        )
        borders = passed_along((inner_pre[-(kernel - 1) :], state_pre[-(kernel - 1) :]), "seq", 1)
        (inner_conv, state_conv), filter_back = jax.vjp(
            filters,
            inner_pre,
            state_pre,
            borders[0],
            borders[1],
            filter_inner[layer],
            filter_inner_bias[layer],
            filter_state[layer],
            filter_state_bias[layer],
        )
        state_full = lax.all_gather(state_conv, "head", axis=1, tiled=True)
        (output, within, local_state, decay), scan_back = jax.vjp(
            scan_local,
            inner_conv,
            state_full,
            step_raw,
            step_bias[layer],
            log_rate[layer],
            skip_gain[layer],
        )
        incoming = prefix(
            (decay, local_state),
            "seq",
            chain,
            (jnp.ones_like(decay), jnp.zeros_like(local_state)),
            False,
        )
        mixer, carry_back = jax.vjp(add_carried, output, within, state_full, incoming[1])
        (gated, squares), gate_back = jax.vjp(gate_squares, mixer, gate)
        total_squares = lax.psum(squares, "head")
        part, out_back = jax.vjp(
            normed_out, gated, total_squares, norm_gain[layer], out_weight[layer]
        )
        branch = lax.psum(part, "head")
        saved.append(
            (
                norm_back,
                project_back,
                filter_back,
                scan_back,
                carry_back,
                gate_back,
                out_back,
                decay,
                incoming[1],
            )
        )
        current = current + branch
    grad = cotangent[0]
    collected = []
    for layer in reversed(range(layers)):
        (
            norm_back,
            project_back,
            filter_back,
            scan_back,
            carry_back,
            gate_back,
            out_back,
            decay,
            incoming,
        ) = saved[layer]
        grad_gated, grad_squares, grad_norm_gain, grad_out_weight = out_back(grad)
        grad_total = lax.psum(grad_squares, "head")
        grad_mixer, grad_gate = gate_back((grad_gated, grad_total))
        grad_output, grad_within, grad_full, grad_incoming = carry_back(grad_mixer)
        later = prefix(
            (decay, grad_incoming),
            "seq",
            chain,
            (jnp.ones_like(decay), jnp.zeros_like(grad_incoming)),
            True,
        )
        grad_local = later[1]
        grad_decay = jnp.sum(grad_local * incoming, axis=(1, 2))
        grad_conv, grad_full_scan, grad_step_raw, grad_step_bias, grad_log_rate, grad_skip_gain = (
            scan_back((grad_output, grad_within, grad_local, grad_decay))
        )
        grad_state_conv = lax.psum_scatter(
            grad_full + grad_full_scan, "head", scatter_dimension=1, tiled=True
        )
        (
            grad_inner_pre,
            grad_state_pre,
            grad_inner_border,
            grad_state_border,
            grad_filter_inner,
            grad_filter_inner_bias,
            grad_filter_state,
            grad_filter_state_bias,
        ) = filter_back((grad_conv, grad_state_conv))
        returned = passed_along((grad_inner_border, grad_state_border), "seq", -1)
        length = grad_inner_pre.shape[0]
        grad_inner_pre = grad_inner_pre + jnp.pad(returned[0], ((length - kernel + 1, 0), (0, 0)))
        grad_state_pre = grad_state_pre + jnp.pad(returned[1], ((length - kernel + 1, 0), (0, 0)))
        grad_normed, grad_gate_weight, grad_inner_weight, grad_state_weight, grad_step_weight = (
            project_back((grad_gate, grad_inner_pre, grad_state_pre, grad_step_raw))
        )
        grad_normed = lax.psum(grad_normed, "head")
        grad_branch, grad_pre_gain = norm_back(grad_normed)
        grad = grad + grad_branch
        rows = (
            lax.psum_scatter(grad_gate_weight, "seq", scatter_dimension=0, tiled=True),
            lax.psum_scatter(grad_inner_weight, "seq", scatter_dimension=0, tiled=True),
            lax.psum_scatter(grad_state_weight, "seq", scatter_dimension=0, tiled=True),
            lax.psum_scatter(grad_step_weight, "seq", scatter_dimension=0, tiled=True),
            lax.psum_scatter(grad_out_weight, "seq", scatter_dimension=0, tiled=True),
        )
        rows = lax.psum((rows[0], rows[1], rows[2], rows[3], rows[4]), "dp")
        smaller = lax.psum(
            (
                grad_pre_gain,
                grad_filter_inner,
                grad_filter_inner_bias,
                grad_filter_state,
                grad_filter_state_bias,
                grad_step_bias,
                grad_log_rate,
                grad_skip_gain,
                grad_norm_gain,
            ),
            ("dp", "seq"),
        )
        collected.append(
            (
                smaller[0],
                rows[0],
                rows[1],
                rows[2],
                rows[3],
                smaller[1],
                smaller[2],
                smaller[3],
                smaller[4],
                smaller[5],
                smaller[6],
                smaller[7],
                smaller[8],
                rows[4],
            )
        )
    collected = collected[::-1]
    stacked = [jnp.stack([entry[number] for entry in collected], axis=0) for number in range(14)]
    return (
        current[None],
        grad[None],
        stacked[0],
        stacked[1],
        stacked[2],
        stacked[3],
        stacked[4],
        stacked[5],
        stacked[6],
        stacked[7],
        stacked[8],
        stacked[9],
        stacked[10],
        stacked[11],
        stacked[12],
        stacked[13],
    )


def solution(mesh):
    placed = (
        P("dp", "seq", None),
        P("dp", "seq", None),
        P(),
        P(None, None, "head"),
        P(None, None, "head"),
        P(None, None, "head"),
        P(None, None, "head"),
        P(None, None, "head"),
        P(None, "head"),
        P(None, None, "head"),
        P(None, "head"),
        P(None, "head"),
        P(None, "head"),
        P(None, "head"),
        P(None, "head"),
        P(None, None, "head"),
    )
    return jax.shard_map(
        body,
        mesh=mesh,
        in_specs=placed,
        out_specs=(
            P("dp", "seq", None),
            P("dp", "seq", None),
            P(),
            P(None, "seq", "head"),
            P(None, "seq", "head"),
            P(None, "seq", "head"),
            P(None, "seq", "head"),
            P(None, None, "head"),
            P(None, "head"),
            P(None, None, "head"),
            P(None, "head"),
            P(None, "head"),
            P(None, "head"),
            P(None, "head"),
            P(None, "head"),
            P(None, "seq", "head"),
        ),
        check_vma=False,
    )
```

profile of v0, /device:TPU:0, one launch (start us, length us, event | category | flops | bytes accessed | tf_op | source)
XLA Modules:
  0.0 2000.5 jit_solution(8246926832603172320)
XLA Ops:
  22.3 10.2 fusion.284
  50.6 10.0 all_gather.46
  105.7 118.4 %while.220 = (s32[]{:T(128)}, f32[12,64,128]{2,1,0:T(8,128)S(1)}, f32[12]{0:T(128)}, f32[2,256,12,64]{1,0,3,2:T(2,128)}, f32[2,256,12]{1,0,2:T(2,128)}, /*index=...) while((s32[]{:T(128)}, f32[12,64,128]{2,1,0:T(8,128)S(1)}, ...), condition=%wide.region_4.6_spmd.clone.clone, body=%wide.region_1.5_spmd.clone.clone.sunk | while | flops 1318170624 | bytes 42479712 | solution.py:124
  133.3 16.8 dynamic_update_slice.509
  192.6 16.8 dynamic_update_slice.509
  230.3 10.6 all-reduce.44
  245.7 15.5 all-gather.11.cloned.1.call-done
  270.6 12.5 multiply_reduce_fusion.21
  292.9 11.4 fusion.276
  304.5 87.6 %all-reduce.55.cloned.1.call-done = f32[512,1536]{1,0:T(8,128)} async-done(((f32[512,1536]{1,0:T(8,128)}), f32[512,1536]{1,0:T(8,128)}) %all-reduce.55.cloned.1.call-update) | async-done | bytes 3145744 | tf_op jit(solution)/shard_map/psum | solution.py:227
  398.0 10.3 fusion.272
  421.4 10.5 all_gather.51
  466.8 83.6 %while.221 = (s32[]{:T(128)}, f32[12,64,128]{2,1,0:T(8,128)S(1)}, f32[12]{0:T(128)}, f32[2,256,12,64]{1,0,3,2:T(2,128)}, f32[2,256,12]{1,0,2:T(2,128)}, /*index=...) while((s32[]{:T(128)}, f32[12,64,128]{2,1,0:T(8,128)S(1)}, ...), condition=%wide.region_14.16_spmd.clone.clone, body=%wide.region_11.15_spmd.clone.clone.sunk | while | flops 1318170624 | bytes 34034452 | solution.py:124
  486.4 16.7 dynamic_update_slice.522
  528.2 16.7 dynamic_update_slice.522
  551.9 10.0 all-reduce.45
  565.4 21.2 %all-gather.13.cloned.1.call-done = f32[48,64,128]{2,1,0:T(8,128)} async-done(((f32[12,64,128]{2,1,0:T(8,128)}), f32[48,64,128]{2,1,0:T(8,128)}) %all-gather.13.cloned.1.call-update) | async-done | bytes 1572880 | tf_op jit(solution)/shard_map/all_gather | solution.py:24
  594.1 13.0 multiply_reduce_fusion.20
  617.0 13.2 multiply_reduce_fusion.4
  659.1 10.8 fusion.266
  669.9 17.3 all-gather.15.cloned.1.call-done
  698.7 121.2 %while.218 = (s32[]{:T(128)}, f32[12,64,128]{2,1,0:T(8,128)S(1)}, f32[12]{0:T(128)}, f32[2,256,12,64]{1,0,3,2:T(2,128)}, f32[2,256,12]{1,0,2:T(2,128)}, /*index=...) while((s32[]{:T(128)}, f32[12,64,128]{2,1,0:T(8,128)S(1)}, ...), condition=%wide.region_38.40_spmd.clone.clone, body=%wide.region_26.39_spmd.clone.clone.sunk | while | flops 2628289536 | bytes 48390292 | solution.py:124
  735.1 16.7 dynamic_update_slice.491
  795.4 16.7 dynamic_update_slice.491
  869.3 86.5 %all-reduce.57.cloned.1.call-done = f32[512,1536]{1,0:T(8,128)} async-done(((f32[512,1536]{1,0:T(8,128)}), f32[512,1536]{1,0:T(8,128)}) %all-reduce.57.cloned.1.call-update) | async-done | bytes 3145744 | tf_op jit(solution)/shard_map/psum | solution.py:292
  997.9 30.6 %all-gather.17.cloned.1.call-done = f32[48,64,128]{2,1,0:T(8,128)} async-done(((f32[12,64,128]{2,1,0:T(8,128)}), f32[48,64,128]{2,1,0:T(8,128)}) %all-gather.17.cloned.1.call-update) | async-done | bytes 1572880 | tf_op jit(solution)/shard_map/all_gather | solution.py:24
  1039.3 118.8 %while.219 = (s32[]{:T(128)}, f32[12,64,128]{2,1,0:T(8,128)S(1)}, f32[12]{0:T(128)}, f32[2,256,12,64]{1,0,3,2:T(2,128)}, f32[2,256,12]{1,0,2:T(2,128)}, /*index=...) while((s32[]{:T(128)}, f32[12,64,128]{2,1,0:T(8,128)S(1)}, ...), condition=%wide.region_60.62_spmd.clone.clone, body=%wide.region_48.61_spmd.clone.clone.sunk | while | flops 2628289536 | bytes 48586956 | solution.py:124
  1074.2 16.7 dynamic_update_slice.496
  1133.3 16.7 dynamic_update_slice.496
  1167.6 11.6 convolution_bitcast_fusion.4
  1181.1 11.3 fusion.452
  1205.5 11.9 fusion.373
  1218.1 11.8 fusion.366
  1230.4 11.3 fusion.322
  1261.4 10.0 fusion.320
  1271.6 11.5 fusion.264
  1286.0 11.3 fusion.278
  1305.1 10.5 fusion.282
  1320.6 62.4 %reduce-scatter.19.cloned.1.call-done = f32[384,768]{1,0:T(8,128)} async-done(((f32[1536,768]{1,0:T(8,128)}), f32[384,768]{1,0:T(8,128)}) %reduce-scatter.19.cloned.1.call-update) | async-done | bytes 1179664 | tf_op jit(solution)/shard_map/reduce_scatter | solution.py:296
  1383.1 23.4 %reduce-scatter.25.cloned.1.call-done = f32[384,64]{0,1:T(8,128)} async-done(((f32[1536,64]{0,1:T(8,128)}), f32[384,64]{0,1:T(8,128)}) %reduce-scatter.25.cloned.1.call-update) | async-done | bytes 98320 | tf_op jit(solution)/shard_map/reduce_scatter | solution.py:298
  1406.4 85.9 %reduce-scatter.23.cloned.1.call-done = f32[384,768]{1,0:T(8,128)} async-done(((f32[1536,768]{1,0:T(8,128)}), f32[384,768]{1,0:T(8,128)}) %reduce-scatter.23.cloned.1.call-update) | async-done | bytes 1179664 | tf_op jit(solution)/shard_map/reduce_scatter | solution.py:297
  1492.3 88.0 %reduce-scatter.33.cloned.1.call-done = f32[384,768]{1,0:T(8,128)} async-done(((f32[1536,768]{1,0:T(8,128)}), f32[384,768]{1,0:T(8,128)}) %reduce-scatter.33.cloned.1.call-update) | async-done | bytes 1179664 | tf_op jit(solution)/shard_map/reduce_scatter | solution.py:300
  1580.3 88.0 %reduce-scatter.17.cloned.1.call-done = f32[384,768]{1,0:T(8,128)} async-done(((f32[1536,768]{1,0:T(8,128)}), f32[384,768]{1,0:T(8,128)}) %reduce-scatter.17.cloned.1.call-update) | async-done | bytes 1179664 | tf_op jit(solution)/shard_map/reduce_scatter | solution.py:296
  1668.2 88.0 %reduce-scatter.21.cloned.1.call-done = f32[384,768]{1,0:T(8,128)} async-done(((f32[1536,768]{1,0:T(8,128)}), f32[384,768]{1,0:T(8,128)}) %reduce-scatter.21.cloned.1.call-update) | async-done | bytes 1179664 | tf_op jit(solution)/shard_map/reduce_scatter | solution.py:297
  1757.6 20.9 %reduce-scatter.31.cloned.1.call-done = f32[384,12]{0,1:T(8,128)} async-done(((f32[1536,12]{0,1:T(8,128)}), f32[384,12]{0,1:T(8,128)}) %reduce-scatter.31.cloned.1.call-update) | async-done | bytes 18448 | tf_op jit(solution)/shard_map/reduce_scatter | solution.py:299
  1778.5 20.1 %reduce-scatter.29.cloned.1.call-done = f32[384,12]{0,1:T(8,128)} async-done(((f32[1536,12]{0,1:T(8,128)}), f32[384,12]{0,1:T(8,128)}) %reduce-scatter.29.cloned.1.call-update) | async-done | bytes 18448 | tf_op jit(solution)/shard_map/reduce_scatter | solution.py:299
  1803.4 136.3 %all-reduce.59.cloned.1.call-done = (f32[512,1536]{1,0:T(8,128)}, f32[512,1536]{1,0:T(8,128)}) async-done(((f32[512,1536]{1,0:T(8,128)}, f32[512,1536]{1,0:T(8,128)}), (f32[512,1536]{1,0:T(8,128)}, f32[512,1536]{1,0:T(8,128)})) %all-reduce.59.cloned.1.call-update) | async-done | bytes 6291472 | tf_op jit(solution)/shard_map/psum | solution.py:227
  1942.4 29.9 %all-reduce.46 = (f32[1,1536]{1,0:T(1,128)S(1)}, f32[1,1536]{1,0:T(1,128)S(1)}, f32[1,4,768]{2,1,0:T(4,128)S(1)}, f32[1,4,768]{2,1,0:T(4,128)S(1)}, f32[1,768]{1...) all-reduce(f32[1,1536]{1,0:T(1,128)S(1)} %stack.127, ...), channel_id=1, replica_groups=mesh['dp'=2,'seq'=4,'head'=4] {'dp','seq'}, use_global_device_ids=true, to_apply=%region_67.69 | all-reduce | flops 13000 | bytes 104000 | tf_op jit(solution)/shard_map/psum | solution.py:303
  (1276 shorter events, 730.9 us)
Async XLA Ops:
  7.2 254.0 %all-gather.11.cloned.1.call-start = ((), (), s32[]{:S(2)}) async-start(), calls=%async_computation.26 | async-start | bytes 1966080 | tf_op jit(solution)/shard_map/all_gather | solution.py:24
  8.6 31.4 %copy-start.72 = (f32[1536]{0:T(1024)}, f32[1536]{0:T(1024)S(1)}, u32[]{:S(2)}) copy-start(f32[1536]{0:T(1024)S(1)} %get-tuple-element.3579) | copy-start | bytes 18436
  11.0 29.1 %copy-start.133 = (f32[512]{0:T(512)}, f32[512]{0:T(512)S(1)}, u32[]{:S(2)}) copy-start(f32[512]{0:T(512)S(1)} %fusion.433) | copy-start | bytes 6148
  16.6 21.5 %copy-start.189 = (f32[2,4,768]{2,1,0:T(4,128)S(1)}, f32[2,4,768]{2,1,0:T(4,128)}, u32[]{:S(2)}) copy-start(f32[2,4,768]{2,1,0:T(4,128)} %param.40) | copy-start | bytes 73732
  16.6 22.1 %copy-start.149 = (f32[2,1536,12]{1,0,2:T(2,128)S(1)}, f32[2,1536,12]{1,0,2:T(2,128)}, u32[]{:S(2)}) copy-start(f32[2,1536,12]{1,0,2:T(2,128)} %param.39) | copy-start | bytes 442372
  16.6 22.9 %copy-start.241 = (f32[2,12]{1,0:T(2,128)S(1)}, f32[2,12]{1,0:T(2,128)}, u32[]{:S(2)}) copy-start(f32[2,12]{1,0:T(2,128)} %param.45) | copy-start | bytes 292
  16.6 22.8 %copy-start.255 = (f32[2,12]{1,0:T(2,128)S(1)}, f32[2,12]{1,0:T(2,128)}, u32[]{:S(2)}) copy-start(f32[2,12]{1,0:T(2,128)} %param.44) | copy-start | bytes 292
  16.6 31.8 %collective-permute-start.1 = (f32[3,64]{0,1:T(8,128)}, f32[3,64]{0,1:T(8,128)}, u32[]{:S(2)}, u32[]{:S(2)}) collective-permute-start(f32[3,64]{0,1:T(8,128)} %slice.377), channel_id=1, source_target_pairs={{0,4},{4,8},{8,12},{1,5},{5,9},{9,13},{2,6},{6,10},{10,14},{3,7},{... | collective-permute-start | bytes 2312 | tf_op jit(solution)/shard_map/ppermute | solution.py:17
  33.2 32.7 %collective-permute-start = (f32[3,768]{1,0:T(4,128)}, f32[3,768]{1,0:T(4,128)S(1)}, u32[]{:S(2)}, u32[]{:S(2)}) collective-permute-start(f32[3,768]{1,0:T(4,128)} %slice.372), channel_id=1, source_target_pairs={{0,4},{4,8},{8,12},{1,5},{5,9},{9,13},{2,6},{6,10},{10,14},{3,7},{... | collective-permute-start | bytes 27656 | tf_op jit(solution)/shard_map/ppermute | solution.py:17
  38.7 27.2 %copy-start.175 = (f32[768]{0:T(1024)}, f32[768]{0:T(1024)S(1)}, u32[]{:S(2)}) copy-start(f32[768]{0:T(1024)S(1)} %get-tuple-element.3572) | copy-start | bytes 9220
  224.9 167.2 %all-reduce.55.cloned.1.call-start = ((), (), s32[]{:S(2)}) async-start(), calls=%async_computation.12 | async-start | bytes 6291456 | tf_op jit(solution)/shard_map/psum | solution.py:227
  228.3 64.6 %copy-start.150 = (f32[768]{0:T(1024)}, f32[768]{0:T(1024)S(1)}, u32[]{:S(2)}) copy-start(f32[768]{0:T(1024)S(1)} %get-tuple-element.3581) | copy-start | bytes 9220
  229.5 34.3 %copy-start.232 = (f32[12]{0:T(128)}, f32[12]{0:T(128)S(1)}, u32[]{:S(2)}) copy-start(f32[12]{0:T(128)S(1)} %get-tuple-element.4011) | copy-start | bytes 148
  304.3 282.3 %all-gather.13.cloned.1.call-start = ((), (), s32[]{:S(2)}) async-start(), calls=%async_computation.27 | async-start | bytes 1966080 | tf_op jit(solution)/shard_map/all_gather | solution.py:24
  304.5 90.0 %copy-start.75 = (f32[1536]{0:T(1024)S(1)}, f32[1536]{0:T(1024)}, u32[]{:S(2)}) copy-start(f32[1536]{0:T(1024)} %get-tuple-element.3578) | copy-start | bytes 18436
  398.0 22.4 %copy-start.81 = (f32[512,64]{0,1:T(8,128)}, f32[512,64]{0,1:T(8,128)S(1)}, u32[]{:S(2)}) copy-start(f32[512,64]{0,1:T(8,128)S(1)} %fusion.398) | copy-start | bytes 393220
  408.3 23.9 %copy-start.53 = (f32[512,768]{1,0:T(8,128)}, f32[512,768]{1,0:T(8,128)S(1)}, u32[]{:S(2)}) copy-start(f32[512,768]{1,0:T(8,128)S(1)} %fusion.272) | copy-start | bytes 4718596
  408.4 12.0 collective-permute-start.3
  411.8 20.3 %collective-permute-start.2 = (f32[3,768]{1,0:T(4,128)S(1)}, f32[3,768]{1,0:T(4,128)S(1)}, u32[]{:S(2)}, u32[]{:S(2)}) collective-permute-start(f32[3,768]{1,0:T(4,128)S(1)} %slice.384), channel_id=1, source_target_pairs={{0,4},{4,8},{8,12},{1,5},{5,9},{9,13},{2,6},{6,10},{10,14},{3,7},{... | collective-permute-start | bytes 27656 | tf_op jit(solution)/shard_map/ppermute | solution.py:17
  551.2 136.1 %all-gather.15.cloned.1.call-start = ((), (), s32[]{:S(2)}) async-start(), calls=%async_computation.28 | async-start | bytes 1966080 | tf_op jit(solution)/shard_map/all_gather | solution.py:24
  565.4 23.7 %copy-start.110 = (f32[2,8,2,256]{3,1,2,0:T(8,128)}, f32[2,8,2,256]{3,1,2,0:T(8,128)S(1)}, u32[]{:S(2)}) copy-start(f32[2,8,2,256]{3,1,2,0:T(8,128)S(1)} %copy.556) | copy-start | bytes 98308
  594.1 22.9 %copy-start.127 = (f32[768]{0:T(1024)S(1)}, f32[768]{0:T(1024)}, u32[]{:S(2)}) copy-start(f32[768]{0:T(1024)} %get-tuple-element.3580) | copy-start | bytes 9220
  617.0 21.4 %copy-start.147 = (f32[512]{0:T(512)}, f32[512]{0:T(512)S(1)}, u32[]{:S(2)}) copy-start(f32[512]{0:T(512)S(1)} %fusion.436) | copy-start | bytes 6148
  649.2 203.9 %reduce-scatter.13.cloned.1.call-start = ((), (), s32[]{:S(2)}) async-start(), calls=%async_computation.13 | async-start | bytes 655360 | tf_op jit(solution)/shard_map/reduce_scatter | solution.py:272
  824.1 131.7 %all-reduce.57.cloned.1.call-start = ((), (), s32[]{:S(2)}) async-start(), calls=%async_computation.14 | async-start | bytes 6291456 | tf_op jit(solution)/shard_map/psum | solution.py:292
  834.3 7.8 collective-permute-start.5
  855.3 6.4 collective-permute-start.4
  862.3 93.5 %copy-start.77 = (f32[1536]{0:T(1024)S(1)}, f32[1536]{0:T(1024)}, u32[]{:S(2)}) copy-start(f32[1536]{0:T(1024)} %get-tuple-element.3578) | copy-start | bytes 18436
  862.3 93.5 %copy-start.138 = (f32[512]{0:T(512)S(1)}, f32[512]{0:T(512)}, u32[]{:S(2)}) copy-start(f32[512]{0:T(512)} %copy-done.136) | copy-start | bytes 6148
  868.8 87.0 %copy-start.4 = (f32[512,1536]{1,0:T(8,128)S(1)}, f32[512,1536]{1,0:T(8,128)}, u32[]{:S(2)}) copy-start(f32[512,1536]{1,0:T(8,128)} %copy-done.2) | copy-start | bytes 9437188
  868.8 90.4 %copy-start.191 = (f32[512]{0:T(512)S(1)}, f32[512]{0:T(512)}, u32[]{:S(2)}) copy-start(f32[512]{0:T(512)} %copy-done.190) | copy-start | bytes 6148
  868.8 159.7 %all-gather.17.cloned.1.call-start = ((), (), s32[]{:S(2)}) async-start(), calls=%async_computation.29 | async-start | bytes 1966080 | tf_op jit(solution)/shard_map/all_gather | solution.py:24
  991.3 201.3 %reduce-scatter.15.cloned.1.call-start = ((), (), s32[]{:S(2)}) async-start(), calls=%async_computation.15 | async-start | bytes 655360 | tf_op jit(solution)/shard_map/reduce_scatter | solution.py:272
  1162.2 158.4 %reduce-scatter.27.cloned.1.call-start = ((), (), s32[]{:S(2)}) async-start(), calls=%async_computation.21 | async-start | bytes 491520 | tf_op jit(solution)/shard_map/reduce_scatter | solution.py:298
  1167.5 153.1 %reduce-scatter.35.cloned.1.call-start = ((), (), s32[]{:S(2)}) async-start(), calls=%async_computation.25 | async-start | bytes 5898240 | tf_op jit(solution)/shard_map/reduce_scatter | solution.py:300
  1179.2 203.9 %reduce-scatter.19.cloned.1.call-start = ((), (), s32[]{:S(2)}) async-start(), calls=%async_computation.17 | async-start | bytes 5898240 | tf_op jit(solution)/shard_map/reduce_scatter | solution.py:296
  1192.5 213.9 %reduce-scatter.25.cloned.1.call-start = ((), (), s32[]{:S(2)}) async-start(), calls=%async_computation.20 | async-start | bytes 491520 | tf_op jit(solution)/shard_map/reduce_scatter | solution.py:298
  1195.2 7.0 collective-permute-start.6
  1205.4 286.9 %reduce-scatter.23.cloned.1.call-start = ((), (), s32[]{:S(2)}) async-start(), calls=%async_computation.19 | async-start | bytes 5898240 | tf_op jit(solution)/shard_map/reduce_scatter | solution.py:297
  1217.4 362.9 %reduce-scatter.33.cloned.1.call-start = ((), (), s32[]{:S(2)}) async-start(), calls=%async_computation.24 | async-start | bytes 5898240 | tf_op jit(solution)/shard_map/reduce_scatter | solution.py:300
  1229.9 438.3 %reduce-scatter.17.cloned.1.call-start = ((), (), s32[]{:S(2)}) async-start(), calls=%async_computation.16 | async-start | bytes 5898240 | tf_op jit(solution)/shard_map/reduce_scatter | solution.py:296
  1241.7 514.5 %reduce-scatter.21.cloned.1.call-start = ((), (), s32[]{:S(2)}) async-start(), calls=%async_computation.18 | async-start | bytes 5898240 | tf_op jit(solution)/shard_map/reduce_scatter | solution.py:297
  1254.0 7.4 collective-permute-start.7
  1271.4 507.1 %reduce-scatter.31.cloned.1.call-start = ((), (), s32[]{:S(2)}) async-start(), calls=%async_computation.23 | async-start | bytes 122880 | tf_op jit(solution)/shard_map/reduce_scatter | solution.py:299
  1285.9 512.7 %reduce-scatter.29.cloned.1.call-start = ((), (), s32[]{:S(2)}) async-start(), calls=%async_computation.22 | async-start | bytes 122880 | tf_op jit(solution)/shard_map/reduce_scatter | solution.py:299
  1304.8 635.0 %all-reduce.59.cloned.1.call-start = ((), (), s32[]{:S(2)}) async-start(), calls=%async_computation.30 | async-start | bytes 12582912 | tf_op jit(solution)/shard_map/psum | solution.py:227
  1320.5 664.8 %all-reduce.61.cloned.1.call-start = ((), (), s32[]{:S(2)}) async-start(), calls=%async_computation.31 | async-start | bytes 14548992 | tf_op jit(solution)/shard_map/psum | solution.py:302
  1939.7 37.3 %copy-start.195 = (f32[512]{0:T(512)S(1)}, f32[512]{0:T(512)}, u32[]{:S(2)}) copy-start(f32[512]{0:T(512)} %copy-done.194) | copy-start | bytes 6148
  (321 other events, 1495.8 us)
Sparse Core Ops, SparseCore 0:
  225.1 36.0 all-gather.10
  304.4 87.6 all-reduce.54
  551.3 35.2 all-gather.12
  649.3 37.9 all-gather.14
  824.2 22.9 reduce-scatter.12
  869.0 86.8 all-reduce.56
  991.4 37.0 all-gather.16
  1162.3 22.9 reduce-scatter.14
  1188.1 20.6 reduce-scatter.26
  1211.1 83.7 reduce-scatter.34
  1297.3 85.7 reduce-scatter.18
  1385.3 21.1 reduce-scatter.24
  1408.7 83.5 reduce-scatter.22
  1494.5 85.7 reduce-scatter.32
  1582.4 85.7 reduce-scatter.16
  1670.4 85.7 reduce-scatter.20
  1758.9 19.5 reduce-scatter.30
  1781.3 17.2 reduce-scatter.28
  1802.7 136.9 all-reduce.58
  1942.9 34.2 all-reduce.60
where the time goes:
time: 2020 us; the launch traced here: 2000 us
  waiting for transfers between devices  888 us (44%)
  local copies, waits for them, and re-layouts  386 us (19%)
  matrix products  383 us (19%)
  other arithmetic  186 us (9%)
  blocking collectives  112 us (6%)
  starting transfers between devices  23.5 us (1%)
    psum x2, waiting for transfers between devices, body(): branch = lax.psum(part, 'head')  224 us
    dot_general x36, matrix products, matmul(): return jnp.dot(left, right, precision=highest)  198 us
    dynamic_update_slice x60, local copies, waits for them, and re-layouts, scan_local(): lax.scan(block_step, start, (split(values), split(steps), split(rates), s...  177 us
    reduce_scatter x2, waiting for transfers between devices, body(): lax.psum_scatter(grad_inner_weight, 'seq', scatter_dimension=0, tiled=True)  174 us
    reduce_scatter x2, waiting for transfers between devices, body(): lax.psum_scatter(grad_gate_weight, 'seq', scatter_dimension=0, tiled=True)  150 us
    reduce_scatter x2, waiting for transfers between devices, body(): lax.psum_scatter(grad_out_weight, 'seq', scatter_dimension=0, tiled=True)  88 us
    psum x1, waiting for transfers between devices, body(): grad_normed = lax.psum(grad_normed, 'head')  86.5 us
    all_gather x4, waiting for transfers between devices, prefix(): gathered = jax.tree.map(lambda a: lax.all_gather(a, axis), part)  84.6 us
  transfers between devices with their start and end apart: 28, of which 18 were waited for; matrix products, arithmetic and copies ran while one was open for 13% of the time, Pallas kernels for 0%

commit v1 on v0

v1 whole, which is shorter than its diff:
```python
import functools

import jax
import jax.numpy as jnp
from jax import lax
from jax.experimental import pallas as pl
from jax.experimental.pallas import tpu as pltpu
from jax.sharding import PartitionSpec as P

INNER = 3072
CHUNK = 128
LANES = 128
PAD = 8
epsilon = 1e-05
HIGH = lax.Precision.HIGH
HIGHEST = lax.Precision.HIGHEST
NEG = -1e30
F32 = jnp.float32


def power_of_two(n):
    return n & (n - 1) == 0


def exchanged(value, axis, distance):
    n = lax.axis_size(axis)
    return lax.ppermute(value, axis, [(i, i ^ distance) for i in range(n)])


def shifted(value, axis, step):
    n = lax.axis_size(axis)
    pairs = [(i, i + step) for i in range(n) if 0 <= i + step < n]
    return lax.ppermute(value, axis, pairs)


def distances(axis):
    n = lax.axis_size(axis)
    return [1 << k for k in range(n.bit_length() - 1)]


def bit_of(axis, distance):
    return (lax.axis_index(axis) // distance) % 2


def small_sum(value, axis):
    if not power_of_two(lax.axis_size(axis)):
        return lax.psum(value, axis)
    for distance in distances(axis):
        value = value + exchanged(value, axis, distance)
    return value


def half(value, which, dim=0):
    size = value.shape[dim] // 2
    return lax.dynamic_slice_in_dim(value, which * size, size, dim)


def joined(mine, other, axis, distance, dim=0):
    first = bit_of(axis, distance) == 0
    return jnp.concatenate(
        [jnp.where(first, mine, other), jnp.where(first, other, mine)], axis=dim
    )


def scatter_sum(value, axis, order):
    offset = 0
    for distance in order:
        bit = bit_of(axis, distance)
        size = value.shape[0] // 2
        value = half(value, bit) + exchanged(half(value, 1 - bit), axis, distance)
        offset = offset + bit * size
    return value, offset


def gather_back(value, axis, order, dim=0):
    for distance in order[::-1]:
        value = joined(value, exchanged(value, axis, distance), axis, distance, dim)
    return value


def head_sum(partial, finish):
    order = distances("head")
    rows = partial.shape[0] // 2
    parts = []
    for number, way in enumerate((order, order[::-1])):
        mine, offset = scatter_sum(partial[number * rows : (number + 1) * rows], "head", way)
        parts.append((finish(mine, number * rows + offset), way))
    return jnp.concatenate([gather_back(mine, "head", way) for mine, way in parts], axis=0)


def line_scatter_sum(value, axis):
    n = lax.axis_size(axis)
    if n > 4:
        return lax.psum_scatter(value, axis, scatter_dimension=0, tiled=True)
    rows = value.shape[0] // n
    place = lax.axis_index(axis)

    def shard(number):
        return lax.dynamic_slice_in_dim(value, jnp.clip(number, 0, n - 1) * rows, rows, 0)

    up = shard(n + place - 1)
    down = shard(place + 1 - n)
    for step in range(1, n):
        got_up = lax.ppermute(up, axis, [(z, z + 1) for z in range(step)])
        got_down = lax.ppermute(down, axis, [(n - 1 - z, n - 2 - z) for z in range(step)])
        if step < n - 1:
            up = got_up + shard(n + place - step - 1)
            down = got_down + shard(place + step + 1 - n)
        else:
            return got_up + got_down + shard(place)
    return value


def state_before(local, decay, reverse):
    n = lax.axis_size("seq")
    state = jnp.zeros_like(local)
    for hop in range(n - 1):
        source, target = (n - 1 - hop, n - 2 - hop) if reverse else (hop, hop + 1)
        state = state + lax.ppermute(decay * state + local, "seq", [(source, target)])
    return state


def call(kernel, outs, scratch, flops, *args):
    shapes = [jax.ShapeDtypeStruct(shape, F32) for shape in outs]
    size = 4 * sum(a.size for a in args) + 4 * sum(s.size for s in shapes)
    return pl.pallas_call(
        kernel,
        out_shape=shapes,
        in_specs=[pl.BlockSpec(memory_space=pltpu.VMEM)] * len(args),
        out_specs=[pl.BlockSpec(memory_space=pltpu.VMEM)] * len(outs),
        scratch_shapes=scratch,
        compiler_params=pltpu.CompilerParams(vmem_limit_bytes=40 * 1024 * 1024),
        cost_estimate=pl.CostEstimate(flops=flops, bytes_accessed=size, transcendentals=0),
    )(*args)


def dot(left, right, dims=((1,), (0,)), precision=HIGH):
    return lax.dot_general(
        left, right, (dims, ((), ())), precision=precision, preferred_element_type=F32
    )


NT = ((1,), (1,))


def sigmoid(value):
    return 1.0 / (1.0 + jnp.exp(-value))


def spread_heads(columns, tile, width):
    each = LANES // width
    lane = lax.broadcasted_iota(jnp.int32, (columns.shape[0], LANES), 1)
    result = columns[:, tile * each : tile * each + 1]
    for k in range(1, each):
        result = jnp.where(lane < k * width, result, columns[:, tile * each + k : tile * each + k + 1])
    return jnp.broadcast_to(result, (columns.shape[0], LANES))


def head_rows(row, width, total):
    tiles = [spread_heads(row, tile, width) for tile in range(total // LANES)]
    return jnp.concatenate(tiles, axis=1)


def filter_tile(scratch, taps, start, rows, cols):
    block = scratch[pl.ds(start, rows + PAD), cols]
    total = taps[4:5, cols] + taps[3:4, cols] * block[PAD:]
    for back in range(1, 4):
        total = total + taps[3 - back : 4 - back, cols] * pltpu.roll(block, back, 0)[PAD:]
    return total


def start_kernel(
    width, ip, ib, sp, sb, ti, ts, hp, v_out, bc_out, dsi, dss, dt_out, cum_out, cumt_out, fresh, local, chdec, padi, pads
):
    length, inner = ip.shape
    states = ts.shape[1]
    n = states // 2
    padi[0:PAD, :] = ib[...]
    padi[PAD:, :] = ip[...]
    pads[0:PAD, :] = sb[...]
    pads[PAD:, :] = sp[:, :states]
    rows = 64

    def filtered(step, _):
        start = pl.multiple_of(step * rows, rows)
        for scratch, taps, out, slope, size in (
            (padi, ti, v_out, dsi, inner),
            (pads, ts, bc_out, dss, states),
        ):
            for tile in range(size // LANES):
                cols = slice(tile * LANES, (tile + 1) * LANES)
                total = filter_tile(scratch, taps, start, rows, cols)
                gate = sigmoid(total)
                value = total * gate
                out[pl.ds(start, rows), cols] = value
                slope[pl.ds(start, rows), cols] = gate + value * (1.0 - gate)
        return 0

    lax.fori_loop(0, length // rows, filtered, 0)
    raw = sp[:, states:] + hp[0:1, :]
    dt = jnp.maximum(raw, 0.0) + jnp.log1p(jnp.exp(-jnp.abs(raw)))
    dt_out[...] = dt
    rate = -jnp.exp(hp[1:2, :]) * dt
    ones = (
        lax.broadcasted_iota(jnp.int32, (CHUNK, CHUNK), 0)
        >= lax.broadcasted_iota(jnp.int32, (CHUNK, CHUNK), 1)
    ).astype(F32)
    chunks = length // CHUNK
    for c in range(chunks):
        span = slice(c * CHUNK, (c + 1) * CHUNK)
        cum = dot(ones, rate[span], precision=HIGHEST)
        cum_out[span, :] = cum
        cumt_out[:, span] = cum.T[: cumt_out.shape[0]]
        last = cum[CHUNK - 1 : CHUNK, :]
        weight = jnp.exp(last - cum) * dt[span]
        maps = bc_out[span, :n].T
        chdec[c : c + 1, :] = head_rows(jnp.exp(last), width, inner)
        for tile in range(inner // LANES):
            cols = slice(tile * LANES, (tile + 1) * LANES)
            weighted = v_out[span, cols] * spread_heads(weight, tile, width)
            fresh[c, :, cols] = dot(maps, weighted)
    state = fresh[0]
    decay = chdec[0:1, :]
    for c in range(1, chunks):
        state = chdec[c : c + 1, :] * state + fresh[c]
        decay = decay * chdec[c : c + 1, :]
    local[...] = state
    chdec[chunks : chunks + 1, :] = decay


def inner_kernel(width, v, bc, dt, cum, cumt, hp, out):
    length, inner = v.shape
    n = bc.shape[1] // 2
    each = LANES // width
    lane = lax.broadcasted_iota(jnp.int32, (CHUNK, LANES), 1)
    lower = lax.broadcasted_iota(jnp.int32, (CHUNK, CHUNK), 0) >= lax.broadcasted_iota(
        jnp.int32, (CHUNK, CHUNK), 1
    )
    for c in range(length // CHUNK):
        span = slice(c * CHUNK, (c + 1) * CHUNK)
        meet = dot(bc[span, n:], bc[span, :n], NT)
        for tile in range(inner // LANES):
            cols = slice(tile * LANES, (tile + 1) * LANES)
            values = v[span, cols]
            stepped = values * spread_heads(dt[span, :], tile, width)
            result = None
            for k in range(each):
                head = tile * each + k
                spread = cum[span, head : head + 1] - cumt[head : head + 1, span]
                mixing = jnp.exp(jnp.where(lower, spread, NEG)) * meet
                part = dot(mixing, stepped)
                result = part if k == 0 else jnp.where(lane < k * width, result, part)
            skip = spread_heads(hp[2:3, :], tile, width)
            out[span, cols] = result + skip * values


def gate_kernel(width, yd, bc, cum, fresh, chdec, entering, gate, gain, y_out, gn_out, states, squares):
    length, inner = yd.shape
    n = bc.shape[1] // 2
    ones = jnp.ones((PAD, LANES), F32)
    for c in range(length // CHUNK):
        span = slice(c * CHUNK, (c + 1) * CHUNK)
        if c == 0:
            states[0] = entering[...]
        else:
            states[c] = chdec[c - 1 : c, :] * states[c - 1] + fresh[c - 1]
        carried = jnp.exp(cum[span, :])
        maps = bc[span, n:]
        total = None
        for tile in range(inner // LANES):
            cols = slice(tile * LANES, (tile + 1) * LANES)
            y = yd[span, cols] + spread_heads(carried, tile, width) * dot(maps, states[c, :, cols])
            y_out[span, cols] = y
            g = gate[span, cols]
            gated = y * (g * sigmoid(g))
            gn_out[span, cols] = gated * gain[0:1, cols]
            total = gated * gated if tile == 0 else total + gated * gated
        squares[:, span] = dot(ones, total, NT, HIGHEST)


def open_kernel(
    width, q, y, gate, gain, scale, slope, bc, cum, chdec, dy_out, dgate, u_out, dgain, adjoint, local
):
    length, inner = q.shape
    n = bc.shape[1] // 2
    chunks = length // CHUNK
    for c in range(chunks):
        span = slice(c * CHUNK, (c + 1) * CHUNK)
        carried = jnp.exp(cum[span, :])
        maps = bc[span, n:].T
        s = scale[span, :]
        t = slope[span, :]
        for tile in range(inner // LANES):
            cols = slice(tile * LANES, (tile + 1) * LANES)
            g = gate[span, cols]
            soft = sigmoid(g)
            silu = g * soft
            out = y[span, cols]
            gated = out * silu
            grad = q[span, cols]
            scaled = gated * s
            u_out[span, cols] = scaled * gain[0:1, cols]
            part = (grad * scaled).reshape(CHUNK // PAD, PAD, LANES).sum(axis=0)
            dgain[:, cols] = part if c == 0 else dgain[:, cols] + part
            dgated = s * (grad * gain[0:1, cols]) - t * gated
            dgate[span, cols] = dgated * out * (soft + silu * (1.0 - soft))
            dy = dgated * silu
            dy_out[span, cols] = dy
            adjoint[c, :, cols] = dot(maps, dy * spread_heads(carried, tile, width))
    state = adjoint[chunks - 1]
    for c in range(chunks - 2, -1, -1):
        state = adjoint[c] + chdec[c : c + 1, :] * state
    local[...] = state


def back_kernel(width, dy, v, bc, dt, cum, cumt, states, du, dbc, gram):
    length, inner = v.shape
    n = bc.shape[1] // 2
    each = LANES // width
    lane = lax.broadcasted_iota(jnp.int32, (CHUNK, LANES), 1)
    upper = lax.broadcasted_iota(jnp.int32, (CHUNK, CHUNK), 0) <= lax.broadcasted_iota(
        jnp.int32, (CHUNK, CHUNK), 1
    )
    for c in range(length // CHUNK):
        span = slice(c * CHUNK, (c + 1) * CHUNK)
        inputs, outputs = bc[span, :n], bc[span, n:]
        meet = dot(inputs, outputs, NT)
        carried = jnp.exp(cum[span, :])
        grad_out = None
        for tile in range(inner // LANES):
            cols = slice(tile * LANES, (tile + 1) * LANES)
            grad = dy[span, cols]
            stepped = v[span, cols] * spread_heads(dt[span, :], tile, width)
            result = None
            for k in range(each):
                head = tile * each + k
                spread = cumt[head : head + 1, span] - cum[span, head : head + 1]
                decay = jnp.exp(jnp.where(upper, spread, NEG))
                part = dot(decay * meet, grad)
                result = part if k == 0 else jnp.where(lane < k * width, result, part)
                own = (lane >= k * width) & (lane < (k + 1) * width)
                cross = decay * dot(jnp.where(own, stepped, 0.0), grad, NT)
                first = tile == 0 and k == 0
                gram[...] = cross if first else gram[...] + cross
            du[span, cols] = result
            part = dot(grad * spread_heads(carried, tile, width), states[c, :, cols], NT)
            grad_out = part if tile == 0 else grad_out + part
        total = gram[...]
        dbc[span, :n] = dot(total, outputs)
        dbc[span, n:] = grad_out + dot(total.T, inputs)


def head_totals(product, width):
    each = LANES // width
    lane = lax.broadcasted_iota(jnp.int32, product.shape, 1)
    result = []
    for k in range(each):
        own = (lane >= k * width) & (lane < (k + 1) * width)
        result.append(jnp.sum(jnp.where(own, product, 0.0), axis=1, keepdims=True))
    return result


def place_heads(columns, shape):
    lane = lax.broadcasted_iota(jnp.int32, shape, 1)
    result = jnp.zeros(shape, F32)
    for head, column in enumerate(columns):
        result = jnp.where(lane == head, column, result)
    return result


def close_kernel(
    width, dy, y, v, bc, dt, cum, sp, hp, du, dbc, dsi, dss, adjoint, chdec, fresh, states, later,
    dti, dts, dstep, rows, leaving,
):
    length, inner = v.shape
    n = bc.shape[1] // 2
    chunks = length // CHUNK
    heads_rate = -jnp.exp(hp[1:2, :])
    final = chdec[chunks - 1 : chunks, :] * states[chunks - 1] + fresh[chunks - 1]
    crossing = jnp.sum(final * later[...], axis=0, keepdims=True)
    columns = []
    for tile in range(inner // LANES):
        columns += head_totals(crossing[:, tile * LANES : (tile + 1) * LANES], width)
    running = place_heads(columns, (1, LANES))
    ones = (
        lax.broadcasted_iota(jnp.int32, (CHUNK, CHUNK), 0)
        <= lax.broadcasted_iota(jnp.int32, (CHUNK, CHUNK), 1)
    ).astype(F32)
    leaving[...] = later[...]
    rows[...] = jnp.zeros_like(rows)
    for c in range(chunks - 1, -1, -1):
        span = slice(c * CHUNK, (c + 1) * CHUNK)
        step = dt[span, :]
        cums = cum[span, :]
        fade = jnp.exp(cums[CHUNK - 1 : CHUNK, :] - cums)
        inputs = bc[span, :n]
        grad_in = dbc[span, :n]
        own, direct = [], []
        for tile in range(inner // LANES):
            cols = slice(tile * LANES, (tile + 1) * LANES)
            adj = leaving[:, cols]
            wide_fade = spread_heads(fade, tile, width)
            wide_step = spread_heads(step, tile, width)
            skip = spread_heads(hp[2:3, :], tile, width)
            values = v[span, cols]
            grad = dy[span, cols]
            dstepped = du[span, cols] + wide_fade * dot(inputs, adj)
            grad_in = grad_in + dot(wide_fade * wide_step * values, adj, NT)
            dti[span, cols] = (wide_step * dstepped + skip * grad) * dsi[span, cols]
            own += head_totals(grad * (y[span, cols] - skip * values), width)
            direct += head_totals(values * dstepped, width)
            part = (grad * values).reshape(CHUNK // PAD, PAD, LANES).sum(axis=0)
            rows[0:PAD, cols] = rows[0:PAD, cols] + part
            leaving[:, cols] = adjoint[c, :, cols] + chdec[c : c + 1, cols] * adj
        dts[span, :n] = grad_in * dss[span, :n]
        dts[span, n:] = dbc[span, n:] * dss[span, n:]
        direct = place_heads(direct, (CHUNK, LANES))
        dcum = place_heads(own, (CHUNK, LANES)) - step * direct
        drate = dot(ones, dcum, precision=HIGHEST) + running
        running = drate[0:1, :]
        dstep_value = direct + drate * heads_rate
        raw = sp[span, 2 * n :] + hp[0:1, :]
        grad_raw = dstep_value * sigmoid(raw)
        dstep[span, :] = grad_raw
        lanes = slice(0, LANES)
        rates = drate * heads_rate * step
        rows[PAD : 2 * PAD, lanes] = rows[PAD : 2 * PAD, lanes] + rates.reshape(
            CHUNK // PAD, PAD, LANES
        ).sum(axis=0)
        rows[2 * PAD : 3 * PAD, lanes] = rows[2 * PAD : 3 * PAD, lanes] + grad_raw.reshape(
            CHUNK // PAD, PAD, LANES
        ).sum(axis=0)


def filter_back_kernel(dti, hi, dts, hs, ip, ib, sp, sb, ti, ts, dip, dsp, ri, rs, padi, pads, padgi, padgs):
    length, inner = ip.shape
    states = dts.shape[1]
    padi[0:PAD, :] = ib[...]
    padi[PAD:, :] = ip[...]
    pads[0:PAD, :] = sb[...]
    pads[PAD:, :] = sp[:, :states]
    padgi[0:length, :] = dti[...]
    padgi[length:, :] = hi[...]
    padgs[0:length, :] = dts[...]
    padgs[length:, :] = hs[...]
    ri[...] = jnp.zeros_like(ri)
    rs[...] = jnp.zeros_like(rs)
    rows = 64

    def folded(value):
        return value.reshape(rows // PAD, PAD, LANES).sum(axis=0)

    def step(number, _):
        start = pl.multiple_of(number * rows, rows)
        for signal, grads, taps, out, sums, size in (
            (padi, padgi, ti, dip, ri, inner),
            (pads, padgs, ts, dsp, rs, states),
        ):
            for tile in range(size // LANES):
                cols = slice(tile * LANES, (tile + 1) * LANES)
                ahead = grads[pl.ds(start, rows + PAD), cols]
                grad = ahead[:rows]
                before = signal[pl.ds(start, rows + PAD), cols]
                total = taps[3:4, cols] * grad
                sums[3 * PAD : 4 * PAD, cols] = sums[3 * PAD : 4 * PAD, cols] + folded(grad * before[PAD:])
                sums[4 * PAD : 5 * PAD, cols] = sums[4 * PAD : 5 * PAD, cols] + folded(grad)
                for back in range(1, 4):
                    tap = 3 - back
                    total = total + taps[tap : tap + 1, cols] * pltpu.roll(ahead, rows + PAD - back, 0)[:rows]
                    place = slice(tap * PAD, (tap + 1) * PAD)
                    sums[place, cols] = sums[place, cols] + folded(
                        grad * pltpu.roll(before, back, 0)[PAD:]
                    )
                out[pl.ds(start, rows), cols] = total
        return 0

    lax.fori_loop(0, length // rows, step, 0)


def matmul(left, right, dims=((1,), (0,))):
    return lax.dot_general(left, right, (dims, ((), ())), precision=HIGH)


def padded_rows(rows, lanes):
    rows = jnp.concatenate(rows, axis=0)
    return jnp.pad(rows, ((0, PAD - rows.shape[0]), (0, lanes - rows.shape[1])))


def forward(current, w):
    length = current.shape[0]
    inner = w["inner"].shape[1]
    heads = w["heads"]
    width = inner // heads
    states = w["taps_s"].shape[1]
    n = states // 2
    chunks = length // CHUNK
    root = lax.rsqrt(jnp.mean(current * current, axis=-1, keepdims=True) + epsilon)
    normed = current * root * w["pre_gain"][None, :]
    ip = matmul(normed, w["inner"])
    sp = matmul(normed, w["maps"])
    border = shifted(
        jnp.concatenate([ip[length - PAD :], sp[length - PAD :, :states]], axis=1), "seq", 1
    )
    ib, sb = border[:, :inner], border[:, inner:]
    gate = matmul(normed, w["gate"])
    v, bc, dsi, dss, dt, cum, cumt, fresh, local, chdec = call(
        functools.partial(start_kernel, width),
        [
            (length, inner),
            (length, states),
            (length, inner),
            (length, states),
            (length, LANES),
            (length, LANES),
            (16, length),
            (chunks, n, inner),
            (n, inner),
            (2 * PAD, inner),
        ],
        [pltpu.VMEM((length + PAD, inner), F32), pltpu.VMEM((length + PAD, states), F32)],
        2 * 3 * length * n * inner,
        ip, ib, sp, sb, w["taps_i"], w["taps_s"], w["heads_rows"],
    )
    decay = chdec[chunks : chunks + 1]
    entering = state_before(local, decay, False)
    (yd,) = call(
        functools.partial(inner_kernel, width),
        [(length, inner)],
        [],
        2 * 6 * length * CHUNK * inner,
        v, bc, dt, cum, cumt, w["heads_rows"],
    )
    y, gn, carried, squares = call(
        functools.partial(gate_kernel, width),
        [(length, inner), (length, inner), (chunks, n, inner), (PAD, length)],
        [],
        2 * 3 * length * n * inner,
        yd, bc, cum, fresh, chdec, entering, gate, w["norm_gain"][None, :],
    )
    part = matmul(gn, w["out"], NT)
    saved = dict(
        current=current, root=root, normed=normed, ip=ip, sp=sp, ib=ib, sb=sb, gate=gate, v=v, bc=bc,
        dsi=dsi, dss=dss, dt=dt, cum=cum, cumt=cumt, fresh=fresh, chdec=chdec, decay=decay, y=y,
        gn=gn, states=carried,
    )
    return part, squares[0], saved


def both_cores(left, right):
    place = lax.axis_index("dp")
    n = lax.axis_size("dp")
    if n != 2:
        return lax.psum(matmul(left, right, ((0,), (0,))), "dp")
    sent = exchanged(matmul(left, half(right, 1 - place, 1), ((0,), (0,))), "dp", 1)
    return matmul(left, half(right, place, 1), ((0,), (0,))) + sent


def weight_grad(left, right):
    total = line_scatter_sum(both_cores(left, right), "seq")
    if lax.axis_size("dp") != 2:
        return total
    return joined(total, exchanged(total, "dp", 1), "dp", 1, 1)


def backward(grad, q, scale, slope, w, saved):
    s = saved
    length, inner = q.shape
    width = inner // w["heads"]
    states = w["taps_s"].shape[1]
    n = states // 2
    chunks = length // CHUNK
    dy, dgate, u, dgain, adjoint, local = call(
        functools.partial(open_kernel, width),
        [(length, inner), (length, inner), (length, inner), (PAD, inner), (chunks, n, inner), (n, inner)],
        [],
        2 * 3 * length * n * inner,
        q, s["y"], s["gate"], w["norm_gain"][None, :], scale[:, None], slope[:, None], s["bc"], s["cum"], s["chdec"],
    )
    later = state_before(local, s["decay"], True)
    du, dbc = call(
        functools.partial(back_kernel, width),
        [(length, inner), (length, states)],
        [pltpu.VMEM((CHUNK, CHUNK), F32)],
        2 * 15 * length * CHUNK * inner,
        dy, s["v"], s["bc"], s["dt"], s["cum"], s["cumt"], s["states"],
    )
    grad_out_weight = weight_grad(grad, u)
    grad_gate_weight = weight_grad(s["normed"], dgate)
    dti, dts, dstep, rows = call(
        functools.partial(close_kernel, width),
        [(length, inner), (length, states), (length, LANES), (3 * PAD, inner)],
        [pltpu.VMEM((n, inner), F32)],
        2 * 6 * length * n * inner,
        dy, s["y"], s["v"], s["bc"], s["dt"], s["cum"], s["sp"], w["heads_rows"], du, dbc, s["dsi"], s["dss"],
        adjoint, s["chdec"], s["fresh"], s["states"], later,
    )
    halo = shifted(jnp.concatenate([dti[:PAD], dts[:PAD]], axis=1), "seq", -1)
    dip, dsp, ri, rs = call(
        filter_back_kernel,
        [(length, inner), (length, states), (5 * PAD, inner), (5 * PAD, states)],
        [
            pltpu.VMEM((length + PAD, inner), F32),
            pltpu.VMEM((length + PAD, states), F32),
            pltpu.VMEM((length + PAD, inner), F32),
            pltpu.VMEM((length + PAD, states), F32),
        ],
        16 * length * inner,
        dti, halo[:, :inner], dts, halo[:, inner:], s["ip"], s["ib"], s["sp"], s["sb"], w["taps_i"], w["taps_s"],
    )
    dnormed = (
        matmul(dgate, w["gate"], NT)
        + matmul(dip, w["inner"], NT)
        + matmul(jnp.concatenate([dsp, dstep], axis=1), w["maps"], NT)
    )
    grad_inner_weight = weight_grad(s["normed"], dip)

    dgain_pre = jnp.sum(dnormed * s["current"] * s["root"], axis=0)

    def finish(rows_grad, offset):
        def take(array):
            return lax.dynamic_slice_in_dim(array, offset, rows_grad.shape[0], 0)

        x, root = take(s["current"]), take(s["root"])
        scaled = rows_grad * w["pre_gain"][None, :]
        along = jnp.mean(scaled * x, axis=-1, keepdims=True)
        return root * scaled - x * (root * root * root * along)

    branch = head_sum(dnormed, finish)

    order = distances("head")
    shared = dsp
    heads_count = lax.axis_size("head")
    if power_of_two(heads_count):
        for distance in order[::-1]:
            bit = bit_of("head", distance)
            shared = half(shared, bit, 1) + exchanged(half(shared, 1 - bit, 1), "head", distance)
    else:
        shared = lax.psum_scatter(shared, "head", scatter_dimension=1, tiled=True)
    small = jnp.concatenate([shared, dstep[:, : w["heads"]]], axis=1)
    grad_small = small_sum(matmul(s["normed"], small, ((0,), (0,))), "dp")
    grad_small = line_scatter_sum(grad_small, "seq")
    own = shared.shape[1]

    def folded(array):
        return array.reshape(-1, PAD, array.shape[1]).sum(axis=1)

    ri, rs, rows = folded(ri), folded(rs), folded(rows)
    over_heads = small_sum(jnp.concatenate([dgain_pre, rs.reshape(-1)]), "head")
    flat = jnp.concatenate(
        [over_heads, ri.reshape(-1), dgain.sum(axis=0), rows[0], rows[1, :LANES], rows[2, :LANES]]
    )
    flat = small_sum(small_sum(flat, "dp"), "seq")
    cut = []
    start = 0
    for size in (dgain_pre.size, rs.size, ri.size, inner, inner, LANES, LANES):
        cut.append(flat[start : start + size])
        start += size
    g_pre, g_rs, g_ri, g_norm, g_skip, g_rate, g_bias = cut
    g_rs = lax.dynamic_slice_in_dim(g_rs.reshape(5, states), lax.axis_index("head") * own, own, 1)
    g_ri = g_ri.reshape(5, inner)
    heads = w["heads"]
    grads = (
        g_pre,
        grad_gate_weight,
        grad_inner_weight,
        grad_small[:, :own],
        grad_small[:, own:],
        g_ri[:4],
        g_ri[4],
        g_rs[:4],
        g_rs[4],
        g_bias[:heads],
        g_rate[:heads],
        g_skip.reshape(heads, width).sum(axis=1),
        g_norm,
        grad_out_weight,
    )
    return grad + branch, grads


def gathered_columns(value):
    if not power_of_two(lax.axis_size("head")):
        return lax.all_gather(value, "head", axis=1, tiled=True)
    return gather_back(value, "head", distances("head")[::-1], 1)


def gathered_all(value):
    return gathered_columns(value)


def body(
    tokens,
    cotangent,
    pre_gain,
    gate_weight,
    inner_weight,
    state_weight,
    step_weight,
    filter_inner,
    filter_inner_bias,
    filter_state,
    filter_state_bias,
    step_bias,
    log_rate,
    skip_gain,
    norm_gain,
    out_weight,
):
    layers = pre_gain.shape[0]
    heads = step_bias.shape[1]
    inner = gate_weight.shape[2]
    taps = jnp.concatenate([filter_state, filter_state_bias[:, None, :]], axis=1)
    taps = gathered_columns(taps.reshape(-1, taps.shape[2]))
    taps = taps.reshape(layers, 5, -1)
    weights = []
    for layer in range(layers):
        maps = jnp.concatenate(
            [
                gathered_columns(state_weight[layer]),
                jnp.pad(step_weight[layer], ((0, 0), (0, LANES - heads))),
            ],
            axis=1,
        )
        weights.append(
            dict(
                heads=heads,
                pre_gain=pre_gain[layer],
                gate=gate_weight[layer],
                inner=inner_weight[layer],
                maps=maps,
                out=out_weight[layer],
                norm_gain=norm_gain[layer],
                taps_i=padded_rows([filter_inner[layer], filter_inner_bias[layer][None]], inner),
                taps_s=padded_rows([taps[layer]], taps.shape[2]),
                heads_rows=padded_rows(
                    [step_bias[layer][None], log_rate[layer][None], skip_gain[layer][None]], LANES
                ),
            )
        )
    current = tokens[0]
    grad = cotangent[0]
    kept = []
    for layer in range(layers):
        w = weights[layer]
        part, squares, saved = forward(current, w)
        last = layer == layers - 1
        if last:
            q = matmul(grad, w["out"])
            both = jnp.stack([squares, jnp.sum(q * saved["gn"], axis=1)])
            both = small_sum(both, "head")
            squares, along = both[0], both[1]
        else:
            squares = small_sum(squares, "head")
        scale = lax.rsqrt(squares / INNER + epsilon)

        def finish(rows, offset, scale=scale):
            return rows * lax.dynamic_slice_in_dim(scale, offset, rows.shape[0], 0)[:, None]

        branch = head_sum(part, finish)
        kept.append((saved, scale, branch))
        current = current + branch
    collected = [None] * layers
    for layer in reversed(range(layers)):
        w = weights[layer]
        saved, scale, branch = kept[layer]
        if layer < layers - 1:
            q = matmul(grad, w["out"])
            slope = jnp.sum(grad * branch, axis=1) * scale * scale / INNER
        else:
            slope = along * scale * scale * scale / INNER
        grad, collected[layer] = backward(grad, q, scale, slope, w, saved)
    stacked = [jnp.stack([entry[number] for entry in collected], axis=0) for number in range(14)]
    return (current[None], grad[None], *stacked)


def solution(mesh):
    placed = (
        P("dp", "seq", None),
        P("dp", "seq", None),
        P(),
        P(None, None, "head"),
        P(None, None, "head"),
        P(None, None, "head"),
        P(None, None, "head"),
        P(None, None, "head"),
        P(None, "head"),
        P(None, None, "head"),
        P(None, "head"),
        P(None, "head"),
        P(None, "head"),
        P(None, "head"),
        P(None, "head"),
        P(None, None, "head"),
    )
    return jax.shard_map(
        body,
        mesh=mesh,
        in_specs=placed,
        out_specs=(
            P("dp", "seq", None),
            P("dp", "seq", None),
            P(),
            P(None, "seq", "head"),
            P(None, "seq", "head"),
            P(None, "seq", "head"),
            P(None, "seq", "head"),
            P(None, None, "head"),
            P(None, "head"),
            P(None, None, "head"),
            P(None, "head"),
            P(None, "head"),
            P(None, "head"),
            P(None, "head"),
            P(None, "head"),
            P(None, "seq", "head"),
        ),
        check_vma=False,
    )
```

time: 2020 us -> 915 us (0.45)
  waiting for transfers between devices: 888 us -> 284 us
  local copies, waits for them, and re-layouts: 386 us -> 88.6 us
  matrix products: 383 us -> 150 us
  starting transfers between devices: 23.5 us -> 239 us
  other arithmetic: 186 us -> 72.1 us
  blocking collectives: 112 us -> 0 us
  Pallas kernels: 0 us -> 63.2 us
    reduce_scatter x12 -> x0, waiting for transfers between devices: 477 us -> none  [the longest x2 174 us: body(): lax.psum_scatter(grad_inner_weight, 'seq', scatter_dimension=0, tiled=True)]
    psum x4 -> x0, waiting for transfers between devices: 310 us -> none  [the longest x2 224 us: body(): branch = lax.psum(part, 'head')]
    ppermute x8 -> x134, waiting for transfers between devices: 15.9 us -> 284 us  [the longest x70 163 us: exchanged(): return lax.ppermute(value, axis, [(i, i ^ distance) for i in range(n)])]
    dot_general x84 -> x30, matrix products: 383 us -> 150 us  [matmul(): return lax.dot_general(left, right, (dims, ((), ())), precision=HIGH)]
    ppermute x8 -> x134, starting transfers between devices: 21.3 us -> 239 us  [the longest x24 110 us: line_scatter_sum(): got_up = lax.ppermute(up, axis, [(z, z + 1) for z in range(step)])]
    dynamic_update_slice x60 -> x0, local copies, waits for them, and re-layouts: 177 us -> none  [scan_local(): lax.scan(block_step, start, (split(values), split(steps), split(rates), s...]
    all_gather x4 -> x0, waiting for transfers between devices: 84.6 us -> none  [prefix(): gathered = jax.tree.map(lambda a: lax.all_gather(a, axis), part)]
    another operation x90 -> x0, local copies, waits for them, and re-layouts: 77.1 us -> none
  transfers between devices with their start and end apart: 28 -> 134, of which waited for: 18 -> 53; matrix products, arithmetic and copies ran while one was open for 13% -> 26% of each run, Pallas kernels for 0% -> 6%
where the time goes in v1:
time: 915 us; the launch traced here: 904 us
  waiting for transfers between devices  284 us (31%)
  starting transfers between devices  239 us (26%)
  matrix products  150 us (16%)
  local copies, waits for them, and re-layouts  88.6 us (10%)
  other arithmetic  72.1 us (8%)
  Pallas kernels  63.2 us (7%)
    ppermute x70, waiting for transfers between devices, exchanged(): return lax.ppermute(value, axis, [(i, i ^ distance) for i in range(n)])  163 us
    dot_general x30, matrix products, matmul(): return lax.dot_general(left, right, (dims, ((), ())), precision=HIGH)  150 us
    ppermute x24, starting transfers between devices, line_scatter_sum(): got_up = lax.ppermute(up, axis, [(z, z + 1) for z in range(step)])  110 us
    ppermute x24, waiting for transfers between devices, line_scatter_sum(): got_up = lax.ppermute(up, axis, [(z, z + 1) for z in range(step)])  82.1 us
    ppermute x70, starting transfers between devices, exchanged(): return lax.ppermute(value, axis, [(i, i ^ distance) for i in range(n)])  67.2 us
    pallas_call x14, Pallas kernels, call(): pl.pallas_call(kernel, out_shape=shapes, in_specs=[pl.BlockSpec(memory_sp...  63.2 us
    unnamed x538, local copies, waits for them, and re-layouts  43.6 us
    ppermute x12, waiting for transfers between devices, state_before(): lax.ppermute(decay * state + local, 'seq', [(source, target)])  22.3 us
  transfers between devices with their start and end apart: 134, of which 53 were waited for; matrix products, arithmetic and copies ran while one was open for 26% of the time, Pallas kernels for 6%

profile of v1, /device:TPU:0, one launch (start us, length us, event | category | flops | bytes accessed | tf_op | source)
XLA Modules:
  0.0 903.6 jit_solution(10209457416825771464)
XLA Ops:
  12.7 6.5 fusion.22.ip
  26.4 16.1 %collective-permute-done.4 = f32[10,128]{1,0:T(8,128)S(1)} collective-permute-done((f32[10,128]{1,0:T(8,128)S(1)}, f32[10,128]{1,0:T(8,128)S(1)}, u32[]{:S(2)}, u32[]{:S(2)}) %collective-permute-start.4) | collective-permute-done | bytes 5152 | tf_op jit(solution)/shard_map/ppermute | solution.py:27
  62.6 5.4 collective-permute-done.5
  71.4 6.5 fusion.18.gate
  89.4 7.1 fusion.14
  100.6 11.7 %collective-permute-done.10 = f32[512]{0:T(512)S(1)} collective-permute-done((f32[512]{0:T(512)S(1)}, f32[512]{0:T(512)S(1)}, u32[]{:S(2)}, u32[]{:S(2)}) %collective-permute-start.10) | collective-permute-done | bytes 2080 | tf_op jit(solution)/shard_map/ppermute | solution.py:27
  119.4 15.1 %collective-permute-done.14 = f32[128,1536]{1,0:T(8,128)S(1)} collective-permute-done((f32[128,1536]{1,0:T(8,128)S(1)}, f32[128,1536]{1,0:T(8,128)S(1)}, u32[]{:S(2)}, u32[]{:S(2)}) %collective-permute-start.14) | collective-permute-done | bytes 786464 | tf_op jit(solution)/shard_map/ppermute | solution.py:27
  149.6 7.6 collective-permute-done.16
  160.1 7.6 collective-permute-done.13
  180.4 10.9 %collective-permute-start.20 = (f32[8,1024]{1,0:T(8,128)S(1)}, f32[8,1024]{1,0:T(8,128)S(1)}, u32[]{:S(2)}, u32[]{:S(2)}) collective-permute-start(f32[8,1024]{1,0:T(8,128)S(1)} %pad_maximum_fusion.17), channel_id=1, source_target_pairs={{0,4},{4,8},{8,12},{1,5},{5,9},{9,13},{2,6},{6,10},{10,14},{3,7},{... | collective-permute-start | bytes 98312 | tf_op jit(solution)/shard_map/ppermute | solution.py:33
  207.3 5.3 collective-permute-done.21
  218.6 8.7 fusion.6.gate
  232.3 7.4 fusion.2
  239.7 7.5 multiply_reduce_fusion.3
  274.7 8.1 fusion.4
  286.7 7.6 shard_map.286
  297.6 5.8 fusion.62
  324.2 11.6 %collective-permute-done.36 = f32[128,768]{1,0:T(8,128)S(1)} collective-permute-done((f32[128,768]{1,0:T(8,128)S(1)}, f32[128,768]{1,0:T(8,128)S(1)}, u32[]{:S(2)}, u32[]{:S(2)}) %collective-permute-start.36) | collective-permute-done | bytes 393248 | tf_op jit(solution)/shard_map/ppermute | solution.py:119
  336.0 10.3 %shard_map.287 = (f32[512,768]{1,0:T(8,128)S(1)}, f32[512,256]{1,0:T(8,128)S(1)}, f32[512,128]{1,0:T(8,128)S(1)}, f32[24,768]{1,0:T(8,128)S(1)}) custom-call(f32[512,768]{1,0:T(8,128)S(1)} %copy-done.56, f32[512,768]{1,0:T(8,128)S(1)} %copy-done.50, f32[512,768]{1,0:T(8,128)S(1)} %copy-done.8, f32[512,256]{1,0:T(8,128)S(1)} %copy-done.18, ...), custom_call_target="tpu_custom_call" | custom-call | flops 603979776 | bytes 18345984 | tf_op jit(solution)/shard_map/pallas_call | solution.py:126
  354.9 6.8 fusion.39
  370.9 5.8 fusion.94
  415.0 6.8 collective-permute-done.109
  428.6 19.6 %collective-permute-done.110 = f32[512,64]{1,0:T(8,128)S(1)} collective-permute-done((f32[512,64]{1,0:T(8,128)S(1)}, f32[512,64]{1,0:T(8,128)S(1)}, u32[]{:S(2)}, u32[]{:S(2)}) %collective-permute-start.110) | collective-permute-done | bytes 131104 | tf_op jit(solution)/shard_map/ppermute | solution.py:27
  472.4 8.8 collective-permute-start.114
  498.2 9.1 %collective-permute-done.40 = f32[64,1536]{1,0:T(8,128)S(1)} collective-permute-done((f32[64,1536]{1,0:T(8,128)S(1)}, f32[64,1536]{1,0:T(8,128)S(1)}, u32[]{:S(2)}, u32[]{:S(2)}) %collective-permute-start.40) | collective-permute-done | bytes 393248 | tf_op jit(solution)/shard_map/ppermute | solution.py:27
  507.9 9.2 %collective-permute-done.44 = f32[64,1536]{1,0:T(8,128)S(1)} collective-permute-done((f32[64,1536]{1,0:T(8,128)S(1)}, f32[64,1536]{1,0:T(8,128)S(1)}, u32[]{:S(2)}, u32[]{:S(2)}) %collective-permute-start.44) | collective-permute-done | bytes 393248 | tf_op jit(solution)/shard_map/ppermute | solution.py:27
  525.8 7.9 collective-permute-done.128
  536.1 8.5 collective-permute-done.78
  544.5 5.2 collective-permute-start.129
  552.3 5.4 collective-permute-start.79
  565.6 8.5 fusion.12.q
  580.5 8.1 fusion.16
  595.0 7.5 shard_map.290
  605.2 8.0 collective-permute-start.93
  633.8 7.5 collective-permute-done.94
  642.5 8.6 collective-permute-start.95
  653.0 10.2 %shard_map.291 = (f32[512,768]{1,0:T(8,128)S(1)}, f32[512,256]{1,0:T(8,128)S(1)}, f32[512,128]{1,0:T(8,128)S(1)}, f32[24,768]{1,0:T(8,128)S(1)}) custom-call(f32[512,768]{1,0:T(8,128)S(1)} %copy-done.54, f32[512,768]{1,0:T(8,128)S(1)} %copy-done.43, f32[512,768]{1,0:T(8,128)S(1)} %copy-done.4, f32[512,256]{1,0:T(8,128)S(1)} %copy-done.13, ...), custom_call_target="tpu_custom_call" | custom-call | flops 603979776 | bytes 18345984 | tf_op jit(solution)/shard_map/pallas_call | solution.py:126
  674.7 7.4 fusion.36
  692.6 5.8 fusion.97
  728.5 8.4 collective-permute-done.50
  756.8 6.4 collective-permute-start.105
  778.2 5.7 collective-permute-done.52
  784.4 7.3 collective-permute-done.56
  804.8 7.2 collective-permute-done.120
  813.7 7.3 collective-permute-done.70
  841.1 18.8 %collective-permute-done.85 = f32[384,384]{0,1:T(8,128)S(1)} collective-permute-done((f32[384,384]{0,1:T(8,128)S(1)}, f32[384,384]{0,1:T(8,128)S(1)}, u32[]{:S(2)}, u32[]{:S(2)}) %collective-permute-start.85) | collective-permute-done | bytes 589856 | tf_op jit(solution)/shard_map/ppermute | solution.py:104
  874.0 6.5 collective-permute-start.87
  888.9 5.7 collective-permute-done.90
  (1084 shorter events, 493.1 us)
Async XLA Ops:
  99.0 60.9 %collective-permute-start.19 = (f32[1536,128]{0,1:T(8,128)S(1)}, f32[1536,128]{0,1:T(8,128)S(1)}, u32[]{:S(2)}, u32[]{:S(2)}) collective-permute-start(f32[1536,128]{0,1:T(8,128)S(1)} %pad_maximum_fusion.7), channel_id=1, source_target_pairs={{0,2},{1,3},{2,0},{3,1},{4,6},{5,7},{6,4},{7,5},{8,10},{9,11},{10,... | collective-permute-start | bytes 2359304 | tf_op jit(solution)/shard_map/ppermute | solution.py:27
  116.8 23.1 %collective-permute-start.9 = (f32[64,1536]{1,0:T(8,128)S(1)}, f32[64,1536]{1,0:T(8,128)S(1)}, u32[]{:S(2)}, u32[]{:S(2)}) collective-permute-start(f32[64,1536]{1,0:T(8,128)S(1)} %constant_dynamic-slice_fusion.38), channel_id=1, source_target_pairs={{0,2},{1,3},{2,0},{3,1},{4,6},{5,7},{6,4},{7,5},{8,10},{9,11},{10,... | collective-permute-start | bytes 1179656 | tf_op jit(solution)/shard_map/ppermute | solution.py:27
  250.0 55.3 %collective-permute-start.24 = (f32[128,1536]{1,0:T(8,128)}, f32[128,1536]{1,0:T(8,128)}, u32[]{:S(2)}, u32[]{:S(2)}) collective-permute-start(f32[128,1536]{1,0:T(8,128)} %constant_dynamic-slice_fusion.35), channel_id=1, source_target_pairs={{0,1},{1,0},{2,3},{3,2},{4,5},{5,4},{6,7},{7,6},{8,9},{9,8},{10,11... | collective-permute-start | bytes 2359304 | tf_op jit(solution)/shard_map/ppermute | solution.py:27
  253.9 55.0 %collective-permute-start.30 = (f32[128,1536]{1,0:T(8,128)}, f32[128,1536]{1,0:T(8,128)}, u32[]{:S(2)}, u32[]{:S(2)}) collective-permute-start(f32[128,1536]{1,0:T(8,128)} %constant_dynamic-slice_fusion.32), channel_id=1, source_target_pairs={{0,2},{1,3},{2,0},{3,1},{4,6},{5,7},{6,4},{7,5},{8,10},{9,11},{10,... | collective-permute-start | bytes 2359304 | tf_op jit(solution)/shard_map/ppermute | solution.py:27
  272.0 31.5 %collective-permute-start.34 = (f32[128,768]{1,0:T(8,128)}, f32[128,768]{1,0:T(8,128)}, u32[]{:S(2)}, u32[]{:S(2)}) collective-permute-start(f32[128,768]{1,0:T(8,128)} %broadcast_add_fusion), channel_id=1, source_target_pairs={{12,8},{13,9},{14,10},{15,11},{28,24},{29,25},{30,26},{31,27}} | collective-permute-start | bytes 1179656 | tf_op jit(solution)/shard_map/ppermute | solution.py:119
  286.6 185.8 %collective-permute-start.76 = (f32[1536,384]{0,1:T(8,128)}, f32[1536,384]{0,1:T(8,128)}, u32[]{:S(2)}, u32[]{:S(2)}) collective-permute-start(f32[1536,384]{0,1:T(8,128)} %fusion.100), channel_id=1, source_target_pairs={{0,16},{16,0},{1,17},{17,1},{2,18},{18,2},{3,19},{19,3},{4,20},{20... | collective-permute-start | bytes 7077896 | tf_op jit(solution)/shard_map/ppermute | solution.py:27
  313.3 22.5 %collective-permute-start.36 = (f32[128,768]{1,0:T(8,128)S(1)}, f32[128,768]{1,0:T(8,128)S(1)}, u32[]{:S(2)}, u32[]{:S(2)}) collective-permute-start(f32[128,768]{1,0:T(8,128)S(1)} %get-tuple-element.216), channel_id=1, source_target_pairs={{4,0},{5,1},{6,2},{7,3},{20,16},{21,17},{22,18},{23,19}} | collective-permute-start | bytes 1179656 | tf_op jit(solution)/shard_map/ppermute | solution.py:119
  319.6 104.0 %collective-permute-start.28 = (f32[64,1536]{1,0:T(8,128)}, f32[64,1536]{1,0:T(8,128)}, u32[]{:S(2)}, u32[]{:S(2)}) collective-permute-start(f32[64,1536]{1,0:T(8,128)} %add_multiply_fusion.5), channel_id=1, source_target_pairs={{0,2},{1,3},{2,0},{3,1},{4,6},{5,7},{6,4},{7,5},{8,10},{9,11},{10,... | collective-permute-start | bytes 1179656 | tf_op jit(solution)/shard_map/ppermute | solution.py:27
  322.7 103.8 %collective-permute-start.32 = (f32[64,1536]{1,0:T(8,128)}, f32[64,1536]{1,0:T(8,128)}, u32[]{:S(2)}, u32[]{:S(2)}) collective-permute-start(f32[64,1536]{1,0:T(8,128)} %add_multiply_fusion.4), channel_id=1, source_target_pairs={{0,1},{1,0},{2,3},{3,2},{4,5},{5,4},{6,7},{7,6},{8,9},{9,8},{10,11... | collective-permute-start | bytes 1179656 | tf_op jit(solution)/shard_map/ppermute | solution.py:27
  396.8 54.6 %collective-permute-start.42 = (f32[128,1536]{1,0:T(8,128)}, f32[128,1536]{1,0:T(8,128)}, u32[]{:S(2)}, u32[]{:S(2)}) collective-permute-start(f32[128,1536]{1,0:T(8,128)} %constant_dynamic-slice_fusion.27), channel_id=1, source_target_pairs={{0,2},{1,3},{2,0},{3,1},{4,6},{5,7},{6,4},{7,5},{8,10},{9,11},{10,... | collective-permute-start | bytes 2359304 | tf_op jit(solution)/shard_map/ppermute | solution.py:27
  421.8 31.0 %collective-permute-start.38 = (f32[128,1536]{1,0:T(8,128)}, f32[128,1536]{1,0:T(8,128)S(1)}, u32[]{:S(2)}, u32[]{:S(2)}) collective-permute-start(f32[128,1536]{1,0:T(8,128)} %constant_dynamic-slice_fusion.29), channel_id=1, source_target_pairs={{0,1},{1,0},{2,3},{3,2},{4,5},{5,4},{6,7},{7,6},{8,9},{9,8},{10,11... | collective-permute-start | bytes 2359304 | tf_op jit(solution)/shard_map/ppermute | solution.py:27
  423.6 24.6 %collective-permute-start.110 = (f32[512,64]{1,0:T(8,128)S(1)}, f32[512,64]{1,0:T(8,128)S(1)}, u32[]{:S(2)}, u32[]{:S(2)}) collective-permute-start(f32[512,64]{1,0:T(8,128)S(1)} %constant_dynamic-slice_fusion.8), channel_id=1, source_target_pairs={{0,1},{1,0},{2,3},{3,2},{4,5},{5,4},{6,7},{7,6},{8,9},{9,8},{10,11... | collective-permute-start | bytes 393224 | tf_op jit(solution)/shard_map/ppermute | solution.py:27
  426.4 41.0 %collective-permute-start.29 = (f32[128,1536]{1,0:T(8,128)S(1)}, f32[128,1536]{1,0:T(8,128)S(1)}, u32[]{:S(2)}, u32[]{:S(2)}) collective-permute-start(f32[128,1536]{1,0:T(8,128)S(1)} %pad_maximum_fusion.8), channel_id=1, source_target_pairs={{0,1},{1,0},{2,3},{3,2},{4,5},{5,4},{6,7},{7,6},{8,9},{9,8},{10,11... | collective-permute-start | bytes 2359304 | tf_op jit(solution)/shard_map/ppermute | solution.py:27
  466.9 85.4 %collective-permute-start.92 = (f32[1536,384]{0,1:T(8,128)S(1)}, f32[1536,384]{0,1:T(8,128)S(1)}, u32[]{:S(2)}, u32[]{:S(2)}) collective-permute-start(f32[1536,384]{0,1:T(8,128)S(1)} %copy-done.200), channel_id=1, source_target_pairs={{0,16},{16,0},{1,17},{17,1},{2,18},{18,2},{3,19},{19,3},{4,20},{20... | collective-permute-start | bytes 7077896 | tf_op jit(solution)/shard_map/ppermute | solution.py:27
  467.5 21.9 %collective-permute-start.43 = (f32[64,1536]{1,0:T(8,128)S(1)}, f32[64,1536]{1,0:T(8,128)S(1)}, u32[]{:S(2)}, u32[]{:S(2)}) collective-permute-start(f32[64,1536]{1,0:T(8,128)S(1)} %constant_dynamic-slice_fusion.26), channel_id=1, source_target_pairs={{0,1},{1,0},{2,3},{3,2},{4,5},{5,4},{6,7},{7,6},{8,9},{9,8},{10,11... | collective-permute-start | bytes 1179656 | tf_op jit(solution)/shard_map/ppermute | solution.py:27
  468.2 25.8 %collective-permute-start.39 = (f32[64,1536]{1,0:T(8,128)S(1)}, f32[64,1536]{1,0:T(8,128)S(1)}, u32[]{:S(2)}, u32[]{:S(2)}) collective-permute-start(f32[64,1536]{1,0:T(8,128)S(1)} %constant_dynamic-slice_fusion.28), channel_id=1, source_target_pairs={{0,2},{1,3},{2,0},{3,1},{4,6},{5,7},{6,4},{7,5},{8,10},{9,11},{10,... | collective-permute-start | bytes 1179656 | tf_op jit(solution)/shard_map/ppermute | solution.py:27
  472.4 22.8 %collective-permute-start.114 = (f32[384,76]{0,1:T(8,128)S(1)}, f32[384,76]{0,1:T(8,128)S(1)}, u32[]{:S(2)}, u32[]{:S(2)}) collective-permute-start(f32[384,76]{0,1:T(8,128)S(1)} %get-tuple-element.337), channel_id=1, source_target_pairs={{0,4},{4,8},{8,12},{1,5},{5,9},{9,13},{2,6},{6,10},{10,14},{3,7},{... | collective-permute-start | bytes 350216 | tf_op jit(solution)/shard_map/ppermute | solution.py:104
  489.4 28.5 %collective-permute-start.127 = (f32[384,384]{0,1:T(8,128)S(1)}, f32[384,384]{0,1:T(8,128)S(1)}, u32[]{:S(2)}, u32[]{:S(2)}) collective-permute-start(f32[384,384]{0,1:T(8,128)S(1)} %get-tuple-element.249), channel_id=1, source_target_pairs={{0,4},{1,5},{2,6},{3,7},{16,20},{17,21},{18,22},{19,23}} | collective-permute-start | bytes 1769480 | tf_op jit(solution)/shard_map/ppermute | solution.py:104
  494.0 23.9 %collective-permute-start.130 = (f32[384,384]{0,1:T(8,128)S(1)}, f32[384,384]{0,1:T(8,128)S(1)}, u32[]{:S(2)}, u32[]{:S(2)}) collective-permute-start(f32[384,384]{0,1:T(8,128)S(1)} %get-tuple-element.248), channel_id=1, source_target_pairs={{12,8},{13,9},{14,10},{15,11},{28,24},{29,25},{30,26},{31,27}} | collective-permute-start | bytes 1769480 | tf_op jit(solution)/shard_map/ppermute | solution.py:105
  495.2 25.5 %collective-permute-start.77 = (f32[384,384]{0,1:T(8,128)S(1)}, f32[384,384]{0,1:T(8,128)S(1)}, u32[]{:S(2)}, u32[]{:S(2)}) collective-permute-start(f32[384,384]{0,1:T(8,128)S(1)} %get-tuple-element.273), channel_id=1, source_target_pairs={{0,4},{1,5},{2,6},{3,7},{16,20},{17,21},{18,22},{19,23}} | collective-permute-start | bytes 1769480 | tf_op jit(solution)/shard_map/ppermute | solution.py:104
  520.9 23.7 %collective-permute-start.78 = (f32[384,384]{0,1:T(8,128)S(1)}, f32[384,384]{0,1:T(8,128)S(1)}, u32[]{:S(2)}, u32[]{:S(2)}) collective-permute-start(f32[384,384]{0,1:T(8,128)S(1)} %get-tuple-element.271), channel_id=1, source_target_pairs={{0,4},{4,8},{1,5},{5,9},{2,6},{6,10},{3,7},{7,11},{16,20},{20,24},... | collective-permute-start | bytes 1769480 | tf_op jit(solution)/shard_map/ppermute | solution.py:104
  524.9 24.9 %collective-permute-start.81 = (f32[384,384]{0,1:T(8,128)S(1)}, f32[384,384]{0,1:T(8,128)S(1)}, u32[]{:S(2)}, u32[]{:S(2)}) collective-permute-start(f32[384,384]{0,1:T(8,128)S(1)} %get-tuple-element.270), channel_id=1, source_target_pairs={{12,8},{8,4},{13,9},{9,5},{14,10},{10,6},{15,11},{11,7},{28,24},{2... | collective-permute-start | bytes 1769480 | tf_op jit(solution)/shard_map/ppermute | solution.py:105
  533.7 27.8 %collective-permute-start.41 = (f32[128,1536]{1,0:T(8,128)S(1)}, f32[128,1536]{1,0:T(8,128)S(1)}, u32[]{:S(2)}, u32[]{:S(2)}) collective-permute-start(f32[128,1536]{1,0:T(8,128)S(1)} %pad_maximum_fusion.10), channel_id=1, source_target_pairs={{0,1},{1,0},{2,3},{3,2},{4,5},{5,4},{6,7},{7,6},{8,9},{9,8},{10,11... | collective-permute-start | bytes 2359304 | tf_op jit(solution)/shard_map/ppermute | solution.py:27
  534.2 28.9 %collective-permute-start.45 = (f32[128,1536]{1,0:T(8,128)S(1)}, f32[128,1536]{1,0:T(8,128)S(1)}, u32[]{:S(2)}, u32[]{:S(2)}) collective-permute-start(f32[128,1536]{1,0:T(8,128)S(1)} %pad_maximum_fusion.11), channel_id=1, source_target_pairs={{0,2},{1,3},{2,0},{3,1},{4,6},{5,7},{6,4},{7,5},{8,10},{9,11},{10,... | collective-permute-start | bytes 2359304 | tf_op jit(solution)/shard_map/ppermute | solution.py:27
  544.5 68.7 %collective-permute-start.129 = (f32[384,384]{0,1:T(8,128)}, f32[384,384]{0,1:T(8,128)}, u32[]{:S(2)}, u32[]{:S(2)}) collective-permute-start(f32[384,384]{0,1:T(8,128)} %get-tuple-element.245), channel_id=1, source_target_pairs={{0,4},{4,8},{8,12},{1,5},{5,9},{9,13},{2,6},{6,10},{10,14},{3,7},{... | collective-permute-start | bytes 1769480 | tf_op jit(solution)/shard_map/ppermute | solution.py:104
  549.8 65.3 %collective-permute-start.132 = (f32[384,384]{0,1:T(8,128)}, f32[384,384]{0,1:T(8,128)}, u32[]{:S(2)}, u32[]{:S(2)}) collective-permute-start(f32[384,384]{0,1:T(8,128)} %get-tuple-element.244), channel_id=1, source_target_pairs={{12,8},{8,4},{4,0},{13,9},{9,5},{5,1},{14,10},{10,6},{6,2},{15,11}... | collective-permute-start | bytes 1769480 | tf_op jit(solution)/shard_map/ppermute | solution.py:105
  552.3 64.4 %collective-permute-start.79 = (f32[384,384]{0,1:T(8,128)}, f32[384,384]{0,1:T(8,128)}, u32[]{:S(2)}, u32[]{:S(2)}) collective-permute-start(f32[384,384]{0,1:T(8,128)} %get-tuple-element.269), channel_id=1, source_target_pairs={{0,4},{4,8},{8,12},{1,5},{5,9},{9,13},{2,6},{6,10},{10,14},{3,7},{... | collective-permute-start | bytes 1769480 | tf_op jit(solution)/shard_map/ppermute | solution.py:104
  561.5 56.1 %collective-permute-start.82 = (f32[384,384]{0,1:T(8,128)}, f32[384,384]{0,1:T(8,128)}, u32[]{:S(2)}, u32[]{:S(2)}) collective-permute-start(f32[384,384]{0,1:T(8,128)} %get-tuple-element.268), channel_id=1, source_target_pairs={{12,8},{8,4},{4,0},{13,9},{9,5},{5,1},{14,10},{10,6},{6,2},{15,11}... | collective-permute-start | bytes 1769480 | tf_op jit(solution)/shard_map/ppermute | solution.py:105
  615.1 136.5 %collective-permute-start.118 = (f32[1536,384]{0,1:T(8,128)}, f32[1536,384]{0,1:T(8,128)}, u32[]{:S(2)}, u32[]{:S(2)}) collective-permute-start(f32[1536,384]{0,1:T(8,128)} %fusion.91), channel_id=1, source_target_pairs={{0,16},{16,0},{1,17},{17,1},{2,18},{18,2},{3,19},{19,3},{4,20},{20... | collective-permute-start | bytes 7077896 | tf_op jit(solution)/shard_map/ppermute | solution.py:27
  629.9 22.9 %collective-permute-start.48 = (f32[128,768]{1,0:T(8,128)S(1)}, f32[128,768]{1,0:T(8,128)S(1)}, u32[]{:S(2)}, u32[]{:S(2)}) collective-permute-start(f32[128,768]{1,0:T(8,128)S(1)} %get-tuple-element.210), channel_id=1, source_target_pairs={{4,0},{5,1},{6,2},{7,3},{20,16},{21,17},{22,18},{23,19}} | collective-permute-start | bytes 1179656 | tf_op jit(solution)/shard_map/ppermute | solution.py:119
  642.5 82.3 %collective-permute-start.95 = (f32[384,384]{0,1:T(8,128)}, f32[384,384]{0,1:T(8,128)}, u32[]{:S(2)}, u32[]{:S(2)}) collective-permute-start(f32[384,384]{0,1:T(8,128)} %get-tuple-element.257), channel_id=1, source_target_pairs={{0,4},{4,8},{8,12},{1,5},{5,9},{9,13},{2,6},{6,10},{10,14},{3,7},{... | collective-permute-start | bytes 1769480 | tf_op jit(solution)/shard_map/ppermute | solution.py:104
  651.1 73.8 %collective-permute-start.98 = (f32[384,384]{0,1:T(8,128)}, f32[384,384]{0,1:T(8,128)}, u32[]{:S(2)}, u32[]{:S(2)}) collective-permute-start(f32[384,384]{0,1:T(8,128)} %get-tuple-element.256), channel_id=1, source_target_pairs={{12,8},{8,4},{4,0},{13,9},{9,5},{5,1},{14,10},{10,6},{6,2},{15,11}... | collective-permute-start | bytes 1769480 | tf_op jit(solution)/shard_map/ppermute | solution.py:105
  685.5 27.3 %collective-permute-start.100 = (f32[512,128]{1,0:T(8,128)}, f32[512,128]{1,0:T(8,128)S(1)}, u32[]{:S(2)}, u32[]{:S(2)}) collective-permute-start(f32[512,128]{1,0:T(8,128)} %constant_dynamic-slice_fusion.13), channel_id=1, source_target_pairs={{0,2},{1,3},{2,0},{3,1},{4,6},{5,7},{6,4},{7,5},{8,10},{9,11},{10,... | collective-permute-start | bytes 786440 | tf_op jit(solution)/shard_map/ppermute | solution.py:27
  724.8 32.0 %collective-permute-start.68 = (f32[1536,384]{0,1:T(8,128)S(1)}, f32[1536,384]{0,1:T(8,128)S(1)}, u32[]{:S(2)}, u32[]{:S(2)}) collective-permute-start(f32[1536,384]{0,1:T(8,128)S(1)} %copy-done.199), channel_id=1, source_target_pairs={{0,16},{16,0},{1,17},{17,1},{2,18},{18,2},{3,19},{19,3},{4,20},{20... | collective-permute-start | bytes 7077896 | tf_op jit(solution)/shard_map/ppermute | solution.py:27
  724.9 102.0 %collective-permute-start.84 = (f32[1536,384]{0,1:T(8,128)S(1)}, f32[1536,384]{0,1:T(8,128)S(1)}, u32[]{:S(2)}, u32[]{:S(2)}) collective-permute-start(f32[1536,384]{0,1:T(8,128)S(1)} %copy-done.201), channel_id=1, source_target_pairs={{0,16},{16,0},{1,17},{17,1},{2,18},{18,2},{3,19},{19,3},{4,20},{20... | collective-permute-start | bytes 7077896 | tf_op jit(solution)/shard_map/ppermute | solution.py:27
  751.6 21.4 %collective-permute-start.51 = (f32[64,1536]{1,0:T(8,128)S(1)}, f32[64,1536]{1,0:T(8,128)S(1)}, u32[]{:S(2)}, u32[]{:S(2)}) collective-permute-start(f32[64,1536]{1,0:T(8,128)S(1)} %constant_dynamic-slice_fusion.24), channel_id=1, source_target_pairs={{0,2},{1,3},{2,0},{3,1},{4,6},{5,7},{6,4},{7,5},{8,10},{9,11},{10,... | collective-permute-start | bytes 1179656 | tf_op jit(solution)/shard_map/ppermute | solution.py:27
  768.3 24.2 %collective-permute-start.119 = (f32[384,384]{0,1:T(8,128)S(1)}, f32[384,384]{0,1:T(8,128)S(1)}, u32[]{:S(2)}, u32[]{:S(2)}) collective-permute-start(f32[384,384]{0,1:T(8,128)S(1)} %get-tuple-element.243), channel_id=1, source_target_pairs={{0,4},{1,5},{2,6},{3,7},{16,20},{17,21},{18,22},{19,23}} | collective-permute-start | bytes 1769480 | tf_op jit(solution)/shard_map/ppermute | solution.py:104
  774.3 25.0 %collective-permute-start.69 = (f32[384,384]{0,1:T(8,128)S(1)}, f32[384,384]{0,1:T(8,128)S(1)}, u32[]{:S(2)}, u32[]{:S(2)}) collective-permute-start(f32[384,384]{0,1:T(8,128)S(1)} %get-tuple-element.267), channel_id=1, source_target_pairs={{0,4},{1,5},{2,6},{3,7},{16,20},{17,21},{18,22},{19,23}} | collective-permute-start | bytes 1769480 | tf_op jit(solution)/shard_map/ppermute | solution.py:104
  799.5 21.5 %collective-permute-start.70 = (f32[384,384]{0,1:T(8,128)S(1)}, f32[384,384]{0,1:T(8,128)S(1)}, u32[]{:S(2)}, u32[]{:S(2)}) collective-permute-start(f32[384,384]{0,1:T(8,128)S(1)} %get-tuple-element.265), channel_id=1, source_target_pairs={{0,4},{4,8},{1,5},{5,9},{2,6},{6,10},{3,7},{7,11},{16,20},{20,24},... | collective-permute-start | bytes 1769480 | tf_op jit(solution)/shard_map/ppermute | solution.py:104
  804.0 21.5 %collective-permute-start.73 = (f32[384,384]{0,1:T(8,128)S(1)}, f32[384,384]{0,1:T(8,128)S(1)}, u32[]{:S(2)}, u32[]{:S(2)}) collective-permute-start(f32[384,384]{0,1:T(8,128)S(1)} %get-tuple-element.264), channel_id=1, source_target_pairs={{12,8},{8,4},{13,9},{9,5},{14,10},{10,6},{15,11},{11,7},{28,24},{2... | collective-permute-start | bytes 1769480 | tf_op jit(solution)/shard_map/ppermute | solution.py:105
  812.0 22.4 %collective-permute-start.53 = (f32[128,1536]{1,0:T(8,128)S(1)}, f32[128,1536]{1,0:T(8,128)S(1)}, u32[]{:S(2)}, u32[]{:S(2)}) collective-permute-start(f32[128,1536]{1,0:T(8,128)S(1)} %pad_maximum_fusion.12), channel_id=1, source_target_pairs={{0,1},{1,0},{2,3},{3,2},{4,5},{5,4},{6,7},{7,6},{8,9},{9,8},{10,11... | collective-permute-start | bytes 2359304 | tf_op jit(solution)/shard_map/ppermute | solution.py:27
  812.7 26.1 %collective-permute-start.57 = (f32[128,1536]{1,0:T(8,128)S(1)}, f32[128,1536]{1,0:T(8,128)S(1)}, u32[]{:S(2)}, u32[]{:S(2)}) collective-permute-start(f32[128,1536]{1,0:T(8,128)S(1)} %pad_maximum_fusion.13), channel_id=1, source_target_pairs={{0,2},{1,3},{2,0},{3,1},{4,6},{5,7},{6,4},{7,5},{8,10},{9,11},{10,... | collective-permute-start | bytes 2359304 | tf_op jit(solution)/shard_map/ppermute | solution.py:27
  826.9 40.5 %collective-permute-start.71 = (f32[384,384]{0,1:T(8,128)S(1)}, f32[384,384]{0,1:T(8,128)S(1)}, u32[]{:S(2)}, u32[]{:S(2)}) collective-permute-start(f32[384,384]{0,1:T(8,128)S(1)} %get-tuple-element.263), channel_id=1, source_target_pairs={{0,4},{4,8},{8,12},{1,5},{5,9},{9,13},{2,6},{6,10},{10,14},{3,7},{... | collective-permute-start | bytes 1769480 | tf_op jit(solution)/shard_map/ppermute | solution.py:104
  834.3 25.5 %collective-permute-start.85 = (f32[384,384]{0,1:T(8,128)S(1)}, f32[384,384]{0,1:T(8,128)S(1)}, u32[]{:S(2)}, u32[]{:S(2)}) collective-permute-start(f32[384,384]{0,1:T(8,128)S(1)} %get-tuple-element.255), channel_id=1, source_target_pairs={{0,4},{1,5},{2,6},{3,7},{16,20},{17,21},{18,22},{19,23}} | collective-permute-start | bytes 1769480 | tf_op jit(solution)/shard_map/ppermute | solution.py:104
  838.7 21.2 %collective-permute-start.88 = (f32[384,384]{0,1:T(8,128)S(1)}, f32[384,384]{0,1:T(8,128)S(1)}, u32[]{:S(2)}, u32[]{:S(2)}) collective-permute-start(f32[384,384]{0,1:T(8,128)S(1)} %get-tuple-element.254), channel_id=1, source_target_pairs={{12,8},{13,9},{14,10},{15,11},{28,24},{29,25},{30,26},{31,27}} | collective-permute-start | bytes 1769480 | tf_op jit(solution)/shard_map/ppermute | solution.py:105
  839.6 27.9 %collective-permute-start.74 = (f32[384,384]{0,1:T(8,128)S(1)}, f32[384,384]{0,1:T(8,128)S(1)}, u32[]{:S(2)}, u32[]{:S(2)}) collective-permute-start(f32[384,384]{0,1:T(8,128)S(1)} %get-tuple-element.262), channel_id=1, source_target_pairs={{12,8},{8,4},{4,0},{13,9},{9,5},{5,1},{14,10},{10,6},{6,2},{15,11}... | collective-permute-start | bytes 1769480 | tf_op jit(solution)/shard_map/ppermute | solution.py:105
  841.0 40.8 %collective-permute-start.125 = (f32[384,384]{0,1:T(8,128)S(1)}, f32[384,384]{0,1:T(8,128)S(1)}, u32[]{:S(2)}, u32[]{:S(2)}) collective-permute-start(f32[384,384]{0,1:T(8,128)S(1)} %dynamic-slice_add_fusion.13), channel_id=1, source_target_pairs={{0,16},{16,0},{1,17},{17,1},{2,18},{18,2},{3,19},{19,3},{4,20},{20... | collective-permute-start | bytes 1769480 | tf_op jit(solution)/shard_map/ppermute | solution.py:27
  867.6 28.7 %collective-permute-start.75 = (f32[384,384]{0,1:T(8,128)S(1)}, f32[384,384]{0,1:T(8,128)}, u32[]{:S(2)}, u32[]{:S(2)}) collective-permute-start(f32[384,384]{0,1:T(8,128)S(1)} %dynamic-slice_add_fusion.33), channel_id=1, source_target_pairs={{0,16},{16,0},{1,17},{17,1},{2,18},{18,2},{3,19},{19,3},{4,20},{20... | collective-permute-start | bytes 1769480 | tf_op jit(solution)/shard_map/ppermute | solution.py:27
  (349 other events, 3846.5 us)

commit v2 on v1

v2 whole, which is shorter than its diff:
```python
import functools

import jax
import jax.numpy as jnp
from jax import lax
from jax.experimental import pallas as pl
from jax.experimental.pallas import tpu as pltpu
from jax.sharding import PartitionSpec as P

INNER = 3072
CHUNK = 128
LANES = 128
PAD = 8
VMEM = 20 * 1024 * 1024
epsilon = 1e-05
HIGH = lax.Precision.HIGH
HIGHEST = lax.Precision.HIGHEST
NEG = -1e30
F32 = jnp.float32


def power_of_two(n):
    return n & (n - 1) == 0


def exchanged(value, axis, distance):
    n = lax.axis_size(axis)
    return lax.ppermute(value, axis, [(i, i ^ distance) for i in range(n)])


def shifted(value, axis, step):
    n = lax.axis_size(axis)
    pairs = [(i, i + step) for i in range(n) if 0 <= i + step < n]
    return lax.ppermute(value, axis, pairs)


def distances(axis):
    n = lax.axis_size(axis)
    return [1 << k for k in range(n.bit_length() - 1)]


def bit_of(axis, distance):
    return (lax.axis_index(axis) // distance) % 2


def small_sum(value, axis):
    if not power_of_two(lax.axis_size(axis)):
        return lax.psum(value, axis)
    for distance in distances(axis):
        value = value + exchanged(value, axis, distance)
    return value


def half(value, which, dim=0):
    size = value.shape[dim] // 2
    return lax.dynamic_slice_in_dim(value, which * size, size, dim)


def joined(mine, other, axis, distance, dim=0):
    first = bit_of(axis, distance) == 0
    return jnp.concatenate(
        [jnp.where(first, mine, other), jnp.where(first, other, mine)], axis=dim
    )


def gather_back(value, axis, order, dim=0):
    for distance in order[::-1]:
        value = joined(value, exchanged(value, axis, distance), axis, distance, dim)
    return value


def tied(value, *others):
    return lax.optimization_barrier((value, *others))


def head_sum(lefts, product, finish):
    order = distances("head")
    rows = lefts[0].shape[0] // 2
    ways = (order, order[::-1])

    def chosen(other):
        picked = []
        for array in lefts:
            pieces = []
            for number, way in enumerate(ways):
                bit = bit_of("head", way[0])
                part = array[number * rows : (number + 1) * rows]
                pieces.append(half(part, 1 - bit if other else bit))
            picked.append(jnp.concatenate(pieces, axis=0))
        return product(*picked)

    sent = chosen(True)
    kept = chosen(False)
    sent, kept = yield sent, kept
    size = rows // 2
    got = [
        exchanged(sent[number * size : (number + 1) * size], "head", way[0])
        for number, way in enumerate(ways)
    ]
    kept = [kept[:size], kept[size:]]
    offsets = [bit_of("head", way[0]) * size + number * rows for number, way in enumerate(ways)]
    got, kept = yield got, kept
    for step in range(1, len(order)):
        bits = [bit_of("head", way[step]) for way in ways]
        sends = [half(k, 1 - bit) + half(g, 1 - bit) for k, g, bit in zip(kept, got, bits)]
        arrived = [exchanged(send, "head", way[step]) for send, way in zip(sends, ways)]
        kept = [half(k, bit) + half(g, bit) for k, g, bit in zip(kept, got, bits)]
        offsets = [o + bit * k.shape[0] for o, bit, k in zip(offsets, bits, kept)]
        got, kept = yield arrived, kept
    mine = [finish(k + g, o) for k, g, o in zip(kept, got, offsets)]
    for step in range(len(order) - 1, -1, -1):
        others = [exchanged(m, "head", way[step]) for m, way in zip(mine, ways)]
        others, mine = yield others, mine
        mine = [joined(m, o, "head", way[step]) for m, o, way in zip(mine, others, ways)]
    return jnp.concatenate(mine, axis=0)


class Steps:
    def __init__(self, steps):
        self.steps = steps
        self.now = next(steps)
        self.result = None

    def advance(self, *others):
        if self.result is not None:
            return others
        if len(others) > 0:
            self.now, *others = tied(self.now, *others)
        try:
            self.now = self.steps.send(self.now)
        except StopIteration as end:
            self.result = end.value
        return others

    def finished(self):
        while self.result is None:
            self.advance()
        return self.result


def after(value, *others):
    return tied(value, *others)[0]


def state_before(local, decay, reverse, windows):
    n = lax.axis_size("seq")
    state = jnp.zeros_like(local)
    done = []
    before = local
    for hop in range(n - 1):
        source, target = (n - 1 - hop, n - 2 - hop) if reverse else (hop, hop + 1)
        got = lax.ppermute(decay * state + local, "seq", [(source, target)])
        if hop < len(windows):
            got, *result = tied(got, *windows[hop](before))
            done.append(result)
        before = got
        state = state + got
    for window in windows[n - 1 :]:
        done.append(window(before))
    return state, done


def rows_of(*shape):
    return pl.BlockSpec(shape, lambda c: (c,) + (0,) * (len(shape) - 1))


def columns_of(*shape):
    return pl.BlockSpec(shape, lambda c: (0, c))


def all_of(*shape):
    return pl.BlockSpec(shape, lambda c: (0,) * len(shape))


def reverse(spec, steps):
    index = spec.index_map
    return pl.BlockSpec(spec.block_shape, lambda c: index(steps - 1 - c))


def call(kernel, steps, outs, scratch, flops, *args, backward=False):
    shapes = [jax.ShapeDtypeStruct(shape, F32) for shape, _ in outs]
    size = 4 * sum(a.size for a, _ in args) + 4 * sum(s.size for s in shapes)

    def spec(blocks):
        return reverse(blocks, steps) if backward else blocks

    return pl.pallas_call(
        kernel,
        grid=(steps,),
        out_shape=shapes,
        in_specs=[spec(blocks) for _, blocks in args],
        out_specs=[spec(blocks) for _, blocks in outs],
        scratch_shapes=scratch,
        compiler_params=pltpu.CompilerParams(vmem_limit_bytes=VMEM),
        cost_estimate=pl.CostEstimate(flops=flops, bytes_accessed=size, transcendentals=0),
    )(*[a for a, _ in args])


def dot(left, right, dims=((1,), (0,)), precision=HIGH):
    return lax.dot_general(
        left, right, (dims, ((), ())), precision=precision, preferred_element_type=F32
    )


NT = ((1,), (1,))


def sigmoid(value):
    return 1.0 / (1.0 + jnp.exp(-value))


def spread_heads(columns, tile, width):
    each = LANES // width
    lane = lax.broadcasted_iota(jnp.int32, (columns.shape[0], LANES), 1)
    result = columns[:, tile * each : tile * each + 1]
    for k in range(1, each):
        result = jnp.where(lane < k * width, result, columns[:, tile * each + k : tile * each + k + 1])
    return jnp.broadcast_to(result, (columns.shape[0], LANES))


def head_rows(row, width, total):
    tiles = [spread_heads(row, tile, width) for tile in range(total // LANES)]
    return jnp.concatenate(tiles, axis=1)


def filter_tile(scratch, taps, start, rows, cols):
    block = scratch[pl.ds(start, rows + PAD), cols]
    total = taps[4:5, cols] + taps[3:4, cols] * block[PAD:]
    for back in range(1, 4):
        total = total + taps[3 - back : 4 - back, cols] * pltpu.roll(block, back, 0)[PAD:]
    return total


def start_kernel(
    width, ip, ib, sp, sb, ti, ts, hp, v_out, bc_out, dsi, dss, dt_out, cum_out, cumt_out, fresh, local, chdec, passed, padi, pads
):
    inner = ip.shape[1]
    states = ts.shape[1]
    n = states // 2
    c = pl.program_id(0)

    @pl.when(c == 0)
    def _():
        padi[0:PAD, :] = ib[...]
        pads[0:PAD, :] = sb[...]
        passed[...] = jnp.ones_like(passed)
        local[...] = jnp.zeros_like(local)

    @pl.when(c > 0)
    def _():
        padi[0:PAD, :] = padi[CHUNK:, :]
        pads[0:PAD, :] = pads[CHUNK:, :]

    padi[PAD:, :] = ip[...]
    pads[PAD:, :] = sp[:, :states]
    rows = 64

    def filtered(step, _):
        start = pl.multiple_of(step * rows, rows)
        for scratch, taps, out, slope, size in (
            (padi, ti, v_out, dsi, inner),
            (pads, ts, bc_out, dss, states),
        ):
            for tile in range(size // LANES):
                cols = slice(tile * LANES, (tile + 1) * LANES)
                total = filter_tile(scratch, taps, start, rows, cols)
                gate = sigmoid(total)
                value = total * gate
                out[pl.ds(start, rows), cols] = value
                slope[pl.ds(start, rows), cols] = gate + value * (1.0 - gate)
        return 0

    lax.fori_loop(0, CHUNK // rows, filtered, 0)
    raw = sp[:, states:] + hp[0:1, :]
    dt = jnp.maximum(raw, 0.0) + jnp.log1p(jnp.exp(-jnp.abs(raw)))
    dt_out[...] = dt
    rate = -jnp.exp(hp[1:2, :]) * dt
    ones = (
        lax.broadcasted_iota(jnp.int32, (CHUNK, CHUNK), 0)
        >= lax.broadcasted_iota(jnp.int32, (CHUNK, CHUNK), 1)
    ).astype(F32)
    cum = dot(ones, rate, precision=HIGHEST)
    cum_out[...] = cum
    cumt_out[...] = cum.T[: cumt_out.shape[0]]
    last = cum[CHUNK - 1 : CHUNK, :]
    weight = jnp.exp(last - cum) * dt
    maps = bc_out[:, :n].T
    decay = head_rows(jnp.exp(last), width, inner)
    chdec[0] = jnp.broadcast_to(decay, (PAD, inner))
    passed[...] = passed[...] * decay
    for tile in range(inner // LANES):
        cols = slice(tile * LANES, (tile + 1) * LANES)
        weighted = v_out[:, cols] * spread_heads(weight, tile, width)
        part = dot(maps, weighted)
        fresh[0, :, cols] = part
        local[:, cols] = decay[:, cols] * local[:, cols] + part


def inner_kernel(width, v, bc, dt, cum, cumt, hp, out):
    inner = v.shape[1]
    n = bc.shape[1] // 2
    each = LANES // width
    lane = lax.broadcasted_iota(jnp.int32, (CHUNK, LANES), 1)
    lower = lax.broadcasted_iota(jnp.int32, (CHUNK, CHUNK), 0) >= lax.broadcasted_iota(
        jnp.int32, (CHUNK, CHUNK), 1
    )
    meet = dot(bc[:, n:], bc[:, :n], NT)
    for tile in range(inner // LANES):
        cols = slice(tile * LANES, (tile + 1) * LANES)
        values = v[:, cols]
        stepped = values * spread_heads(dt[...], tile, width)
        result = None
        for k in range(each):
            head = tile * each + k
            spread = cum[:, head : head + 1] - cumt[head : head + 1, :]
            mixing = jnp.exp(jnp.where(lower, spread, NEG)) * meet
            part = dot(mixing, stepped)
            result = part if k == 0 else jnp.where(lane < k * width, result, part)
        out[:, cols] = result + spread_heads(hp[2:3, :], tile, width) * values


def gate_kernel(width, yd, bc, cum, fresh, chdec, entering, gate, gain, y_out, gn_out, states, squares, final):
    inner = yd.shape[1]
    n = bc.shape[1] // 2
    ones = jnp.ones((PAD, LANES), F32)
    c = pl.program_id(0)

    @pl.when(c == 0)
    def _():
        final[...] = entering[...]

    carried = jnp.exp(cum[...])
    maps = bc[:, n:]
    total = None
    for tile in range(inner // LANES):
        cols = slice(tile * LANES, (tile + 1) * LANES)
        state = final[:, cols]
        states[0, :, cols] = state
        final[:, cols] = chdec[0, 0:1, cols] * state + fresh[0, :, cols]
        y = yd[:, cols] + spread_heads(carried, tile, width) * dot(maps, state)
        y_out[:, cols] = y
        g = gate[:, cols]
        gated = y * (g * sigmoid(g))
        gn_out[:, cols] = gated * gain[0:1, cols]
        total = gated * gated if tile == 0 else total + gated * gated
    squares[...] = dot(ones, total, NT, HIGHEST)


def open_kernel(
    width, q, y, gate, gain, factors, bc, cum, chdec, dy_out, dgate, u_out, dgain, adjoint, local, passed
):
    inner = q.shape[1]
    n = bc.shape[1] // 2
    c = pl.program_id(0)

    @pl.when(c == 0)
    def _():
        dgain[...] = jnp.zeros_like(dgain)
        local[...] = jnp.zeros_like(local)
        passed[...] = jnp.ones_like(passed)

    carried = jnp.exp(cum[...])
    maps = bc[:, n:].T
    turned = factors[...].T
    s = turned[:, 0:1]
    t = turned[:, 1:2]
    for tile in range(inner // LANES):
        cols = slice(tile * LANES, (tile + 1) * LANES)
        g = gate[:, cols]
        soft = sigmoid(g)
        silu = g * soft
        out = y[:, cols]
        gated = out * silu
        grad = q[:, cols]
        scaled = gated * s
        u_out[:, cols] = scaled * gain[0:1, cols]
        dgain[:, cols] = dgain[:, cols] + (grad * scaled).reshape(CHUNK // PAD, PAD, LANES).sum(axis=0)
        dgated = s * (grad * gain[0:1, cols]) - t * gated
        dgate[:, cols] = dgated * out * (soft + silu * (1.0 - soft))
        dy = dgated * silu
        dy_out[:, cols] = dy
        part = dot(maps, dy * spread_heads(carried, tile, width))
        adjoint[0, :, cols] = part
        local[:, cols] = local[:, cols] + passed[0:1, cols] * part
    passed[...] = passed[...] * chdec[0]


def back_kernel(width, dy, v, bc, dt, cum, cumt, states, du, dbc, gram):
    inner = v.shape[1]
    n = bc.shape[1] // 2
    each = LANES // width
    lane = lax.broadcasted_iota(jnp.int32, (CHUNK, LANES), 1)
    upper = lax.broadcasted_iota(jnp.int32, (CHUNK, CHUNK), 0) <= lax.broadcasted_iota(
        jnp.int32, (CHUNK, CHUNK), 1
    )
    inputs, outputs = bc[:, :n], bc[:, n:]
    meet = dot(inputs, outputs, NT)
    carried = jnp.exp(cum[...])
    grad_out = None
    for tile in range(inner // LANES):
        cols = slice(tile * LANES, (tile + 1) * LANES)
        grad = dy[:, cols]
        stepped = v[:, cols] * spread_heads(dt[...], tile, width)
        result = None
        for k in range(each):
            head = tile * each + k
            spread = cumt[head : head + 1, :] - cum[:, head : head + 1]
            decay = jnp.exp(jnp.where(upper, spread, NEG))
            part = dot(decay * meet, grad)
            result = part if k == 0 else jnp.where(lane < k * width, result, part)
            own = (lane >= k * width) & (lane < (k + 1) * width)
            cross = decay * dot(jnp.where(own, stepped, 0.0), grad, NT)
            first = tile == 0 and k == 0
            gram[...] = cross if first else gram[...] + cross
        du[:, cols] = result
        part = dot(grad * spread_heads(carried, tile, width), states[0, :, cols], NT)
        grad_out = part if tile == 0 else grad_out + part
    total = gram[...]
    dbc[:, :n] = dot(total, outputs)
    dbc[:, n:] = grad_out + dot(total.T, inputs)


def head_totals(product, width):
    each = LANES // width
    lane = lax.broadcasted_iota(jnp.int32, product.shape, 1)
    result = []
    for k in range(each):
        own = (lane >= k * width) & (lane < (k + 1) * width)
        result.append(jnp.sum(jnp.where(own, product, 0.0), axis=1, keepdims=True))
    return result


def place_heads(columns, shape):
    lane = lax.broadcasted_iota(jnp.int32, shape, 1)
    result = jnp.zeros(shape, F32)
    for head, column in enumerate(columns):
        result = jnp.where(lane == head, column, result)
    return result


def close_kernel(
    width, dy, y, v, du, dsi, adjoint, bc, dt, cum, sp, hp, dbc, dss, chdec, final, later,
    dti, dts, dstep, rows, leaving, running,
):
    inner = v.shape[1]
    n = bc.shape[1] // 2
    heads_rate = -jnp.exp(hp[1:2, :])

    @pl.when(pl.program_id(0) == 0)
    def _():
        crossing = jnp.sum(final[...] * later[...], axis=0, keepdims=True)
        columns = []
        for tile in range(inner // LANES):
            columns += head_totals(crossing[:, tile * LANES : (tile + 1) * LANES], width)
        running[...] = jnp.broadcast_to(place_heads(columns, (1, LANES)), running.shape)
        leaving[...] = later[...]
        rows[...] = jnp.zeros_like(rows)

    ones = (
        lax.broadcasted_iota(jnp.int32, (CHUNK, CHUNK), 0)
        <= lax.broadcasted_iota(jnp.int32, (CHUNK, CHUNK), 1)
    ).astype(F32)
    step = dt[...]
    cums = cum[...]
    fade = jnp.exp(cums[CHUNK - 1 : CHUNK, :] - cums)
    inputs = bc[:, :n]
    grad_in = dbc[:, :n]
    own, direct = [], []
    for tile in range(inner // LANES):
        cols = slice(tile * LANES, (tile + 1) * LANES)
        adj = leaving[:, cols]
        wide_fade = spread_heads(fade, tile, width)
        wide_step = spread_heads(step, tile, width)
        skip = spread_heads(hp[2:3, :], tile, width)
        values = v[:, cols]
        grad = dy[:, cols]
        dstepped = du[:, cols] + wide_fade * dot(inputs, adj)
        grad_in = grad_in + dot(wide_fade * wide_step * values, adj, NT)
        dti[:, cols] = (wide_step * dstepped + skip * grad) * dsi[:, cols]
        own += head_totals(grad * (y[:, cols] - skip * values), width)
        direct += head_totals(values * dstepped, width)
        part = (grad * values).reshape(CHUNK // PAD, PAD, LANES).sum(axis=0)
        rows[0:PAD, cols] = rows[0:PAD, cols] + part
        leaving[:, cols] = adjoint[0, :, cols] + chdec[0, 0:1, cols] * adj
    dts[:, :n] = grad_in * dss[:, :n]
    dts[:, n:] = dbc[:, n:] * dss[:, n:]
    direct = place_heads(direct, (CHUNK, LANES))
    dcum = place_heads(own, (CHUNK, LANES)) - step * direct
    drate = dot(ones, dcum, precision=HIGHEST) + running[0:1, :]
    running[...] = jnp.broadcast_to(drate[0:1, :], running.shape)
    dstep_value = direct + drate * heads_rate
    raw = sp[:, 2 * n :] + hp[0:1, :]
    grad_raw = dstep_value * sigmoid(raw)
    dstep[...] = grad_raw
    lanes = slice(0, LANES)
    rates = drate * heads_rate * step
    rows[PAD : 2 * PAD, lanes] = rows[PAD : 2 * PAD, lanes] + rates.reshape(
        CHUNK // PAD, PAD, LANES
    ).sum(axis=0)
    rows[2 * PAD : 3 * PAD, lanes] = rows[2 * PAD : 3 * PAD, lanes] + grad_raw.reshape(
        CHUNK // PAD, PAD, LANES
    ).sum(axis=0)


def filter_back_kernel(
    dti, hi, dts, hs, ip, pi, ib, sp, ps, sb, ti, ts, dip, dsp, ri, rs, padi, pads, padgi, padgs
):
    inner = ip.shape[1]
    states = dts.shape[1]
    place = pl.program_id(0)

    @pl.when(place == 0)
    def _():
        padgi[CHUNK:, :] = hi[...]
        padgs[CHUNK:, :] = hs[...]
        ri[...] = jnp.zeros_like(ri)
        rs[...] = jnp.zeros_like(rs)

    @pl.when(place > 0)
    def _():
        padgi[CHUNK:, :] = padgi[0:PAD, :]
        padgs[CHUNK:, :] = padgs[0:PAD, :]

    @pl.when(place == pl.num_programs(0) - 1)
    def _():
        padi[0:PAD, :] = ib[...]
        pads[0:PAD, :] = sb[...]

    @pl.when(place < pl.num_programs(0) - 1)
    def _():
        padi[0:PAD, :] = pi[...]
        pads[0:PAD, :] = ps[:, :states]

    padi[PAD:, :] = ip[...]
    pads[PAD:, :] = sp[:, :states]
    padgi[0:CHUNK, :] = dti[...]
    padgs[0:CHUNK, :] = dts[...]
    rows = 64

    def folded(value):
        return value.reshape(rows // PAD, PAD, LANES).sum(axis=0)

    def step(number, _):
        start = pl.multiple_of(number * rows, rows)
        for signal, grads, taps, out, sums, size in (
            (padi, padgi, ti, dip, ri, inner),
            (pads, padgs, ts, dsp, rs, states),
        ):
            for tile in range(size // LANES):
                cols = slice(tile * LANES, (tile + 1) * LANES)
                ahead = grads[pl.ds(start, rows + PAD), cols]
                grad = ahead[:rows]
                before = signal[pl.ds(start, rows + PAD), cols]
                total = taps[3:4, cols] * grad
                sums[3 * PAD : 4 * PAD, cols] = sums[3 * PAD : 4 * PAD, cols] + folded(grad * before[PAD:])
                sums[4 * PAD : 5 * PAD, cols] = sums[4 * PAD : 5 * PAD, cols] + folded(grad)
                for back in range(1, 4):
                    tap = 3 - back
                    total = total + taps[tap : tap + 1, cols] * pltpu.roll(ahead, rows + PAD - back, 0)[:rows]
                    place = slice(tap * PAD, (tap + 1) * PAD)
                    sums[place, cols] = sums[place, cols] + folded(
                        grad * pltpu.roll(before, back, 0)[PAD:]
                    )
                out[pl.ds(start, rows), cols] = total
        return 0

    lax.fori_loop(0, CHUNK // rows, step, 0)


def matmul(left, right, dims=((1,), (0,)), precision=HIGH):
    return lax.dot_general(left, right, (dims, ((), ())), precision=precision)


def padded_rows(rows, lanes):
    rows = jnp.concatenate(rows, axis=0)
    return jnp.pad(rows, ((0, PAD - rows.shape[0]), (0, lanes - rows.shape[1])))


def forward(current, w, first, extra, other_maps, taps):
    length = current.shape[0]
    inner = w["inner"].shape[1]
    heads = w["heads"]
    width = inner // heads
    states = w["states"]
    n = states // 2
    chunks = length // CHUNK
    root = lax.rsqrt(jnp.mean(current * current, axis=-1, keepdims=True) + epsilon)
    normed = current * root * w["pre_gain"][None, :]
    if first:
        whole = matmul(normed, w["state"], precision=HIGHEST)
        whole = jnp.concatenate([whole, taps], axis=0)
        ip = matmul(after(normed, whole), w["inner"])
        if power_of_two(lax.axis_size("head")):
            wait = whole
            for distance in distances("head"):
                other = exchanged(whole, "head", distance)
                if distance == 1:
                    other, ip = tied(other, ip)
                    wait = other
                whole = joined(whole, other, "head", distance, 1)
        else:
            whole = gathered_columns(whole)
            wait = whole
        gate = matmul(after(normed, wait), w["gate"])
        whole, gate = tied(whole, gate)
        taps = whole[length:]
        sp = whole[:length]
    else:
        ip = matmul(normed, w["inner"])
        sp = matmul(normed, w["maps"], NT, HIGHEST)
        gate = None
    border = shifted(
        jnp.concatenate([ip[length - PAD :], sp[length - PAD :, :states]], axis=1), "seq", 1
    )
    if first:
        step = matmul(after(normed, sp), w["step"], precision=HIGHEST)
        border, step = tied(border, step)
        sp = jnp.concatenate([sp, step], axis=1)
    else:
        gate = matmul(after(normed, ip, sp), w["gate"])
        border, gate = tied(border, gate)
    ib, sb = border[:, :inner], border[:, inner:]
    taps_s = taps[w["layer"] * PAD : (w["layer"] + 1) * PAD]
    b_inner, b_states, b_lanes = (rows_of(CHUNK, size) for size in (inner, states, LANES))
    b_heads, b_sp = columns_of(16, CHUNK), rows_of(CHUNK, states + LANES)
    b_block, b_state = rows_of(1, n, inner), all_of(n, inner)
    b_decay = rows_of(1, PAD, inner)
    v, bc, dsi, dss, dt, cum, cumt, fresh, local, chdec, decay = call(
        functools.partial(start_kernel, width),
        chunks,
        [
            ((length, inner), b_inner),
            ((length, states), b_states),
            ((length, inner), b_inner),
            ((length, states), b_states),
            ((length, LANES), b_lanes),
            ((length, LANES), b_lanes),
            ((16, length), b_heads),
            ((chunks, n, inner), b_block),
            ((n, inner), b_state),
            ((chunks, PAD, inner), b_decay),
            ((PAD, inner), all_of(PAD, inner)),
        ],
        [pltpu.VMEM((CHUNK + PAD, inner), F32), pltpu.VMEM((CHUNK + PAD, states), F32)],
        2 * 3 * length * n * inner,
        (ip, b_inner),
        (ib, all_of(PAD, inner)),
        (sp, b_sp),
        (sb, all_of(PAD, states)),
        (w["taps_i"], all_of(PAD, inner)),
        (taps_s, all_of(PAD, states)),
        (w["heads_rows"], all_of(PAD, LANES)),
    )
    decay = decay[0:1]

    def inside(before):
        return call(
            functools.partial(inner_kernel, width),
            chunks,
            [((length, inner), b_inner)],
            [],
            2 * 6 * length * CHUNK * inner,
            (v, b_inner),
            (bc, b_states),
            (dt, b_lanes),
            (cum, b_lanes),
            (cumt, b_heads),
            (w["heads_rows"], all_of(PAD, LANES)),
        )

    other_maps = gathered_rows(after(other_maps, chdec).T)

    def aside(before):
        return [matmul(after(extra, before), w["last_out"])] if first else [extra]

    entering, ((yd,), (extra,), (other_maps,)) = state_before(
        local, decay, False, [inside, aside, lambda before: [other_maps]]
    )
    y, gn, carried, squares, final = call(
        functools.partial(gate_kernel, width),
        chunks,
        [
            ((length, inner), b_inner),
            ((length, inner), b_inner),
            ((chunks, n, inner), b_block),
            ((PAD, length), columns_of(PAD, CHUNK)),
            ((n, inner), b_state),
        ],
        [],
        2 * 3 * length * n * inner,
        (yd, b_inner),
        (bc, b_states),
        (cum, b_lanes),
        (fresh, b_block),
        (chdec, b_decay),
        (entering, b_state),
        (gate, b_inner),
        (w["norm_gain"][None, :], all_of(1, inner)),
    )
    saved = dict(
        current=current, root=root, normed=normed, ip=ip, sp=sp, ib=ib, sb=sb, gate=gate, v=v, bc=bc,
        dsi=dsi, dss=dss, dt=dt, cum=cum, cumt=cumt, fresh=fresh, chdec=chdec, decay=decay, y=y,
        gn=gn, states=carried, taps_s=taps_s, final=final,
    )
    return gn, squares[0:1], saved, extra, other_maps, taps


def core_products(left, right):
    place = lax.axis_index("dp")
    if lax.axis_size("dp") != 2:
        total = matmul(left, right, ((0,), (0,)))
        return total, total
    return (
        matmul(left, half(right, 1 - place, 1), ((0,), (0,))),
        matmul(left, half(right, place, 1), ((0,), (0,))),
    )


def over_cores(sent, kept):
    if lax.axis_size("dp") != 2:
        return lax.psum(kept, "dp")
    return kept + exchanged(sent, "dp", 1)


def over_seq(total):
    return lax.psum_scatter(total, "seq", scatter_dimension=0, tiled=True)


def place_kernel(*refs):
    *parts, out = refs
    first = lax.axis_index("dp") == 0
    width = out.shape[2] // 2
    for layer in range(len(parts) // 2):
        mine, other = parts[2 * layer], parts[2 * layer + 1]

        @pl.when(first)
        def _():
            out[layer, :, :width] = mine[...]
            out[layer, :, width:] = other[...]

        @pl.when(jnp.logical_not(first))
        def _():
            out[layer, :, :width] = other[...]
            out[layer, :, width:] = mine[...]


def cores_joined(pairs, start, width):
    if lax.axis_size("dp") != 2:
        return jnp.stack([mine[:, start : start + width] for mine, _ in pairs], axis=0)
    pieces = [piece for pair in pairs for piece in pair]
    rows = pieces[0].shape[0]
    tile = 96 if rows % 96 == 0 else rows
    return pl.pallas_call(
        place_kernel,
        grid=(rows // tile,),
        out_shape=jax.ShapeDtypeStruct((len(pairs), rows, 2 * width), F32),
        in_specs=[pl.BlockSpec((tile, width), lambda i: (i, start // width))] * len(pieces),
        out_specs=pl.BlockSpec((len(pairs), tile, 2 * width), lambda i: (0, i, 0)),
        compiler_params=pltpu.CompilerParams(vmem_limit_bytes=24 * 1024 * 1024),
    )(*pieces)


def backward(grad, q, scale, slope, w, saved, beside, waiting):
    s = saved
    length, inner = q.shape
    width = inner // w["heads"]
    states = w["states"]
    n = states // 2
    chunks = length // CHUNK
    factors = jnp.pad(jnp.concatenate([scale, slope], axis=0), ((0, PAD - 2), (0, 0)))
    b_inner, b_states, b_lanes = (rows_of(CHUNK, size) for size in (inner, states, LANES))
    b_heads, b_sp = columns_of(16, CHUNK), rows_of(CHUNK, states + LANES)
    b_block, b_state = rows_of(1, n, inner), all_of(n, inner)
    b_decay = rows_of(1, PAD, inner)
    dy, dgate, u, dgain, adjoint, local = call(
        functools.partial(open_kernel, width),
        chunks,
        [
            ((length, inner), b_inner),
            ((length, inner), b_inner),
            ((length, inner), b_inner),
            ((PAD, inner), all_of(PAD, inner)),
            ((chunks, n, inner), b_block),
            ((n, inner), b_state),
        ],
        [pltpu.VMEM((PAD, inner), F32)],
        2 * 3 * length * n * inner,
        (q, b_inner),
        (s["y"], b_inner),
        (s["gate"], b_inner),
        (w["norm_gain"][None, :], all_of(1, inner)),
        (factors, columns_of(PAD, CHUNK)),
        (s["bc"], b_states),
        (s["cum"], b_lanes),
        (s["chdec"], b_decay),
    )

    def cross_out(before):
        return core_products(grad, after(u, before))

    def cross_gate(before):
        result = core_products(s["normed"], after(dgate, before))
        return beside.advance(*result) if beside is not None else result

    def inside(before):
        result = call(
            functools.partial(back_kernel, width),
            chunks,
            [((length, inner), b_inner), ((length, states), b_states)],
            [pltpu.VMEM((CHUNK, CHUNK), F32)],
            2 * 15 * length * CHUNK * inner,
            (after(dy, before), b_inner),
            (s["v"], b_inner),
            (s["bc"], b_states),
            (s["dt"], b_lanes),
            (s["cum"], b_lanes),
            (s["cumt"], b_heads),
            (s["states"], b_block),
        )
        return beside.advance(*result) if beside is not None else result

    later, (halves_out, halves_gate, (du, dbc)) = state_before(
        local, s["decay"], True, [cross_out, cross_gate, inside]
    )
    pair = jnp.concatenate([over_cores(*halves_out), over_cores(*halves_gate)], axis=1)
    if waiting is not None:
        pair = after(pair, waiting)
    pair = over_seq(pair)
    dti, dts, dstep, rows = call(
        functools.partial(close_kernel, width),
        chunks,
        [
            ((length, inner), b_inner),
            ((length, states), b_states),
            ((length, LANES), b_lanes),
            ((3 * PAD, inner), all_of(3 * PAD, inner)),
        ],
        [pltpu.VMEM((n, inner), F32), pltpu.VMEM((PAD, LANES), F32)],
        2 * 6 * length * n * inner,
        (dy, b_inner),
        (s["y"], b_inner),
        (s["v"], b_inner),
        (du, b_inner),
        (s["dsi"], b_inner),
        (adjoint, b_block),
        (s["bc"], b_states),
        (s["dt"], b_lanes),
        (s["cum"], b_lanes),
        (s["sp"], b_sp),
        (w["heads_rows"], all_of(PAD, LANES)),
        (dbc, b_states),
        (s["dss"], b_states),
        (s["chdec"], b_decay),
        (s["final"], b_state),
        (later, b_state),
        backward=True,
    )
    if beside is not None:
        dti, dts = beside.advance(dti, dts)
    halo = shifted(jnp.concatenate([dti[:PAD], dts[:PAD]], axis=1), "seq", -1)
    base = matmul(after(dgate, dti), w["gate"], NT)
    halo, base = tied(halo, base)
    def edge(size):
        return pl.BlockSpec((PAD, size), lambda c: (jnp.maximum(c * (CHUNK // PAD) - 1, 0), 0))

    dip, dsp, ri, rs = call(
        filter_back_kernel,
        chunks,
        [
            ((length, inner), b_inner),
            ((length, states), b_states),
            ((5 * PAD, inner), all_of(5 * PAD, inner)),
            ((5 * PAD, states), all_of(5 * PAD, states)),
        ],
        [pltpu.VMEM((CHUNK + PAD, size), F32) for size in (inner, states, inner, states)],
        16 * length * inner,
        (dti, b_inner),
        (halo[:, :inner], all_of(PAD, inner)),
        (dts, b_states),
        (halo[:, inner:], all_of(PAD, states)),
        (s["ip"], b_inner),
        (s["ip"], edge(inner)),
        (s["ib"], all_of(PAD, inner)),
        (s["sp"], b_sp),
        (s["sp"], edge(states + LANES)),
        (s["sb"], all_of(PAD, states)),
        (w["taps_i"], all_of(PAD, inner)),
        (s["taps_s"], all_of(PAD, states)),
        backward=True,
    )
    if beside is not None:
        (dip,) = beside.advance(dip)

    def product(base, dip, dmaps):
        return base + matmul(dip, w["inner"], NT) + matmul(dmaps, w["maps"])

    gains = []

    def finish(rows_grad, offset):
        def take(array):
            return lax.dynamic_slice_in_dim(array, offset, rows_grad.shape[0], 0)

        x, root = take(s["current"]), take(s["root"])
        scaled = rows_grad * w["pre_gain"][None, :]
        along = jnp.mean(scaled * x, axis=-1, keepdims=True)
        gains.append(jnp.sum(rows_grad * x * root, axis=0))
        return root * scaled - x * (root * root * root * along)

    shared = dsp
    own = states // lax.axis_size("head")
    lefts = [base, dip, jnp.concatenate([dsp, dstep], axis=1)]
    if power_of_two(lax.axis_size("head")):
        way = distances("head")[::-1]
        for number, distance in enumerate(way):
            bit = bit_of("head", distance)
            other = exchanged(half(shared, 1 - bit, 1), "head", distance)
            if number == 0:
                steps = Steps(head_sum(lefts, product, finish))
                (other,) = steps.advance(other)
            shared = half(shared, bit, 1) + other
    else:
        shared = lax.psum_scatter(shared, "head", scatter_dimension=1, tiled=True)
        steps = Steps(head_sum(lefts, product, finish))
        steps.advance()
    halves = core_products(s["normed"], after(dip, shared))
    if waiting is None:
        (pair,) = steps.advance(pair)
    else:
        steps.advance()
    small = jnp.concatenate([shared, dstep[:, : LANES - own]], axis=1)
    total_small = small_sum(matmul(s["normed"], after(small, halves), ((0,), (0,))), "dp")
    last = jnp.concatenate([over_cores(*halves), total_small], axis=1)
    if waiting is None:
        (last,) = steps.advance(last)
    else:
        last, pair = steps.advance(last, pair)
    last = over_seq(after(last, pair))
    branch = steps.finished()
    grad = grad + branch

    def folded(array):
        return array.reshape(-1, PAD, array.shape[1]).sum(axis=1)

    ri, rs, rows = folded(ri), folded(rs), folded(rows)
    over_heads = jnp.concatenate([gains[0] + gains[1], rs.reshape(-1)])
    flat = jnp.concatenate(
        [ri.reshape(-1), dgain.sum(axis=0), rows[0], rows[1, :LANES], rows[2, :LANES]]
    )
    return grad, pair, last, over_heads, flat, own


def small_grads(over_heads, flat, own, w):
    model, inner = w["inner"].shape
    states = w["states"]
    heads = w["heads"]
    g_pre, g_rs = over_heads[:model], over_heads[model:]
    cut = []
    start = 0
    for size in (5 * inner, inner, inner, LANES, LANES):
        cut.append(flat[start : start + size])
        start += size
    g_ri, g_norm, g_skip, g_rate, g_bias = cut
    g_rs = lax.dynamic_slice_in_dim(g_rs.reshape(5, states), lax.axis_index("head") * own, own, 1)
    g_ri = g_ri.reshape(5, inner)
    return (
        g_pre,
        g_ri[:4],
        g_ri[4],
        g_rs[:4],
        g_rs[4],
        g_bias[:heads],
        g_rate[:heads],
        g_skip.reshape(heads, -1).sum(axis=1),
        g_norm,
    )


def gathered_columns(value):
    if not power_of_two(lax.axis_size("head")):
        return lax.all_gather(value, "head", axis=1, tiled=True)
    return gather_back(value, "head", distances("head")[::-1], 1)


def gathered_rows(value):
    if not power_of_two(lax.axis_size("head")):
        return lax.all_gather(value, "head", axis=0, tiled=True)
    return gather_back(value, "head", distances("head")[::-1], 0)


def body(
    tokens,
    cotangent,
    pre_gain,
    gate_weight,
    inner_weight,
    state_weight,
    step_weight,
    filter_inner,
    filter_inner_bias,
    filter_state,
    filter_state_bias,
    step_bias,
    log_rate,
    skip_gain,
    norm_gain,
    out_weight,
):
    layers = pre_gain.shape[0]
    heads = step_bias.shape[1]
    inner = gate_weight.shape[2]
    taps = jnp.concatenate([filter_state, filter_state_bias[:, None, :]], axis=1)
    taps = jnp.pad(taps, ((0, 0), (0, PAD - taps.shape[1]), (0, 0))).reshape(layers * PAD, -1)
    weights = []
    for layer in range(layers):
        steps = jnp.pad(step_weight[layer], ((0, 0), (0, LANES - heads)))
        weights.append(
            dict(
                layer=layer,
                heads=heads,
                states=state_weight.shape[2] * lax.axis_size("head"),
                pre_gain=pre_gain[layer],
                gate=gate_weight[layer],
                inner=inner_weight[layer],
                state=state_weight[layer],
                step=steps,
                out=out_weight[layer],
                norm_gain=norm_gain[layer],
                taps_i=padded_rows([filter_inner[layer], filter_inner_bias[layer][None]], inner),
                heads_rows=padded_rows(
                    [step_bias[layer][None], log_rate[layer][None], skip_gain[layer][None]], LANES
                ),
            )
        )
    current = tokens[0]
    grad = cotangent[0]
    kept = []
    weights[0]["last_out"] = weights[layers - 1]["out"]
    extra = grad
    for layer in range(layers):
        w = weights[layer]
        other = weights[(layer + 1) % layers]
        gn, squares, saved, extra, maps, taps = forward(
            current, w, layer == 0, extra, other["state"], taps
        )
        other["maps"] = jnp.concatenate([maps, after(other["step"], maps).T], axis=0)
        last = layer == layers - 1
        if last:
            both = jnp.concatenate([squares, jnp.sum(extra * gn, axis=1)[None, :]], axis=0)
            both = small_sum(both, "head")
            squares, along = both[0:1], both[1:2]
        else:
            squares = small_sum(squares, "head")
        scale = lax.rsqrt(squares / INNER + epsilon)

        def finish(rows, offset, scale=scale):
            return rows * lax.dynamic_slice_in_dim(scale[0], offset, rows.shape[0], 0)[:, None]

        steps = Steps(head_sum([gn], lambda rows, w=w: matmul(rows, w["out"], NT), finish))
        if last:
            scale = after(scale, steps.now)
            steps.advance(scale)
        branch = None if last else steps.finished()
        kept.append((saved, scale, branch))
        if not last:
            current = current + branch
    collected = [None] * layers
    waiting = None
    for layer in reversed(range(layers)):
        w = weights[layer]
        saved, scale, branch = kept[layer]
        if layer < layers - 1:
            q, waiting = tied(matmul(grad, w["out"]), waiting)
            collected[layer + 1][1] = waiting
            slope = jnp.sum(grad * branch, axis=1)[None, :] * scale * scale / INNER
        else:
            q = extra
            slope = along * scale * scale * scale / INNER
        grad, *collected[layer] = backward(
            grad, q, scale, slope, w, saved, steps if layer == layers - 1 else None, waiting
        )
        waiting = collected[layer][1]
    current = current + steps.finished()
    over_heads = jnp.concatenate([entry[2] for entry in collected])
    flat = jnp.concatenate([small_sum(over_heads, "head")] + [entry[3] for entry in collected])
    flat = small_sum(small_sum(flat, "dp"), "seq")
    size = collected[0][2].size
    rest = collected[0][3].size
    results = []
    for layer in range(layers):
        start = layers * size + layer * rest
        results.append(
            small_grads(
                flat[layer * size : (layer + 1) * size],
                flat[start : start + rest],
                collected[layer][4],
                weights[layer],
            )
        )
    stacked = [jnp.stack([entry[number] for entry in results], axis=0) for number in range(9)]
    two = lax.axis_size("dp") == 2

    def with_other(part):
        return part, exchanged(part, "dp", 1) if two else part

    pairs = [[with_other(entry[0]) for entry in collected]]
    half_width = inner // 2 if two else inner
    large = {
        "out": cores_joined(pairs[0], 0, half_width),
        "gate": cores_joined(pairs[0], half_width, half_width),
    }
    collected[0][1], current, grad, stacked, large = tied(
        collected[0][1], current, grad, stacked, large
    )
    pairs.append([with_other(entry[1]) for entry in collected])
    large["inner"] = cores_joined(pairs[1], 0, half_width)
    small = jnp.stack([entry[1][:, half_width : half_width + LANES] for entry in collected], axis=0)
    own = collected[0][4]
    return (
        current[None],
        grad[None],
        stacked[0],
        large["gate"],
        large["inner"],
        small[:, :, :own],
        small[:, :, own : own + heads],
        *stacked[1:],
        large["out"],
    )


def solution(mesh):
    placed = (
        P("dp", "seq", None),
        P("dp", "seq", None),
        P(),
        P(None, None, "head"),
        P(None, None, "head"),
        P(None, None, "head"),
        P(None, None, "head"),
        P(None, None, "head"),
        P(None, "head"),
        P(None, None, "head"),
        P(None, "head"),
        P(None, "head"),
        P(None, "head"),
        P(None, "head"),
        P(None, "head"),
        P(None, None, "head"),
    )
    return jax.shard_map(
        body,
        mesh=mesh,
        in_specs=placed,
        out_specs=(
            P("dp", "seq", None),
            P("dp", "seq", None),
            P(),
            P(None, "seq", "head"),
            P(None, "seq", "head"),
            P(None, "seq", "head"),
            P(None, "seq", "head"),
            P(None, None, "head"),
            P(None, "head"),
            P(None, None, "head"),
            P(None, "head"),
            P(None, "head"),
            P(None, "head"),
            P(None, "head"),
            P(None, "head"),
            P(None, "seq", "head"),
        ),
        check_vma=False,
    )
```

time: 915 us -> 708 us (0.77)
  starting transfers between devices: 239 us -> 91.7 us
  waiting for transfers between devices: 284 us -> 182 us
  other arithmetic: 72.1 us -> 92.6 us
  Pallas kernels: 63.2 us -> 76.5 us
  between operations: 6.16 us -> 17.9 us
    ppermute x60 -> x12, starting transfers between devices: 155 us -> 16.4 us  [state_before(): got = lax.ppermute(decay * state + local, 'seq', [(source, target)])]
    ppermute x60 -> x12, waiting for transfers between devices: 110 us -> 1.6 us  [state_before(): got = lax.ppermute(decay * state + local, 'seq', [(source, target)])]
    reduce_scatter x0 -> x4, waiting for transfers between devices: none -> 27.1 us  [over_seq(): return lax.psum_scatter(total, 'seq', scatter_dimension=0, tiled=True)]
    ppermute x70 -> x63, waiting for transfers between devices: 163 us -> 148 us  [exchanged(): return lax.ppermute(value, axis, [(i, i ^ distance) for i in range(n)])]
    pallas_call x14 -> x17, Pallas kernels: 63.2 us -> 76.5 us  [the longest x14 65.5 us: call(): pl.pallas_call(kernel, grid=(steps,), out_shape=shapes, in_specs=[spec(bl...]
    unnamed x538 -> x477, local copies, waits for them, and re-layouts: 43.6 us -> 54.4 us
    dot_general x30 -> x37, matrix products: 150 us -> 145 us  [matmul(): return lax.dot_general(left, right, (dims, ((), ())), precision=precision)]
    add x54 -> x38, other arithmetic: 35.2 us -> 31.6 us  [the longest x6 8.67 us: over_cores(): return kept + exchanged(sent, 'dp', 1)]
  transfers between devices with their start and end apart: 134 -> 83, of which waited for: 53 -> 38; matrix products, arithmetic and copies ran while one was open for 26% -> 37% of each run, Pallas kernels for 6% -> 8%
where the time goes in v2:
time: 708 us; the launch traced here: 696 us
  waiting for transfers between devices  182 us (26%)
  matrix products  145 us (20%)
  other arithmetic  92.6 us (13%)
  starting transfers between devices  91.7 us (13%)
  local copies, waits for them, and re-layouts  90.5 us (13%)
  Pallas kernels  76.5 us (11%)
  between operations  17.9 us (3%)
    ppermute x63, waiting for transfers between devices, exchanged(): return lax.ppermute(value, axis, [(i, i ^ distance) for i in range(n)])  148 us
    dot_general x37, matrix products, matmul(): return lax.dot_general(left, right, (dims, ((), ())), precision=precision)  145 us
    pallas_call x14, Pallas kernels, call(): pl.pallas_call(kernel, grid=(steps,), out_shape=shapes, in_specs=[spec(bl...  65.5 us
    ppermute x63, starting transfers between devices, exchanged(): return lax.ppermute(value, axis, [(i, i ^ distance) for i in range(n)])  65 us
    unnamed x477, local copies, waits for them, and re-layouts  54.4 us
    reduce_scatter x4, waiting for transfers between devices, over_seq(): return lax.psum_scatter(total, 'seq', scatter_dimension=0, tiled=True)  27.1 us
    ppermute x12, starting transfers between devices, state_before(): got = lax.ppermute(decay * state + local, 'seq', [(source, target)])  16.4 us
  transfers between devices with their start and end apart: 83, of which 38 were waited for; matrix products, arithmetic and copies ran while one was open for 37% of the time, Pallas kernels for 8%

profile of v2, /device:TPU:0, one launch (start us, length us, event | category | flops | bytes accessed | tf_op | source)
XLA Modules:
  0.0 695.8 jit_solution(9573826945245831481)
XLA Ops:
  11.0 3.8 fusion.66
  20.0 4.1 fusion.30.ip.pi
  28.3 8.5 %fusion.24.gate = f32[512,768]{1,0:T(8,128)} fusion(f32[512,1536]{1,0:T(8,128)} %copy-done.117, f32[2,1536,768]{2,1,0:T(8,128)} %param.19), kind=kOutput, calls=%fused_computation.26 | convolution fusion | flops 3623878656 | bytes 9437184 | tf_op jit(solution)/shard_map/dot_general | solution.py:571
  45.0 5.5 shard_map.279
  55.9 4.2 collective-permute-start.3
  72.3 7.9 %fusion.20.q = f32[512,768]{1,0:T(8,128)} fusion(f32[512,1536]{1,0:T(8,128)S(1)} %bitcast.271, f32[2,1536,768]{2,1,0:T(8,128)} %param.31), kind=kOutput, calls=%fused_computation.22 | convolution fusion | flops 3623878656 | bytes 9437184 | tf_op jit(solution)/shard_map/dot_general | solution.py:571
  82.2 6.3 collective-permute-done.7
  102.9 9.1 %collective-permute-done.14 = f32[128,1536]{1,0:T(8,128)S(1)} collective-permute-done((f32[128,1536]{1,0:T(8,128)S(1)}, f32[128,1536]{1,0:T(8,128)S(1)}, u32[]{:S(2)}, u32[]{:S(2)}) %collective-permute-start.14) | collective-permute-done | bytes 786464 | tf_op jit(solution)/shard_map/ppermute | solution.py:28
  113.7 6.6 collective-permute-done.8
  121.9 4.9 collective-permute-done.15
  127.2 4.0 collective-permute-done.9
  138.1 5.4 collective-permute-done.12
  145.2 7.5 %collective-permute-done.17 = f32[128,1536]{1,0:T(8,128)S(1)} collective-permute-done((f32[128,1536]{1,0:T(8,128)S(1)}, f32[128,1536]{1,0:T(8,128)S(1)}, u32[]{:S(2)}, u32[]{:S(2)}) %collective-permute-start.17) | collective-permute-done | bytes 786464 | tf_op jit(solution)/shard_map/ppermute | solution.py:28
  158.6 5.4 fusion.104.sp.ps
  164.1 6.2 fusion.8.ip.pi
  170.3 3.7 collective-permute-start.18
  174.1 5.3 fusion.2.gate
  179.4 5.5 shard_map.282
  203.9 6.5 collective-permute-done.23
  219.7 4.4 fusion.18
  225.8 4.4 fusion.16
  255.7 8.1 %shard_map.286 = (f32[512,768]{1,0:T(8,128)S(1)}, f32[512,256]{1,0:T(8,128)S(1)}) custom-call(f32[512,768]{1,0:T(8,128)S(1)} %get-tuple-element.277.dy, f32[512,768]{1,0:T(8,128)S(1)} %copy-done.6, f32[512,256]{1,0:T(8,128)S(1)} %copy-done.15, f32[512,128]{1,0:T(8,128)S(1)} %copy-done.46, f32[512,128]{1,0:T(8,128)S(1)} %copy-done.18, ...), custom_call_target="tpu_custom_call" | custom-call | flops 1509949440 | bytes 7897088 | tf_op jit(solution)/shard_map/pallas_call | solution.py:187
  288.7 7.3 %shard_map.287 = (f32[512,768]{1,0:T(8,128)S(1)}, f32[512,256]{1,0:T(8,128)S(1)}, f32[512,128]{1,0:T(8,128)S(1)}, f32[24,768]{1,0:T(8,128)S(1)}) custom-call(f32[512,768]{1,0:T(8,128)S(1)} %copy-done.30, f32[512,768]{1,0:T(8,128)S(1)} %copy-done.28, f32[512,768]{1,0:T(8,128)S(1)} %copy-done.7, f32[512,768]{1,0:T(8,128)S(1)} %copy-done.57, ...), custom_call_target="tpu_custom_call" | custom-call | flops 603979776 | bytes 15642624 | tf_op jit(solution)/shard_map/pallas_call | solution.py:187
  300.0 6.0 fusion
  318.3 8.4 %collective-permute-done.37 = f32[128,1536]{1,0:T(8,128)S(1)} collective-permute-done((f32[128,1536]{1,0:T(8,128)S(1)}, f32[128,1536]{1,0:T(8,128)S(1)}, u32[]{:S(2)}, u32[]{:S(2)}) %collective-permute-start.37) | collective-permute-done | bytes 786464 | tf_op jit(solution)/shard_map/ppermute | solution.py:28
  334.4 4.9 collective-permute-done.45
  339.5 4.1 fusion.141
  346.5 3.9 fusion.143
  355.2 8.6 %collective-permute-done.39 = f32[128,1536]{1,0:T(8,128)} collective-permute-done((f32[128,1536]{1,0:T(8,128)S(1)}, f32[128,1536]{1,0:T(8,128)}, u32[]{:S(2)}, u32[]{:S(2)}) %collective-permute-start.39) | collective-permute-done | bytes 786464 | tf_op jit(solution)/shard_map/ppermute | solution.py:28
  386.8 7.7 %collective-permute-done.50 = f32[64,1536]{1,0:T(8,128)S(1)} collective-permute-done((f32[64,1536]{1,0:T(8,128)S(1)}, f32[64,1536]{1,0:T(8,128)S(1)}, u32[]{:S(2)}, u32[]{:S(2)}) %collective-permute-start.50) | collective-permute-done | bytes 393248 | tf_op jit(solution)/shard_map/ppermute | solution.py:28
  397.2 15.2 %collective-permute-done.51 = f32[128,1536]{1,0:T(8,128)S(1)} collective-permute-done((f32[128,1536]{1,0:T(8,128)S(1)}, f32[128,1536]{1,0:T(8,128)S(1)}, u32[]{:S(2)}, u32[]{:S(2)}) %collective-permute-start.51) | collective-permute-done | bytes 786464 | tf_op jit(solution)/shard_map/ppermute | solution.py:28
  415.5 5.4 fusion.10.q
  420.9 27.1 %reduce-scatter.7.cloned.1.call-done.refs_2_ = f32[384,512]{1,0:T(8,128)} async-done(((f32[1536,512]{1,0:T(8,128)}), f32[384,512]{1,0:T(8,128)}) %reduce-scatter.7.cloned.1.call-update) | async-done | bytes 786448 | tf_op jit(solution)/shard_map/reduce_scatter | solution.py:726
  454.8 4.2 fusion.139
  459.0 4.2 fusion.137
  464.4 4.1 fusion.135
  468.6 4.1 fusion.133
  492.0 8.1 %shard_map.290 = (f32[512,768]{1,0:T(8,128)S(1)}, f32[512,256]{1,0:T(8,128)S(1)}) custom-call(f32[512,768]{1,0:T(8,128)S(1)} %copy-done.32, f32[512,768]{1,0:T(8,128)S(1)} %copy-done.4, f32[512,256]{1,0:T(8,128)S(1)} %copy-done.13, f32[512,128]{1,0:T(8,128)S(1)} %copy-done.44, f32[512,128]{1,0:T(8,128)S(1)} %get-tuple-element.223.cum, ...), custom_call_target="tpu_custom_call" | custom-call | flops 1509949440 | bytes 7897088 | tf_op jit(solution)/shard_map/pallas_call | solution.py:187
  501.4 7.3 %shard_map.291 = (f32[512,768]{1,0:T(8,128)S(1)}, f32[512,256]{1,0:T(8,128)S(1)}, f32[512,128]{1,0:T(8,128)S(1)}, f32[24,768]{1,0:T(8,128)S(1)}) custom-call(f32[512,768]{1,0:T(8,128)S(1)} %copy-done.32, f32[512,768]{1,0:T(8,128)S(1)} %copy-done.26, f32[512,768]{1,0:T(8,128)S(1)} %copy-done.4, f32[512,768]{1,0:T(8,128)S(1)} %get-tuple-element.343.du, ...), custom_call_target="tpu_custom_call" | custom-call | flops 603979776 | bytes 15642624 | tf_op jit(solution)/shard_map/pallas_call | solution.py:187
  510.8 6.0 fusion.22
  516.8 4.6 collective-permute-done.55
  544.1 4.0 collective-permute-done.61
  549.2 6.1 fusion.129
  565.1 10.5 %collective-permute-done.57 = f32[128,1536]{1,0:T(8,128)S(1)} collective-permute-done((f32[128,1536]{1,0:T(8,128)S(1)}, f32[128,1536]{1,0:T(8,128)S(1)}, u32[]{:S(2)}, u32[]{:S(2)}) %collective-permute-start.57) | collective-permute-done | bytes 786464 | tf_op jit(solution)/shard_map/ppermute | solution.py:28
  620.6 5.8 collective-permute-done.73
  631.5 5.5 collective-permute-done.74
  664.2 3.7 shard_map.293
  671.5 7.1 %collective-permute-done.69 = f32[128,1536]{1,0:T(8,128)S(1)} collective-permute-done((f32[128,1536]{1,0:T(8,128)S(1)}, f32[128,1536]{1,0:T(8,128)S(1)}, u32[]{:S(2)}, u32[]{:S(2)}) %collective-permute-start.69) | collective-permute-done | bytes 786464 | tf_op jit(solution)/shard_map/ppermute | solution.py:28
  (919 shorter events, 366.8 us)
Async XLA Ops:
  7.2 357.8 %reduce-scatter.5.cloned.1.call-start = ((), (), s32[]{:S(2)}) async-start(), calls=%async_computation.4 | async-start | bytes 5898240 | tf_op jit(solution)/shard_map/reduce_scatter | solution.py:726
  71.8 16.7 %collective-permute-start.7 = (f32[128,1536]{1,0:T(8,128)S(1)}, f32[128,1536]{1,0:T(8,128)S(1)}, u32[]{:S(2)}, u32[]{:S(2)}) collective-permute-start(f32[128,1536]{1,0:T(8,128)S(1)} %pad_maximum_fusion.15), channel_id=1, source_target_pairs={{0,2},{1,3},{2,0},{3,1},{4,6},{5,7},{6,4},{7,5},{8,10},{9,11},{10,... | collective-permute-start | bytes 2359304 | tf_op jit(solution)/shard_map/ppermute | solution.py:28
  96.2 15.8 %collective-permute-start.14 = (f32[128,1536]{1,0:T(8,128)S(1)}, f32[128,1536]{1,0:T(8,128)S(1)}, u32[]{:S(2)}, u32[]{:S(2)}) collective-permute-start(f32[128,1536]{1,0:T(8,128)S(1)} %get-tuple-element.527), channel_id=1, source_target_pairs={{0,2},{1,3},{2,0},{3,1},{4,6},{5,7},{6,4},{7,5},{8,10},{9,11},{10,... | collective-permute-start | bytes 2359304 | tf_op jit(solution)/shard_map/ppermute | solution.py:28
  100.8 19.5 %collective-permute-start.8 = (f32[128,1536]{1,0:T(8,128)S(1)}, f32[128,1536]{1,0:T(8,128)S(1)}, u32[]{:S(2)}, u32[]{:S(2)}) collective-permute-start(f32[128,1536]{1,0:T(8,128)S(1)} %get-tuple-element.526), channel_id=1, source_target_pairs={{0,1},{1,0},{2,3},{3,2},{4,5},{5,4},{6,7},{7,6},{8,9},{9,8},{10,11... | collective-permute-start | bytes 2359304 | tf_op jit(solution)/shard_map/ppermute | solution.py:28
  101.4 12.2 %collective-permute-start.11 = (f32[1,512]{1,0:T(1,128)S(1)}, f32[1,512]{1,0:T(1,128)S(1)}, u32[]{:S(2)}, u32[]{:S(2)}) collective-permute-start(f32[1,512]{1,0:T(1,128)S(1)} %slice_add_fusion), channel_id=1, source_target_pairs={{0,2},{1,3},{2,0},{3,1},{4,6},{5,7},{6,4},{7,5},{8,10},{9,11},{10,... | collective-permute-start | bytes 6152 | tf_op jit(solution)/shard_map/ppermute | solution.py:28
  112.1 14.7 %collective-permute-start.15 = (f32[64,1536]{1,0:T(8,128)S(1)}, f32[64,1536]{1,0:T(8,128)S(1)}, u32[]{:S(2)}, u32[]{:S(2)}) collective-permute-start(f32[64,1536]{1,0:T(8,128)S(1)} %dynamic-slice_add_fusion.12), channel_id=1, source_target_pairs={{0,1},{1,0},{2,3},{3,2},{4,5},{5,4},{6,7},{7,6},{8,9},{9,8},{10,11... | collective-permute-start | bytes 1179656 | tf_op jit(solution)/shard_map/ppermute | solution.py:28
  131.4 12.1 %collective-permute-start.12 = (f32[64,1536]{1,0:T(8,128)S(1)}, f32[64,1536]{1,0:T(8,128)S(1)}, u32[]{:S(2)}, u32[]{:S(2)}) collective-permute-start(f32[64,1536]{1,0:T(8,128)S(1)} %add_multiply_fusion.3), channel_id=1, source_target_pairs={{0,2},{1,3},{2,0},{3,1},{4,6},{5,7},{6,4},{7,5},{8,10},{9,11},{10,... | collective-permute-start | bytes 1179656 | tf_op jit(solution)/shard_map/ppermute | solution.py:28
  136.4 16.3 %collective-permute-start.17 = (f32[128,1536]{1,0:T(8,128)S(1)}, f32[128,1536]{1,0:T(8,128)S(1)}, u32[]{:S(2)}, u32[]{:S(2)}) collective-permute-start(f32[128,1536]{1,0:T(8,128)S(1)} %pad_maximum_fusion.17), channel_id=1, source_target_pairs={{0,2},{1,3},{2,0},{3,1},{4,6},{5,7},{6,4},{7,5},{8,10},{9,11},{10,... | collective-permute-start | bytes 2359304 | tf_op jit(solution)/shard_map/ppermute | solution.py:28
  143.6 12.1 %collective-permute-start.13 = (f32[128,1536]{1,0:T(8,128)S(1)}, f32[128,1536]{1,0:T(8,128)S(1)}, u32[]{:S(2)}, u32[]{:S(2)}) collective-permute-start(f32[128,1536]{1,0:T(8,128)S(1)} %pad_maximum_fusion.16), channel_id=1, source_target_pairs={{0,1},{1,0},{2,3},{3,2},{4,5},{5,4},{6,7},{7,6},{8,9},{9,8},{10,11... | collective-permute-start | bytes 2359304 | tf_op jit(solution)/shard_map/ppermute | solution.py:28
  198.1 12.3 %collective-permute-start.23 = (f32[128,1536]{1,0:T(8,128)}, f32[128,1536]{1,0:T(8,128)}, u32[]{:S(2)}, u32[]{:S(2)}) collective-permute-start(f32[128,1536]{1,0:T(8,128)} %pad_maximum_fusion.18), channel_id=1, source_target_pairs={{0,2},{1,3},{2,0},{3,1},{4,6},{5,7},{6,4},{7,5},{8,10},{9,11},{10,... | collective-permute-start | bytes 2359304 | tf_op jit(solution)/shard_map/ppermute | solution.py:28
  230.4 17.6 %collective-permute-start.26 = (f32[128,1536]{1,0:T(8,128)S(1)}, f32[128,1536]{1,0:T(8,128)S(1)}, u32[]{:S(2)}, u32[]{:S(2)}) collective-permute-start(f32[128,1536]{1,0:T(8,128)S(1)} %get-tuple-element.517), channel_id=1, source_target_pairs={{0,1},{1,0},{2,3},{3,2},{4,5},{5,4},{6,7},{7,6},{8,9},{9,8},{10,11... | collective-permute-start | bytes 2359304 | tf_op jit(solution)/shard_map/ppermute | solution.py:28
  230.8 17.2 %collective-permute-start.27 = (f32[128,1536]{1,0:T(8,128)S(1)}, f32[128,1536]{1,0:T(8,128)S(1)}, u32[]{:S(2)}, u32[]{:S(2)}) collective-permute-start(f32[128,1536]{1,0:T(8,128)S(1)} %get-tuple-element.516), channel_id=1, source_target_pairs={{0,2},{1,3},{2,0},{3,1},{4,6},{5,7},{6,4},{7,5},{8,10},{9,11},{10,... | collective-permute-start | bytes 2359304 | tf_op jit(solution)/shard_map/ppermute | solution.py:28
  245.2 20.9 %collective-permute-start.41 = (f32[1536,384]{1,0:T(8,128)S(1)}, f32[1536,384]{1,0:T(8,128)S(1)}, u32[]{:S(2)}, u32[]{:S(2)}) collective-permute-start(f32[1536,384]{1,0:T(8,128)S(1)} %convolution_bitcast_fusion.1), channel_id=1, source_target_pairs={{0,16},{16,0},{1,17},{17,1},{2,18},{18,2},{3,19},{19,3},{4,20},{20... | collective-permute-start | bytes 7077896 | tf_op jit(solution)/shard_map/ppermute | solution.py:28
  248.1 18.4 %collective-permute-start.42 = (f32[1536,384]{1,0:T(8,128)S(1)}, f32[1536,384]{1,0:T(8,128)S(1)}, u32[]{:S(2)}, u32[]{:S(2)}) collective-permute-start(f32[1536,384]{1,0:T(8,128)S(1)} %fusion.147), channel_id=1, source_target_pairs={{0,16},{16,0},{1,17},{17,1},{2,18},{18,2},{3,19},{19,3},{4,20},{20... | collective-permute-start | bytes 7077896 | tf_op jit(solution)/shard_map/ppermute | solution.py:28
  249.3 15.3 %collective-permute-start.29 = (f32[64,1536]{1,0:T(8,128)S(1)}, f32[64,1536]{1,0:T(8,128)S(1)}, u32[]{:S(2)}, u32[]{:S(2)}) collective-permute-start(f32[64,1536]{1,0:T(8,128)S(1)} %get-tuple-element.513), channel_id=1, source_target_pairs={{0,2},{1,3},{2,0},{3,1},{4,6},{5,7},{6,4},{7,5},{8,10},{9,11},{10,... | collective-permute-start | bytes 1179656 | tf_op jit(solution)/shard_map/ppermute | solution.py:28
  251.5 13.1 %collective-permute-start.30 = (f32[64,1536]{1,0:T(8,128)S(1)}, f32[64,1536]{1,0:T(8,128)S(1)}, u32[]{:S(2)}, u32[]{:S(2)}) collective-permute-start(f32[64,1536]{1,0:T(8,128)S(1)} %get-tuple-element.511), channel_id=1, source_target_pairs={{0,1},{1,0},{2,3},{3,2},{4,5},{5,4},{6,7},{7,6},{8,9},{9,8},{10,11... | collective-permute-start | bytes 1179656 | tf_op jit(solution)/shard_map/ppermute | solution.py:28
  254.2 18.3 %collective-permute-start.34 = (f32[128,768]{1,0:T(8,128)}, f32[128,768]{1,0:T(8,128)}, u32[]{:S(2)}, u32[]{:S(2)}) collective-permute-start(f32[128,768]{1,0:T(8,128)} %get-tuple-element.454), channel_id=1, source_target_pairs={{4,0},{5,1},{6,2},{7,3},{20,16},{21,17},{22,18},{23,19}} | collective-permute-start | bytes 1179656 | tf_op jit(solution)/shard_map/ppermute | solution.py:152
  265.6 31.0 %collective-permute-start.32 = (f32[64,1536]{1,0:T(8,128)}, f32[64,1536]{1,0:T(8,128)}, u32[]{:S(2)}, u32[]{:S(2)}) collective-permute-start(f32[64,1536]{1,0:T(8,128)} %add_multiply_fusion.1), channel_id=1, source_target_pairs={{0,2},{1,3},{2,0},{3,1},{4,6},{5,7},{6,4},{7,5},{8,10},{9,11},{10,... | collective-permute-start | bytes 1179656 | tf_op jit(solution)/shard_map/ppermute | solution.py:28
  269.4 178.6 %reduce-scatter.7.cloned.1.call-start = ((), (), s32[]{:S(2)}) async-start(), calls=%async_computation.5 | async-start | bytes 3932160 | tf_op jit(solution)/shard_map/reduce_scatter | solution.py:726
  270.8 25.8 %collective-permute-start.33 = (f32[64,1536]{1,0:T(8,128)S(1)}, f32[64,1536]{1,0:T(8,128)S(1)}, u32[]{:S(2)}, u32[]{:S(2)}) collective-permute-start(f32[64,1536]{1,0:T(8,128)S(1)} %add_multiply_fusion), channel_id=1, source_target_pairs={{0,1},{1,0},{2,3},{3,2},{4,5},{5,4},{6,7},{7,6},{8,9},{9,8},{10,11... | collective-permute-start | bytes 1179656 | tf_op jit(solution)/shard_map/ppermute | solution.py:28
  299.3 19.0 %collective-permute-start.36 = (f32[128,1536]{1,0:T(8,128)S(1)}, f32[128,1536]{1,0:T(8,128)S(1)}, u32[]{:S(2)}, u32[]{:S(2)}) collective-permute-start(f32[128,1536]{1,0:T(8,128)S(1)} %pad_maximum_fusion.19), channel_id=1, source_target_pairs={{0,1},{1,0},{2,3},{3,2},{4,5},{5,4},{6,7},{7,6},{8,9},{9,8},{10,11... | collective-permute-start | bytes 2359304 | tf_op jit(solution)/shard_map/ppermute | solution.py:28
  306.1 20.5 %collective-permute-start.37 = (f32[128,1536]{1,0:T(8,128)S(1)}, f32[128,1536]{1,0:T(8,128)S(1)}, u32[]{:S(2)}, u32[]{:S(2)}) collective-permute-start(f32[128,1536]{1,0:T(8,128)S(1)} %pad_maximum_fusion.20), channel_id=1, source_target_pairs={{0,2},{1,3},{2,0},{3,1},{4,6},{5,7},{6,4},{7,5},{8,10},{9,11},{10,... | collective-permute-start | bytes 2359304 | tf_op jit(solution)/shard_map/ppermute | solution.py:28
  311.4 21.3 %collective-permute-start.38 = (f32[512,128]{1,0:T(8,128)S(1)}, f32[512,128]{1,0:T(8,128)S(1)}, u32[]{:S(2)}, u32[]{:S(2)}) collective-permute-start(f32[512,128]{1,0:T(8,128)S(1)} %constant_dynamic-slice_fusion.15), channel_id=1, source_target_pairs={{0,2},{1,3},{2,0},{3,1},{4,6},{5,7},{6,4},{7,5},{8,10},{9,11},{10,... | collective-permute-start | bytes 786440 | tf_op jit(solution)/shard_map/ppermute | solution.py:28
  343.6 32.4 %collective-permute-start.46 = (f32[1536,384]{1,0:T(8,128)}, f32[1536,384]{1,0:T(8,128)}, u32[]{:S(2)}, u32[]{:S(2)}) collective-permute-start(f32[1536,384]{1,0:T(8,128)} %fusion.141), channel_id=1, source_target_pairs={{0,16},{16,0},{1,17},{17,1},{2,18},{18,2},{3,19},{19,3},{4,20},{20... | collective-permute-start | bytes 7077896 | tf_op jit(solution)/shard_map/ppermute | solution.py:28
  343.7 20.1 %collective-permute-start.39 = (f32[128,1536]{1,0:T(8,128)S(1)}, f32[128,1536]{1,0:T(8,128)}, u32[]{:S(2)}, u32[]{:S(2)}) collective-permute-start(f32[128,1536]{1,0:T(8,128)S(1)} %get-tuple-element.503), channel_id=1, source_target_pairs={{0,1},{1,0},{2,3},{3,2},{4,5},{5,4},{6,7},{7,6},{8,9},{9,8},{10,11... | collective-permute-start | bytes 2359304 | tf_op jit(solution)/shard_map/ppermute | solution.py:28
  345.2 19.8 %collective-permute-start.40 = (f32[128,1536]{1,0:T(8,128)S(1)}, f32[128,1536]{1,0:T(8,128)}, u32[]{:S(2)}, u32[]{:S(2)}) collective-permute-start(f32[128,1536]{1,0:T(8,128)S(1)} %get-tuple-element.502), channel_id=1, source_target_pairs={{0,2},{1,3},{2,0},{3,1},{4,6},{5,7},{6,4},{7,5},{8,10},{9,11},{10,... | collective-permute-start | bytes 2359304 | tf_op jit(solution)/shard_map/ppermute | solution.py:28
  353.9 20.5 %collective-permute-start.47 = (f32[1536,128]{1,0:T(8,128)}, f32[1536,128]{1,0:T(8,128)}, u32[]{:S(2)}, u32[]{:S(2)}) collective-permute-start(f32[1536,128]{1,0:T(8,128)} %fusion.250), channel_id=1, source_target_pairs={{0,16},{16,0},{1,17},{17,1},{2,18},{18,2},{3,19},{19,3},{4,20},{20... | collective-permute-start | bytes 2359304 | tf_op jit(solution)/shard_map/ppermute | solution.py:28
  367.2 13.4 %collective-permute-start.43 = (f32[64,1536]{1,0:T(8,128)}, f32[64,1536]{1,0:T(8,128)S(1)}, u32[]{:S(2)}, u32[]{:S(2)}) collective-permute-start(f32[64,1536]{1,0:T(8,128)} %get-tuple-element.499), channel_id=1, source_target_pairs={{0,2},{1,3},{2,0},{3,1},{4,6},{5,7},{6,4},{7,5},{8,10},{9,11},{10,... | collective-permute-start | bytes 1179656 | tf_op jit(solution)/shard_map/ppermute | solution.py:28
  380.9 207.9 %reduce-scatter.9.cloned.1.call-start = ((), (), s32[]{:S(2)}) async-start(), calls=%async_computation.6 | async-start | bytes 5898240 | tf_op jit(solution)/shard_map/reduce_scatter | solution.py:726
  394.7 17.7 %collective-permute-start.51 = (f32[128,1536]{1,0:T(8,128)S(1)}, f32[128,1536]{1,0:T(8,128)S(1)}, u32[]{:S(2)}, u32[]{:S(2)}) collective-permute-start(f32[128,1536]{1,0:T(8,128)S(1)} %pad_maximum_fusion.22), channel_id=1, source_target_pairs={{0,2},{1,3},{2,0},{3,1},{4,6},{5,7},{6,4},{7,5},{8,10},{9,11},{10,... | collective-permute-start | bytes 2359304 | tf_op jit(solution)/shard_map/ppermute | solution.py:28
  395.9 17.0 %collective-permute-start.49 = (f32[128,1536]{1,0:T(8,128)S(1)}, f32[128,1536]{1,0:T(8,128)S(1)}, u32[]{:S(2)}, u32[]{:S(2)}) collective-permute-start(f32[128,1536]{1,0:T(8,128)S(1)} %pad_maximum_fusion.21), channel_id=1, source_target_pairs={{0,1},{1,0},{2,3},{3,2},{4,5},{5,4},{6,7},{7,6},{8,9},{9,8},{10,11... | collective-permute-start | bytes 2359304 | tf_op jit(solution)/shard_map/ppermute | solution.py:28
  468.5 13.9 %collective-permute-start.64 = (f32[1536,384]{1,0:T(8,128)}, f32[1536,384]{1,0:T(8,128)}, u32[]{:S(2)}, u32[]{:S(2)}) collective-permute-start(f32[1536,384]{1,0:T(8,128)} %fusion.139), channel_id=1, source_target_pairs={{0,16},{16,0},{1,17},{17,1},{2,18},{18,2},{3,19},{19,3},{4,20},{20... | collective-permute-start | bytes 7077896 | tf_op jit(solution)/shard_map/ppermute | solution.py:28
  481.0 19.1 %collective-permute-start.54 = (f32[128,768]{1,0:T(8,128)}, f32[128,768]{1,0:T(8,128)}, u32[]{:S(2)}, u32[]{:S(2)}) collective-permute-start(f32[128,768]{1,0:T(8,128)} %get-tuple-element.450), channel_id=1, source_target_pairs={{4,0},{5,1},{6,2},{7,3},{20,16},{21,17},{22,18},{23,19}} | collective-permute-start | bytes 1179656 | tf_op jit(solution)/shard_map/ppermute | solution.py:152
  489.1 193.5 %reduce-scatter.11.cloned.1.call-start = ((), (), s32[]{:S(2)}) async-start(), calls=%async_computation.7 | async-start | bytes 3932160 | tf_op jit(solution)/shard_map/reduce_scatter | solution.py:726
  509.4 12.0 %collective-permute-start.55 = (f32[8,1024]{1,0:T(8,128)S(1)}, f32[8,1024]{1,0:T(8,128)S(1)}, u32[]{:S(2)}, u32[]{:S(2)}) collective-permute-start(f32[8,1024]{1,0:T(8,128)S(1)} %pad_maximum_fusion.34), channel_id=1, source_target_pairs={{4,0},{8,4},{12,8},{5,1},{9,5},{13,9},{6,2},{10,6},{14,10},{7,3},{... | collective-permute-start | bytes 98312 | tf_op jit(solution)/shard_map/ppermute | solution.py:34
  524.1 14.7 %collective-permute-start.56 = (f32[512,128]{1,0:T(8,128)S(1)}, f32[512,128]{1,0:T(8,128)S(1)}, u32[]{:S(2)}, u32[]{:S(2)}) collective-permute-start(f32[512,128]{1,0:T(8,128)S(1)} %constant_dynamic-slice_fusion), channel_id=1, source_target_pairs={{0,2},{1,3},{2,0},{3,1},{4,6},{5,7},{6,4},{7,5},{8,10},{9,11},{10,... | collective-permute-start | bytes 786440 | tf_op jit(solution)/shard_map/ppermute | solution.py:28
  543.4 120.7 %collective-permute-start.76 = (f32[384,768]{1,0:T(8,128)S(1)}, f32[384,768]{1,0:T(8,128)}, u32[]{:S(2)}, u32[]{:S(2)}) collective-permute-start(f32[384,768]{1,0:T(8,128)S(1)} %copy-done.36), channel_id=1, source_target_pairs={{0,16},{16,0},{1,17},{17,1},{2,18},{18,2},{3,19},{19,3},{4,20},{20... | collective-permute-start | bytes 3538952 | tf_op jit(solution)/shard_map/ppermute | solution.py:28
  555.3 29.0 %collective-permute-start.62 = (f32[1536,384]{1,0:T(8,128)}, f32[1536,384]{1,0:T(8,128)}, u32[]{:S(2)}, u32[]{:S(2)}) collective-permute-start(f32[1536,384]{1,0:T(8,128)} %fusion.129), channel_id=1, source_target_pairs={{0,16},{16,0},{1,17},{17,1},{2,18},{18,2},{3,19},{19,3},{4,20},{20... | collective-permute-start | bytes 7077896 | tf_op jit(solution)/shard_map/ppermute | solution.py:28
  555.7 20.0 %collective-permute-start.57 = (f32[128,1536]{1,0:T(8,128)S(1)}, f32[128,1536]{1,0:T(8,128)S(1)}, u32[]{:S(2)}, u32[]{:S(2)}) collective-permute-start(f32[128,1536]{1,0:T(8,128)S(1)} %get-tuple-element.485), channel_id=1, source_target_pairs={{0,1},{1,0},{2,3},{3,2},{4,5},{5,4},{6,7},{7,6},{8,9},{9,8},{10,11... | collective-permute-start | bytes 2359304 | tf_op jit(solution)/shard_map/ppermute | solution.py:28
  557.2 19.9 %collective-permute-start.59 = (f32[128,1536]{1,0:T(8,128)S(1)}, f32[128,1536]{1,0:T(8,128)S(1)}, u32[]{:S(2)}, u32[]{:S(2)}) collective-permute-start(f32[128,1536]{1,0:T(8,128)S(1)} %get-tuple-element.484), channel_id=1, source_target_pairs={{0,2},{1,3},{2,0},{3,1},{4,6},{5,7},{6,4},{7,5},{8,10},{9,11},{10,... | collective-permute-start | bytes 2359304 | tf_op jit(solution)/shard_map/ppermute | solution.py:28
  565.0 17.6 %collective-permute-start.63 = (f32[1536,128]{1,0:T(8,128)}, f32[1536,128]{1,0:T(8,128)}, u32[]{:S(2)}, u32[]{:S(2)}) collective-permute-start(f32[1536,128]{1,0:T(8,128)} %fusion.251), channel_id=1, source_target_pairs={{0,16},{16,0},{1,17},{17,1},{2,18},{18,2},{3,19},{19,3},{4,20},{20... | collective-permute-start | bytes 2359304 | tf_op jit(solution)/shard_map/ppermute | solution.py:28
  576.5 12.2 %collective-permute-start.58 = (f32[64,1536]{1,0:T(8,128)}, f32[64,1536]{1,0:T(8,128)S(1)}, u32[]{:S(2)}, u32[]{:S(2)}) collective-permute-start(f32[64,1536]{1,0:T(8,128)} %get-tuple-element.481), channel_id=1, source_target_pairs={{0,2},{1,3},{2,0},{3,1},{4,6},{5,7},{6,4},{7,5},{8,10},{9,11},{10,... | collective-permute-start | bytes 1179656 | tf_op jit(solution)/shard_map/ppermute | solution.py:28
  582.6 102.8 %collective-permute-start.78 = (f32[384,512]{1,0:T(8,128)S(1)}, f32[384,512]{1,0:T(8,128)}, u32[]{:S(2)}, u32[]{:S(2)}) collective-permute-start(f32[384,512]{1,0:T(8,128)S(1)} %copy-done.64), channel_id=1, source_target_pairs={{0,16},{16,0},{1,17},{17,1},{2,18},{18,2},{3,19},{19,3},{4,20},{20... | collective-permute-start | bytes 2359304 | tf_op jit(solution)/shard_map/ppermute | solution.py:28
  597.6 66.6 %collective-permute-start.75 = (f32[384,768]{1,0:T(8,128)}, f32[384,768]{1,0:T(8,128)S(1)}, u32[]{:S(2)}, u32[]{:S(2)}) collective-permute-start(f32[384,768]{1,0:T(8,128)} %reduce-scatter.9.cloned.1.call-done.refs_0_), channel_id=1, source_target_pairs={{0,16},{16,0},{1,17},{17,1},{2,18},{18,2},{3,19},{19,3},{4,20},{20... | collective-permute-start | bytes 3538952 | tf_op jit(solution)/shard_map/ppermute | solution.py:28
  630.0 28.5 %collective-permute-start.68 = (f32[64,1536]{1,0:T(8,128)}, f32[64,1536]{1,0:T(8,128)}, u32[]{:S(2)}, u32[]{:S(2)}) collective-permute-start(f32[64,1536]{1,0:T(8,128)} %get-tuple-element.463), channel_id=1, source_target_pairs={{0,1},{1,0},{2,3},{3,2},{4,5},{5,4},{6,7},{7,6},{8,9},{9,8},{10,11... | collective-permute-start | bytes 1179656 | tf_op jit(solution)/shard_map/ppermute | solution.py:28
  637.0 23.4 %collective-permute-start.66 = (f32[64,1536]{1,0:T(8,128)}, f32[64,1536]{1,0:T(8,128)S(1)}, u32[]{:S(2)}, u32[]{:S(2)}) collective-permute-start(f32[64,1536]{1,0:T(8,128)} %get-tuple-element.462), channel_id=1, source_target_pairs={{0,2},{1,3},{2,0},{3,1},{4,6},{5,7},{6,4},{7,5},{8,10},{9,11},{10,... | collective-permute-start | bytes 1179656 | tf_op jit(solution)/shard_map/ppermute | solution.py:28
  659.8 18.8 %collective-permute-start.69 = (f32[128,1536]{1,0:T(8,128)S(1)}, f32[128,1536]{1,0:T(8,128)S(1)}, u32[]{:S(2)}, u32[]{:S(2)}) collective-permute-start(f32[128,1536]{1,0:T(8,128)S(1)} %pad_maximum_fusion.24), channel_id=1, source_target_pairs={{0,2},{1,3},{2,0},{3,1},{4,6},{5,7},{6,4},{7,5},{8,10},{9,11},{10,... | collective-permute-start | bytes 2359304 | tf_op jit(solution)/shard_map/ppermute | solution.py:28
  661.5 18.7 %collective-permute-start.67 = (f32[128,1536]{1,0:T(8,128)S(1)}, f32[128,1536]{1,0:T(8,128)S(1)}, u32[]{:S(2)}, u32[]{:S(2)}) collective-permute-start(f32[128,1536]{1,0:T(8,128)S(1)} %pad_maximum_fusion.23), channel_id=1, source_target_pairs={{0,1},{1,0},{2,3},{3,2},{4,5},{5,4},{6,7},{7,6},{8,9},{9,8},{10,11... | collective-permute-start | bytes 2359304 | tf_op jit(solution)/shard_map/ppermute | solution.py:28
  (267 other events, 2196.9 us)
Sparse Core Ops, SparseCore 0:
  269.5 90.9 reduce-scatter.4
  381.0 66.8 reduce-scatter.6
  489.2 90.8 reduce-scatter.8
  597.8 64.8 reduce-scatter.10

commit v3 on v2

--- a/solution.py
+++ b/solution.py
@@ -11,7 +11,10 @@
 CHUNK = 128
 LANES = 128
 PAD = 8
+SMALL = 96
+COST = 4
 VMEM = 20 * 1024 * 1024
+LARGE = 56 * 1024 * 1024
 epsilon = 1e-05
 HIGH = lax.Precision.HIGH
 HIGHEST = lax.Precision.HIGHEST
@@ -144,20 +147,21 @@
 
 def state_before(local, decay, reverse, windows):
     n = lax.axis_size("seq")
-    state = jnp.zeros_like(local)
     done = []
+    arrived = []
     before = local
     for hop in range(n - 1):
         source, target = (n - 1 - hop, n - 2 - hop) if reverse else (hop, hop + 1)
-        got = lax.ppermute(decay * state + local, "seq", [(source, target)])
+        leaving = local if hop == 0 else decay * before + local
+        got = lax.ppermute(leaving, "seq", [(source, target)])
         if hop < len(windows):
-            got, *result = tied(got, *windows[hop](before))
+            got, *result = tied(got, *windows[hop](before, done))
             done.append(result)
         before = got
-        state = state + got
+        arrived.append(got)
     for window in windows[n - 1 :]:
-        done.append(window(before))
-    return state, done
+        done.append(window(before, done))
+    return sum(arrived) if len(arrived) > 0 else jnp.zeros_like(local), done
 
 
 def rows_of(*shape):
@@ -177,7 +181,7 @@
     return pl.BlockSpec(spec.block_shape, lambda c: index(steps - 1 - c))
 
 
-def call(kernel, steps, outs, scratch, flops, *args, backward=False):
+def call(kernel, steps, outs, scratch, flops, *args, backward=False, vmem=VMEM):
     shapes = [jax.ShapeDtypeStruct(shape, F32) for shape, _ in outs]
     size = 4 * sum(a.size for a, _ in args) + 4 * sum(s.size for s in shapes)
 
@@ -191,8 +195,8 @@
         in_specs=[spec(blocks) for _, blocks in args],
         out_specs=[spec(blocks) for _, blocks in outs],
         scratch_shapes=scratch,
-        compiler_params=pltpu.CompilerParams(vmem_limit_bytes=VMEM),
-        cost_estimate=pl.CostEstimate(flops=flops, bytes_accessed=size, transcendentals=0),
+        compiler_params=pltpu.CompilerParams(vmem_limit_bytes=vmem),
+        cost_estimate=pl.CostEstimate(flops=flops // COST, bytes_accessed=size // COST, transcendentals=0),
     )(*[a for a, _ in args])
 
 
@@ -291,7 +295,7 @@
     for tile in range(inner // LANES):
         cols = slice(tile * LANES, (tile + 1) * LANES)
         weighted = v_out[:, cols] * spread_heads(weight, tile, width)
-        part = dot(maps, weighted)
+        part = dot(maps, weighted, precision=HIGHEST)
         fresh[0, :, cols] = part
         local[:, cols] = decay[:, cols] * local[:, cols] + part
 
@@ -304,7 +308,7 @@
     lower = lax.broadcasted_iota(jnp.int32, (CHUNK, CHUNK), 0) >= lax.broadcasted_iota(
         jnp.int32, (CHUNK, CHUNK), 1
     )
-    meet = dot(bc[:, n:], bc[:, :n], NT)
+    meet = dot(bc[:, n:], bc[:, :n], NT, HIGHEST)
     for tile in range(inner // LANES):
         cols = slice(tile * LANES, (tile + 1) * LANES)
         values = v[:, cols]
@@ -314,7 +318,7 @@
             head = tile * each + k
             spread = cum[:, head : head + 1] - cumt[head : head + 1, :]
             mixing = jnp.exp(jnp.where(lower, spread, NEG)) * meet
-            part = dot(mixing, stepped)
+            part = dot(mixing, stepped, precision=HIGHEST)
             result = part if k == 0 else jnp.where(lane < k * width, result, part)
         out[:, cols] = result + spread_heads(hp[2:3, :], tile, width) * values
 
@@ -337,7 +341,7 @@
         state = final[:, cols]
         states[0, :, cols] = state
         final[:, cols] = chdec[0, 0:1, cols] * state + fresh[0, :, cols]
-        y = yd[:, cols] + spread_heads(carried, tile, width) * dot(maps, state)
+        y = yd[:, cols] + spread_heads(carried, tile, width) * dot(maps, state, precision=HIGHEST)
         y_out[:, cols] = y
         g = gate[:, cols]
         gated = y * (g * sigmoid(g))
@@ -576,7 +580,7 @@
     return jnp.pad(rows, ((0, PAD - rows.shape[0]), (0, lanes - rows.shape[1])))
 
 
-def forward(current, w, first, extra, other_maps, taps):
+def forward(current, w, first, taps, beside):
     length = current.shape[0]
     inner = w["inner"].shape[1]
     heads = w["heads"]
@@ -589,7 +593,7 @@
     if first:
         whole = matmul(normed, w["state"], precision=HIGHEST)
         whole = jnp.concatenate([whole, taps], axis=0)
-        ip = matmul(after(normed, whole), w["inner"])
+        ip = matmul(after(normed, whole), w["inner"], precision=HIGHEST)
         if power_of_two(lax.axis_size("head")):
             wait = whole
             for distance in distances("head"):
@@ -601,7 +605,7 @@
         else:
             whole = gathered_columns(whole)
             wait = whole
-        gate = matmul(after(normed, wait), w["gate"])
+        gate = matmul(after(normed, wait), w["gate"], precision=HIGHEST)
         whole, gate = tied(whole, gate)
         taps = whole[length:]
         sp = whole[:length]
@@ -650,10 +654,11 @@
         (w["taps_i"], all_of(PAD, inner)),
         (taps_s, all_of(PAD, states)),
         (w["heads_rows"], all_of(PAD, LANES)),
+        vmem=LARGE,
     )
     decay = decay[0:1]
 
-    def inside(before):
+    def inside(before, done):
         return call(
             functools.partial(inner_kernel, width),
             chunks,
@@ -666,16 +671,13 @@
             (cum, b_lanes),
             (cumt, b_heads),
             (w["heads_rows"], all_of(PAD, LANES)),
+            vmem=LARGE,
         )
 
-    other_maps = gathered_rows(after(other_maps, chdec).T)
-
-    def aside(before):
-        return [matmul(after(extra, before), w["last_out"])] if first else [extra]
-
-    entering, ((yd,), (extra,), (other_maps,)) = state_before(
-        local, decay, False, [inside, aside, lambda before: [other_maps]]
-    )
+    def aside(before, done):
+        return [beside]
+
+    entering, ((yd,), (beside,)) = state_before(local, decay, False, [inside, aside])
     y, gn, carried, squares, final = call(
         functools.partial(gate_kernel, width),
         chunks,
@@ -702,7 +704,7 @@
         dsi=dsi, dss=dss, dt=dt, cum=cum, cumt=cumt, fresh=fresh, chdec=chdec, decay=decay, y=y,
         gn=gn, states=carried, taps_s=taps_s, final=final,
     )
-    return gn, squares[0:1], saved, extra, other_maps, taps
+    return gn, squares[0:1], saved, taps, beside
 
 
 def core_products(left, right):
@@ -722,6 +724,67 @@
     return kept + exchanged(sent, "dp", 1)
 
 
+def pair_kernel(one, a, two, b, sent, kept):
+    width = a.shape[1] // 2
+    first = lax.axis_index("dp") == 0
+    for number, (left, right) in enumerate(((one, a), (two, b))):
+        product = dot(left[...].T, right[...])
+        cols = slice(number * width, (number + 1) * width)
+        sent[:, cols] = jnp.where(first, product[:, width:], product[:, :width])
+        kept[:, cols] = jnp.where(first, product[:, :width], product[:, width:])
+
+
+def pair_products(one, a, two, b):
+    length, model = one.shape
+    inner = a.shape[1]
+    tile = 256
+    out = ((model, inner), rows_of(tile, inner))
+    return call(
+        pair_kernel,
+        model // tile,
+        [out, out],
+        [],
+        4 * length * model * inner,
+        (one, columns_of(length, tile)),
+        (a, all_of(length, inner)),
+        (two, columns_of(length, tile)),
+        (b, all_of(length, inner)),
+        vmem=LARGE,
+    )
+
+
+def last_kernel(left, right, small, sent, kept):
+    width = right.shape[1] // 2
+    rows = left.shape[1]
+    first = lax.axis_index("dp") == 0
+    turned = left[...].T
+    product = dot(turned, right[...])
+    sent[0, :rows, :] = jnp.where(first, product[:, width:], product[:, :width])
+    kept[0, :rows, :] = jnp.where(first, product[:, :width], product[:, width:])
+    below = dot(small[...].T, left[...])
+    size = SMALL // 2
+    sent[0, rows:, :] = jnp.where(first, below[size : 2 * size], below[:size])
+    kept[0, rows:, :] = jnp.where(first, below[:size], below[size : 2 * size])
+
+
+def last_products(left, right, small):
+    length, model = left.shape
+    inner = right.shape[1]
+    shards = lax.axis_size("seq")
+    rows = model // shards
+    out = ((shards, rows + SMALL // 2, inner // 2), rows_of(1, rows + SMALL // 2, inner // 2))
+    return call(
+        last_kernel,
+        shards,
+        [out, out],
+        [],
+        2 * length * model * (inner + LANES),
+        (left, columns_of(length, rows)),
+        (right, all_of(length, inner)),
+        (small, all_of(length, LANES)),
+    )
+
+
 def over_seq(total):
     return lax.psum_scatter(total, "seq", scatter_dimension=0, tiled=True)
 
@@ -744,11 +807,10 @@
             out[layer, :, width:] = mine[...]
 
 
-def cores_joined(pairs, start, width):
+def cores_joined(pairs, start, width, rows):
     if lax.axis_size("dp") != 2:
-        return jnp.stack([mine[:, start : start + width] for mine, _ in pairs], axis=0)
+        return jnp.stack([mine[:rows, start : start + width] for mine, _ in pairs], axis=0)
     pieces = [piece for pair in pairs for piece in pair]
-    rows = pieces[0].shape[0]
     tile = 96 if rows % 96 == 0 else rows
     return pl.pallas_call(
         place_kernel,
@@ -760,7 +822,7 @@
     )(*pieces)
 
 
-def backward(grad, q, scale, slope, w, saved, beside, waiting):
+def backward(grad, q, scale, slope, w, saved, beside, waiting, earlier, final):
     s = saved
     length, inner = q.shape
     width = inner // w["heads"]
@@ -795,14 +857,19 @@
         (s["chdec"], b_decay),
     )
 
-    def cross_out(before):
-        return core_products(grad, after(u, before))
-
-    def cross_gate(before):
-        result = core_products(s["normed"], after(dgate, before))
+    def cross(before, done):
+        if lax.axis_size("dp") == 2:
+            result = pair_products(grad, after(u, before), s["normed"], dgate)
+        else:
+            result = [
+                jnp.concatenate(both, axis=1)
+                for both in zip(core_products(grad, u), core_products(s["normed"], dgate))
+            ]
+        if waiting is not None:
+            result = (*result, waiting)
         return beside.advance(*result) if beside is not None else result
 
-    def inside(before):
+    def inside(before, done):
         result = call(
             functools.partial(back_kernel, width),
             chunks,
@@ -819,12 +886,12 @@
         )
         return beside.advance(*result) if beside is not None else result
 
-    later, (halves_out, halves_gate, (du, dbc)) = state_before(
-        local, s["decay"], True, [cross_out, cross_gate, inside]
-    )
-    pair = jnp.concatenate([over_cores(*halves_out), over_cores(*halves_gate)], axis=1)
-    if waiting is not None:
-        pair = after(pair, waiting)
+    def summed(before, done):
+        result = [over_cores(*done[0][:2])]
+        return beside.advance(*result) if beside is not None else result
+
+
+    later, (_, (du, dbc), (pair, *_)) = state_before(local, s["decay"], True, [cross, inside, summed])
     pair = over_seq(pair)
     dti, dts, dstep, rows = call(
         functools.partial(close_kernel, width),
@@ -854,6 +921,7 @@
         (s["final"], b_state),
         (later, b_state),
         backward=True,
+        vmem=LARGE,
     )
     if beside is not None:
         dti, dts = beside.advance(dti, dts)
@@ -888,13 +956,12 @@
         (s["taps_s"], all_of(PAD, states)),
         backward=True,
     )
-    if beside is not None:
-        (dip,) = beside.advance(dip)
-
-    def product(base, dip, dmaps):
-        return base + matmul(dip, w["inner"], NT) + matmul(dmaps, w["maps"])
-
     gains = []
+
+    def product(base, dip, dmaps, scaled):
+        total = base + matmul(dip, w["inner"], NT) + matmul(dmaps, w["maps"])
+        gains.append(jnp.sum(total * scaled, axis=0))
+        return total
 
     def finish(rows_grad, offset):
         def take(array):
@@ -903,12 +970,11 @@
         x, root = take(s["current"]), take(s["root"])
         scaled = rows_grad * w["pre_gain"][None, :]
         along = jnp.mean(scaled * x, axis=-1, keepdims=True)
-        gains.append(jnp.sum(rows_grad * x * root, axis=0))
         return root * scaled - x * (root * root * root * along)
 
     shared = dsp
     own = states // lax.axis_size("head")
-    lefts = [base, dip, jnp.concatenate([dsp, dstep], axis=1)]
+    lefts = [base, dip, jnp.concatenate([dsp, dstep], axis=1), s["current"] * s["root"]]
     if power_of_two(lax.axis_size("head")):
         way = distances("head")[::-1]
         for number, distance in enumerate(way):
@@ -922,31 +988,54 @@
         shared = lax.psum_scatter(shared, "head", scatter_dimension=1, tiled=True)
         steps = Steps(head_sum(lefts, product, finish))
         steps.advance()
-    halves = core_products(s["normed"], after(dip, shared))
-    if waiting is None:
-        (pair,) = steps.advance(pair)
+    def folded(array):
+        return array.reshape(-1, PAD, array.shape[1]).sum(axis=1)
+
+    ri, rs, rows = folded(ri), folded(rs), folded(rows)
+    over_heads = jnp.concatenate([gains[0] + gains[1], rs.reshape(-1)])
+    flat = jnp.concatenate(
+        [ri.reshape(-1), dgain.sum(axis=0), rows[0], rows[1, :LANES], rows[2, :LANES]]
+    )
+    small_parts = [*earlier, (over_heads, flat)]
+    (dip,) = steps.advance(dip)
+    if final:
+        over_heads = jnp.concatenate([part[0] for part in small_parts])
+        over_heads = small_sum(after(over_heads, dip), "head")
+    shards = lax.axis_size("seq")
+    model = s["normed"].shape[1]
+    small = jnp.concatenate([shared, dstep[:, : LANES - own]], axis=1)
+    if lax.axis_size("dp") == 2 and model // shards % LANES == 0:
+        sent, kept = last_products(s["normed"], dip, small)
+        if final:
+            sent, pair = tied(sent, pair)
+        last = over_cores(sent, kept)
     else:
-        steps.advance()
-    small = jnp.concatenate([shared, dstep[:, : LANES - own]], axis=1)
-    total_small = small_sum(matmul(s["normed"], after(small, halves), ((0,), (0,))), "dp")
-    last = jnp.concatenate([over_cores(*halves), total_small], axis=1)
-    if waiting is None:
+        last = over_cores(*core_products(s["normed"], dip)).reshape(shards, -1, inner // lax.axis_size("dp"))
+        small = matmul(small[:, :SMALL], s["normed"], ((0,), (0,)))
+        small = jnp.transpose(small.reshape(SMALL, shards, -1), (1, 0, 2))
+        if lax.axis_size("dp") == 2:
+            place = lax.axis_index("dp")
+            small = over_cores(half(small, 1 - place, 1), half(small, place, 1))
+        else:
+            small = lax.psum(small, "dp")
+        small = jnp.pad(small, ((0, 0), (0, 0), (0, last.shape[2] - small.shape[2])))
+        last = jnp.concatenate([last, small], axis=1)
+    last = last.reshape(-1, last.shape[2])
+    if final:
         (last,) = steps.advance(last)
     else:
         last, pair = steps.advance(last, pair)
     last = over_seq(after(last, pair))
+    if not final:
+        branch = steps.finished()
+        return grad + branch, pair, last, small_parts, own
+    (over_heads,) = steps.advance(over_heads)
+    flat = jnp.concatenate([over_heads] + [part[1] for part in small_parts])
+    flat = small_sum(small_sum(flat, "dp"), "seq")
+    flat, last = steps.advance(flat, last)
     branch = steps.finished()
-    grad = grad + branch
-
-    def folded(array):
-        return array.reshape(-1, PAD, array.shape[1]).sum(axis=1)
-
-    ri, rs, rows = folded(ri), folded(rs), folded(rows)
-    over_heads = jnp.concatenate([gains[0] + gains[1], rs.reshape(-1)])
-    flat = jnp.concatenate(
-        [ri.reshape(-1), dgain.sum(axis=0), rows[0], rows[1, :LANES], rows[2, :LANES]]
-    )
-    return grad, pair, last, over_heads, flat, own
+    sizes = (small_parts[0][0].size, small_parts[0][1].size)
+    return grad + branch, pair, last, (flat, sizes), own
 
 
 def small_grads(over_heads, flat, own, w):
@@ -979,12 +1068,6 @@
     if not power_of_two(lax.axis_size("head")):
         return lax.all_gather(value, "head", axis=1, tiled=True)
     return gather_back(value, "head", distances("head")[::-1], 1)
-
-
-def gathered_rows(value):
-    if not power_of_two(lax.axis_size("head")):
-        return lax.all_gather(value, "head", axis=0, tiled=True)
-    return gather_back(value, "head", distances("head")[::-1], 0)
 
 
 def body(
@@ -1031,18 +1114,20 @@
                 ),
             )
         )
+    maps = jnp.concatenate([state_weight[layer].T for layer in range(layers)], axis=1)
+    maps = lax.all_gather(maps, "head", axis=0, tiled=True)
     current = tokens[0]
     grad = cotangent[0]
     kept = []
-    weights[0]["last_out"] = weights[layers - 1]["out"]
-    extra = grad
+    extra = None
     for layer in range(layers):
         w = weights[layer]
-        other = weights[(layer + 1) % layers]
-        gn, squares, saved, extra, maps, taps = forward(
-            current, w, layer == 0, extra, other["state"], taps
-        )
-        other["maps"] = jnp.concatenate([maps, after(other["step"], maps).T], axis=0)
+        gn, squares, saved, taps, maps = forward(current, w, layer == 0, taps, maps)
+        if layer == 0:
+            for number, other in enumerate(weights):
+                size = other["inner"].shape[0]
+                cut = maps[:, number * size : (number + 1) * size]
+                other["maps"] = jnp.concatenate([cut, other["step"].T], axis=0)
         last = layer == layers - 1
         if last:
             both = jnp.concatenate([squares, jnp.sum(extra * gn, axis=1)[None, :]], axis=0)
@@ -1055,44 +1140,49 @@
         def finish(rows, offset, scale=scale):
             return rows * lax.dynamic_slice_in_dim(scale[0], offset, rows.shape[0], 0)[:, None]
 
-        steps = Steps(head_sum([gn], lambda rows, w=w: matmul(rows, w["out"], NT), finish))
+        steps = Steps(head_sum([gn], lambda rows, w=w, p=HIGH if last else HIGHEST: matmul(rows, w["out"], NT, p), finish))
         if last:
             scale = after(scale, steps.now)
-            steps.advance(scale)
+        if layer == 0:
+            product = matmul(after(grad, steps.now), weights[layers - 1]["out"])
+            if not last:
+                steps.advance()
+                (product,) = steps.advance(product)
+            extra = product
         branch = None if last else steps.finished()
         kept.append((saved, scale, branch))
         if not last:
             current = current + branch
     collected = [None] * layers
     waiting = None
+    earlier = []
     for layer in reversed(range(layers)):
         w = weights[layer]
         saved, scale, branch = kept[layer]
         if layer < layers - 1:
-            q, waiting = tied(matmul(grad, w["out"]), waiting)
-            collected[layer + 1][1] = waiting
+            if layer == layers - 2:
+                (grad,) = steps.advance(grad)
+            q = matmul(grad, w["out"])
             slope = jnp.sum(grad * branch, axis=1)[None, :] * scale * scale / INNER
         else:
             q = extra
             slope = along * scale * scale * scale / INNER
         grad, *collected[layer] = backward(
-            grad, q, scale, slope, w, saved, steps if layer == layers - 1 else None, waiting
+            grad, q, scale, slope, w, saved, steps if layer == layers - 2 else None, waiting, earlier, layer == 0
         )
         waiting = collected[layer][1]
+        earlier = collected[layer][2]
     current = current + steps.finished()
-    over_heads = jnp.concatenate([entry[2] for entry in collected])
-    flat = jnp.concatenate([small_sum(over_heads, "head")] + [entry[3] for entry in collected])
-    flat = small_sum(small_sum(flat, "dp"), "seq")
-    size = collected[0][2].size
-    rest = collected[0][3].size
+    flat, (size, rest) = earlier
     results = []
     for layer in range(layers):
-        start = layers * size + layer * rest
+        number = layers - 1 - layer
+        start = layers * size + number * rest
         results.append(
             small_grads(
-                flat[layer * size : (layer + 1) * size],
+                flat[number * size : (number + 1) * size],
                 flat[start : start + rest],
-                collected[layer][4],
+                collected[layer][3],
                 weights[layer],
             )
         )
@@ -1104,17 +1194,27 @@
 
     pairs = [[with_other(entry[0]) for entry in collected]]
     half_width = inner // 2 if two else inner
+    rows = gate_weight.shape[1] // lax.axis_size("seq")
     large = {
-        "out": cores_joined(pairs[0], 0, half_width),
-        "gate": cores_joined(pairs[0], half_width, half_width),
+        "out": cores_joined(pairs[0], 0, half_width, rows),
+        "gate": cores_joined(pairs[0], half_width, half_width, rows),
     }
     collected[0][1], current, grad, stacked, large = tied(
         collected[0][1], current, grad, stacked, large
     )
     pairs.append([with_other(entry[1]) for entry in collected])
-    large["inner"] = cores_joined(pairs[1], 0, half_width)
-    small = jnp.stack([entry[1][:, half_width : half_width + LANES] for entry in collected], axis=0)
-    own = collected[0][4]
+    large["inner"] = cores_joined(pairs[1], 0, half_width, rows)
+    small = []
+    for mine, other in pairs[1]:
+        mine, other = mine[rows:, :rows], other[rows:, :rows]
+        if two:
+            mine = jnp.concatenate(
+                [jnp.where(lax.axis_index("dp") == 0, a, b) for a, b in ((mine, other), (other, mine))],
+                axis=0,
+            )
+        small.append(mine.T)
+    small = jnp.stack(small, axis=0)
+    own = collected[0][3]
     return (
         current[None],
         grad[None],

time: 708 us -> 670 us (0.946)
  Pallas kernels: 76.5 us -> 132 us
  matrix products: 145 us -> 100 us
  waiting for transfers between devices: 182 us -> 162 us
  local copies, waits for them, and re-layouts: 90.5 us -> 78.7 us
  other arithmetic: 92.6 us -> 81.3 us
    pallas_call x14 -> x18, Pallas kernels: 65.5 us -> 124 us  [call(): pl.pallas_call(kernel, grid=(steps,), out_shape=shapes, in_specs=[spec(bl...]
    dot_general x37 -> x23, matrix products: 145 us -> 100 us  [matmul(): return lax.dot_general(left, right, (dims, ((), ())), precision=precision)]
    ppermute x12, waiting for transfers between devices: 1.6 us -> 24.9 us  [state_before(): got = lax.ppermute(leaving, 'seq', [(source, target)])]
    reduce_scatter x4, waiting for transfers between devices: 27.1 us -> 5.04 us  [over_seq(): return lax.psum_scatter(total, 'seq', scatter_dimension=0, tiled=True)]
    ppermute x63 -> x55, starting transfers between devices: 65 us -> 49 us  [exchanged(): return lax.ppermute(value, axis, [(i, i ^ distance) for i in range(n)])]
    ppermute x63 -> x55, waiting for transfers between devices: 148 us -> 132 us  [exchanged(): return lax.ppermute(value, axis, [(i, i ^ distance) for i in range(n)])]
    unnamed x477 -> x409, local copies, waits for them, and re-layouts: 54.4 us -> 46.1 us
    ppermute x12, starting transfers between devices: 16.4 us -> 24.5 us  [state_before(): got = lax.ppermute(leaving, 'seq', [(source, target)])]
  transfers between devices with their start and end apart: 83 -> 76, of which waited for: 38 -> 33; matrix products, arithmetic and copies ran while one was open for 37% -> 29% of each run, Pallas kernels for 8% -> 17%
where the time goes in v3:
time: 670 us; the launch traced here: 664 us
  waiting for transfers between devices  162 us (24%)
  Pallas kernels  132 us (20%)
  matrix products  100 us (15%)
  starting transfers between devices  91.8 us (14%)
  other arithmetic  81.3 us (12%)
  local copies, waits for them, and re-layouts  78.7 us (12%)
  between operations  17.4 us (3%)
    ppermute x55, waiting for transfers between devices, exchanged(): return lax.ppermute(value, axis, [(i, i ^ distance) for i in range(n)])  132 us
    pallas_call x18, Pallas kernels, call(): pl.pallas_call(kernel, grid=(steps,), out_shape=shapes, in_specs=[spec(bl...  124 us
    dot_general x23, matrix products, matmul(): return lax.dot_general(left, right, (dims, ((), ())), precision=precision)  100 us
    ppermute x55, starting transfers between devices, exchanged(): return lax.ppermute(value, axis, [(i, i ^ distance) for i in range(n)])  49 us
    unnamed x409, local copies, waits for them, and re-layouts  46.1 us
    ppermute x12, waiting for transfers between devices, state_before(): got = lax.ppermute(leaving, 'seq', [(source, target)])  24.9 us
    ppermute x12, starting transfers between devices, state_before(): got = lax.ppermute(leaving, 'seq', [(source, target)])  24.5 us
    ppermute x4, starting transfers between devices, shifted(): return lax.ppermute(value, axis, pairs)  17.9 us
  transfers between devices with their start and end apart: 76, of which 33 were waited for; matrix products, arithmetic and copies ran while one was open for 29% of the time, Pallas kernels for 17%

profile of v3, /device:TPU:0, one launch (start us, length us, event | category | flops | bytes accessed | tf_op | source)
XLA Modules:
  0.0 664.1 jit_solution(16034715699694268110)
XLA Ops:
  19.3 4.2 broadcast_multiply_fusion.2
  27.0 9.0 %fusion.30.ip.pi = f32[512,768]{1,0:T(8,128)} fusion(f32[512,1536]{1,0:T(8,128)S(1)} %get-tuple-element.228.two.left, f32[2,1536,768]{2,1,0:T(8,128)S(1)} %copy-done.83), kind=kOutput, calls=%fused_computation.30 | convolution fusion | flops 7247757312 | bytes 9437184 | tf_op jit(solution)/shard_map/dot_general | solution.py:575
  40.0 10.1 %fusion.24.gate = f32[512,768]{1,0:T(8,128)} fusion(f32[512,1536]{1,0:T(8,128)S(1)} %get-tuple-element.228.two.left, f32[2,1536,768]{2,1,0:T(8,128)} %param.19), kind=kOutput, calls=%fused_computation.24 | convolution fusion | flops 7247757312 | bytes 9437184 | tf_op jit(solution)/shard_map/dot_general | solution.py:575
  51.0 4.0 collective-permute-start.2
  59.8 8.0 %shard_map.279 = (f32[512,768]{1,0:T(8,128)}, f32[512,256]{1,0:T(8,128)}, f32[512,768]{1,0:T(8,128)}, f32[512,256]{1,0:T(8,128)}, f32[512,128]{1,0:T(8,128)}, /*...) custom-call(f32[512,768]{1,0:T(8,128)} %fusion.30.ip.pi, ...), custom_call_target="tpu_custom_call" | custom-call | flops 75497472 | bytes 2317312 | tf_op jit(solution)/shard_map/pallas_call | solution.py:191
  67.9 3.6 collective-permute-start.3
  71.5 7.0 %shard_map.280.yd = f32[512,768]{1,0:T(8,128)} custom-call(f32[512,768]{1,0:T(8,128)} %get-tuple-element.232.v, f32[512,256]{1,0:T(8,128)} %get-tuple-element.233.bc, f32[512,128]{1,0:T(8,128)} %get-tuple-element.234.dt, f32[512,128]{1,0:T(8,128)} %get-tuple-element.235.cum, f32[16,512]{1,0:T(8,128)} %get-tuple-element.236.cumt, f32[8,128]{1,0:T(8,128)} %get-tuple-element.686.hp), custom_call_target="tpu_custom_call" | custom-call | flops 150994944 | bytes 1057792 | tf_op jit(solution)/shard_map/pallas_call | solution.py:191
  91.6 6.9 %fusion.20 = f32[256,1536]{1,0:T(8,128)S(1)} fusion(f32[2,1536,768]{2,1,0:T(8,128)} %param.31, f32[128,768]{1,0:T(8,128)S(1)} %get-tuple-element.619, f32[128,768]{1,0:T(8,128)S(1)} %get-tuple-element.617), kind=kOutput, calls=%fused_computation.20 | convolution fusion | flops 3624075264 | bytes 7077888 | tf_op jit(solution)/shard_map/dot_general | solution.py:575
  99.7 4.1 fusion.18
  105.7 4.1 fusion.14.q
  109.8 7.0 %collective-permute-done.9 = f32[1,512]{1,0:T(1,128)S(1)} collective-permute-done((f32[1,512]{1,0:T(1,128)S(1)}, f32[1,512]{1,0:T(1,128)S(1)}, u32[]{:S(2)}, u32[]{:S(2)}) %collective-permute-start.9) | collective-permute-done | bytes 2080 | tf_op jit(solution)/shard_map/ppermute | solution.py:31
  121.3 5.3 collective-permute-done.8
  130.6 4.0 collective-permute-done.11
  136.0 6.1 collective-permute-done.14
  144.1 9.8 %collective-permute-done.12 = f32[128,1536]{1,0:T(8,128)S(1)} collective-permute-done((f32[128,1536]{1,0:T(8,128)S(1)}, f32[128,1536]{1,0:T(8,128)S(1)}, u32[]{:S(2)}, u32[]{:S(2)}) %collective-permute-start.12) | collective-permute-done | bytes 786464 | tf_op jit(solution)/shard_map/ppermute | solution.py:31
  157.9 5.6 fusion.99.sp.ps
  163.7 4.3 fusion.8.ip.pi
  168.0 10.8 %collective-permute-start.16 = (f32[8,1024]{1,0:T(8,128)S(1)}, f32[8,1024]{1,0:T(8,128)S(1)}, u32[]{:S(2)}, u32[]{:S(2)}) collective-permute-start(f32[8,1024]{1,0:T(8,128)S(1)} %pad_maximum_fusion.25), channel_id=1, source_target_pairs={{0,4},{4,8},{8,12},{1,5},{5,9},{9,13},{2,6},{6,10},{10,14},{3,7},{... | collective-permute-start | bytes 98312 | tf_op jit(solution)/shard_map/ppermute | solution.py:37
  178.8 6.4 fusion.2.gate
  186.5 8.2 %shard_map.282 = (f32[512,768]{1,0:T(8,128)}, f32[512,256]{1,0:T(8,128)}, f32[512,768]{1,0:T(8,128)}, f32[512,256]{1,0:T(8,128)}, f32[512,128]{1,0:T(8,128)}, /*...) custom-call(f32[512,768]{1,0:T(8,128)} %copy-done.8, ...), custom_call_target="tpu_custom_call" | custom-call | flops 75497472 | bytes 2317312 | tf_op jit(solution)/shard_map/pallas_call | solution.py:191
  194.7 11.3 %collective-permute-start.17 = (f32[128,768]{1,0:T(8,128)}, f32[128,768]{1,0:T(8,128)S(1)}, u32[]{:S(2)}, u32[]{:S(2)}) collective-permute-start(f32[128,768]{1,0:T(8,128)} %get-tuple-element.254), channel_id=1, source_target_pairs={{0,4},{1,5},{2,6},{3,7},{16,20},{17,21},{18,22},{19,23}} | collective-permute-start | bytes 1179656 | tf_op jit(solution)/shard_map/ppermute | solution.py:156
  206.1 7.1 %shard_map.283.yd = f32[512,768]{1,0:T(8,128)} custom-call(f32[512,768]{1,0:T(8,128)} %get-tuple-element.255.v, f32[512,256]{1,0:T(8,128)} %get-tuple-element.256.bc, f32[512,128]{1,0:T(8,128)} %get-tuple-element.257.dt, f32[512,128]{1,0:T(8,128)} %get-tuple-element.258.cum, f32[16,512]{1,0:T(8,128)} %get-tuple-element.259.cumt, f32[8,128]{1,0:T(8,128)} %get-tuple-element.685.hp), custom_call_target="tpu_custom_call" | custom-call | flops 150994944 | bytes 1057792 | tf_op jit(solution)/shard_map/pallas_call | solution.py:191
  221.1 6.1 fusion.10
  231.2 3.9 shard_map.285
  239.3 13.4 %shard_map.286 = (f32[1536,768]{1,0:T(8,128)}, f32[1536,768]{1,0:T(8,128)}) custom-call(f32[512,1536]{1,0:T(8,128)} %bitcast.252, f32[512,768]{1,0:T(8,128)} %copy-done.41, f32[512,1536]{1,0:T(8,128)} %copy-done, f32[512,768]{1,0:T(8,128)} %copy-done.18), custom_call_target="tpu_custom_call" | custom-call | flops 603979776 | bytes 4718592 | tf_op jit(solution)/shard_map/pallas_call | solution.py:191
  254.7 8.1 %shard_map.287 = (f32[512,768]{1,0:T(8,128)S(1)}, f32[512,256]{1,0:T(8,128)S(1)}) custom-call(f32[512,768]{1,0:T(8,128)S(1)} %get-tuple-element.280.dy, f32[512,768]{1,0:T(8,128)S(1)} %copy-done.11, f32[512,256]{1,0:T(8,128)S(1)} %copy-done.13, f32[512,128]{1,0:T(8,128)S(1)} %copy-done.34, f32[512,128]{1,0:T(8,128)S(1)} %copy-done.15, ...), custom_call_target="tpu_custom_call" | custom-call | flops 377487360 | bytes 1974272 | tf_op jit(solution)/shard_map/pallas_call | solution.py:191
  272.3 20.9 %collective-permute-done.24 = f32[128,768]{1,0:T(8,128)S(1)} collective-permute-done((f32[128,768]{1,0:T(8,128)S(1)}, f32[128,768]{1,0:T(8,128)S(1)}, u32[]{:S(2)}, u32[]{:S(2)}) %collective-permute-start.24) | collective-permute-done | bytes 393248 | tf_op jit(solution)/shard_map/ppermute | solution.py:156
  298.9 10.2 %shard_map.288 = (f32[512,768]{1,0:T(8,128)}, f32[512,256]{1,0:T(8,128)}, f32[512,128]{1,0:T(8,128)}, f32[24,768]{1,0:T(8,128)}) custom-call(f32[512,768]{1,0:T(8,128)} %copy-done.26, f32[512,768]{1,0:T(8,128)} %copy-done.24, f32[512,768]{1,0:T(8,128)} %get-tuple-element.255.v, f32[512,768]{1,0:T(8,128)} %copy-done.40, f32[512,768]{1,0:T(8,128)} %get-tuple-element.285.dsi, ...), custom_call_target="tpu_custom_call" | custom-call | flops 150994944 | bytes 3910656 | tf_op jit(solution)/shard_map/pallas_call | solution.py:191
  312.2 6.4 fusion
  338.8 6.4 collective-permute-done.32
  345.5 15.5 %collective-permute-done.28 = f32[128,1536]{1,0:T(8,128)S(1)} collective-permute-done((f32[128,1536]{1,0:T(8,128)S(1)}, f32[128,1536]{1,0:T(8,128)S(1)}, u32[]{:S(2)}, u32[]{:S(2)}) %collective-permute-start.28) | collective-permute-done | bytes 786464 | tf_op jit(solution)/shard_map/ppermute | solution.py:31
  361.0 6.0 shard_map.290
  373.8 4.9 collective-permute-done.31
  384.1 9.0 %collective-permute-done.34 = f32[64,1536]{1,0:T(8,128)S(1)} collective-permute-done((f32[64,1536]{1,0:T(8,128)S(1)}, f32[64,1536]{1,0:T(8,128)S(1)}, u32[]{:S(2)}, u32[]{:S(2)}) %collective-permute-start.34) | collective-permute-done | bytes 393248 | tf_op jit(solution)/shard_map/ppermute | solution.py:31
  395.1 16.1 %collective-permute-done.35 = f32[128,1536]{1,0:T(8,128)S(1)} collective-permute-done((f32[128,1536]{1,0:T(8,128)S(1)}, f32[128,1536]{1,0:T(8,128)S(1)}, u32[]{:S(2)}, u32[]{:S(2)}) %collective-permute-start.35) | collective-permute-done | bytes 786464 | tf_op jit(solution)/shard_map/ppermute | solution.py:31
  418.3 4.3 fusion.16.q
  432.0 13.3 %shard_map.292 = (f32[1536,768]{1,0:T(8,128)}, f32[1536,768]{1,0:T(8,128)}) custom-call(f32[512,1536]{1,0:T(8,128)} %copy-done.77, f32[512,768]{1,0:T(8,128)} %copy-done.42, f32[512,1536]{1,0:T(8,128)} %copy-done.2, f32[512,768]{1,0:T(8,128)} %copy-done.16), custom_call_target="tpu_custom_call" | custom-call | flops 603979776 | bytes 4718592 | tf_op jit(solution)/shard_map/pallas_call | solution.py:191
  453.4 8.1 %shard_map.293 = (f32[512,768]{1,0:T(8,128)S(1)}, f32[512,256]{1,0:T(8,128)S(1)}) custom-call(f32[512,768]{1,0:T(8,128)S(1)} %copy-done.23, f32[512,768]{1,0:T(8,128)S(1)} %copy-done.10, f32[512,256]{1,0:T(8,128)S(1)} %copy-done.12, f32[512,128]{1,0:T(8,128)S(1)} %copy-done.33, f32[512,128]{1,0:T(8,128)S(1)} %copy-done.14, f32[16,512]{1,0:T(8,128)S(1)} %copy-done.62, ...), custom_call_target="tpu_custom_call" | custom-call | flops 377487360 | bytes 1974272 | tf_op jit(solution)/shard_map/pallas_call | solution.py:191
  476.6 4.0 collective-permute-done.49
  490.2 10.2 %shard_map.294 = (f32[512,768]{1,0:T(8,128)}, f32[512,256]{1,0:T(8,128)}, f32[512,128]{1,0:T(8,128)}, f32[24,768]{1,0:T(8,128)}) custom-call(f32[512,768]{1,0:T(8,128)} %copy-done.22, f32[512,768]{1,0:T(8,128)} %copy-done.20, f32[512,768]{1,0:T(8,128)} %get-tuple-element.232.v, f32[512,768]{1,0:T(8,128)} %copy-done.38, f32[512,768]{1,0:T(8,128)} %get-tuple-element.355.dsi, ...), custom_call_target="tpu_custom_call" | custom-call | flops 150994944 | bytes 3910656 | tf_op jit(solution)/shard_map/pallas_call | solution.py:191
  505.7 6.4 fusion.22
  532.3 4.9 collective-permute-done.56
  537.5 11.5 %collective-permute-done.52 = f32[128,1536]{1,0:T(8,128)S(1)} collective-permute-done((f32[128,1536]{1,0:T(8,128)S(1)}, f32[128,1536]{1,0:T(8,128)S(1)}, u32[]{:S(2)}, u32[]{:S(2)}) %collective-permute-start.52) | collective-permute-done | bytes 786464 | tf_op jit(solution)/shard_map/ppermute | solution.py:31
  550.2 6.0 shard_map.296
  559.2 4.9 reduce-scatter.9.cloned.1.call-done.refs_0_
  576.5 4.3 add.569
  622.0 6.3 collective-permute-done.65
  653.6 3.7 shard_map.299
  (812 shorter events, 284.7 us)
Async XLA Ops:
  7.2 74.6 %all-gather.2.cloned.1.call-start = ((), (), s32[]{:S(2)}) async-start(), calls=%async_computation.4 | async-start | bytes 3932160 | tf_op jit(solution)/shard_map/all_gather | solution.py:1118
  14.9 22.4 %collective-permute-start = (f32[528,64]{1,0:T(8,128)}, f32[528,64]{1,0:T(8,128)}, u32[]{:S(2)}, u32[]{:S(2)}) collective-permute-start(f32[528,64]{1,0:T(8,128)} %pad_maximum_fusion.19), channel_id=1, source_target_pairs={{0,1},{1,0},{2,3},{3,2},{4,5},{5,4},{6,7},{7,6},{8,9},{9,8},{10,11... | collective-permute-start | bytes 405512 | tf_op jit(solution)/shard_map/ppermute | solution.py:31
  18.9 360.9 %reduce-scatter.5.cloned.1.call-start = ((), (), s32[]{:S(2)}) async-start(), calls=%async_computation.5 | async-start | bytes 5898240 | tf_op jit(solution)/shard_map/reduce_scatter | solution.py:789
  38.4 11.7 %collective-permute-start.1 = (f32[528,128]{1,0:T(8,128)S(1)}, f32[528,128]{1,0:T(8,128)S(1)}, u32[]{:S(2)}, u32[]{:S(2)}) collective-permute-start(f32[528,128]{1,0:T(8,128)S(1)} %pad_maximum_fusion.20), channel_id=1, source_target_pairs={{0,2},{1,3},{2,0},{3,1},{4,6},{5,7},{6,4},{7,5},{8,10},{9,11},{10,... | collective-permute-start | bytes 811016 | tf_op jit(solution)/shard_map/ppermute | solution.py:31
  67.9 11.6 %collective-permute-start.3 = (f32[128,768]{1,0:T(8,128)}, f32[128,768]{1,0:T(8,128)S(1)}, u32[]{:S(2)}, u32[]{:S(2)}) collective-permute-start(f32[128,768]{1,0:T(8,128)} %get-tuple-element.231), channel_id=1, source_target_pairs={{0,4},{1,5},{2,6},{3,7},{16,20},{17,21},{18,22},{19,23}} | collective-permute-start | bytes 1179656 | tf_op jit(solution)/shard_map/ppermute | solution.py:156
  98.7 18.7 %collective-permute-start.6 = (f32[128,1536]{1,0:T(8,128)S(1)}, f32[128,1536]{1,0:T(8,128)S(1)}, u32[]{:S(2)}, u32[]{:S(2)}) collective-permute-start(f32[128,1536]{1,0:T(8,128)S(1)} %get-tuple-element.577), channel_id=1, source_target_pairs={{0,1},{1,0},{2,3},{3,2},{4,5},{5,4},{6,7},{7,6},{8,9},{9,8},{10,11... | collective-permute-start | bytes 2359304 | tf_op jit(solution)/shard_map/ppermute | solution.py:31
  99.2 18.2 %collective-permute-start.7 = (f32[128,1536]{1,0:T(8,128)S(1)}, f32[128,1536]{1,0:T(8,128)S(1)}, u32[]{:S(2)}, u32[]{:S(2)}) collective-permute-start(f32[128,1536]{1,0:T(8,128)S(1)} %get-tuple-element.576), channel_id=1, source_target_pairs={{0,2},{1,3},{2,0},{3,1},{4,6},{5,7},{6,4},{7,5},{8,10},{9,11},{10,... | collective-permute-start | bytes 2359304 | tf_op jit(solution)/shard_map/ppermute | solution.py:31
  104.0 12.9 %collective-permute-start.9 = (f32[1,512]{1,0:T(1,128)S(1)}, f32[1,512]{1,0:T(1,128)S(1)}, u32[]{:S(2)}, u32[]{:S(2)}) collective-permute-start(f32[1,512]{1,0:T(1,128)S(1)} %slice.491), channel_id=1, source_target_pairs={{0,1},{1,0},{2,3},{3,2},{4,5},{5,4},{6,7},{7,6},{8,9},{9,8},{10,11... | collective-permute-start | bytes 6152 | tf_op jit(solution)/shard_map/ppermute | solution.py:31
  130.0 12.0 %collective-permute-start.14 = (f32[64,1536]{1,0:T(8,128)S(1)}, f32[64,1536]{1,0:T(8,128)S(1)}, u32[]{:S(2)}, u32[]{:S(2)}) collective-permute-start(f32[64,1536]{1,0:T(8,128)S(1)} %add_multiply_fusion.6), channel_id=1, source_target_pairs={{0,1},{1,0},{2,3},{3,2},{4,5},{5,4},{6,7},{7,6},{8,9},{9,8},{10,11... | collective-permute-start | bytes 1179656 | tf_op jit(solution)/shard_map/ppermute | solution.py:31
  134.7 19.2 %collective-permute-start.12 = (f32[128,1536]{1,0:T(8,128)S(1)}, f32[128,1536]{1,0:T(8,128)S(1)}, u32[]{:S(2)}, u32[]{:S(2)}) collective-permute-start(f32[128,1536]{1,0:T(8,128)S(1)} %pad_maximum_fusion.10), channel_id=1, source_target_pairs={{0,1},{1,0},{2,3},{3,2},{4,5},{5,4},{6,7},{7,6},{8,9},{9,8},{10,11... | collective-permute-start | bytes 2359304 | tf_op jit(solution)/shard_map/ppermute | solution.py:31
  142.2 12.1 %collective-permute-start.15 = (f32[128,1536]{1,0:T(8,128)S(1)}, f32[128,1536]{1,0:T(8,128)S(1)}, u32[]{:S(2)}, u32[]{:S(2)}) collective-permute-start(f32[128,1536]{1,0:T(8,128)S(1)} %pad_maximum_fusion.11), channel_id=1, source_target_pairs={{0,2},{1,3},{2,0},{3,1},{4,6},{5,7},{6,4},{7,5},{8,10},{9,11},{10,... | collective-permute-start | bytes 2359304 | tf_op jit(solution)/shard_map/ppermute | solution.py:31
  168.0 17.3 %collective-permute-start.16 = (f32[8,1024]{1,0:T(8,128)S(1)}, f32[8,1024]{1,0:T(8,128)S(1)}, u32[]{:S(2)}, u32[]{:S(2)}) collective-permute-start(f32[8,1024]{1,0:T(8,128)S(1)} %pad_maximum_fusion.25), channel_id=1, source_target_pairs={{0,4},{4,8},{8,12},{1,5},{5,9},{9,13},{2,6},{6,10},{10,14},{3,7},{... | collective-permute-start | bytes 98312 | tf_op jit(solution)/shard_map/ppermute | solution.py:37
  194.7 19.3 %collective-permute-start.17 = (f32[128,768]{1,0:T(8,128)}, f32[128,768]{1,0:T(8,128)S(1)}, u32[]{:S(2)}, u32[]{:S(2)}) collective-permute-start(f32[128,768]{1,0:T(8,128)} %get-tuple-element.254), channel_id=1, source_target_pairs={{0,4},{1,5},{2,6},{3,7},{16,20},{17,21},{18,22},{19,23}} | collective-permute-start | bytes 1179656 | tf_op jit(solution)/shard_map/ppermute | solution.py:156
  238.6 14.1 %collective-permute-start.22 = (f32[128,768]{1,0:T(8,128)}, f32[128,768]{1,0:T(8,128)S(1)}, u32[]{:S(2)}, u32[]{:S(2)}) collective-permute-start(f32[128,768]{1,0:T(8,128)} %get-tuple-element.273), channel_id=1, source_target_pairs={{12,8},{13,9},{14,10},{15,11},{28,24},{29,25},{30,26},{31,27}} | collective-permute-start | bytes 1179656 | tf_op jit(solution)/shard_map/ppermute | solution.py:156
  252.7 15.3 %collective-permute-start.25 = (f32[1536,768]{1,0:T(8,128)}, f32[1536,768]{1,0:T(8,128)S(1)}, u32[]{:S(2)}, u32[]{:S(2)}) collective-permute-start(f32[1536,768]{1,0:T(8,128)} %get-tuple-element.292), channel_id=1, source_target_pairs={{0,16},{16,0},{1,17},{17,1},{2,18},{18,2},{3,19},{19,3},{4,20},{20... | collective-permute-start | bytes 14155784 | tf_op jit(solution)/shard_map/ppermute | solution.py:31
  265.3 27.9 %collective-permute-start.24 = (f32[128,768]{1,0:T(8,128)S(1)}, f32[128,768]{1,0:T(8,128)S(1)}, u32[]{:S(2)}, u32[]{:S(2)}) collective-permute-start(f32[128,768]{1,0:T(8,128)S(1)} %multiply_add_fusion.2), channel_id=1, source_target_pairs={{4,0},{5,1},{6,2},{7,3},{20,16},{21,17},{22,18},{23,19}} | collective-permute-start | bytes 1179656 | tf_op jit(solution)/shard_map/ppermute | solution.py:156
  293.2 153.4 %reduce-scatter.7.cloned.1.call-start = ((), (), s32[]{:S(2)}) async-start(), calls=%async_computation.6 | async-start | bytes 3317760 | tf_op jit(solution)/shard_map/reduce_scatter | solution.py:789
  321.5 14.3 %collective-permute-start.27 = (f32[512,128]{1,0:T(8,128)S(1)}, f32[512,128]{1,0:T(8,128)S(1)}, u32[]{:S(2)}, u32[]{:S(2)}) collective-permute-start(f32[512,128]{1,0:T(8,128)S(1)} %constant_dynamic-slice_fusion.26), channel_id=1, source_target_pairs={{0,2},{1,3},{2,0},{3,1},{4,6},{5,7},{6,4},{7,5},{8,10},{9,11},{10,... | collective-permute-start | bytes 786440 | tf_op jit(solution)/shard_map/ppermute | solution.py:31
  337.5 23.5 %collective-permute-start.28 = (f32[128,1536]{1,0:T(8,128)S(1)}, f32[128,1536]{1,0:T(8,128)S(1)}, u32[]{:S(2)}, u32[]{:S(2)}) collective-permute-start(f32[128,1536]{1,0:T(8,128)S(1)} %get-tuple-element.561), channel_id=1, source_target_pairs={{0,1},{1,0},{2,3},{3,2},{4,5},{5,4},{6,7},{7,6},{8,9},{9,8},{10,11... | collective-permute-start | bytes 2359304 | tf_op jit(solution)/shard_map/ppermute | solution.py:31
  338.2 22.8 %collective-permute-start.29 = (f32[128,1536]{1,0:T(8,128)S(1)}, f32[128,1536]{1,0:T(8,128)S(1)}, u32[]{:S(2)}, u32[]{:S(2)}) collective-permute-start(f32[128,1536]{1,0:T(8,128)S(1)} %get-tuple-element.560), channel_id=1, source_target_pairs={{0,2},{1,3},{2,0},{3,1},{4,6},{5,7},{6,4},{7,5},{8,10},{9,11},{10,... | collective-permute-start | bytes 2359304 | tf_op jit(solution)/shard_map/ppermute | solution.py:31
  367.2 11.6 %collective-permute-start.31 = (f32[64,1536]{1,0:T(8,128)S(1)}, f32[64,1536]{1,0:T(8,128)S(1)}, u32[]{:S(2)}, u32[]{:S(2)}) collective-permute-start(f32[64,1536]{1,0:T(8,128)S(1)} %get-tuple-element.555), channel_id=1, source_target_pairs={{0,1},{1,0},{2,3},{3,2},{4,5},{5,4},{6,7},{7,6},{8,9},{9,8},{10,11... | collective-permute-start | bytes 1179656 | tf_op jit(solution)/shard_map/ppermute | solution.py:31
  368.6 11.3 %collective-permute-start.30 = (f32[64,1536]{1,0:T(8,128)S(1)}, f32[64,1536]{1,0:T(8,128)S(1)}, u32[]{:S(2)}, u32[]{:S(2)}) collective-permute-start(f32[64,1536]{1,0:T(8,128)S(1)} %get-tuple-element.557), channel_id=1, source_target_pairs={{0,2},{1,3},{2,0},{3,1},{4,6},{5,7},{6,4},{7,5},{8,10},{9,11},{10,... | collective-permute-start | bytes 1179656 | tf_op jit(solution)/shard_map/ppermute | solution.py:31
  383.2 180.9 %reduce-scatter.9.cloned.1.call-start = ((), (), s32[]{:S(2)}) async-start(), calls=%async_computation.7 | async-start | bytes 5898240 | tf_op jit(solution)/shard_map/reduce_scatter | solution.py:789
  393.2 18.1 %collective-permute-start.35 = (f32[128,1536]{1,0:T(8,128)S(1)}, f32[128,1536]{1,0:T(8,128)S(1)}, u32[]{:S(2)}, u32[]{:S(2)}) collective-permute-start(f32[128,1536]{1,0:T(8,128)S(1)} %pad_maximum_fusion.12), channel_id=1, source_target_pairs={{0,1},{1,0},{2,3},{3,2},{4,5},{5,4},{6,7},{7,6},{8,9},{9,8},{10,11... | collective-permute-start | bytes 2359304 | tf_op jit(solution)/shard_map/ppermute | solution.py:31
  394.2 17.8 %collective-permute-start.37 = (f32[128,1536]{1,0:T(8,128)S(1)}, f32[128,1536]{1,0:T(8,128)S(1)}, u32[]{:S(2)}, u32[]{:S(2)}) collective-permute-start(f32[128,1536]{1,0:T(8,128)S(1)} %pad_maximum_fusion.13), channel_id=1, source_target_pairs={{0,2},{1,3},{2,0},{3,1},{4,6},{5,7},{6,4},{7,5},{8,10},{9,11},{10,... | collective-permute-start | bytes 2359304 | tf_op jit(solution)/shard_map/ppermute | solution.py:31
  413.7 32.9 %collective-permute-start.38 = (f32[128,1536]{1,0:T(8,128)S(1)}, f32[128,1536]{1,0:T(8,128)}, u32[]{:S(2)}, u32[]{:S(2)}) collective-permute-start(f32[128,1536]{1,0:T(8,128)S(1)} %get-tuple-element.549), channel_id=1, source_target_pairs={{0,1},{1,0},{2,3},{3,2},{4,5},{5,4},{6,7},{7,6},{8,9},{9,8},{10,11... | collective-permute-start | bytes 2359304 | tf_op jit(solution)/shard_map/ppermute | solution.py:31
  415.0 31.6 %collective-permute-start.39 = (f32[128,1536]{1,0:T(8,128)S(1)}, f32[128,1536]{1,0:T(8,128)}, u32[]{:S(2)}, u32[]{:S(2)}) collective-permute-start(f32[128,1536]{1,0:T(8,128)S(1)} %get-tuple-element.548), channel_id=1, source_target_pairs={{0,2},{1,3},{2,0},{3,1},{4,6},{5,7},{6,4},{7,5},{8,10},{9,11},{10,... | collective-permute-start | bytes 2359304 | tf_op jit(solution)/shard_map/ppermute | solution.py:31
  430.5 16.1 %collective-permute-start.42 = (f32[128,768]{1,0:T(8,128)S(1)}, f32[128,768]{1,0:T(8,128)}, u32[]{:S(2)}, u32[]{:S(2)}) collective-permute-start(f32[128,768]{1,0:T(8,128)S(1)} %get-tuple-element.322), channel_id=1, source_target_pairs={{12,8},{13,9},{14,10},{15,11},{28,24},{29,25},{30,26},{31,27}} | collective-permute-start | bytes 1179656 | tf_op jit(solution)/shard_map/ppermute | solution.py:156
  446.6 22.4 %collective-permute-start.45 = (f32[1536,768]{1,0:T(8,128)}, f32[1536,768]{1,0:T(8,128)S(1)}, u32[]{:S(2)}, u32[]{:S(2)}) collective-permute-start(f32[1536,768]{1,0:T(8,128)} %get-tuple-element.347), channel_id=1, source_target_pairs={{0,16},{16,0},{1,17},{17,1},{2,18},{18,2},{3,19},{19,3},{4,20},{20... | collective-permute-start | bytes 14155784 | tf_op jit(solution)/shard_map/ppermute | solution.py:31
  448.3 14.4 %collective-permute-start.41 = (f32[64,1536]{1,0:T(8,128)S(1)}, f32[64,1536]{1,0:T(8,128)S(1)}, u32[]{:S(2)}, u32[]{:S(2)}) collective-permute-start(f32[64,1536]{1,0:T(8,128)S(1)} %get-tuple-element.543), channel_id=1, source_target_pairs={{0,1},{1,0},{2,3},{3,2},{4,5},{5,4},{6,7},{7,6},{8,9},{9,8},{10,11... | collective-permute-start | bytes 1179656 | tf_op jit(solution)/shard_map/ppermute | solution.py:31
  451.0 11.7 %collective-permute-start.40 = (f32[64,1536]{1,0:T(8,128)S(1)}, f32[64,1536]{1,0:T(8,128)S(1)}, u32[]{:S(2)}, u32[]{:S(2)}) collective-permute-start(f32[64,1536]{1,0:T(8,128)S(1)} %get-tuple-element.545), channel_id=1, source_target_pairs={{0,2},{1,3},{2,0},{3,1},{4,6},{5,7},{6,4},{7,5},{8,10},{9,11},{10,... | collective-permute-start | bytes 1179656 | tf_op jit(solution)/shard_map/ppermute | solution.py:31
  463.8 11.1 %collective-permute-start.44 = (f32[64,1536]{1,0:T(8,128)}, f32[64,1536]{1,0:T(8,128)}, u32[]{:S(2)}, u32[]{:S(2)}) collective-permute-start(f32[64,1536]{1,0:T(8,128)} %add_multiply_fusion.2), channel_id=1, source_target_pairs={{0,1},{1,0},{2,3},{3,2},{4,5},{5,4},{6,7},{7,6},{8,9},{9,8},{10,11... | collective-permute-start | bytes 1179656 | tf_op jit(solution)/shard_map/ppermute | solution.py:31
  467.8 12.8 %collective-permute-start.49 = (f32[128,768]{1,0:T(8,128)}, f32[128,768]{1,0:T(8,128)}, u32[]{:S(2)}, u32[]{:S(2)}) collective-permute-start(f32[128,768]{1,0:T(8,128)} %multiply_add_fusion), channel_id=1, source_target_pairs={{4,0},{5,1},{6,2},{7,3},{20,16},{21,17},{22,18},{23,19}} | collective-permute-start | bytes 1179656 | tf_op jit(solution)/shard_map/ppermute | solution.py:156
  480.6 158.9 %reduce-scatter.11.cloned.1.call-start = ((), (), s32[]{:S(2)}) async-start(), calls=%async_computation.8 | async-start | bytes 3317760 | tf_op jit(solution)/shard_map/reduce_scatter | solution.py:789
  483.4 17.2 %collective-permute-start.47 = (f32[128,1536]{1,0:T(8,128)S(1)}, f32[128,1536]{1,0:T(8,128)S(1)}, u32[]{:S(2)}, u32[]{:S(2)}) collective-permute-start(f32[128,1536]{1,0:T(8,128)S(1)} %pad_maximum_fusion.15), channel_id=1, source_target_pairs={{0,2},{1,3},{2,0},{3,1},{4,6},{5,7},{6,4},{7,5},{8,10},{9,11},{10,... | collective-permute-start | bytes 2359304 | tf_op jit(solution)/shard_map/ppermute | solution.py:31
  485.8 16.8 %collective-permute-start.46 = (f32[128,1536]{1,0:T(8,128)S(1)}, f32[128,1536]{1,0:T(8,128)S(1)}, u32[]{:S(2)}, u32[]{:S(2)}) collective-permute-start(f32[128,1536]{1,0:T(8,128)S(1)} %pad_maximum_fusion.14), channel_id=1, source_target_pairs={{0,1},{1,0},{2,3},{3,2},{4,5},{5,4},{6,7},{7,6},{8,9},{9,8},{10,11... | collective-permute-start | bytes 2359304 | tf_op jit(solution)/shard_map/ppermute | solution.py:31
  514.8 12.9 %collective-permute-start.51 = (f32[512,128]{1,0:T(8,128)S(1)}, f32[512,128]{1,0:T(8,128)S(1)}, u32[]{:S(2)}, u32[]{:S(2)}) collective-permute-start(f32[512,128]{1,0:T(8,128)S(1)} %constant_dynamic-slice_fusion.2), channel_id=1, source_target_pairs={{0,2},{1,3},{2,0},{3,1},{4,6},{5,7},{6,4},{7,5},{8,10},{9,11},{10,... | collective-permute-start | bytes 786440 | tf_op jit(solution)/shard_map/ppermute | solution.py:31
  529.6 19.5 %collective-permute-start.52 = (f32[128,1536]{1,0:T(8,128)S(1)}, f32[128,1536]{1,0:T(8,128)S(1)}, u32[]{:S(2)}, u32[]{:S(2)}) collective-permute-start(f32[128,1536]{1,0:T(8,128)S(1)} %get-tuple-element.535), channel_id=1, source_target_pairs={{0,1},{1,0},{2,3},{3,2},{4,5},{5,4},{6,7},{7,6},{8,9},{9,8},{10,11... | collective-permute-start | bytes 2359304 | tf_op jit(solution)/shard_map/ppermute | solution.py:31
  530.2 18.9 %collective-permute-start.53 = (f32[128,1536]{1,0:T(8,128)S(1)}, f32[128,1536]{1,0:T(8,128)S(1)}, u32[]{:S(2)}, u32[]{:S(2)}) collective-permute-start(f32[128,1536]{1,0:T(8,128)S(1)} %get-tuple-element.534), channel_id=1, source_target_pairs={{0,2},{1,3},{2,0},{3,1},{4,6},{5,7},{6,4},{7,5},{8,10},{9,11},{10,... | collective-permute-start | bytes 2359304 | tf_op jit(solution)/shard_map/ppermute | solution.py:31
  564.1 12.4 %collective-permute-start.57 = (f32[4,432,384]{2,1,0:T(8,128)}, f32[4,432,384]{2,1,0:T(8,128)}, u32[]{:S(2)}, u32[]{:S(2)}) collective-permute-start(f32[4,432,384]{2,1,0:T(8,128)} %copy-done.76), channel_id=1, source_target_pairs={{0,16},{16,0},{1,17},{17,1},{2,18},{18,2},{3,19},{19,3},{4,20},{20... | collective-permute-start | bytes 7962632 | tf_op jit(solution)/shard_map/ppermute | solution.py:31
  566.1 65.7 %collective-permute-start.68 = (f32[384,768]{1,0:T(8,128)S(1)}, f32[384,768]{1,0:T(8,128)S(1)}, u32[]{:S(2)}, u32[]{:S(2)}) collective-permute-start(f32[384,768]{1,0:T(8,128)S(1)} %copy-done.30), channel_id=1, source_target_pairs={{0,16},{16,0},{1,17},{17,1},{2,18},{18,2},{3,19},{19,3},{4,20},{20... | collective-permute-start | bytes 3538952 | tf_op jit(solution)/shard_map/ppermute | solution.py:31
  569.4 11.6 %collective-permute-start.55 = (f32[64,1536]{1,0:T(8,128)}, f32[64,1536]{1,0:T(8,128)}, u32[]{:S(2)}, u32[]{:S(2)}) collective-permute-start(f32[64,1536]{1,0:T(8,128)} %get-tuple-element.529), channel_id=1, source_target_pairs={{0,1},{1,0},{2,3},{3,2},{4,5},{5,4},{6,7},{7,6},{8,9},{9,8},{10,11... | collective-permute-start | bytes 1179656 | tf_op jit(solution)/shard_map/ppermute | solution.py:31
  575.9 16.3 %collective-permute-start.60 = (f32[5632]{0:T(1024)}, f32[5632]{0:T(1024)}, u32[]{:S(2)}, u32[]{:S(2)}) collective-permute-start(f32[5632]{0:T(1024)} %pad_maximum_fusion.28), channel_id=1, source_target_pairs={{0,1},{1,0},{2,3},{3,2},{4,5},{5,4},{6,7},{7,6},{8,9},{9,8},{10,11... | collective-permute-start | bytes 67592 | tf_op jit(solution)/shard_map/ppermute | solution.py:31
  588.8 11.6 %collective-permute-start.58 = (f32[64,1536]{1,0:T(8,128)}, f32[64,1536]{1,0:T(8,128)}, u32[]{:S(2)}, u32[]{:S(2)}) collective-permute-start(f32[64,1536]{1,0:T(8,128)} %get-tuple-element.392), channel_id=1, source_target_pairs={{0,2},{1,3},{2,0},{3,1},{4,6},{5,7},{6,4},{7,5},{8,10},{9,11},{10,... | collective-permute-start | bytes 1179656 | tf_op jit(solution)/shard_map/ppermute | solution.py:31
  600.3 31.5 %collective-permute-start.67 = (f32[384,768]{1,0:T(8,128)S(1)}, f32[384,768]{1,0:T(8,128)S(1)}, u32[]{:S(2)}, u32[]{:S(2)}) collective-permute-start(f32[384,768]{1,0:T(8,128)S(1)} %copy-done.31), channel_id=1, source_target_pairs={{0,16},{16,0},{1,17},{17,1},{2,18},{18,2},{3,19},{19,3},{4,20},{20... | collective-permute-start | bytes 3538952 | tf_op jit(solution)/shard_map/ppermute | solution.py:31
  616.7 21.9 %collective-permute-start.63 = (f32[128,1536]{1,0:T(8,128)S(1)}, f32[128,1536]{1,0:T(8,128)S(1)}, u32[]{:S(2)}, u32[]{:S(2)}) collective-permute-start(f32[128,1536]{1,0:T(8,128)S(1)} %pad_maximum_fusion.17), channel_id=1, source_target_pairs={{0,2},{1,3},{2,0},{3,1},{4,6},{5,7},{6,4},{7,5},{8,10},{9,11},{10,... | collective-permute-start | bytes 2359304 | tf_op jit(solution)/shard_map/ppermute | solution.py:31
  619.6 19.8 %collective-permute-start.62 = (f32[128,1536]{1,0:T(8,128)S(1)}, f32[128,1536]{1,0:T(8,128)}, u32[]{:S(2)}, u32[]{:S(2)}) collective-permute-start(f32[128,1536]{1,0:T(8,128)S(1)} %pad_maximum_fusion.16), channel_id=1, source_target_pairs={{0,1},{1,0},{2,3},{3,2},{4,5},{5,4},{6,7},{7,6},{8,9},{9,8},{10,11... | collective-permute-start | bytes 2359304 | tf_op jit(solution)/shard_map/ppermute | solution.py:31
  631.8 18.4 %collective-permute-start.70 = (f32[432,384]{1,0:T(8,128)}, f32[432,384]{1,0:T(8,128)}, u32[]{:S(2)}, u32[]{:S(2)}) collective-permute-start(f32[432,384]{1,0:T(8,128)} %reduce-scatter.7.cloned.1.call-done.refs_2_), channel_id=1, source_target_pairs={{0,16},{16,0},{1,17},{17,1},{2,18},{18,2},{3,19},{19,3},{4,20},{20... | collective-permute-start | bytes 1990664 | tf_op jit(solution)/shard_map/ppermute | solution.py:31
  (226 other events, 2011.7 us)
Sparse Core Ops, SparseCore 0:
  19.0 44.5 all-gather.1
  293.3 83.6 reduce-scatter.4
  383.3 50.6 reduce-scatter.6
  480.7 83.3 reduce-scatter.8
  584.3 55.1 reduce-scatter.10

commit v4 on v3

--- a/solution.py
+++ b/solution.py
@@ -595,34 +595,29 @@
         whole = jnp.concatenate([whole, taps], axis=0)
         ip = matmul(after(normed, whole), w["inner"], precision=HIGHEST)
         if power_of_two(lax.axis_size("head")):
-            wait = whole
+            step = None
             for distance in distances("head"):
                 other = exchanged(whole, "head", distance)
                 if distance == 1:
                     other, ip = tied(other, ip)
-                    wait = other
+                elif step is None:
+                    step = matmul(after(normed, whole), w["step"], precision=HIGHEST)
+                    other, step = tied(other, step)
                 whole = joined(whole, other, "head", distance, 1)
         else:
             whole = gathered_columns(whole)
-            wait = whole
-        gate = matmul(after(normed, wait), w["gate"], precision=HIGHEST)
-        whole, gate = tied(whole, gate)
+        if not power_of_two(lax.axis_size("head")) or step is None:
+            step = matmul(normed, w["step"], precision=HIGHEST)
         taps = whole[length:]
         sp = whole[:length]
     else:
         ip = matmul(normed, w["inner"])
         sp = matmul(normed, w["maps"], NT, HIGHEST)
-        gate = None
     border = shifted(
         jnp.concatenate([ip[length - PAD :], sp[length - PAD :, :states]], axis=1), "seq", 1
     )
     if first:
-        step = matmul(after(normed, sp), w["step"], precision=HIGHEST)
-        border, step = tied(border, step)
         sp = jnp.concatenate([sp, step], axis=1)
-    else:
-        gate = matmul(after(normed, ip, sp), w["gate"])
-        border, gate = tied(border, gate)
     ib, sb = border[:, :inner], border[:, inner:]
     taps_s = taps[w["layer"] * PAD : (w["layer"] + 1) * PAD]
     b_inner, b_states, b_lanes = (rows_of(CHUNK, size) for size in (inner, states, LANES))
@@ -675,9 +670,10 @@
         )
 
     def aside(before, done):
-        return [beside]
-
-    entering, ((yd,), (beside,)) = state_before(local, decay, False, [inside, aside])
+        gate = matmul(after(normed, before), w["gate"], precision=HIGHEST if first else HIGH)
+        return [gate, beside]
+
+    entering, ((yd,), (gate, beside)) = state_before(local, decay, False, [inside, aside])
     y, gn, carried, squares, final = call(
         functools.partial(gate_kernel, width),
         chunks,
@@ -749,7 +745,6 @@
         (a, all_of(length, inner)),
         (two, columns_of(length, tile)),
         (b, all_of(length, inner)),
-        vmem=LARGE,
     )
 
 
@@ -819,6 +814,7 @@
         in_specs=[pl.BlockSpec((tile, width), lambda i: (i, start // width))] * len(pieces),
         out_specs=pl.BlockSpec((len(pairs), tile, 2 * width), lambda i: (0, i, 0)),
         compiler_params=pltpu.CompilerParams(vmem_limit_bytes=24 * 1024 * 1024),
+        cost_estimate=pl.CostEstimate(flops=0, bytes_accessed=0, transcendentals=0),
     )(*pieces)
 
 
@@ -1007,7 +1003,7 @@
     if lax.axis_size("dp") == 2 and model // shards % LANES == 0:
         sent, kept = last_products(s["normed"], dip, small)
         if final:
-            sent, pair = tied(sent, pair)
+            kept, pair = tied(kept, pair)
         last = over_cores(sent, kept)
     else:
         last = over_cores(*core_products(s["normed"], dip)).reshape(shards, -1, inner // lax.axis_size("dp"))
@@ -1032,36 +1028,74 @@
     (over_heads,) = steps.advance(over_heads)
     flat = jnp.concatenate([over_heads] + [part[1] for part in small_parts])
     flat = small_sum(small_sum(flat, "dp"), "seq")
-    flat, last = steps.advance(flat, last)
+    flat, last = tied(flat, last)
     branch = steps.finished()
     sizes = (small_parts[0][0].size, small_parts[0][1].size)
     return grad + branch, pair, last, (flat, sizes), own
 
 
-def small_grads(over_heads, flat, own, w):
-    model, inner = w["inner"].shape
-    states = w["states"]
-    heads = w["heads"]
-    g_pre, g_rs = over_heads[:model], over_heads[model:]
-    cut = []
-    start = 0
-    for size in (5 * inner, inner, inner, LANES, LANES):
-        cut.append(flat[start : start + size])
-        start += size
-    g_ri, g_norm, g_skip, g_rate, g_bias = cut
-    g_rs = lax.dynamic_slice_in_dim(g_rs.reshape(5, states), lax.axis_index("head") * own, own, 1)
-    g_ri = g_ri.reshape(5, inner)
-    return (
-        g_pre,
-        g_ri[:4],
-        g_ri[4],
-        g_rs[:4],
-        g_rs[4],
-        g_bias[:heads],
-        g_rate[:heads],
-        g_skip.reshape(heads, -1).sum(axis=1),
-        g_norm,
-    )
+def unpack_kernel(width, size, flat, pre, fi, fib, fs, fsb, bias, rate, skip, norm):
+    layers, model = pre.shape
+    inner = norm.shape[1]
+    own = fs.shape[2]
+    heads = bias.shape[1]
+    place = lax.axis_index("head")
+    shares = size // LANES - model // LANES
+    shares = shares * LANES // 5 // own
+    rest = 7 * inner // LANES + 2
+
+    def row(number):
+        return flat[number : number + 1, :]
+
+    for layer in range(layers):
+        number = layers - 1 - layer
+        base = number * size // LANES
+        for k in range(model // LANES):
+            pre[layer : layer + 1, k * LANES : (k + 1) * LANES] = row(base + k)
+        base += model // LANES
+        for tap in range(5):
+            chosen = None
+            for share in range(shares):
+                start = (tap * shares + share) * own
+                line, lane = divmod(start, LANES)
+                piece = row(base + line)[:, lane : lane + own]
+                chosen = piece if share == 0 else jnp.where(place == share, piece, chosen)
+            if tap < 4:
+                fs[layer, tap : tap + 1, :] = chosen
+            else:
+                fsb[layer : layer + 1, :] = chosen
+        base = layers * size // LANES + number * rest
+        sums = []
+        for k in range(inner // LANES):
+            cols = slice(k * LANES, (k + 1) * LANES)
+            for tap in range(4):
+                fi[layer, tap : tap + 1, cols] = row(base + tap * (inner // LANES) + k)
+            fib[layer : layer + 1, cols] = row(base + 4 * (inner // LANES) + k)
+            norm[layer : layer + 1, cols] = row(base + 5 * (inner // LANES) + k)
+            sums += head_totals(row(base + 6 * (inner // LANES) + k), width)
+        skip[layer : layer + 1, :] = place_heads(sums, (1, LANES))[:, :heads]
+        rate[layer : layer + 1, :] = row(base + rest - 2)[:, :heads]
+        bias[layer : layer + 1, :] = row(base + rest - 1)[:, :heads]
+
+
+def unpacked(flat, size, layers, model, inner, own, heads):
+    shapes = [
+        (layers, model),
+        (layers, 4, inner),
+        (layers, inner),
+        (layers, 4, own),
+        (layers, own),
+        (layers, heads),
+        (layers, heads),
+        (layers, heads),
+        (layers, inner),
+    ]
+    return pl.pallas_call(
+        functools.partial(unpack_kernel, inner // heads, size),
+        out_shape=[jax.ShapeDtypeStruct(shape, F32) for shape in shapes],
+        compiler_params=pltpu.CompilerParams(vmem_limit_bytes=VMEM),
+        cost_estimate=pl.CostEstimate(flops=0, bytes_accessed=0, transcendentals=0),
+    )(flat.reshape(-1, LANES))
 
 
 def gathered_columns(value):
@@ -1173,20 +1207,9 @@
         waiting = collected[layer][1]
         earlier = collected[layer][2]
     current = current + steps.finished()
-    flat, (size, rest) = earlier
-    results = []
-    for layer in range(layers):
-        number = layers - 1 - layer
-        start = layers * size + number * rest
-        results.append(
-            small_grads(
-                flat[number * size : (number + 1) * size],
-                flat[start : start + rest],
-                collected[layer][3],
-                weights[layer],
-            )
-        )
-    stacked = [jnp.stack([entry[number] for entry in results], axis=0) for number in range(9)]
+    flat, (size, _) = earlier
+    own = collected[0][3]
+    stacked = unpacked(flat, size, layers, gate_weight.shape[1], inner, own, heads)
     two = lax.axis_size("dp") == 2
 
     def with_other(part):
@@ -1199,9 +1222,7 @@
         "out": cores_joined(pairs[0], 0, half_width, rows),
         "gate": cores_joined(pairs[0], half_width, half_width, rows),
     }
-    collected[0][1], current, grad, stacked, large = tied(
-        collected[0][1], current, grad, stacked, large
-    )
+    collected[0][1], current, large = tied(collected[0][1], current, large)
     pairs.append([with_other(entry[1]) for entry in collected])
     large["inner"] = cores_joined(pairs[1], 0, half_width, rows)
     small = []
@@ -1214,7 +1235,6 @@
             )
         small.append(mine.T)
     small = jnp.stack(small, axis=0)
-    own = collected[0][3]
     return (
         current[None],
         grad[None],

time: 670 us -> 656 us (0.979)
  local copies, waits for them, and re-layouts: 78.7 us -> 64.9 us
  waiting for transfers between devices: 162 us -> 155 us
    unnamed x409 -> x391, local copies, waits for them, and re-layouts: 46.1 us -> 32.1 us
    ppermute x55, starting transfers between devices: 49 us -> 60.7 us  [exchanged(): return lax.ppermute(value, axis, [(i, i ^ distance) for i in range(n)])]
    ppermute x12, waiting for transfers between devices: 24.9 us -> 16.3 us  [state_before(): got = lax.ppermute(leaving, 'seq', [(source, target)])]
    ppermute x4, starting transfers between devices: 17.9 us -> 10.6 us  [shifted(): return lax.ppermute(value, axis, pairs)]
  transfers between devices with their start and end apart: 76 -> 76, of which waited for: 33 -> 34; matrix products, arithmetic and copies ran while one was open for 29% -> 29% of each run, Pallas kernels for 17% -> 17%
where the time goes in v4:
time: 656 us; the launch traced here: 650 us
  waiting for transfers between devices  155 us (24%)
  Pallas kernels  130 us (20%)
  matrix products  102 us (16%)
  starting transfers between devices  92.4 us (14%)
  other arithmetic  87.8 us (13%)
  local copies, waits for them, and re-layouts  64.9 us (10%)
  between operations  17.3 us (3%)
    ppermute x55, waiting for transfers between devices, exchanged(): return lax.ppermute(value, axis, [(i, i ^ distance) for i in range(n)])  130 us
    pallas_call x18, Pallas kernels, call(): pl.pallas_call(kernel, grid=(steps,), out_shape=shapes, in_specs=[spec(bl...  119 us
    dot_general x23, matrix products, matmul(): return lax.dot_general(left, right, (dims, ((), ())), precision=precision)  102 us
    ppermute x55, starting transfers between devices, exchanged(): return lax.ppermute(value, axis, [(i, i ^ distance) for i in range(n)])  60.7 us
    unnamed x391, local copies, waits for them, and re-layouts  32.1 us
    ppermute x12, starting transfers between devices, state_before(): got = lax.ppermute(leaving, 'seq', [(source, target)])  20.6 us
    ppermute x12, waiting for transfers between devices, state_before(): got = lax.ppermute(leaving, 'seq', [(source, target)])  16.3 us
    select_n x18, other arithmetic, joined(): jnp.where(first, mine, other)  15.9 us
  transfers between devices with their start and end apart: 76, of which 34 were waited for; matrix products, arithmetic and copies ran while one was open for 29% of the time, Pallas kernels for 17%

profile of v4, /device:TPU:0, one launch (start us, length us, event | category | flops | bytes accessed | tf_op | source)
XLA Modules:
  0.0 649.9 jit_solution(15375133802072451695)
XLA Ops:
  19.3 4.2 broadcast_multiply_fusion.2
  27.0 9.0 %fusion.30.ip.pi = f32[512,768]{1,0:T(8,128)} fusion(f32[512,1536]{1,0:T(8,128)S(1)} %get-tuple-element.233.two.left, f32[2,1536,768]{2,1,0:T(8,128)S(1)} %copy-done.81), kind=kOutput, calls=%fused_computation.30 | convolution fusion | flops 7247757312 | bytes 9437184 | tf_op jit(solution)/shard_map/dot_general | solution.py:575
  42.5 5.5 collective-permute-done.1
  54.2 8.0 %shard_map.279 = (f32[512,768]{1,0:T(8,128)}, f32[512,256]{1,0:T(8,128)}, f32[512,768]{1,0:T(8,128)}, f32[512,256]{1,0:T(8,128)}, f32[512,128]{1,0:T(8,128)}, /*...) custom-call(f32[512,768]{1,0:T(8,128)} %fusion.30.ip.pi, ...), custom_call_target="tpu_custom_call" | custom-call | flops 75497472 | bytes 2317312 | tf_op jit(solution)/shard_map/pallas_call | solution.py:191
  62.3 4.7 collective-permute-start.3
  68.6 7.0 %shard_map.280.yd = f32[512,768]{1,0:T(8,128)} custom-call(f32[512,768]{1,0:T(8,128)} %get-tuple-element.223.v, f32[512,256]{1,0:T(8,128)} %get-tuple-element.224.bc, f32[512,128]{1,0:T(8,128)} %get-tuple-element.225.dt, f32[512,128]{1,0:T(8,128)} %get-tuple-element.226.cum, f32[16,512]{1,0:T(8,128)} %get-tuple-element.227.cumt, f32[8,128]{1,0:T(8,128)} %get-tuple-element.637.hp), custom_call_target="tpu_custom_call" | custom-call | flops 150994944 | bytes 1057792 | tf_op jit(solution)/shard_map/pallas_call | solution.py:191
  77.9 10.1 %fusion.24.gate = f32[512,768]{1,0:T(8,128)} fusion(f32[512,1536]{1,0:T(8,128)S(1)} %get-tuple-element.233.two.left, f32[2,1536,768]{2,1,0:T(8,128)} %param.19), kind=kOutput, calls=%fused_computation.24 | convolution fusion | flops 7247757312 | bytes 9437184 | tf_op jit(solution)/shard_map/dot_general | solution.py:575
  101.1 6.9 %fusion.20 = f32[256,1536]{1,0:T(8,128)S(1)} fusion(f32[2,1536,768]{2,1,0:T(8,128)} %param.31, f32[128,768]{1,0:T(8,128)S(1)} %get-tuple-element.589, f32[128,768]{1,0:T(8,128)S(1)} %get-tuple-element.587), kind=kOutput, calls=%fused_computation.20 | convolution fusion | flops 3624075264 | bytes 7077888 | tf_op jit(solution)/shard_map/dot_general | solution.py:575
  110.8 4.1 fusion.18
  117.1 5.4 fusion.14.q
  129.7 7.5 %collective-permute-done.8 = f32[64,1536]{1,0:T(8,128)S(1)} collective-permute-done((f32[64,1536]{1,0:T(8,128)S(1)}, f32[64,1536]{1,0:T(8,128)S(1)}, u32[]{:S(2)}, u32[]{:S(2)}) %collective-permute-start.8) | collective-permute-done | bytes 393248 | tf_op jit(solution)/shard_map/ppermute | solution.py:31
  141.5 6.1 collective-permute-done.11
  155.2 7.2 %collective-permute-done.12 = f32[128,1536]{1,0:T(8,128)S(1)} collective-permute-done((f32[128,1536]{1,0:T(8,128)S(1)}, f32[128,1536]{1,0:T(8,128)S(1)}, u32[]{:S(2)}, u32[]{:S(2)}) %collective-permute-start.12) | collective-permute-done | bytes 786464 | tf_op jit(solution)/shard_map/ppermute | solution.py:31
  168.5 5.5 fusion.100.sp.ps
  174.2 4.3 fusion.8.ip.pi
  179.7 3.9 collective-permute-start.16
  186.4 8.1 %shard_map.282 = (f32[512,768]{1,0:T(8,128)}, f32[512,256]{1,0:T(8,128)}, f32[512,768]{1,0:T(8,128)}, f32[512,256]{1,0:T(8,128)}, f32[512,128]{1,0:T(8,128)}, /*...) custom-call(f32[512,768]{1,0:T(8,128)} %copy-done.9, ...), custom_call_target="tpu_custom_call" | custom-call | flops 75497472 | bytes 2317312 | tf_op jit(solution)/shard_map/pallas_call | solution.py:191
  194.5 5.9 collective-permute-start.17
  200.3 7.0 %shard_map.283.yd = f32[512,768]{1,0:T(8,128)} custom-call(f32[512,768]{1,0:T(8,128)} %get-tuple-element.245.v, f32[512,256]{1,0:T(8,128)} %get-tuple-element.246.bc, f32[512,128]{1,0:T(8,128)} %get-tuple-element.247.dt, f32[512,128]{1,0:T(8,128)} %get-tuple-element.248.cum, f32[16,512]{1,0:T(8,128)} %get-tuple-element.249.cumt, f32[8,128]{1,0:T(8,128)} %get-tuple-element.636.hp), custom_call_target="tpu_custom_call" | custom-call | flops 150994944 | bytes 1057792 | tf_op jit(solution)/shard_map/pallas_call | solution.py:191
  209.9 6.5 %fusion.2.gate = f32[512,768]{1,0:T(8,128)S(1)} fusion(f32[512,1536]{1,0:T(8,128)S(1)} %get-tuple-element.255.two.left, f32[2,1536,768]{2,1,0:T(8,128)} %param.19), kind=kOutput, calls=%fused_computation.2 | convolution fusion | flops 3623878656 | bytes 9437184 | tf_op jit(solution)/shard_map/dot_general | solution.py:575
  222.6 6.1 fusion.10
  238.0 9.8 %shard_map.286 = (f32[1536,768]{1,0:T(8,128)S(1)}, f32[1536,768]{1,0:T(8,128)S(1)}) custom-call(f32[512,1536]{1,0:T(8,128)S(1)} %bitcast.229, f32[512,768]{1,0:T(8,128)S(1)} %get-tuple-element.266.a, f32[512,1536]{1,0:T(8,128)S(1)} %get-tuple-element.255.two.left, f32[512,768]{1,0:T(8,128)S(1)} %get-tuple-element.287.b), custom_call_target="tpu_custom_call" | custom-call | flops 603979776 | bytes 4718592 | tf_op jit(solution)/shard_map/pallas_call | solution.py:191
  248.8 8.1 %shard_map.287 = (f32[512,768]{1,0:T(8,128)S(1)}, f32[512,256]{1,0:T(8,128)S(1)}) custom-call(f32[512,768]{1,0:T(8,128)S(1)} %get-tuple-element.271.dy, f32[512,768]{1,0:T(8,128)S(1)} %copy-done.12, f32[512,256]{1,0:T(8,128)S(1)} %copy-done.17, f32[512,128]{1,0:T(8,128)S(1)} %copy-done.39, f32[512,128]{1,0:T(8,128)S(1)} %copy-done.19, ...), custom_call_target="tpu_custom_call" | custom-call | flops 377487360 | bytes 1974272 | tf_op jit(solution)/shard_map/pallas_call | solution.py:191
  264.9 16.2 %collective-permute-done.24 = f32[128,768]{1,0:T(8,128)} collective-permute-done((f32[128,768]{1,0:T(8,128)}, f32[128,768]{1,0:T(8,128)}, u32[]{:S(2)}, u32[]{:S(2)}) %collective-permute-start.24) | collective-permute-done | bytes 393248 | tf_op jit(solution)/shard_map/ppermute | solution.py:156
  287.1 10.3 %shard_map.288 = (f32[512,768]{1,0:T(8,128)}, f32[512,256]{1,0:T(8,128)}, f32[512,128]{1,0:T(8,128)}, f32[24,768]{1,0:T(8,128)}) custom-call(f32[512,768]{1,0:T(8,128)} %copy-done.29, f32[512,768]{1,0:T(8,128)} %copy-done.28, f32[512,768]{1,0:T(8,128)} %get-tuple-element.245.v, f32[512,768]{1,0:T(8,128)} %copy-done.45, f32[512,768]{1,0:T(8,128)} %get-tuple-element.276.dsi, ...), custom_call_target="tpu_custom_call" | custom-call | flops 150994944 | bytes 3910656 | tf_op jit(solution)/shard_map/pallas_call | solution.py:191
  300.8 6.0 fusion
  327.4 6.1 collective-permute-done.32
  333.8 15.5 %collective-permute-done.28 = f32[128,1536]{1,0:T(8,128)S(1)} collective-permute-done((f32[128,1536]{1,0:T(8,128)S(1)}, f32[128,1536]{1,0:T(8,128)S(1)}, u32[]{:S(2)}, u32[]{:S(2)}) %collective-permute-start.28) | collective-permute-done | bytes 786464 | tf_op jit(solution)/shard_map/ppermute | solution.py:31
  349.3 6.3 shard_map.290
  362.5 5.7 collective-permute-done.31
  376.5 9.3 %collective-permute-done.34 = f32[64,1536]{1,0:T(8,128)S(1)} collective-permute-done((f32[64,1536]{1,0:T(8,128)}, f32[64,1536]{1,0:T(8,128)S(1)}, u32[]{:S(2)}, u32[]{:S(2)}) %collective-permute-start.34) | collective-permute-done | bytes 393248 | tf_op jit(solution)/shard_map/ppermute | solution.py:31
  388.4 16.6 %collective-permute-done.35 = f32[128,1536]{1,0:T(8,128)S(1)} collective-permute-done((f32[128,1536]{1,0:T(8,128)S(1)}, f32[128,1536]{1,0:T(8,128)S(1)}, u32[]{:S(2)}, u32[]{:S(2)}) %collective-permute-start.35) | collective-permute-done | bytes 786464 | tf_op jit(solution)/shard_map/ppermute | solution.py:31
  410.6 4.3 fusion.16.q
  415.0 3.9 shard_map.291
  422.6 9.8 %shard_map.292 = (f32[1536,768]{1,0:T(8,128)S(1)}, f32[1536,768]{1,0:T(8,128)S(1)}) custom-call(f32[512,1536]{1,0:T(8,128)S(1)} %maximum_add_fusion.1.one, f32[512,768]{1,0:T(8,128)S(1)} %get-tuple-element.314.a, f32[512,1536]{1,0:T(8,128)S(1)} %copy-done.1, f32[512,768]{1,0:T(8,128)S(1)} %get-tuple-element.358.b), custom_call_target="tpu_custom_call" | custom-call | flops 603979776 | bytes 4718592 | tf_op jit(solution)/shard_map/pallas_call | solution.py:191
  445.6 8.1 %shard_map.293 = (f32[512,768]{1,0:T(8,128)S(1)}, f32[512,256]{1,0:T(8,128)S(1)}) custom-call(f32[512,768]{1,0:T(8,128)S(1)} %copy-done.27, f32[512,768]{1,0:T(8,128)S(1)} %copy-done.11, f32[512,256]{1,0:T(8,128)S(1)} %copy-done.16, f32[512,128]{1,0:T(8,128)S(1)} %copy-done.38, f32[512,128]{1,0:T(8,128)S(1)} %copy-done.18, f32[16,512]{1,0:T(8,128)S(1)} %copy-done.63, ...), custom_call_target="tpu_custom_call" | custom-call | flops 377487360 | bytes 1974272 | tf_op jit(solution)/shard_map/pallas_call | solution.py:191
  483.4 11.0 %shard_map.294 = (f32[512,768]{1,0:T(8,128)}, f32[512,256]{1,0:T(8,128)}, f32[512,128]{1,0:T(8,128)}, f32[24,768]{1,0:T(8,128)}) custom-call(f32[512,768]{1,0:T(8,128)} %copy-done.26, f32[512,768]{1,0:T(8,128)} %copy-done.24, f32[512,768]{1,0:T(8,128)} %get-tuple-element.223.v, f32[512,768]{1,0:T(8,128)} %copy-done.43, f32[512,768]{1,0:T(8,128)} %get-tuple-element.346.dsi, ...), custom_call_target="tpu_custom_call" | custom-call | flops 150994944 | bytes 3910656 | tf_op jit(solution)/shard_map/pallas_call | solution.py:191
  497.6 6.4 fusion.22
  525.8 5.2 collective-permute-done.56
  531.3 10.2 %collective-permute-done.52 = f32[128,1536]{1,0:T(8,128)S(1)} collective-permute-done((f32[128,1536]{1,0:T(8,128)S(1)}, f32[128,1536]{1,0:T(8,128)S(1)}, u32[]{:S(2)}, u32[]{:S(2)}) %collective-permute-start.52) | collective-permute-done | bytes 786464 | tf_op jit(solution)/shard_map/ppermute | solution.py:31
  542.4 6.9 %shard_map.296 = (f32[4,432,384]{2,1,0:T(8,128)}, f32[4,432,384]{2,1,0:T(8,128)S(1)}) custom-call(f32[512,1536]{1,0:T(8,128)S(1)} %copy-done.2, f32[512,768]{1,0:T(8,128)S(1)} %get-tuple-element.370.right, f32[512,128]{1,0:T(8,128)S(1)} %pad_maximum_fusion.21.small), custom_call_target="tpu_custom_call" | custom-call | flops 352321536 | bytes 2572288 | tf_op jit(solution)/shard_map/pallas_call | solution.py:191
  568.7 4.3 add.565
  585.6 4.6 collective-permute-done.61
  596.4 4.9 collective-permute-start.63
  603.7 3.9 collective-permute-done.63
  610.6 8.0 %collective-permute-done.64 = f32[16896]{0:T(1024)S(1)} collective-permute-done((f32[16896]{0:T(1024)S(1)}, f32[16896]{0:T(1024)S(1)}, u32[]{:S(2)}, u32[]{:S(2)}) %collective-permute-start.64) | collective-permute-done | bytes 67616 | tf_op jit(solution)/shard_map/ppermute | solution.py:31
  627.3 5.8 reduce-scatter.11.cloned.1.call-done.refs_0_
  639.4 3.7 shard_map.300
  (761 shorter events, 288.5 us)
Async XLA Ops:
  7.2 80.8 %all-gather.2.cloned.1.call-start = ((), (), s32[]{:S(2)}) async-start(), calls=%async_computation.4 | async-start | bytes 3932160 | tf_op jit(solution)/shard_map/all_gather | solution.py:1152
  14.9 22.3 %collective-permute-start = (f32[528,64]{1,0:T(8,128)}, f32[528,64]{1,0:T(8,128)}, u32[]{:S(2)}, u32[]{:S(2)}) collective-permute-start(f32[528,64]{1,0:T(8,128)} %pad_maximum_fusion.18), channel_id=1, source_target_pairs={{0,1},{1,0},{2,3},{3,2},{4,5},{5,4},{6,7},{7,6},{8,9},{9,8},{10,11... | collective-permute-start | bytes 405512 | tf_op jit(solution)/shard_map/ppermute | solution.py:31
  18.9 351.3 %reduce-scatter.5.cloned.1.call-start = ((), (), s32[]{:S(2)}) async-start(), calls=%async_computation.5 | async-start | bytes 5898240 | tf_op jit(solution)/shard_map/reduce_scatter | solution.py:784
  62.3 14.1 %collective-permute-start.3 = (f32[128,768]{1,0:T(8,128)}, f32[128,768]{1,0:T(8,128)S(1)}, u32[]{:S(2)}, u32[]{:S(2)}) collective-permute-start(f32[128,768]{1,0:T(8,128)} %get-tuple-element.222), channel_id=1, source_target_pairs={{0,4},{1,5},{2,6},{3,7},{16,20},{17,21},{18,22},{19,23}} | collective-permute-start | bytes 1179656 | tf_op jit(solution)/shard_map/ppermute | solution.py:156
  76.4 11.6 %collective-permute-start.4 = (f32[128,768]{1,0:T(8,128)S(1)}, f32[128,768]{1,0:T(8,128)}, u32[]{:S(2)}, u32[]{:S(2)}) collective-permute-start(f32[128,768]{1,0:T(8,128)S(1)} %multiply_add_fusion.7), channel_id=1, source_target_pairs={{4,8},{5,9},{6,10},{7,11},{20,24},{21,25},{22,26},{23,27}} | collective-permute-start | bytes 1179656 | tf_op jit(solution)/shard_map/ppermute | solution.py:156
  108.2 17.3 %collective-permute-start.6 = (f32[128,1536]{1,0:T(8,128)S(1)}, f32[128,1536]{1,0:T(8,128)S(1)}, u32[]{:S(2)}, u32[]{:S(2)}) collective-permute-start(f32[128,1536]{1,0:T(8,128)S(1)} %get-tuple-element.547), channel_id=1, source_target_pairs={{0,1},{1,0},{2,3},{3,2},{4,5},{5,4},{6,7},{7,6},{8,9},{9,8},{10,11... | collective-permute-start | bytes 2359304 | tf_op jit(solution)/shard_map/ppermute | solution.py:31
  108.3 18.0 %collective-permute-start.7 = (f32[128,1536]{1,0:T(8,128)S(1)}, f32[128,1536]{1,0:T(8,128)S(1)}, u32[]{:S(2)}, u32[]{:S(2)}) collective-permute-start(f32[128,1536]{1,0:T(8,128)S(1)} %get-tuple-element.546), channel_id=1, source_target_pairs={{0,2},{1,3},{2,0},{3,1},{4,6},{5,7},{6,4},{7,5},{8,10},{9,11},{10,... | collective-permute-start | bytes 2359304 | tf_op jit(solution)/shard_map/ppermute | solution.py:31
  126.3 11.0 %collective-permute-start.8 = (f32[64,1536]{1,0:T(8,128)S(1)}, f32[64,1536]{1,0:T(8,128)S(1)}, u32[]{:S(2)}, u32[]{:S(2)}) collective-permute-start(f32[64,1536]{1,0:T(8,128)S(1)} %dynamic-slice_add_fusion.13), channel_id=1, source_target_pairs={{0,2},{1,3},{2,0},{3,1},{4,6},{5,7},{6,4},{7,5},{8,10},{9,11},{10,... | collective-permute-start | bytes 1179656 | tf_op jit(solution)/shard_map/ppermute | solution.py:31
  128.1 11.4 %collective-permute-start.13 = (f32[64,1536]{1,0:T(8,128)S(1)}, f32[64,1536]{1,0:T(8,128)S(1)}, u32[]{:S(2)}, u32[]{:S(2)}) collective-permute-start(f32[64,1536]{1,0:T(8,128)S(1)} %dynamic-slice_add_fusion.12), channel_id=1, source_target_pairs={{0,1},{1,0},{2,3},{3,2},{4,5},{5,4},{6,7},{7,6},{8,9},{9,8},{10,11... | collective-permute-start | bytes 1179656 | tf_op jit(solution)/shard_map/ppermute | solution.py:31
  139.6 12.1 %collective-permute-start.14 = (f32[64,1536]{1,0:T(8,128)S(1)}, f32[64,1536]{1,0:T(8,128)S(1)}, u32[]{:S(2)}, u32[]{:S(2)}) collective-permute-start(f32[64,1536]{1,0:T(8,128)S(1)} %add_multiply_fusion.6), channel_id=1, source_target_pairs={{0,1},{1,0},{2,3},{3,2},{4,5},{5,4},{6,7},{7,6},{8,9},{9,8},{10,11... | collective-permute-start | bytes 1179656 | tf_op jit(solution)/shard_map/ppermute | solution.py:31
  147.7 14.6 %collective-permute-start.12 = (f32[128,1536]{1,0:T(8,128)S(1)}, f32[128,1536]{1,0:T(8,128)S(1)}, u32[]{:S(2)}, u32[]{:S(2)}) collective-permute-start(f32[128,1536]{1,0:T(8,128)S(1)} %pad_maximum_fusion.10), channel_id=1, source_target_pairs={{0,1},{1,0},{2,3},{3,2},{4,5},{5,4},{6,7},{7,6},{8,9},{9,8},{10,11... | collective-permute-start | bytes 2359304 | tf_op jit(solution)/shard_map/ppermute | solution.py:31
  151.8 12.1 %collective-permute-start.15 = (f32[128,1536]{1,0:T(8,128)S(1)}, f32[128,1536]{1,0:T(8,128)S(1)}, u32[]{:S(2)}, u32[]{:S(2)}) collective-permute-start(f32[128,1536]{1,0:T(8,128)S(1)} %pad_maximum_fusion.11), channel_id=1, source_target_pairs={{0,2},{1,3},{2,0},{3,1},{4,6},{5,7},{6,4},{7,5},{8,10},{9,11},{10,... | collective-permute-start | bytes 2359304 | tf_op jit(solution)/shard_map/ppermute | solution.py:31
  194.5 13.6 %collective-permute-start.17 = (f32[128,768]{1,0:T(8,128)}, f32[128,768]{1,0:T(8,128)S(1)}, u32[]{:S(2)}, u32[]{:S(2)}) collective-permute-start(f32[128,768]{1,0:T(8,128)} %get-tuple-element.244), channel_id=1, source_target_pairs={{0,4},{1,5},{2,6},{3,7},{16,20},{17,21},{18,22},{19,23}} | collective-permute-start | bytes 1179656 | tf_op jit(solution)/shard_map/ppermute | solution.py:156
  247.9 14.2 %collective-permute-start.25 = (f32[1536,768]{1,0:T(8,128)S(1)}, f32[1536,768]{1,0:T(8,128)S(1)}, u32[]{:S(2)}, u32[]{:S(2)}) collective-permute-start(f32[1536,768]{1,0:T(8,128)S(1)} %get-tuple-element.283), channel_id=1, source_target_pairs={{0,16},{16,0},{1,17},{17,1},{2,18},{18,2},{3,19},{19,3},{4,20},{20... | collective-permute-start | bytes 14155784 | tf_op jit(solution)/shard_map/ppermute | solution.py:31
  258.9 22.1 %collective-permute-start.24 = (f32[128,768]{1,0:T(8,128)}, f32[128,768]{1,0:T(8,128)}, u32[]{:S(2)}, u32[]{:S(2)}) collective-permute-start(f32[128,768]{1,0:T(8,128)} %multiply_add_fusion.2), channel_id=1, source_target_pairs={{4,0},{5,1},{6,2},{7,3},{20,16},{21,17},{22,18},{23,19}} | collective-permute-start | bytes 1179656 | tf_op jit(solution)/shard_map/ppermute | solution.py:156
  281.1 157.2 %reduce-scatter.7.cloned.1.call-start = ((), (), s32[]{:S(2)}) async-start(), calls=%async_computation.6 | async-start | bytes 3317760 | tf_op jit(solution)/shard_map/reduce_scatter | solution.py:784
  309.5 14.6 %collective-permute-start.27 = (f32[512,128]{1,0:T(8,128)S(1)}, f32[512,128]{1,0:T(8,128)S(1)}, u32[]{:S(2)}, u32[]{:S(2)}) collective-permute-start(f32[512,128]{1,0:T(8,128)S(1)} %constant_dynamic-slice_fusion.25), channel_id=1, source_target_pairs={{0,2},{1,3},{2,0},{3,1},{4,6},{5,7},{6,4},{7,5},{8,10},{9,11},{10,... | collective-permute-start | bytes 786440 | tf_op jit(solution)/shard_map/ppermute | solution.py:31
  325.9 23.4 %collective-permute-start.28 = (f32[128,1536]{1,0:T(8,128)S(1)}, f32[128,1536]{1,0:T(8,128)S(1)}, u32[]{:S(2)}, u32[]{:S(2)}) collective-permute-start(f32[128,1536]{1,0:T(8,128)S(1)} %get-tuple-element.531), channel_id=1, source_target_pairs={{0,1},{1,0},{2,3},{3,2},{4,5},{5,4},{6,7},{7,6},{8,9},{9,8},{10,11... | collective-permute-start | bytes 2359304 | tf_op jit(solution)/shard_map/ppermute | solution.py:31
  326.5 22.8 %collective-permute-start.29 = (f32[128,1536]{1,0:T(8,128)S(1)}, f32[128,1536]{1,0:T(8,128)S(1)}, u32[]{:S(2)}, u32[]{:S(2)}) collective-permute-start(f32[128,1536]{1,0:T(8,128)S(1)} %get-tuple-element.530), channel_id=1, source_target_pairs={{0,2},{1,3},{2,0},{3,1},{4,6},{5,7},{6,4},{7,5},{8,10},{9,11},{10,... | collective-permute-start | bytes 2359304 | tf_op jit(solution)/shard_map/ppermute | solution.py:31
  356.5 11.6 %collective-permute-start.31 = (f32[64,1536]{1,0:T(8,128)S(1)}, f32[64,1536]{1,0:T(8,128)}, u32[]{:S(2)}, u32[]{:S(2)}) collective-permute-start(f32[64,1536]{1,0:T(8,128)S(1)} %get-tuple-element.525), channel_id=1, source_target_pairs={{0,1},{1,0},{2,3},{3,2},{4,5},{5,4},{6,7},{7,6},{8,9},{9,8},{10,11... | collective-permute-start | bytes 1179656 | tf_op jit(solution)/shard_map/ppermute | solution.py:31
  358.9 11.3 %collective-permute-start.30 = (f32[64,1536]{1,0:T(8,128)S(1)}, f32[64,1536]{1,0:T(8,128)}, u32[]{:S(2)}, u32[]{:S(2)}) collective-permute-start(f32[64,1536]{1,0:T(8,128)S(1)} %get-tuple-element.527), channel_id=1, source_target_pairs={{0,2},{1,3},{2,0},{3,1},{4,6},{5,7},{6,4},{7,5},{8,10},{9,11},{10,... | collective-permute-start | bytes 1179656 | tf_op jit(solution)/shard_map/ppermute | solution.py:31
  375.8 192.9 %reduce-scatter.9.cloned.1.call-start = ((), (), s32[]{:S(2)}) async-start(), calls=%async_computation.7 | async-start | bytes 5898240 | tf_op jit(solution)/shard_map/reduce_scatter | solution.py:784
  375.8 11.7 %collective-permute-start.36 = (f32[64,1536]{1,0:T(8,128)}, f32[64,1536]{1,0:T(8,128)S(1)}, u32[]{:S(2)}, u32[]{:S(2)}) collective-permute-start(f32[64,1536]{1,0:T(8,128)} %get-tuple-element.471), channel_id=1, source_target_pairs={{0,1},{1,0},{2,3},{3,2},{4,5},{5,4},{6,7},{7,6},{8,9},{9,8},{10,11... | collective-permute-start | bytes 1179656 | tf_op jit(solution)/shard_map/ppermute | solution.py:31
  386.9 18.1 %collective-permute-start.35 = (f32[128,1536]{1,0:T(8,128)S(1)}, f32[128,1536]{1,0:T(8,128)S(1)}, u32[]{:S(2)}, u32[]{:S(2)}) collective-permute-start(f32[128,1536]{1,0:T(8,128)S(1)} %pad_maximum_fusion.12), channel_id=1, source_target_pairs={{0,1},{1,0},{2,3},{3,2},{4,5},{5,4},{6,7},{7,6},{8,9},{9,8},{10,11... | collective-permute-start | bytes 2359304 | tf_op jit(solution)/shard_map/ppermute | solution.py:31
  387.7 17.8 %collective-permute-start.37 = (f32[128,1536]{1,0:T(8,128)S(1)}, f32[128,1536]{1,0:T(8,128)S(1)}, u32[]{:S(2)}, u32[]{:S(2)}) collective-permute-start(f32[128,1536]{1,0:T(8,128)S(1)} %pad_maximum_fusion.13), channel_id=1, source_target_pairs={{0,2},{1,3},{2,0},{3,1},{4,6},{5,7},{6,4},{7,5},{8,10},{9,11},{10,... | collective-permute-start | bytes 2359304 | tf_op jit(solution)/shard_map/ppermute | solution.py:31
  407.2 31.1 %collective-permute-start.38 = (f32[128,1536]{1,0:T(8,128)S(1)}, f32[128,1536]{1,0:T(8,128)}, u32[]{:S(2)}, u32[]{:S(2)}) collective-permute-start(f32[128,1536]{1,0:T(8,128)S(1)} %get-tuple-element.519), channel_id=1, source_target_pairs={{0,1},{1,0},{2,3},{3,2},{4,5},{5,4},{6,7},{7,6},{8,9},{9,8},{10,11... | collective-permute-start | bytes 2359304 | tf_op jit(solution)/shard_map/ppermute | solution.py:31
  408.7 29.5 %collective-permute-start.39 = (f32[128,1536]{1,0:T(8,128)S(1)}, f32[128,1536]{1,0:T(8,128)}, u32[]{:S(2)}, u32[]{:S(2)}) collective-permute-start(f32[128,1536]{1,0:T(8,128)S(1)} %get-tuple-element.518), channel_id=1, source_target_pairs={{0,2},{1,3},{2,0},{3,1},{4,6},{5,7},{6,4},{7,5},{8,10},{9,11},{10,... | collective-permute-start | bytes 2359304 | tf_op jit(solution)/shard_map/ppermute | solution.py:31
  421.2 17.1 %collective-permute-start.42 = (f32[128,768]{1,0:T(8,128)}, f32[128,768]{1,0:T(8,128)}, u32[]{:S(2)}, u32[]{:S(2)}) collective-permute-start(f32[128,768]{1,0:T(8,128)} %get-tuple-element.313), channel_id=1, source_target_pairs={{12,8},{13,9},{14,10},{15,11},{28,24},{29,25},{30,26},{31,27}} | collective-permute-start | bytes 1179656 | tf_op jit(solution)/shard_map/ppermute | solution.py:156
  438.4 25.5 %collective-permute-start.45 = (f32[1536,768]{1,0:T(8,128)}, f32[1536,768]{1,0:T(8,128)S(1)}, u32[]{:S(2)}, u32[]{:S(2)}) collective-permute-start(f32[1536,768]{1,0:T(8,128)} %copy-done.75), channel_id=1, source_target_pairs={{0,16},{16,0},{1,17},{17,1},{2,18},{18,2},{3,19},{19,3},{4,20},{20... | collective-permute-start | bytes 14155784 | tf_op jit(solution)/shard_map/ppermute | solution.py:31
  440.0 13.8 %collective-permute-start.41 = (f32[64,1536]{1,0:T(8,128)S(1)}, f32[64,1536]{1,0:T(8,128)S(1)}, u32[]{:S(2)}, u32[]{:S(2)}) collective-permute-start(f32[64,1536]{1,0:T(8,128)S(1)} %get-tuple-element.513), channel_id=1, source_target_pairs={{0,1},{1,0},{2,3},{3,2},{4,5},{5,4},{6,7},{7,6},{8,9},{9,8},{10,11... | collective-permute-start | bytes 1179656 | tf_op jit(solution)/shard_map/ppermute | solution.py:31
  443.0 11.1 %collective-permute-start.40 = (f32[64,1536]{1,0:T(8,128)S(1)}, f32[64,1536]{1,0:T(8,128)S(1)}, u32[]{:S(2)}, u32[]{:S(2)}) collective-permute-start(f32[64,1536]{1,0:T(8,128)S(1)} %get-tuple-element.515), channel_id=1, source_target_pairs={{0,2},{1,3},{2,0},{3,1},{4,6},{5,7},{6,4},{7,5},{8,10},{9,11},{10,... | collective-permute-start | bytes 1179656 | tf_op jit(solution)/shard_map/ppermute | solution.py:31
  457.1 13.6 %collective-permute-start.49 = (f32[128,768]{1,0:T(8,128)}, f32[128,768]{1,0:T(8,128)}, u32[]{:S(2)}, u32[]{:S(2)}) collective-permute-start(f32[128,768]{1,0:T(8,128)} %multiply_add_fusion), channel_id=1, source_target_pairs={{4,0},{5,1},{6,2},{7,3},{20,16},{21,17},{22,18},{23,19}} | collective-permute-start | bytes 1179656 | tf_op jit(solution)/shard_map/ppermute | solution.py:156
  472.9 21.6 %collective-permute-start.47 = (f32[128,1536]{1,0:T(8,128)}, f32[128,1536]{1,0:T(8,128)}, u32[]{:S(2)}, u32[]{:S(2)}) collective-permute-start(f32[128,1536]{1,0:T(8,128)} %pad_maximum_fusion.15), channel_id=1, source_target_pairs={{0,2},{1,3},{2,0},{3,1},{4,6},{5,7},{6,4},{7,5},{8,10},{9,11},{10,... | collective-permute-start | bytes 2359304 | tf_op jit(solution)/shard_map/ppermute | solution.py:31
  476.3 18.2 %collective-permute-start.46 = (f32[128,1536]{1,0:T(8,128)}, f32[128,1536]{1,0:T(8,128)}, u32[]{:S(2)}, u32[]{:S(2)}) collective-permute-start(f32[128,1536]{1,0:T(8,128)} %pad_maximum_fusion.14), channel_id=1, source_target_pairs={{0,1},{1,0},{2,3},{3,2},{4,5},{5,4},{6,7},{7,6},{8,9},{9,8},{10,11... | collective-permute-start | bytes 2359304 | tf_op jit(solution)/shard_map/ppermute | solution.py:31
  477.8 155.2 %reduce-scatter.11.cloned.1.call-start = ((), (), s32[]{:S(2)}) async-start(), calls=%async_computation.8 | async-start | bytes 3317760 | tf_op jit(solution)/shard_map/reduce_scatter | solution.py:784
  508.4 13.1 %collective-permute-start.51 = (f32[512,128]{1,0:T(8,128)S(1)}, f32[512,128]{1,0:T(8,128)S(1)}, u32[]{:S(2)}, u32[]{:S(2)}) collective-permute-start(f32[512,128]{1,0:T(8,128)S(1)} %constant_dynamic-slice_fusion.3), channel_id=1, source_target_pairs={{0,2},{1,3},{2,0},{3,1},{4,6},{5,7},{6,4},{7,5},{8,10},{9,11},{10,... | collective-permute-start | bytes 786440 | tf_op jit(solution)/shard_map/ppermute | solution.py:31
  523.3 18.2 %collective-permute-start.52 = (f32[128,1536]{1,0:T(8,128)S(1)}, f32[128,1536]{1,0:T(8,128)S(1)}, u32[]{:S(2)}, u32[]{:S(2)}) collective-permute-start(f32[128,1536]{1,0:T(8,128)S(1)} %get-tuple-element.505), channel_id=1, source_target_pairs={{0,1},{1,0},{2,3},{3,2},{4,5},{5,4},{6,7},{7,6},{8,9},{9,8},{10,11... | collective-permute-start | bytes 2359304 | tf_op jit(solution)/shard_map/ppermute | solution.py:31
  524.0 17.6 %collective-permute-start.53 = (f32[128,1536]{1,0:T(8,128)S(1)}, f32[128,1536]{1,0:T(8,128)S(1)}, u32[]{:S(2)}, u32[]{:S(2)}) collective-permute-start(f32[128,1536]{1,0:T(8,128)S(1)} %get-tuple-element.504), channel_id=1, source_target_pairs={{0,2},{1,3},{2,0},{3,1},{4,6},{5,7},{6,4},{7,5},{8,10},{9,11},{10,... | collective-permute-start | bytes 2359304 | tf_op jit(solution)/shard_map/ppermute | solution.py:31
  550.8 17.9 %collective-permute-start.57 = (f32[4,432,384]{2,1,0:T(8,128)}, f32[4,432,384]{2,1,0:T(8,128)}, u32[]{:S(2)}, u32[]{:S(2)}) collective-permute-start(f32[4,432,384]{2,1,0:T(8,128)} %get-tuple-element.375), channel_id=1, source_target_pairs={{0,16},{16,0},{1,17},{17,1},{2,18},{18,2},{3,19},{19,3},{4,20},{20... | collective-permute-start | bytes 7962632 | tf_op jit(solution)/shard_map/ppermute | solution.py:31
  553.6 65.1 %collective-permute-start.66 = (f32[384,768]{1,0:T(8,128)}, f32[384,768]{1,0:T(8,128)}, u32[]{:S(2)}, u32[]{:S(2)}) collective-permute-start(f32[384,768]{1,0:T(8,128)} %reduce-scatter.5.cloned.1.call-done.refs_2_), channel_id=1, source_target_pairs={{0,16},{16,0},{1,17},{17,1},{2,18},{18,2},{3,19},{19,3},{4,20},{20... | collective-permute-start | bytes 3538952 | tf_op jit(solution)/shard_map/ppermute | solution.py:31
  561.9 11.7 %collective-permute-start.55 = (f32[64,1536]{1,0:T(8,128)}, f32[64,1536]{1,0:T(8,128)}, u32[]{:S(2)}, u32[]{:S(2)}) collective-permute-start(f32[64,1536]{1,0:T(8,128)} %get-tuple-element.499), channel_id=1, source_target_pairs={{0,1},{1,0},{2,3},{3,2},{4,5},{5,4},{6,7},{7,6},{8,9},{9,8},{10,11... | collective-permute-start | bytes 1179656 | tf_op jit(solution)/shard_map/ppermute | solution.py:31
  563.6 11.2 %collective-permute-start.54 = (f32[64,1536]{1,0:T(8,128)}, f32[64,1536]{1,0:T(8,128)}, u32[]{:S(2)}, u32[]{:S(2)}) collective-permute-start(f32[64,1536]{1,0:T(8,128)} %get-tuple-element.501), channel_id=1, source_target_pairs={{0,2},{1,3},{2,0},{3,1},{4,6},{5,7},{6,4},{7,5},{8,10},{9,11},{10,... | collective-permute-start | bytes 1179656 | tf_op jit(solution)/shard_map/ppermute | solution.py:31
  568.0 16.4 %collective-permute-start.60 = (f32[5632]{0:T(1024)S(1)}, f32[5632]{0:T(1024)S(1)}, u32[]{:S(2)}, u32[]{:S(2)}) collective-permute-start(f32[5632]{0:T(1024)S(1)} %pad_maximum_fusion.27), channel_id=1, source_target_pairs={{0,1},{1,0},{2,3},{3,2},{4,5},{5,4},{6,7},{7,6},{8,9},{9,8},{10,11... | collective-permute-start | bytes 67592 | tf_op jit(solution)/shard_map/ppermute | solution.py:31
  590.3 28.4 %collective-permute-start.65 = (f32[384,768]{1,0:T(8,128)}, f32[384,768]{1,0:T(8,128)S(1)}, u32[]{:S(2)}, u32[]{:S(2)}) collective-permute-start(f32[384,768]{1,0:T(8,128)} %reduce-scatter.9.cloned.1.call-done.refs_0_), channel_id=1, source_target_pairs={{0,16},{16,0},{1,17},{17,1},{2,18},{18,2},{3,19},{19,3},{4,20},{20... | collective-permute-start | bytes 3538952 | tf_op jit(solution)/shard_map/ppermute | solution.py:31
  594.3 31.7 %collective-permute-start.67 = (f32[128,1536]{1,0:T(8,128)S(1)}, f32[128,1536]{1,0:T(8,128)S(1)}, u32[]{:S(2)}, u32[]{:S(2)}) collective-permute-start(f32[128,1536]{1,0:T(8,128)S(1)} %pad_maximum_fusion.16), channel_id=1, source_target_pairs={{0,1},{1,0},{2,3},{3,2},{4,5},{5,4},{6,7},{7,6},{8,9},{9,8},{10,11... | collective-permute-start | bytes 2359304 | tf_op jit(solution)/shard_map/ppermute | solution.py:31
  596.4 11.2 %collective-permute-start.63 = (f32[16896]{0:T(1024)S(1)}, f32[16896]{0:T(1024)S(1)}, u32[]{:S(2)}, u32[]{:S(2)}) collective-permute-start(f32[16896]{0:T(1024)S(1)} %add.572), channel_id=1, source_target_pairs={{0,4},{4,0},{8,12},{12,8},{1,5},{5,1},{9,13},{13,9},{2,6},{6,2},{1... | collective-permute-start | bytes 202760 | tf_op jit(solution)/shard_map/ppermute | solution.py:31
  602.3 30.7 %collective-permute-start.68 = (f32[128,1536]{1,0:T(8,128)}, f32[128,1536]{1,0:T(8,128)}, u32[]{:S(2)}, u32[]{:S(2)}) collective-permute-start(f32[128,1536]{1,0:T(8,128)} %pad_maximum_fusion.17), channel_id=1, source_target_pairs={{0,2},{1,3},{2,0},{3,1},{4,6},{5,7},{6,4},{7,5},{8,10},{9,11},{10,... | collective-permute-start | bytes 2359304 | tf_op jit(solution)/shard_map/ppermute | solution.py:31
  607.6 11.0 %collective-permute-start.64 = (f32[16896]{0:T(1024)S(1)}, f32[16896]{0:T(1024)S(1)}, u32[]{:S(2)}, u32[]{:S(2)}) collective-permute-start(f32[16896]{0:T(1024)S(1)} %add.573), channel_id=1, source_target_pairs={{0,8},{4,12},{8,0},{12,4},{1,9},{5,13},{9,1},{13,5},{2,10},{6,14},... | collective-permute-start | bytes 202760 | tf_op jit(solution)/shard_map/ppermute | solution.py:31
  (217 other events, 1861.1 us)
Sparse Core Ops, SparseCore 0:
  19.0 44.5 all-gather.1
  281.2 83.3 reduce-scatter.4
  375.9 51.1 reduce-scatter.6
  478.0 86.5 reduce-scatter.8
  574.9 58.0 reduce-scatter.10

commit v5 on v4

--- a/solution.py
+++ b/solution.py
@@ -601,13 +601,14 @@
                 if distance == 1:
                     other, ip = tied(other, ip)
                 elif step is None:
-                    step = matmul(after(normed, whole), w["step"], precision=HIGHEST)
+                    step = matmul(after(normed, whole), w["own_step"], precision=HIGHEST)
                     other, step = tied(other, step)
                 whole = joined(whole, other, "head", distance, 1)
         else:
             whole = gathered_columns(whole)
         if not power_of_two(lax.axis_size("head")) or step is None:
-            step = matmul(normed, w["step"], precision=HIGHEST)
+            step = matmul(normed, w["own_step"], precision=HIGHEST)
+        step = jnp.pad(step, ((0, 0), (0, LANES - heads)))
         taps = whole[length:]
         sp = whole[:length]
     else:
@@ -818,7 +819,7 @@
     )(*pieces)
 
 
-def backward(grad, q, scale, slope, w, saved, beside, waiting, earlier, final):
+def backward(grad, q, scale, slope, w, saved, beside, idle, waiting, earlier, final):
     s = saved
     length, inner = q.shape
     width = inner // w["heads"]
@@ -954,10 +955,8 @@
     )
     gains = []
 
-    def product(base, dip, dmaps, scaled):
-        total = base + matmul(dip, w["inner"], NT) + matmul(dmaps, w["maps"])
-        gains.append(jnp.sum(total * scaled, axis=0))
-        return total
+    def product(base, dip, dmaps):
+        return base + matmul(dip, w["inner"], NT) + matmul(dmaps, w["maps"])
 
     def finish(rows_grad, offset):
         def take(array):
@@ -966,11 +965,12 @@
         x, root = take(s["current"]), take(s["root"])
         scaled = rows_grad * w["pre_gain"][None, :]
         along = jnp.mean(scaled * x, axis=-1, keepdims=True)
+        gains.append(jnp.sum(rows_grad * x * root, axis=0))
         return root * scaled - x * (root * root * root * along)
 
     shared = dsp
     own = states // lax.axis_size("head")
-    lefts = [base, dip, jnp.concatenate([dsp, dstep], axis=1), s["current"] * s["root"]]
+    lefts = [base, dip, jnp.concatenate([dsp, dstep], axis=1)]
     if power_of_two(lax.axis_size("head")):
         way = distances("head")[::-1]
         for number, distance in enumerate(way):
@@ -984,19 +984,8 @@
         shared = lax.psum_scatter(shared, "head", scatter_dimension=1, tiled=True)
         steps = Steps(head_sum(lefts, product, finish))
         steps.advance()
-    def folded(array):
-        return array.reshape(-1, PAD, array.shape[1]).sum(axis=1)
-
-    ri, rs, rows = folded(ri), folded(rs), folded(rows)
-    over_heads = jnp.concatenate([gains[0] + gains[1], rs.reshape(-1)])
-    flat = jnp.concatenate(
-        [ri.reshape(-1), dgain.sum(axis=0), rows[0], rows[1, :LANES], rows[2, :LANES]]
-    )
-    small_parts = [*earlier, (over_heads, flat)]
+    over, rest = packed(ri, rs, dgain, rows)
     (dip,) = steps.advance(dip)
-    if final:
-        over_heads = jnp.concatenate([part[0] for part in small_parts])
-        over_heads = small_sum(after(over_heads, dip), "head")
     shards = lax.axis_size("seq")
     model = s["normed"].shape[1]
     small = jnp.concatenate([shared, dstep[:, : LANES - own]], axis=1)
@@ -1022,16 +1011,51 @@
     else:
         last, pair = steps.advance(last, pair)
     last = over_seq(after(last, pair))
+    over_heads = jnp.concatenate([sum(gains).reshape(-1, LANES), over], axis=0)
+    small_parts = [*earlier, (over_heads, rest)]
     if not final:
+        steps.advance()
+        if idle is not None:
+            (idle.now,) = steps.advance(idle.now)
         branch = steps.finished()
         return grad + branch, pair, last, small_parts, own
-    (over_heads,) = steps.advance(over_heads)
-    flat = jnp.concatenate([over_heads] + [part[1] for part in small_parts])
+    over_heads = small_sum(jnp.concatenate([part[0] for part in small_parts], axis=0), "head")
+    steps.advance()
+    flat = jnp.concatenate([over_heads] + [part[1] for part in small_parts], axis=0)
     flat = small_sum(small_sum(flat, "dp"), "seq")
     flat, last = tied(flat, last)
     branch = steps.finished()
     sizes = (small_parts[0][0].size, small_parts[0][1].size)
     return grad + branch, pair, last, (flat, sizes), own
+
+
+def pack_kernel(ri, rs, dgain, rows, over, rest):
+    def line(array, number, k):
+        part = array[number * PAD : (number + 1) * PAD, k * LANES : (k + 1) * LANES]
+        return jnp.sum(part, axis=0, keepdims=True)
+
+    tiles = ri.shape[1] // LANES
+    maps = rs.shape[1] // LANES
+    for tap in range(5):
+        for k in range(tiles):
+            rest[tap * tiles + k : tap * tiles + k + 1, :] = line(ri, tap, k)
+        for k in range(maps):
+            over[tap * maps + k : tap * maps + k + 1, :] = line(rs, tap, k)
+    for k in range(tiles):
+        rest[5 * tiles + k : 5 * tiles + k + 1, :] = line(dgain, 0, k)
+        rest[6 * tiles + k : 6 * tiles + k + 1, :] = line(rows, 0, k)
+    for k in range(2):
+        rest[7 * tiles + k : 7 * tiles + k + 1, :] = line(rows, 1 + k, 0)
+
+
+def packed(ri, rs, dgain, rows):
+    counts = (5 * rs.shape[1] // LANES, 7 * ri.shape[1] // LANES + 2)
+    return pl.pallas_call(
+        pack_kernel,
+        out_shape=[jax.ShapeDtypeStruct((count, LANES), F32) for count in counts],
+        compiler_params=pltpu.CompilerParams(vmem_limit_bytes=VMEM),
+        cost_estimate=pl.CostEstimate(flops=0, bytes_accessed=0, transcendentals=0),
+    )(ri, rs, dgain, rows)
 
 
 def unpack_kernel(width, size, flat, pre, fi, fib, fs, fsb, bias, rate, skip, norm):
@@ -1095,7 +1119,7 @@
         out_shape=[jax.ShapeDtypeStruct(shape, F32) for shape in shapes],
         compiler_params=pltpu.CompilerParams(vmem_limit_bytes=VMEM),
         cost_estimate=pl.CostEstimate(flops=0, bytes_accessed=0, transcendentals=0),
-    )(flat.reshape(-1, LANES))
+    )(flat)
 
 
 def gathered_columns(value):
@@ -1140,6 +1164,7 @@
                 inner=inner_weight[layer],
                 state=state_weight[layer],
                 step=steps,
+                own_step=step_weight[layer],
                 out=out_weight[layer],
                 norm_gain=norm_gain[layer],
                 taps_i=padded_rows([filter_inner[layer], filter_inner_bias[layer][None]], inner),
@@ -1161,7 +1186,7 @@
             for number, other in enumerate(weights):
                 size = other["inner"].shape[0]
                 cut = maps[:, number * size : (number + 1) * size]
-                other["maps"] = jnp.concatenate([cut, other["step"].T], axis=0)
+                other["maps"] = jnp.concatenate([cut, after(other["step"], gn).T], axis=0)
         last = layer == layers - 1
         if last:
             both = jnp.concatenate([squares, jnp.sum(extra * gn, axis=1)[None, :]], axis=0)
@@ -1175,8 +1200,6 @@
             return rows * lax.dynamic_slice_in_dim(scale[0], offset, rows.shape[0], 0)[:, None]
 
         steps = Steps(head_sum([gn], lambda rows, w=w, p=HIGH if last else HIGHEST: matmul(rows, w["out"], NT, p), finish))
-        if last:
-            scale = after(scale, steps.now)
         if layer == 0:
             product = matmul(after(grad, steps.now), weights[layers - 1]["out"])
             if not last:
@@ -1202,7 +1225,17 @@
             q = extra
             slope = along * scale * scale * scale / INNER
         grad, *collected[layer] = backward(
-            grad, q, scale, slope, w, saved, steps if layer == layers - 2 else None, waiting, earlier, layer == 0
+            grad,
+            q,
+            scale,
+            slope,
+            w,
+            saved,
+            steps if layer == layers - 2 else None,
+            steps if layer == layers - 1 else None,
+            waiting,
+            earlier,
+            layer == 0,
         )
         waiting = collected[layer][1]
         earlier = collected[layer][2]

time: 656 us -> 647 us (0.986)
  other arithmetic: 87.8 us -> 76.2 us
  local copies, waits for them, and re-layouts: 64.9 us -> 53.7 us
  waiting for transfers between devices: 155 us -> 165 us
    reduce_scatter x4, waiting for transfers between devices: 5.8 us -> 13.8 us  [over_seq(): return lax.psum_scatter(total, 'seq', scatter_dimension=0, tiled=True)]
    dynamic_slice x24 -> x20, local copies, waits for them, and re-layouts: 9.3 us -> 1.37 us  [half(): return lax.dynamic_slice_in_dim(value, which * size, size, dim)]
    unnamed x391 -> x351, local copies, waits for them, and re-layouts: 32.1 us -> 31.8 us
  transfers between devices with their start and end apart: 76 -> 76, of which waited for: 34 -> 38; matrix products, arithmetic and copies ran while one was open for 29% -> 26% of each run, Pallas kernels for 17% -> 17%
where the time goes in v5:
time: 647 us; the launch traced here: 637 us
  waiting for transfers between devices  165 us (26%)
  Pallas kernels  131 us (20%)
  matrix products  101 us (16%)
  starting transfers between devices  92.4 us (14%)
  other arithmetic  76.2 us (12%)
  local copies, waits for them, and re-layouts  53.7 us (8%)
  between operations  17.2 us (3%)
    ppermute x55, waiting for transfers between devices, exchanged(): return lax.ppermute(value, axis, [(i, i ^ distance) for i in range(n)])  128 us
    pallas_call x18, Pallas kernels, call(): pl.pallas_call(kernel, grid=(steps,), out_shape=shapes, in_specs=[spec(bl...  119 us
    dot_general x23, matrix products, matmul(): return lax.dot_general(left, right, (dims, ((), ())), precision=precision)  101 us
    ppermute x55, starting transfers between devices, exchanged(): return lax.ppermute(value, axis, [(i, i ^ distance) for i in range(n)])  58.9 us
    unnamed x351, local copies, waits for them, and re-layouts  31.8 us
    ppermute x12, starting transfers between devices, state_before(): got = lax.ppermute(leaving, 'seq', [(source, target)])  22 us
    ppermute x12, waiting for transfers between devices, state_before(): got = lax.ppermute(leaving, 'seq', [(source, target)])  18 us
    reduce_scatter x4, waiting for transfers between devices, over_seq(): return lax.psum_scatter(total, 'seq', scatter_dimension=0, tiled=True)  13.8 us
  transfers between devices with their start and end apart: 76, of which 38 were waited for; matrix products, arithmetic and copies ran while one was open for 26% of the time, Pallas kernels for 17%

profile of v5, /device:TPU:0, one launch (start us, length us, event | category | flops | bytes accessed | tf_op | source)
XLA Modules:
  0.0 636.5 jit_solution(12668977909977944456)
XLA Ops:
  23.0 10.1 %fusion.30.ip.pi = f32[512,768]{1,0:T(8,128)} fusion(f32[512,1536]{1,0:T(8,128)S(1)} %fusion.62.two.left, f32[2,1536,768]{2,1,0:T(8,128)} %param.20), kind=kOutput, calls=%fused_computation.30 | convolution fusion | flops 7247757312 | bytes 9437184 | tf_op jit(solution)/shard_map/dot_general | solution.py:575
  53.5 8.0 %shard_map.279 = (f32[512,768]{1,0:T(8,128)}, f32[512,256]{1,0:T(8,128)}, f32[512,768]{1,0:T(8,128)}, f32[512,256]{1,0:T(8,128)}, f32[512,128]{1,0:T(8,128)}, /*...) custom-call(f32[512,768]{1,0:T(8,128)} %fusion.30.ip.pi, ...), custom_call_target="tpu_custom_call" | custom-call | flops 75497472 | bytes 2317312 | tf_op jit(solution)/shard_map/pallas_call | solution.py:191
  61.6 4.5 collective-permute-start.3
  66.1 7.0 %shard_map.280.yd = f32[512,768]{1,0:T(8,128)} custom-call(f32[512,768]{1,0:T(8,128)} %get-tuple-element.228.v, f32[512,256]{1,0:T(8,128)} %get-tuple-element.229.bc, f32[512,128]{1,0:T(8,128)} %get-tuple-element.230.dt, f32[512,128]{1,0:T(8,128)} %get-tuple-element.231.cum, f32[16,512]{1,0:T(8,128)} %get-tuple-element.232.cumt, f32[8,128]{1,0:T(8,128)} %get-tuple-element.627.hp), custom_call_target="tpu_custom_call" | custom-call | flops 150994944 | bytes 1057792 | tf_op jit(solution)/shard_map/pallas_call | solution.py:191
  75.5 10.1 %fusion.24.gate = f32[512,768]{1,0:T(8,128)} fusion(f32[512,1536]{1,0:T(8,128)S(1)} %fusion.62.two.left, f32[2,1536,768]{2,1,0:T(8,128)} %param.19), kind=kOutput, calls=%fused_computation.24 | convolution fusion | flops 7247757312 | bytes 9437184 | tf_op jit(solution)/shard_map/dot_general | solution.py:575
  97.7 7.0 %fusion.20 = f32[256,1536]{1,0:T(8,128)S(1)} fusion(f32[2,1536,768]{2,1,0:T(8,128)} %param.31, f32[128,768]{1,0:T(8,128)S(1)} %get-tuple-element.585, f32[128,768]{1,0:T(8,128)S(1)} %get-tuple-element.583), kind=kOutput, calls=%fused_computation.20 | convolution fusion | flops 3624075264 | bytes 7077888 | tf_op jit(solution)/shard_map/dot_general | solution.py:575
  106.9 4.1 fusion.18
  112.9 5.3 fusion.14.q
  118.2 4.3 collective-permute-done.9
  128.2 5.0 collective-permute-done.8
  141.7 6.2 collective-permute-done.14
  150.6 9.7 %collective-permute-done.12 = f32[128,1536]{1,0:T(8,128)S(1)} collective-permute-done((f32[128,1536]{1,0:T(8,128)S(1)}, f32[128,1536]{1,0:T(8,128)S(1)}, u32[]{:S(2)}, u32[]{:S(2)}) %collective-permute-start.12) | collective-permute-done | bytes 786464 | tf_op jit(solution)/shard_map/ppermute | solution.py:31
  163.6 5.5 fusion.97.sp.ps
  169.3 4.3 fusion.8.ip.pi
  174.8 3.9 collective-permute-start.16
  181.5 8.0 %shard_map.282 = (f32[512,768]{1,0:T(8,128)}, f32[512,256]{1,0:T(8,128)}, f32[512,768]{1,0:T(8,128)}, f32[512,256]{1,0:T(8,128)}, f32[512,128]{1,0:T(8,128)}, /*...) custom-call(f32[512,768]{1,0:T(8,128)} %copy-done.9, ...), custom_call_target="tpu_custom_call" | custom-call | flops 75497472 | bytes 2317312 | tf_op jit(solution)/shard_map/pallas_call | solution.py:191
  189.6 7.2 %collective-permute-start.17 = (f32[128,768]{1,0:T(8,128)}, f32[128,768]{1,0:T(8,128)S(1)}, u32[]{:S(2)}, u32[]{:S(2)}) collective-permute-start(f32[128,768]{1,0:T(8,128)} %get-tuple-element.251), channel_id=1, source_target_pairs={{0,4},{1,5},{2,6},{3,7},{16,20},{17,21},{18,22},{19,23}} | collective-permute-start | bytes 1179656 | tf_op jit(solution)/shard_map/ppermute | solution.py:156
  196.8 7.0 %shard_map.283.yd = f32[512,768]{1,0:T(8,128)} custom-call(f32[512,768]{1,0:T(8,128)} %get-tuple-element.252.v, f32[512,256]{1,0:T(8,128)} %get-tuple-element.253.bc, f32[512,128]{1,0:T(8,128)} %get-tuple-element.254.dt, f32[512,128]{1,0:T(8,128)} %get-tuple-element.255.cum, f32[16,512]{1,0:T(8,128)} %get-tuple-element.256.cumt, f32[8,128]{1,0:T(8,128)} %get-tuple-element.626.hp), custom_call_target="tpu_custom_call" | custom-call | flops 150994944 | bytes 1057792 | tf_op jit(solution)/shard_map/pallas_call | solution.py:191
  206.3 6.6 %fusion.2.gate = f32[512,768]{1,0:T(8,128)S(1)} fusion(f32[512,1536]{1,0:T(8,128)S(1)} %multiply_multiply_fusion.two.left, f32[2,1536,768]{2,1,0:T(8,128)} %param.19), kind=kOutput, calls=%fused_computation.2 | convolution fusion | flops 3623878656 | bytes 9437184 | tf_op jit(solution)/shard_map/dot_general | solution.py:575
  230.8 9.8 %shard_map.286 = (f32[1536,768]{1,0:T(8,128)S(1)}, f32[1536,768]{1,0:T(8,128)S(1)}) custom-call(f32[512,1536]{1,0:T(8,128)S(1)} %bitcast.204, f32[512,768]{1,0:T(8,128)S(1)} %get-tuple-element.271.a, f32[512,1536]{1,0:T(8,128)S(1)} %multiply_multiply_fusion.two.left, f32[512,768]{1,0:T(8,128)S(1)} %get-tuple-element.292.b), custom_call_target="tpu_custom_call" | custom-call | flops 603979776 | bytes 4718592 | tf_op jit(solution)/shard_map/pallas_call | solution.py:191
  241.6 8.1 %shard_map.287 = (f32[512,768]{1,0:T(8,128)S(1)}, f32[512,256]{1,0:T(8,128)S(1)}) custom-call(f32[512,768]{1,0:T(8,128)S(1)} %get-tuple-element.276.dy, f32[512,768]{1,0:T(8,128)S(1)} %copy-done.12, f32[512,256]{1,0:T(8,128)S(1)} %copy-done.17, f32[512,128]{1,0:T(8,128)S(1)} %copy-done.41, f32[512,128]{1,0:T(8,128)S(1)} %copy-done.19, ...), custom_call_target="tpu_custom_call" | custom-call | flops 377487360 | bytes 1974272 | tf_op jit(solution)/shard_map/pallas_call | solution.py:191
  255.9 18.0 %collective-permute-done.24 = f32[128,768]{1,0:T(8,128)} collective-permute-done((f32[128,768]{1,0:T(8,128)}, f32[128,768]{1,0:T(8,128)}, u32[]{:S(2)}, u32[]{:S(2)}) %collective-permute-start.24) | collective-permute-done | bytes 393248 | tf_op jit(solution)/shard_map/ppermute | solution.py:156
  275.9 11.0 %shard_map.288 = (f32[512,768]{1,0:T(8,128)}, f32[512,256]{1,0:T(8,128)}, f32[512,128]{1,0:T(8,128)}, f32[24,768]{1,0:T(8,128)}) custom-call(f32[512,768]{1,0:T(8,128)} %copy-done.30, f32[512,768]{1,0:T(8,128)} %copy-done.29, f32[512,768]{1,0:T(8,128)} %get-tuple-element.252.v, f32[512,768]{1,0:T(8,128)} %copy-done.47, f32[512,768]{1,0:T(8,128)} %get-tuple-element.281.dsi, ...), custom_call_target="tpu_custom_call" | custom-call | flops 150994944 | bytes 3910656 | tf_op jit(solution)/shard_map/pallas_call | solution.py:191
  290.5 6.0 fusion
  317.2 4.9 collective-permute-done.32
  322.4 12.8 %collective-permute-done.28 = f32[128,1536]{1,0:T(8,128)S(1)} collective-permute-done((f32[128,1536]{1,0:T(8,128)S(1)}, f32[128,1536]{1,0:T(8,128)S(1)}, u32[]{:S(2)}, u32[]{:S(2)}) %collective-permute-start.28) | collective-permute-done | bytes 786464 | tf_op jit(solution)/shard_map/ppermute | solution.py:31
  335.2 6.3 shard_map.290
  348.4 4.9 collective-permute-done.31
  366.1 8.0 %collective-permute-done.36 = f32[64,1536]{1,0:T(8,128)} collective-permute-done((f32[64,1536]{1,0:T(8,128)}, f32[64,1536]{1,0:T(8,128)}, u32[]{:S(2)}, u32[]{:S(2)}) %collective-permute-start.36) | collective-permute-done | bytes 393248 | tf_op jit(solution)/shard_map/ppermute | solution.py:31
  378.5 4.4 fusion.10
  383.0 4.5 fusion.12
  387.5 6.4 %collective-permute-done.37 = f32[128,1536]{1,0:T(8,128)S(1)} collective-permute-done((f32[128,1536]{1,0:T(8,128)S(1)}, f32[128,1536]{1,0:T(8,128)S(1)}, u32[]{:S(2)}, u32[]{:S(2)}) %collective-permute-start.37) | collective-permute-done | bytes 786464 | tf_op jit(solution)/shard_map/ppermute | solution.py:31
  400.4 4.3 fusion.16.q
  404.8 3.9 shard_map.292
  412.7 9.8 %shard_map.293 = (f32[1536,768]{1,0:T(8,128)S(1)}, f32[1536,768]{1,0:T(8,128)S(1)}) custom-call(f32[512,1536]{1,0:T(8,128)S(1)} %maximum_add_fusion.1.one, f32[512,768]{1,0:T(8,128)S(1)} %get-tuple-element.330.a, f32[512,1536]{1,0:T(8,128)S(1)} %copy-done.1, f32[512,768]{1,0:T(8,128)S(1)} %get-tuple-element.374.b), custom_call_target="tpu_custom_call" | custom-call | flops 603979776 | bytes 4718592 | tf_op jit(solution)/shard_map/pallas_call | solution.py:191
  435.4 8.1 %shard_map.294 = (f32[512,768]{1,0:T(8,128)S(1)}, f32[512,256]{1,0:T(8,128)S(1)}) custom-call(f32[512,768]{1,0:T(8,128)S(1)} %copy-done.27, f32[512,768]{1,0:T(8,128)S(1)} %copy-done.11, f32[512,256]{1,0:T(8,128)S(1)} %copy-done.16, f32[512,128]{1,0:T(8,128)S(1)} %copy-done.40, f32[512,128]{1,0:T(8,128)S(1)} %copy-done.18, f32[16,512]{1,0:T(8,128)S(1)} %copy-done.65, ...), custom_call_target="tpu_custom_call" | custom-call | flops 377487360 | bytes 1974272 | tf_op jit(solution)/shard_map/pallas_call | solution.py:191
  468.8 10.8 %shard_map.295 = (f32[512,768]{1,0:T(8,128)}, f32[512,256]{1,0:T(8,128)}, f32[512,128]{1,0:T(8,128)}, f32[24,768]{1,0:T(8,128)}) custom-call(f32[512,768]{1,0:T(8,128)} %copy-done.26, f32[512,768]{1,0:T(8,128)} %copy-done.24, f32[512,768]{1,0:T(8,128)} %get-tuple-element.228.v, f32[512,768]{1,0:T(8,128)} %copy-done.45, f32[512,768]{1,0:T(8,128)} %get-tuple-element.362.dsi, ...), custom_call_target="tpu_custom_call" | custom-call | flops 150994944 | bytes 3910656 | tf_op jit(solution)/shard_map/pallas_call | solution.py:191
  486.1 6.0 fusion.22
  513.4 3.8 collective-permute-done.56
  517.5 11.1 %collective-permute-done.52 = f32[128,1536]{1,0:T(8,128)S(1)} collective-permute-done((f32[128,1536]{1,0:T(8,128)S(1)}, f32[128,1536]{1,0:T(8,128)S(1)}, u32[]{:S(2)}, u32[]{:S(2)}) %collective-permute-start.52) | collective-permute-done | bytes 786464 | tf_op jit(solution)/shard_map/ppermute | solution.py:31
  529.6 6.9 %shard_map.297 = (f32[4,432,384]{2,1,0:T(8,128)}, f32[4,432,384]{2,1,0:T(8,128)S(1)}) custom-call(f32[512,1536]{1,0:T(8,128)S(1)} %copy-done.2, f32[512,768]{1,0:T(8,128)S(1)} %get-tuple-element.387.right, f32[512,128]{1,0:T(8,128)S(1)} %pad_maximum_fusion.20.small), custom_call_target="tpu_custom_call" | custom-call | flops 352321536 | bytes 2572288 | tf_op jit(solution)/shard_map/pallas_call | solution.py:191
  539.9 4.2 collective-permute-done.70.refs_3_
  554.7 4.3 add.561
  580.2 4.1 collective-permute-done.61
  587.5 3.9 collective-permute-done.67
  602.9 5.0 collective-permute-done.66
  609.1 10.6 %reduce-scatter.11.cloned.1.call-done.refs_0_ = f32[432,384]{1,0:T(8,128)} async-done(((f32[1728,384]{1,0:T(8,128)}), f32[432,384]{1,0:T(8,128)}) %reduce-scatter.11.cloned.1.call-update) | async-done | bytes 663568 | tf_op jit(solution)/shard_map/reduce_scatter | solution.py:785
  626.1 3.7 shard_map.302
  (706 shorter events, 289.8 us)
Async XLA Ops:
  7.2 78.5 %all-gather.2.cloned.1.call-start = ((), (), s32[]{:S(2)}) async-start(), calls=%async_computation.4 | async-start | bytes 3932160 | tf_op jit(solution)/shard_map/all_gather | solution.py:1177
  14.9 19.4 %collective-permute-start = (f32[528,64]{1,0:T(8,128)S(1)}, f32[528,64]{1,0:T(8,128)}, u32[]{:S(2)}, u32[]{:S(2)}) collective-permute-start(f32[528,64]{1,0:T(8,128)S(1)} %pad_maximum_fusion.17), channel_id=1, source_target_pairs={{0,1},{1,0},{2,3},{3,2},{4,5},{5,4},{6,7},{7,6},{8,9},{9,8},{10,11... | collective-permute-start | bytes 405512 | tf_op jit(solution)/shard_map/ppermute | solution.py:31
  19.0 338.4 %reduce-scatter.5.cloned.1.call-start = ((), (), s32[]{:S(2)}) async-start(), calls=%async_computation.5 | async-start | bytes 5898240 | tf_op jit(solution)/shard_map/reduce_scatter | solution.py:785
  61.6 12.3 %collective-permute-start.3 = (f32[128,768]{1,0:T(8,128)}, f32[128,768]{1,0:T(8,128)S(1)}, u32[]{:S(2)}, u32[]{:S(2)}) collective-permute-start(f32[128,768]{1,0:T(8,128)} %get-tuple-element.227), channel_id=1, source_target_pairs={{0,4},{1,5},{2,6},{3,7},{16,20},{17,21},{18,22},{19,23}} | collective-permute-start | bytes 1179656 | tf_op jit(solution)/shard_map/ppermute | solution.py:156
  74.0 11.7 %collective-permute-start.4 = (f32[128,768]{1,0:T(8,128)S(1)}, f32[128,768]{1,0:T(8,128)}, u32[]{:S(2)}, u32[]{:S(2)}) collective-permute-start(f32[128,768]{1,0:T(8,128)S(1)} %multiply_add_fusion.7), channel_id=1, source_target_pairs={{4,8},{5,9},{6,10},{7,11},{20,24},{21,25},{22,26},{23,27}} | collective-permute-start | bytes 1179656 | tf_op jit(solution)/shard_map/ppermute | solution.py:156
  104.7 18.8 %collective-permute-start.6 = (f32[128,1536]{1,0:T(8,128)S(1)}, f32[128,1536]{1,0:T(8,128)S(1)}, u32[]{:S(2)}, u32[]{:S(2)}) collective-permute-start(f32[128,1536]{1,0:T(8,128)S(1)} %get-tuple-element.543), channel_id=1, source_target_pairs={{0,1},{1,0},{2,3},{3,2},{4,5},{5,4},{6,7},{7,6},{8,9},{9,8},{10,11... | collective-permute-start | bytes 2359304 | tf_op jit(solution)/shard_map/ppermute | solution.py:31
  106.2 17.7 %collective-permute-start.7 = (f32[128,1536]{1,0:T(8,128)S(1)}, f32[128,1536]{1,0:T(8,128)S(1)}, u32[]{:S(2)}, u32[]{:S(2)}) collective-permute-start(f32[128,1536]{1,0:T(8,128)S(1)} %get-tuple-element.542), channel_id=1, source_target_pairs={{0,2},{1,3},{2,0},{3,1},{4,6},{5,7},{6,4},{7,5},{8,10},{9,11},{10,... | collective-permute-start | bytes 2359304 | tf_op jit(solution)/shard_map/ppermute | solution.py:31
  111.1 11.4 %collective-permute-start.9 = (f32[1,512]{1,0:T(1,128)S(1)}, f32[1,512]{1,0:T(1,128)S(1)}, u32[]{:S(2)}, u32[]{:S(2)}) collective-permute-start(f32[1,512]{1,0:T(1,128)S(1)} %slice.322), channel_id=1, source_target_pairs={{0,1},{1,0},{2,3},{3,2},{4,5},{5,4},{6,7},{7,6},{8,9},{9,8},{10,11... | collective-permute-start | bytes 6152 | tf_op jit(solution)/shard_map/ppermute | solution.py:31
  135.8 12.1 %collective-permute-start.14 = (f32[64,1536]{1,0:T(8,128)S(1)}, f32[64,1536]{1,0:T(8,128)S(1)}, u32[]{:S(2)}, u32[]{:S(2)}) collective-permute-start(f32[64,1536]{1,0:T(8,128)S(1)} %add_multiply_fusion.2), channel_id=1, source_target_pairs={{0,1},{1,0},{2,3},{3,2},{4,5},{5,4},{6,7},{7,6},{8,9},{9,8},{10,11... | collective-permute-start | bytes 1179656 | tf_op jit(solution)/shard_map/ppermute | solution.py:31
  141.3 19.1 %collective-permute-start.12 = (f32[128,1536]{1,0:T(8,128)S(1)}, f32[128,1536]{1,0:T(8,128)S(1)}, u32[]{:S(2)}, u32[]{:S(2)}) collective-permute-start(f32[128,1536]{1,0:T(8,128)S(1)} %pad_maximum_fusion.9), channel_id=1, source_target_pairs={{0,1},{1,0},{2,3},{3,2},{4,5},{5,4},{6,7},{7,6},{8,9},{9,8},{10,11... | collective-permute-start | bytes 2359304 | tf_op jit(solution)/shard_map/ppermute | solution.py:31
  148.0 12.4 %collective-permute-start.15 = (f32[128,1536]{1,0:T(8,128)S(1)}, f32[128,1536]{1,0:T(8,128)S(1)}, u32[]{:S(2)}, u32[]{:S(2)}) collective-permute-start(f32[128,1536]{1,0:T(8,128)S(1)} %pad_maximum_fusion.10), channel_id=1, source_target_pairs={{0,2},{1,3},{2,0},{3,1},{4,6},{5,7},{6,4},{7,5},{8,10},{9,11},{10,... | collective-permute-start | bytes 2359304 | tf_op jit(solution)/shard_map/ppermute | solution.py:31
  189.6 14.9 %collective-permute-start.17 = (f32[128,768]{1,0:T(8,128)}, f32[128,768]{1,0:T(8,128)S(1)}, u32[]{:S(2)}, u32[]{:S(2)}) collective-permute-start(f32[128,768]{1,0:T(8,128)} %get-tuple-element.251), channel_id=1, source_target_pairs={{0,4},{1,5},{2,6},{3,7},{16,20},{17,21},{18,22},{19,23}} | collective-permute-start | bytes 1179656 | tf_op jit(solution)/shard_map/ppermute | solution.py:156
  240.7 12.4 %collective-permute-start.25 = (f32[1536,768]{1,0:T(8,128)S(1)}, f32[1536,768]{1,0:T(8,128)S(1)}, u32[]{:S(2)}, u32[]{:S(2)}) collective-permute-start(f32[1536,768]{1,0:T(8,128)S(1)} %get-tuple-element.288), channel_id=1, source_target_pairs={{0,16},{16,0},{1,17},{17,1},{2,18},{18,2},{3,19},{19,3},{4,20},{20... | collective-permute-start | bytes 14155784 | tf_op jit(solution)/shard_map/ppermute | solution.py:31
  251.8 22.0 %collective-permute-start.24 = (f32[128,768]{1,0:T(8,128)}, f32[128,768]{1,0:T(8,128)}, u32[]{:S(2)}, u32[]{:S(2)}) collective-permute-start(f32[128,768]{1,0:T(8,128)} %multiply_add_fusion.2), channel_id=1, source_target_pairs={{4,0},{5,1},{6,2},{7,3},{20,16},{21,17},{22,18},{23,19}} | collective-permute-start | bytes 1179656 | tf_op jit(solution)/shard_map/ppermute | solution.py:156
  273.8 154.5 %reduce-scatter.7.cloned.1.call-start = ((), (), s32[]{:S(2)}) async-start(), calls=%async_computation.6 | async-start | bytes 3317760 | tf_op jit(solution)/shard_map/reduce_scatter | solution.py:785
  301.0 11.6 %collective-permute-start.27 = (f32[512,128]{1,0:T(8,128)S(1)}, f32[512,128]{1,0:T(8,128)S(1)}, u32[]{:S(2)}, u32[]{:S(2)}) collective-permute-start(f32[512,128]{1,0:T(8,128)S(1)} %constant_dynamic-slice_fusion.18), channel_id=1, source_target_pairs={{0,2},{1,3},{2,0},{3,1},{4,6},{5,7},{6,4},{7,5},{8,10},{9,11},{10,... | collective-permute-start | bytes 786440 | tf_op jit(solution)/shard_map/ppermute | solution.py:31
  314.5 20.7 %collective-permute-start.28 = (f32[128,1536]{1,0:T(8,128)S(1)}, f32[128,1536]{1,0:T(8,128)S(1)}, u32[]{:S(2)}, u32[]{:S(2)}) collective-permute-start(f32[128,1536]{1,0:T(8,128)S(1)} %get-tuple-element.529), channel_id=1, source_target_pairs={{0,1},{1,0},{2,3},{3,2},{4,5},{5,4},{6,7},{7,6},{8,9},{9,8},{10,11... | collective-permute-start | bytes 2359304 | tf_op jit(solution)/shard_map/ppermute | solution.py:31
  315.1 20.1 %collective-permute-start.29 = (f32[128,1536]{1,0:T(8,128)S(1)}, f32[128,1536]{1,0:T(8,128)S(1)}, u32[]{:S(2)}, u32[]{:S(2)}) collective-permute-start(f32[128,1536]{1,0:T(8,128)S(1)} %get-tuple-element.528), channel_id=1, source_target_pairs={{0,2},{1,3},{2,0},{3,1},{4,6},{5,7},{6,4},{7,5},{8,10},{9,11},{10,... | collective-permute-start | bytes 2359304 | tf_op jit(solution)/shard_map/ppermute | solution.py:31
  341.7 11.6 %collective-permute-start.31 = (f32[64,1536]{1,0:T(8,128)S(1)}, f32[64,1536]{1,0:T(8,128)S(1)}, u32[]{:S(2)}, u32[]{:S(2)}) collective-permute-start(f32[64,1536]{1,0:T(8,128)S(1)} %get-tuple-element.523), channel_id=1, source_target_pairs={{0,1},{1,0},{2,3},{3,2},{4,5},{5,4},{6,7},{7,6},{8,9},{9,8},{10,11... | collective-permute-start | bytes 1179656 | tf_op jit(solution)/shard_map/ppermute | solution.py:31
  342.9 11.3 %collective-permute-start.30 = (f32[64,1536]{1,0:T(8,128)S(1)}, f32[64,1536]{1,0:T(8,128)S(1)}, u32[]{:S(2)}, u32[]{:S(2)}) collective-permute-start(f32[64,1536]{1,0:T(8,128)S(1)} %get-tuple-element.525), channel_id=1, source_target_pairs={{0,2},{1,3},{2,0},{3,1},{4,6},{5,7},{6,4},{7,5},{8,10},{9,11},{10,... | collective-permute-start | bytes 1179656 | tf_op jit(solution)/shard_map/ppermute | solution.py:31
  362.9 11.2 %collective-permute-start.36 = (f32[64,1536]{1,0:T(8,128)}, f32[64,1536]{1,0:T(8,128)}, u32[]{:S(2)}, u32[]{:S(2)}) collective-permute-start(f32[64,1536]{1,0:T(8,128)} %get-tuple-element.478), channel_id=1, source_target_pairs={{0,1},{1,0},{2,3},{3,2},{4,5},{5,4},{6,7},{7,6},{8,9},{9,8},{10,11... | collective-permute-start | bytes 1179656 | tf_op jit(solution)/shard_map/ppermute | solution.py:31
  364.5 190.1 %reduce-scatter.9.cloned.1.call-start = ((), (), s32[]{:S(2)}) async-start(), calls=%async_computation.7 | async-start | bytes 5898240 | tf_op jit(solution)/shard_map/reduce_scatter | solution.py:785
  364.6 12.4 %collective-permute-start.34 = (f32[64,1536]{1,0:T(8,128)}, f32[64,1536]{1,0:T(8,128)S(1)}, u32[]{:S(2)}, u32[]{:S(2)}) collective-permute-start(f32[64,1536]{1,0:T(8,128)} %get-tuple-element.479), channel_id=1, source_target_pairs={{0,2},{1,3},{2,0},{3,1},{4,6},{5,7},{6,4},{7,5},{8,10},{9,11},{10,... | collective-permute-start | bytes 1179656 | tf_op jit(solution)/shard_map/ppermute | solution.py:31
  375.3 18.5 %collective-permute-start.37 = (f32[128,1536]{1,0:T(8,128)S(1)}, f32[128,1536]{1,0:T(8,128)S(1)}, u32[]{:S(2)}, u32[]{:S(2)}) collective-permute-start(f32[128,1536]{1,0:T(8,128)S(1)} %pad_maximum_fusion.12), channel_id=1, source_target_pairs={{0,2},{1,3},{2,0},{3,1},{4,6},{5,7},{6,4},{7,5},{8,10},{9,11},{10,... | collective-permute-start | bytes 2359304 | tf_op jit(solution)/shard_map/ppermute | solution.py:31
  377.1 18.4 %collective-permute-start.35 = (f32[128,1536]{1,0:T(8,128)S(1)}, f32[128,1536]{1,0:T(8,128)S(1)}, u32[]{:S(2)}, u32[]{:S(2)}) collective-permute-start(f32[128,1536]{1,0:T(8,128)S(1)} %pad_maximum_fusion.11), channel_id=1, source_target_pairs={{0,1},{1,0},{2,3},{3,2},{4,5},{5,4},{6,7},{7,6},{8,9},{9,8},{10,11... | collective-permute-start | bytes 2359304 | tf_op jit(solution)/shard_map/ppermute | solution.py:31
  396.6 31.7 %collective-permute-start.38 = (f32[128,1536]{1,0:T(8,128)S(1)}, f32[128,1536]{1,0:T(8,128)}, u32[]{:S(2)}, u32[]{:S(2)}) collective-permute-start(f32[128,1536]{1,0:T(8,128)S(1)} %get-tuple-element.515), channel_id=1, source_target_pairs={{0,1},{1,0},{2,3},{3,2},{4,5},{5,4},{6,7},{7,6},{8,9},{9,8},{10,11... | collective-permute-start | bytes 2359304 | tf_op jit(solution)/shard_map/ppermute | solution.py:31
  397.7 30.5 %collective-permute-start.39 = (f32[128,1536]{1,0:T(8,128)S(1)}, f32[128,1536]{1,0:T(8,128)}, u32[]{:S(2)}, u32[]{:S(2)}) collective-permute-start(f32[128,1536]{1,0:T(8,128)S(1)} %get-tuple-element.514), channel_id=1, source_target_pairs={{0,2},{1,3},{2,0},{3,1},{4,6},{5,7},{6,4},{7,5},{8,10},{9,11},{10,... | collective-permute-start | bytes 2359304 | tf_op jit(solution)/shard_map/ppermute | solution.py:31
  411.0 17.3 %collective-permute-start.42 = (f32[128,768]{1,0:T(8,128)}, f32[128,768]{1,0:T(8,128)}, u32[]{:S(2)}, u32[]{:S(2)}) collective-permute-start(f32[128,768]{1,0:T(8,128)} %get-tuple-element.329), channel_id=1, source_target_pairs={{12,8},{13,9},{14,10},{15,11},{28,24},{29,25},{30,26},{31,27}} | collective-permute-start | bytes 1179656 | tf_op jit(solution)/shard_map/ppermute | solution.py:156
  428.4 24.4 %collective-permute-start.45 = (f32[1536,768]{1,0:T(8,128)}, f32[1536,768]{1,0:T(8,128)S(1)}, u32[]{:S(2)}, u32[]{:S(2)}) collective-permute-start(f32[1536,768]{1,0:T(8,128)} %copy-done.81), channel_id=1, source_target_pairs={{0,16},{16,0},{1,17},{17,1},{2,18},{18,2},{3,19},{19,3},{4,20},{20... | collective-permute-start | bytes 14155784 | tf_op jit(solution)/shard_map/ppermute | solution.py:31
  430.0 15.4 %collective-permute-start.41 = (f32[64,1536]{1,0:T(8,128)S(1)}, f32[64,1536]{1,0:T(8,128)S(1)}, u32[]{:S(2)}, u32[]{:S(2)}) collective-permute-start(f32[64,1536]{1,0:T(8,128)S(1)} %get-tuple-element.509), channel_id=1, source_target_pairs={{0,1},{1,0},{2,3},{3,2},{4,5},{5,4},{6,7},{7,6},{8,9},{9,8},{10,11... | collective-permute-start | bytes 1179656 | tf_op jit(solution)/shard_map/ppermute | solution.py:31
  432.6 12.8 %collective-permute-start.40 = (f32[64,1536]{1,0:T(8,128)S(1)}, f32[64,1536]{1,0:T(8,128)S(1)}, u32[]{:S(2)}, u32[]{:S(2)}) collective-permute-start(f32[64,1536]{1,0:T(8,128)S(1)} %get-tuple-element.511), channel_id=1, source_target_pairs={{0,2},{1,3},{2,0},{3,1},{4,6},{5,7},{6,4},{7,5},{8,10},{9,11},{10,... | collective-permute-start | bytes 1179656 | tf_op jit(solution)/shard_map/ppermute | solution.py:31
  434.6 14.9 %collective-permute-start.48 = (f32[128,768]{1,0:T(8,128)S(1)}, f32[128,768]{1,0:T(8,128)S(1)}, u32[]{:S(2)}, u32[]{:S(2)}) collective-permute-start(f32[128,768]{1,0:T(8,128)S(1)} %multiply_add_fusion.1), channel_id=1, source_target_pairs={{8,4},{9,5},{10,6},{11,7},{24,20},{25,21},{26,22},{27,23}} | collective-permute-start | bytes 1179656 | tf_op jit(solution)/shard_map/ppermute | solution.py:156
  451.4 14.2 %collective-permute-start.49 = (f32[128,768]{1,0:T(8,128)}, f32[128,768]{1,0:T(8,128)}, u32[]{:S(2)}, u32[]{:S(2)}) collective-permute-start(f32[128,768]{1,0:T(8,128)} %multiply_add_fusion), channel_id=1, source_target_pairs={{4,0},{5,1},{6,2},{7,3},{20,16},{21,17},{22,18},{23,19}} | collective-permute-start | bytes 1179656 | tf_op jit(solution)/shard_map/ppermute | solution.py:156
  460.7 18.9 %collective-permute-start.47 = (f32[128,1536]{1,0:T(8,128)}, f32[128,1536]{1,0:T(8,128)}, u32[]{:S(2)}, u32[]{:S(2)}) collective-permute-start(f32[128,1536]{1,0:T(8,128)} %pad_maximum_fusion.14), channel_id=1, source_target_pairs={{0,2},{1,3},{2,0},{3,1},{4,6},{5,7},{6,4},{7,5},{8,10},{9,11},{10,... | collective-permute-start | bytes 2359304 | tf_op jit(solution)/shard_map/ppermute | solution.py:31
  464.6 18.1 %collective-permute-start.46 = (f32[128,1536]{1,0:T(8,128)}, f32[128,1536]{1,0:T(8,128)}, u32[]{:S(2)}, u32[]{:S(2)}) collective-permute-start(f32[128,1536]{1,0:T(8,128)} %pad_maximum_fusion.13), channel_id=1, source_target_pairs={{0,1},{1,0},{2,3},{3,2},{4,5},{5,4},{6,7},{7,6},{8,9},{9,8},{10,11... | collective-permute-start | bytes 2359304 | tf_op jit(solution)/shard_map/ppermute | solution.py:31
  465.7 154.0 %reduce-scatter.11.cloned.1.call-start = ((), (), s32[]{:S(2)}) async-start(), calls=%async_computation.8 | async-start | bytes 3317760 | tf_op jit(solution)/shard_map/reduce_scatter | solution.py:785
  509.2 19.4 %collective-permute-start.52 = (f32[128,1536]{1,0:T(8,128)S(1)}, f32[128,1536]{1,0:T(8,128)S(1)}, u32[]{:S(2)}, u32[]{:S(2)}) collective-permute-start(f32[128,1536]{1,0:T(8,128)S(1)} %get-tuple-element.501), channel_id=1, source_target_pairs={{0,1},{1,0},{2,3},{3,2},{4,5},{5,4},{6,7},{7,6},{8,9},{9,8},{10,11... | collective-permute-start | bytes 2359304 | tf_op jit(solution)/shard_map/ppermute | solution.py:31
  510.2 18.5 %collective-permute-start.53 = (f32[128,1536]{1,0:T(8,128)S(1)}, f32[128,1536]{1,0:T(8,128)S(1)}, u32[]{:S(2)}, u32[]{:S(2)}) collective-permute-start(f32[128,1536]{1,0:T(8,128)S(1)} %get-tuple-element.500), channel_id=1, source_target_pairs={{0,2},{1,3},{2,0},{3,1},{4,6},{5,7},{6,4},{7,5},{8,10},{9,11},{10,... | collective-permute-start | bytes 2359304 | tf_op jit(solution)/shard_map/ppermute | solution.py:31
  537.9 16.8 %collective-permute-start.57 = (f32[4,432,384]{2,1,0:T(8,128)}, f32[4,432,384]{2,1,0:T(8,128)}, u32[]{:S(2)}, u32[]{:S(2)}) collective-permute-start(f32[4,432,384]{2,1,0:T(8,128)} %get-tuple-element.392), channel_id=1, source_target_pairs={{0,16},{16,0},{1,17},{17,1},{2,18},{18,2},{3,19},{19,3},{4,20},{20... | collective-permute-start | bytes 7962632 | tf_op jit(solution)/shard_map/ppermute | solution.py:31
  539.8 55.7 %collective-permute-start.64 = (f32[384,768]{1,0:T(8,128)}, f32[384,768]{1,0:T(8,128)}, u32[]{:S(2)}, u32[]{:S(2)}) collective-permute-start(f32[384,768]{1,0:T(8,128)} %reduce-scatter.5.cloned.1.call-done.refs_2_), channel_id=1, source_target_pairs={{0,16},{16,0},{1,17},{17,1},{2,18},{18,2},{3,19},{19,3},{4,20},{20... | collective-permute-start | bytes 3538952 | tf_op jit(solution)/shard_map/ppermute | solution.py:31
  548.1 11.6 %collective-permute-start.55 = (f32[64,1536]{1,0:T(8,128)}, f32[64,1536]{1,0:T(8,128)}, u32[]{:S(2)}, u32[]{:S(2)}) collective-permute-start(f32[64,1536]{1,0:T(8,128)} %get-tuple-element.495), channel_id=1, source_target_pairs={{0,1},{1,0},{2,3},{3,2},{4,5},{5,4},{6,7},{7,6},{8,9},{9,8},{10,11... | collective-permute-start | bytes 1179656 | tf_op jit(solution)/shard_map/ppermute | solution.py:31
  550.6 11.3 %collective-permute-start.54 = (f32[64,1536]{1,0:T(8,128)}, f32[64,1536]{1,0:T(8,128)}, u32[]{:S(2)}, u32[]{:S(2)}) collective-permute-start(f32[64,1536]{1,0:T(8,128)} %get-tuple-element.497), channel_id=1, source_target_pairs={{0,2},{1,3},{2,0},{3,1},{4,6},{5,7},{6,4},{7,5},{8,10},{9,11},{10,... | collective-permute-start | bytes 1179656 | tf_op jit(solution)/shard_map/ppermute | solution.py:31
  573.7 13.6 %collective-permute-start.65 = (f32[64,1536]{1,0:T(8,128)S(1)}, f32[64,1536]{1,0:T(8,128)S(1)}, u32[]{:S(2)}, u32[]{:S(2)}) collective-permute-start(f32[64,1536]{1,0:T(8,128)S(1)} %get-tuple-element.476), channel_id=1, source_target_pairs={{0,2},{1,3},{2,0},{3,1},{4,6},{5,7},{6,4},{7,5},{8,10},{9,11},{10,... | collective-permute-start | bytes 1179656 | tf_op jit(solution)/shard_map/ppermute | solution.py:31
  579.4 16.2 %collective-permute-start.63 = (f32[384,768]{1,0:T(8,128)S(1)}, f32[384,768]{1,0:T(8,128)S(1)}, u32[]{:S(2)}, u32[]{:S(2)}) collective-permute-start(f32[384,768]{1,0:T(8,128)S(1)} %copy-done.38), channel_id=1, source_target_pairs={{0,16},{16,0},{1,17},{17,1},{2,18},{18,2},{3,19},{19,3},{4,20},{20... | collective-permute-start | bytes 3538952 | tf_op jit(solution)/shard_map/ppermute | solution.py:31
  579.5 12.0 %collective-permute-start.67 = (f32[64,1536]{1,0:T(8,128)S(1)}, f32[64,1536]{1,0:T(8,128)S(1)}, u32[]{:S(2)}, u32[]{:S(2)}) collective-permute-start(f32[64,1536]{1,0:T(8,128)S(1)} %get-tuple-element.477), channel_id=1, source_target_pairs={{0,1},{1,0},{2,3},{3,2},{4,5},{5,4},{6,7},{7,6},{8,9},{9,8},{10,11... | collective-permute-start | bytes 1179656 | tf_op jit(solution)/shard_map/ppermute | solution.py:31
  584.3 11.2 %collective-permute-start.62 = (f32[132,128]{1,0:T(8,128)S(1)}, f32[132,128]{1,0:T(8,128)S(1)}, u32[]{:S(2)}, u32[]{:S(2)}) collective-permute-start(f32[132,128]{1,0:T(8,128)S(1)} %add.569), channel_id=1, source_target_pairs={{0,8},{4,12},{8,0},{12,4},{1,9},{5,13},{9,1},{13,5},{2,10},{6,14},... | collective-permute-start | bytes 202760 | tf_op jit(solution)/shard_map/ppermute | solution.py:31
  587.4 20.5 %collective-permute-start.66 = (f32[128,1536]{1,0:T(8,128)S(1)}, f32[128,1536]{1,0:T(8,128)S(1)}, u32[]{:S(2)}, u32[]{:S(2)}) collective-permute-start(f32[128,1536]{1,0:T(8,128)S(1)} %pad_maximum_fusion.15), channel_id=1, source_target_pairs={{0,1},{1,0},{2,3},{3,2},{4,5},{5,4},{6,7},{7,6},{8,9},{9,8},{10,11... | collective-permute-start | bytes 2359304 | tf_op jit(solution)/shard_map/ppermute | solution.py:31
  592.6 27.1 %collective-permute-start.68 = (f32[128,1536]{1,0:T(8,128)}, f32[128,1536]{1,0:T(8,128)}, u32[]{:S(2)}, u32[]{:S(2)}) collective-permute-start(f32[128,1536]{1,0:T(8,128)} %pad_maximum_fusion.16), channel_id=1, source_target_pairs={{0,2},{1,3},{2,0},{3,1},{4,6},{5,7},{6,4},{7,5},{8,10},{9,11},{10,... | collective-permute-start | bytes 2359304 | tf_op jit(solution)/shard_map/ppermute | solution.py:31
  (203 other events, 1677.8 us)
Sparse Core Ops, SparseCore 0:
  19.0 44.7 all-gather.1
  274.0 83.3 reduce-scatter.4
  364.7 52.2 reduce-scatter.6
  465.8 87.5 reduce-scatter.8
  562.0 57.6 reduce-scatter.10

commit v6 on v5

--- a/solution.py
+++ b/solution.py
@@ -1007,7 +1007,7 @@
         last = jnp.concatenate([last, small], axis=1)
     last = last.reshape(-1, last.shape[2])
     if final:
-        (last,) = steps.advance(last)
+        steps.advance()
     else:
         last, pair = steps.advance(last, pair)
     last = over_seq(after(last, pair))

time: 647 us -> 644 us (level)
    reduce_scatter x4, waiting for transfers between devices: 13.8 us -> 4.9 us  [over_seq(): return lax.psum_scatter(total, 'seq', scatter_dimension=0, tiled=True)]
    unnamed x351 -> x347, local copies, waits for them, and re-layouts: 31.8 us -> 31.7 us
  transfers between devices with their start and end apart: 76 -> 76, of which waited for: 38 -> 37; matrix products, arithmetic and copies ran while one was open for 26% -> 26% of each run, Pallas kernels for 17% -> 17%
where the time goes in v6:
time: 644 us; the launch traced here: 633 us
  waiting for transfers between devices  159 us (25%)
  Pallas kernels  131 us (20%)
  matrix products  101 us (16%)
  starting transfers between devices  94.8 us (15%)
  other arithmetic  76.5 us (12%)
  local copies, waits for them, and re-layouts  53.5 us (8%)
  between operations  17.1 us (3%)
    ppermute x55, waiting for transfers between devices, exchanged(): return lax.ppermute(value, axis, [(i, i ^ distance) for i in range(n)])  131 us
    pallas_call x18, Pallas kernels, call(): pl.pallas_call(kernel, grid=(steps,), out_shape=shapes, in_specs=[spec(bl...  119 us
    dot_general x23, matrix products, matmul(): return lax.dot_general(left, right, (dims, ((), ())), precision=precision)  101 us
    ppermute x55, starting transfers between devices, exchanged(): return lax.ppermute(value, axis, [(i, i ^ distance) for i in range(n)])  61.4 us
    unnamed x347, local copies, waits for them, and re-layouts  31.7 us
    ppermute x12, starting transfers between devices, state_before(): got = lax.ppermute(leaving, 'seq', [(source, target)])  22 us
    ppermute x12, waiting for transfers between devices, state_before(): got = lax.ppermute(leaving, 'seq', [(source, target)])  18 us
    select_n x18, other arithmetic, joined(): jnp.where(first, mine, other)  13.7 us
  transfers between devices with their start and end apart: 76, of which 37 were waited for; matrix products, arithmetic and copies ran while one was open for 26% of the time, Pallas kernels for 17%

profile of v6, /device:TPU:0, one launch (start us, length us, event | category | flops | bytes accessed | tf_op | source)
XLA Modules:
  0.0 633.5 jit_solution(6606286550753705745)
XLA Ops:
  10.5 3.6 fusion.59
  23.0 10.1 %fusion.30.ip.pi = f32[512,768]{1,0:T(8,128)} fusion(f32[512,1536]{1,0:T(8,128)S(1)} %fusion.62.two.left, f32[2,1536,768]{2,1,0:T(8,128)} %param.20), kind=kOutput, calls=%fused_computation.30 | convolution fusion | flops 7247757312 | bytes 9437184 | tf_op jit(solution)/shard_map/dot_general | solution.py:575
  53.5 8.0 %shard_map.279 = (f32[512,768]{1,0:T(8,128)}, f32[512,256]{1,0:T(8,128)}, f32[512,768]{1,0:T(8,128)}, f32[512,256]{1,0:T(8,128)}, f32[512,128]{1,0:T(8,128)}, /*...) custom-call(f32[512,768]{1,0:T(8,128)} %fusion.30.ip.pi, ...), custom_call_target="tpu_custom_call" | custom-call | flops 75497472 | bytes 2317312 | tf_op jit(solution)/shard_map/pallas_call | solution.py:191
  61.6 4.5 collective-permute-start.3
  66.1 7.0 %shard_map.280.yd = f32[512,768]{1,0:T(8,128)} custom-call(f32[512,768]{1,0:T(8,128)} %get-tuple-element.223.v, f32[512,256]{1,0:T(8,128)} %get-tuple-element.224.bc, f32[512,128]{1,0:T(8,128)} %get-tuple-element.225.dt, f32[512,128]{1,0:T(8,128)} %get-tuple-element.226.cum, f32[16,512]{1,0:T(8,128)} %get-tuple-element.227.cumt, f32[8,128]{1,0:T(8,128)} %get-tuple-element.615.hp), custom_call_target="tpu_custom_call" | custom-call | flops 150994944 | bytes 1057792 | tf_op jit(solution)/shard_map/pallas_call | solution.py:191
  75.5 10.1 %fusion.24.gate = f32[512,768]{1,0:T(8,128)} fusion(f32[512,1536]{1,0:T(8,128)S(1)} %fusion.62.two.left, f32[2,1536,768]{2,1,0:T(8,128)} %param.19), kind=kOutput, calls=%fused_computation.24 | convolution fusion | flops 7247757312 | bytes 9437184 | tf_op jit(solution)/shard_map/dot_general | solution.py:575
  97.6 7.0 %fusion.20 = f32[256,1536]{1,0:T(8,128)S(1)} fusion(f32[2,1536,768]{2,1,0:T(8,128)} %param.31, f32[128,768]{1,0:T(8,128)S(1)} %get-tuple-element.573, f32[128,768]{1,0:T(8,128)S(1)} %get-tuple-element.571), kind=kOutput, calls=%fused_computation.20 | convolution fusion | flops 3624075264 | bytes 7077888 | tf_op jit(solution)/shard_map/dot_general | solution.py:575
  106.9 4.1 fusion.18
  112.9 5.4 fusion.14.q
  118.2 4.3 collective-permute-done.9
  128.2 5.0 collective-permute-done.8
  141.7 6.2 collective-permute-done.14
  150.6 9.7 %collective-permute-done.12 = f32[128,1536]{1,0:T(8,128)S(1)} collective-permute-done((f32[128,1536]{1,0:T(8,128)S(1)}, f32[128,1536]{1,0:T(8,128)S(1)}, u32[]{:S(2)}, u32[]{:S(2)}) %collective-permute-start.12) | collective-permute-done | bytes 786464 | tf_op jit(solution)/shard_map/ppermute | solution.py:31
  163.6 5.6 fusion.97.sp.ps
  169.3 4.3 fusion.8.ip.pi
  174.8 3.9 collective-permute-start.16
  181.5 8.0 %shard_map.282 = (f32[512,768]{1,0:T(8,128)}, f32[512,256]{1,0:T(8,128)}, f32[512,768]{1,0:T(8,128)}, f32[512,256]{1,0:T(8,128)}, f32[512,128]{1,0:T(8,128)}, /*...) custom-call(f32[512,768]{1,0:T(8,128)} %copy-done.9, ...), custom_call_target="tpu_custom_call" | custom-call | flops 75497472 | bytes 2317312 | tf_op jit(solution)/shard_map/pallas_call | solution.py:191
  189.6 7.1 %collective-permute-start.17 = (f32[128,768]{1,0:T(8,128)}, f32[128,768]{1,0:T(8,128)S(1)}, u32[]{:S(2)}, u32[]{:S(2)}) collective-permute-start(f32[128,768]{1,0:T(8,128)} %get-tuple-element.246), channel_id=1, source_target_pairs={{0,4},{1,5},{2,6},{3,7},{16,20},{17,21},{18,22},{19,23}} | collective-permute-start | bytes 1179656 | tf_op jit(solution)/shard_map/ppermute | solution.py:156
  196.7 7.0 %shard_map.283.yd = f32[512,768]{1,0:T(8,128)} custom-call(f32[512,768]{1,0:T(8,128)} %get-tuple-element.247.v, f32[512,256]{1,0:T(8,128)} %get-tuple-element.248.bc, f32[512,128]{1,0:T(8,128)} %get-tuple-element.249.dt, f32[512,128]{1,0:T(8,128)} %get-tuple-element.250.cum, f32[16,512]{1,0:T(8,128)} %get-tuple-element.251.cumt, f32[8,128]{1,0:T(8,128)} %get-tuple-element.614.hp), custom_call_target="tpu_custom_call" | custom-call | flops 150994944 | bytes 1057792 | tf_op jit(solution)/shard_map/pallas_call | solution.py:191
  206.3 6.6 %fusion.2.gate = f32[512,768]{1,0:T(8,128)S(1)} fusion(f32[512,1536]{1,0:T(8,128)S(1)} %multiply_multiply_fusion.two.left, f32[2,1536,768]{2,1,0:T(8,128)} %param.19), kind=kOutput, calls=%fused_computation.2 | convolution fusion | flops 3623878656 | bytes 9437184 | tf_op jit(solution)/shard_map/dot_general | solution.py:575
  230.8 9.8 %shard_map.286 = (f32[1536,768]{1,0:T(8,128)S(1)}, f32[1536,768]{1,0:T(8,128)S(1)}) custom-call(f32[512,1536]{1,0:T(8,128)S(1)} %bitcast.204, f32[512,768]{1,0:T(8,128)S(1)} %get-tuple-element.266.a, f32[512,1536]{1,0:T(8,128)S(1)} %multiply_multiply_fusion.two.left, f32[512,768]{1,0:T(8,128)S(1)} %get-tuple-element.287.b), custom_call_target="tpu_custom_call" | custom-call | flops 603979776 | bytes 4718592 | tf_op jit(solution)/shard_map/pallas_call | solution.py:191
  241.5 8.1 %shard_map.287 = (f32[512,768]{1,0:T(8,128)S(1)}, f32[512,256]{1,0:T(8,128)S(1)}) custom-call(f32[512,768]{1,0:T(8,128)S(1)} %get-tuple-element.271.dy, f32[512,768]{1,0:T(8,128)S(1)} %copy-done.12, f32[512,256]{1,0:T(8,128)S(1)} %copy-done.17, f32[512,128]{1,0:T(8,128)S(1)} %copy-done.41, f32[512,128]{1,0:T(8,128)S(1)} %copy-done.19, ...), custom_call_target="tpu_custom_call" | custom-call | flops 377487360 | bytes 1974272 | tf_op jit(solution)/shard_map/pallas_call | solution.py:191
  255.8 17.9 %collective-permute-done.24 = f32[128,768]{1,0:T(8,128)} collective-permute-done((f32[128,768]{1,0:T(8,128)}, f32[128,768]{1,0:T(8,128)}, u32[]{:S(2)}, u32[]{:S(2)}) %collective-permute-start.24) | collective-permute-done | bytes 393248 | tf_op jit(solution)/shard_map/ppermute | solution.py:156
  275.9 11.0 %shard_map.288 = (f32[512,768]{1,0:T(8,128)}, f32[512,256]{1,0:T(8,128)}, f32[512,128]{1,0:T(8,128)}, f32[24,768]{1,0:T(8,128)}) custom-call(f32[512,768]{1,0:T(8,128)} %copy-done.30, f32[512,768]{1,0:T(8,128)} %copy-done.29, f32[512,768]{1,0:T(8,128)} %get-tuple-element.247.v, f32[512,768]{1,0:T(8,128)} %copy-done.47, f32[512,768]{1,0:T(8,128)} %get-tuple-element.276.dsi, ...), custom_call_target="tpu_custom_call" | custom-call | flops 150994944 | bytes 3910656 | tf_op jit(solution)/shard_map/pallas_call | solution.py:191
  290.4 6.0 fusion
  317.2 4.9 collective-permute-done.32
  322.4 12.8 %collective-permute-done.28 = f32[128,1536]{1,0:T(8,128)S(1)} collective-permute-done((f32[128,1536]{1,0:T(8,128)S(1)}, f32[128,1536]{1,0:T(8,128)S(1)}, u32[]{:S(2)}, u32[]{:S(2)}) %collective-permute-start.28) | collective-permute-done | bytes 786464 | tf_op jit(solution)/shard_map/ppermute | solution.py:31
  335.2 6.3 shard_map.290
  348.4 4.9 collective-permute-done.31
  366.1 7.9 %collective-permute-done.36 = f32[64,1536]{1,0:T(8,128)} collective-permute-done((f32[64,1536]{1,0:T(8,128)}, f32[64,1536]{1,0:T(8,128)}, u32[]{:S(2)}, u32[]{:S(2)}) %collective-permute-start.36) | collective-permute-done | bytes 393248 | tf_op jit(solution)/shard_map/ppermute | solution.py:31
  378.5 4.4 fusion.10
  383.0 4.5 fusion.12
  387.5 6.3 collective-permute-done.37
  400.0 4.3 fusion.16.q
  404.4 3.9 shard_map.292
  412.4 9.8 %shard_map.293 = (f32[1536,768]{1,0:T(8,128)S(1)}, f32[1536,768]{1,0:T(8,128)S(1)}) custom-call(f32[512,1536]{1,0:T(8,128)S(1)} %maximum_add_fusion.1.one, f32[512,768]{1,0:T(8,128)S(1)} %get-tuple-element.325.a, f32[512,1536]{1,0:T(8,128)S(1)} %copy-done.1, f32[512,768]{1,0:T(8,128)S(1)} %get-tuple-element.369.b), custom_call_target="tpu_custom_call" | custom-call | flops 603979776 | bytes 4718592 | tf_op jit(solution)/shard_map/pallas_call | solution.py:191
  435.3 8.1 %shard_map.294 = (f32[512,768]{1,0:T(8,128)S(1)}, f32[512,256]{1,0:T(8,128)S(1)}) custom-call(f32[512,768]{1,0:T(8,128)S(1)} %copy-done.27, f32[512,768]{1,0:T(8,128)S(1)} %copy-done.11, f32[512,256]{1,0:T(8,128)S(1)} %copy-done.16, f32[512,128]{1,0:T(8,128)S(1)} %copy-done.40, f32[512,128]{1,0:T(8,128)S(1)} %copy-done.18, f32[16,512]{1,0:T(8,128)S(1)} %copy-done.65, ...), custom_call_target="tpu_custom_call" | custom-call | flops 377487360 | bytes 1974272 | tf_op jit(solution)/shard_map/pallas_call | solution.py:191
  468.8 10.8 %shard_map.295 = (f32[512,768]{1,0:T(8,128)}, f32[512,256]{1,0:T(8,128)}, f32[512,128]{1,0:T(8,128)}, f32[24,768]{1,0:T(8,128)}) custom-call(f32[512,768]{1,0:T(8,128)} %copy-done.26, f32[512,768]{1,0:T(8,128)} %copy-done.24, f32[512,768]{1,0:T(8,128)} %get-tuple-element.223.v, f32[512,768]{1,0:T(8,128)} %copy-done.45, f32[512,768]{1,0:T(8,128)} %get-tuple-element.357.dsi, ...), custom_call_target="tpu_custom_call" | custom-call | flops 150994944 | bytes 3910656 | tf_op jit(solution)/shard_map/pallas_call | solution.py:191
  485.8 6.0 fusion.22
  513.1 3.8 collective-permute-done.61
  517.1 11.3 %collective-permute-done.52 = f32[128,1536]{1,0:T(8,128)S(1)} collective-permute-done((f32[128,1536]{1,0:T(8,128)S(1)}, f32[128,1536]{1,0:T(8,128)S(1)}, u32[]{:S(2)}, u32[]{:S(2)}) %collective-permute-start.52) | collective-permute-done | bytes 786464 | tf_op jit(solution)/shard_map/ppermute | solution.py:31
  529.4 6.9 %shard_map.298 = (f32[4,432,384]{2,1,0:T(8,128)}, f32[4,432,384]{2,1,0:T(8,128)S(1)}) custom-call(f32[512,1536]{1,0:T(8,128)S(1)} %copy-done.2, f32[512,768]{1,0:T(8,128)S(1)} %get-tuple-element.389.right, f32[512,128]{1,0:T(8,128)S(1)} %pad_maximum_fusion.20.small), custom_call_target="tpu_custom_call" | custom-call | flops 352321536 | bytes 2572288 | tf_op jit(solution)/shard_map/pallas_call | solution.py:191
  539.8 4.2 collective-permute-done.70.refs_3_
  555.1 4.3 add.570
  595.7 10.7 %collective-permute-done.66 = f32[128,1536]{1,0:T(8,128)S(1)} collective-permute-done((f32[128,1536]{1,0:T(8,128)S(1)}, f32[128,1536]{1,0:T(8,128)S(1)}, u32[]{:S(2)}, u32[]{:S(2)}) %collective-permute-start.66) | collective-permute-done | bytes 786464 | tf_op jit(solution)/shard_map/ppermute | solution.py:31
  607.7 3.7 shard_map.300
  611.4 3.6 shard_map.299
  623.0 3.7 shard_map.302
  (702 shorter events, 288.6 us)
Async XLA Ops:
  7.2 78.5 %all-gather.2.cloned.1.call-start = ((), (), s32[]{:S(2)}) async-start(), calls=%async_computation.4 | async-start | bytes 3932160 | tf_op jit(solution)/shard_map/all_gather | solution.py:1177
  14.9 19.4 %collective-permute-start = (f32[528,64]{1,0:T(8,128)S(1)}, f32[528,64]{1,0:T(8,128)}, u32[]{:S(2)}, u32[]{:S(2)}) collective-permute-start(f32[528,64]{1,0:T(8,128)S(1)} %pad_maximum_fusion.17), channel_id=1, source_target_pairs={{0,1},{1,0},{2,3},{3,2},{4,5},{5,4},{6,7},{7,6},{8,9},{9,8},{10,11... | collective-permute-start | bytes 405512 | tf_op jit(solution)/shard_map/ppermute | solution.py:31
  19.0 338.4 %reduce-scatter.5.cloned.1.call-start = ((), (), s32[]{:S(2)}) async-start(), calls=%async_computation.5 | async-start | bytes 5898240 | tf_op jit(solution)/shard_map/reduce_scatter | solution.py:785
  61.6 12.3 %collective-permute-start.3 = (f32[128,768]{1,0:T(8,128)}, f32[128,768]{1,0:T(8,128)S(1)}, u32[]{:S(2)}, u32[]{:S(2)}) collective-permute-start(f32[128,768]{1,0:T(8,128)} %get-tuple-element.222), channel_id=1, source_target_pairs={{0,4},{1,5},{2,6},{3,7},{16,20},{17,21},{18,22},{19,23}} | collective-permute-start | bytes 1179656 | tf_op jit(solution)/shard_map/ppermute | solution.py:156
  73.9 11.7 %collective-permute-start.4 = (f32[128,768]{1,0:T(8,128)S(1)}, f32[128,768]{1,0:T(8,128)}, u32[]{:S(2)}, u32[]{:S(2)}) collective-permute-start(f32[128,768]{1,0:T(8,128)S(1)} %multiply_add_fusion.7), channel_id=1, source_target_pairs={{4,8},{5,9},{6,10},{7,11},{20,24},{21,25},{22,26},{23,27}} | collective-permute-start | bytes 1179656 | tf_op jit(solution)/shard_map/ppermute | solution.py:156
  104.7 18.8 %collective-permute-start.6 = (f32[128,1536]{1,0:T(8,128)S(1)}, f32[128,1536]{1,0:T(8,128)S(1)}, u32[]{:S(2)}, u32[]{:S(2)}) collective-permute-start(f32[128,1536]{1,0:T(8,128)S(1)} %get-tuple-element.531), channel_id=1, source_target_pairs={{0,1},{1,0},{2,3},{3,2},{4,5},{5,4},{6,7},{7,6},{8,9},{9,8},{10,11... | collective-permute-start | bytes 2359304 | tf_op jit(solution)/shard_map/ppermute | solution.py:31
  106.2 17.7 %collective-permute-start.7 = (f32[128,1536]{1,0:T(8,128)S(1)}, f32[128,1536]{1,0:T(8,128)S(1)}, u32[]{:S(2)}, u32[]{:S(2)}) collective-permute-start(f32[128,1536]{1,0:T(8,128)S(1)} %get-tuple-element.530), channel_id=1, source_target_pairs={{0,2},{1,3},{2,0},{3,1},{4,6},{5,7},{6,4},{7,5},{8,10},{9,11},{10,... | collective-permute-start | bytes 2359304 | tf_op jit(solution)/shard_map/ppermute | solution.py:31
  111.1 11.4 %collective-permute-start.9 = (f32[1,512]{1,0:T(1,128)S(1)}, f32[1,512]{1,0:T(1,128)S(1)}, u32[]{:S(2)}, u32[]{:S(2)}) collective-permute-start(f32[1,512]{1,0:T(1,128)S(1)} %slice.322), channel_id=1, source_target_pairs={{0,1},{1,0},{2,3},{3,2},{4,5},{5,4},{6,7},{7,6},{8,9},{9,8},{10,11... | collective-permute-start | bytes 6152 | tf_op jit(solution)/shard_map/ppermute | solution.py:31
  135.8 12.1 %collective-permute-start.14 = (f32[64,1536]{1,0:T(8,128)S(1)}, f32[64,1536]{1,0:T(8,128)S(1)}, u32[]{:S(2)}, u32[]{:S(2)}) collective-permute-start(f32[64,1536]{1,0:T(8,128)S(1)} %add_multiply_fusion.2), channel_id=1, source_target_pairs={{0,1},{1,0},{2,3},{3,2},{4,5},{5,4},{6,7},{7,6},{8,9},{9,8},{10,11... | collective-permute-start | bytes 1179656 | tf_op jit(solution)/shard_map/ppermute | solution.py:31
  141.3 19.1 %collective-permute-start.12 = (f32[128,1536]{1,0:T(8,128)S(1)}, f32[128,1536]{1,0:T(8,128)S(1)}, u32[]{:S(2)}, u32[]{:S(2)}) collective-permute-start(f32[128,1536]{1,0:T(8,128)S(1)} %pad_maximum_fusion.9), channel_id=1, source_target_pairs={{0,1},{1,0},{2,3},{3,2},{4,5},{5,4},{6,7},{7,6},{8,9},{9,8},{10,11... | collective-permute-start | bytes 2359304 | tf_op jit(solution)/shard_map/ppermute | solution.py:31
  148.0 12.4 %collective-permute-start.15 = (f32[128,1536]{1,0:T(8,128)S(1)}, f32[128,1536]{1,0:T(8,128)S(1)}, u32[]{:S(2)}, u32[]{:S(2)}) collective-permute-start(f32[128,1536]{1,0:T(8,128)S(1)} %pad_maximum_fusion.10), channel_id=1, source_target_pairs={{0,2},{1,3},{2,0},{3,1},{4,6},{5,7},{6,4},{7,5},{8,10},{9,11},{10,... | collective-permute-start | bytes 2359304 | tf_op jit(solution)/shard_map/ppermute | solution.py:31
  189.6 14.9 %collective-permute-start.17 = (f32[128,768]{1,0:T(8,128)}, f32[128,768]{1,0:T(8,128)S(1)}, u32[]{:S(2)}, u32[]{:S(2)}) collective-permute-start(f32[128,768]{1,0:T(8,128)} %get-tuple-element.246), channel_id=1, source_target_pairs={{0,4},{1,5},{2,6},{3,7},{16,20},{17,21},{18,22},{19,23}} | collective-permute-start | bytes 1179656 | tf_op jit(solution)/shard_map/ppermute | solution.py:156
  240.6 12.4 %collective-permute-start.25 = (f32[1536,768]{1,0:T(8,128)S(1)}, f32[1536,768]{1,0:T(8,128)S(1)}, u32[]{:S(2)}, u32[]{:S(2)}) collective-permute-start(f32[1536,768]{1,0:T(8,128)S(1)} %get-tuple-element.283), channel_id=1, source_target_pairs={{0,16},{16,0},{1,17},{17,1},{2,18},{18,2},{3,19},{19,3},{4,20},{20... | collective-permute-start | bytes 14155784 | tf_op jit(solution)/shard_map/ppermute | solution.py:31
  251.8 22.0 %collective-permute-start.24 = (f32[128,768]{1,0:T(8,128)}, f32[128,768]{1,0:T(8,128)}, u32[]{:S(2)}, u32[]{:S(2)}) collective-permute-start(f32[128,768]{1,0:T(8,128)} %multiply_add_fusion.2), channel_id=1, source_target_pairs={{4,0},{5,1},{6,2},{7,3},{20,16},{21,17},{22,18},{23,19}} | collective-permute-start | bytes 1179656 | tf_op jit(solution)/shard_map/ppermute | solution.py:156
  273.8 154.1 %reduce-scatter.7.cloned.1.call-start = ((), (), s32[]{:S(2)}) async-start(), calls=%async_computation.6 | async-start | bytes 3317760 | tf_op jit(solution)/shard_map/reduce_scatter | solution.py:785
  301.0 11.6 %collective-permute-start.27 = (f32[512,128]{1,0:T(8,128)S(1)}, f32[512,128]{1,0:T(8,128)S(1)}, u32[]{:S(2)}, u32[]{:S(2)}) collective-permute-start(f32[512,128]{1,0:T(8,128)S(1)} %constant_dynamic-slice_fusion.19), channel_id=1, source_target_pairs={{0,2},{1,3},{2,0},{3,1},{4,6},{5,7},{6,4},{7,5},{8,10},{9,11},{10,... | collective-permute-start | bytes 786440 | tf_op jit(solution)/shard_map/ppermute | solution.py:31
  314.5 20.7 %collective-permute-start.28 = (f32[128,1536]{1,0:T(8,128)S(1)}, f32[128,1536]{1,0:T(8,128)S(1)}, u32[]{:S(2)}, u32[]{:S(2)}) collective-permute-start(f32[128,1536]{1,0:T(8,128)S(1)} %get-tuple-element.517), channel_id=1, source_target_pairs={{0,1},{1,0},{2,3},{3,2},{4,5},{5,4},{6,7},{7,6},{8,9},{9,8},{10,11... | collective-permute-start | bytes 2359304 | tf_op jit(solution)/shard_map/ppermute | solution.py:31
  315.0 20.2 %collective-permute-start.29 = (f32[128,1536]{1,0:T(8,128)S(1)}, f32[128,1536]{1,0:T(8,128)S(1)}, u32[]{:S(2)}, u32[]{:S(2)}) collective-permute-start(f32[128,1536]{1,0:T(8,128)S(1)} %get-tuple-element.516), channel_id=1, source_target_pairs={{0,2},{1,3},{2,0},{3,1},{4,6},{5,7},{6,4},{7,5},{8,10},{9,11},{10,... | collective-permute-start | bytes 2359304 | tf_op jit(solution)/shard_map/ppermute | solution.py:31
  341.7 11.6 %collective-permute-start.31 = (f32[64,1536]{1,0:T(8,128)S(1)}, f32[64,1536]{1,0:T(8,128)S(1)}, u32[]{:S(2)}, u32[]{:S(2)}) collective-permute-start(f32[64,1536]{1,0:T(8,128)S(1)} %get-tuple-element.511), channel_id=1, source_target_pairs={{0,1},{1,0},{2,3},{3,2},{4,5},{5,4},{6,7},{7,6},{8,9},{9,8},{10,11... | collective-permute-start | bytes 1179656 | tf_op jit(solution)/shard_map/ppermute | solution.py:31
  342.9 11.3 %collective-permute-start.30 = (f32[64,1536]{1,0:T(8,128)S(1)}, f32[64,1536]{1,0:T(8,128)S(1)}, u32[]{:S(2)}, u32[]{:S(2)}) collective-permute-start(f32[64,1536]{1,0:T(8,128)S(1)} %get-tuple-element.513), channel_id=1, source_target_pairs={{0,2},{1,3},{2,0},{3,1},{4,6},{5,7},{6,4},{7,5},{8,10},{9,11},{10,... | collective-permute-start | bytes 1179656 | tf_op jit(solution)/shard_map/ppermute | solution.py:31
  362.8 11.2 %collective-permute-start.36 = (f32[64,1536]{1,0:T(8,128)}, f32[64,1536]{1,0:T(8,128)}, u32[]{:S(2)}, u32[]{:S(2)}) collective-permute-start(f32[64,1536]{1,0:T(8,128)} %get-tuple-element.470), channel_id=1, source_target_pairs={{0,1},{1,0},{2,3},{3,2},{4,5},{5,4},{6,7},{7,6},{8,9},{9,8},{10,11... | collective-permute-start | bytes 1179656 | tf_op jit(solution)/shard_map/ppermute | solution.py:31
  364.5 190.6 %reduce-scatter.9.cloned.1.call-start = ((), (), s32[]{:S(2)}) async-start(), calls=%async_computation.7 | async-start | bytes 5898240 | tf_op jit(solution)/shard_map/reduce_scatter | solution.py:785
  364.5 12.3 %collective-permute-start.34 = (f32[64,1536]{1,0:T(8,128)}, f32[64,1536]{1,0:T(8,128)S(1)}, u32[]{:S(2)}, u32[]{:S(2)}) collective-permute-start(f32[64,1536]{1,0:T(8,128)} %get-tuple-element.471), channel_id=1, source_target_pairs={{0,2},{1,3},{2,0},{3,1},{4,6},{5,7},{6,4},{7,5},{8,10},{9,11},{10,... | collective-permute-start | bytes 1179656 | tf_op jit(solution)/shard_map/ppermute | solution.py:31
  375.3 18.5 %collective-permute-start.37 = (f32[128,1536]{1,0:T(8,128)S(1)}, f32[128,1536]{1,0:T(8,128)S(1)}, u32[]{:S(2)}, u32[]{:S(2)}) collective-permute-start(f32[128,1536]{1,0:T(8,128)S(1)} %pad_maximum_fusion.12), channel_id=1, source_target_pairs={{0,2},{1,3},{2,0},{3,1},{4,6},{5,7},{6,4},{7,5},{8,10},{9,11},{10,... | collective-permute-start | bytes 2359304 | tf_op jit(solution)/shard_map/ppermute | solution.py:31
  376.9 18.2 %collective-permute-start.35 = (f32[128,1536]{1,0:T(8,128)S(1)}, f32[128,1536]{1,0:T(8,128)S(1)}, u32[]{:S(2)}, u32[]{:S(2)}) collective-permute-start(f32[128,1536]{1,0:T(8,128)S(1)} %pad_maximum_fusion.11), channel_id=1, source_target_pairs={{0,1},{1,0},{2,3},{3,2},{4,5},{5,4},{6,7},{7,6},{8,9},{9,8},{10,11... | collective-permute-start | bytes 2359304 | tf_op jit(solution)/shard_map/ppermute | solution.py:31
  396.3 31.7 %collective-permute-start.38 = (f32[128,1536]{1,0:T(8,128)S(1)}, f32[128,1536]{1,0:T(8,128)}, u32[]{:S(2)}, u32[]{:S(2)}) collective-permute-start(f32[128,1536]{1,0:T(8,128)S(1)} %get-tuple-element.503), channel_id=1, source_target_pairs={{0,1},{1,0},{2,3},{3,2},{4,5},{5,4},{6,7},{7,6},{8,9},{9,8},{10,11... | collective-permute-start | bytes 2359304 | tf_op jit(solution)/shard_map/ppermute | solution.py:31
  397.8 30.1 %collective-permute-start.39 = (f32[128,1536]{1,0:T(8,128)S(1)}, f32[128,1536]{1,0:T(8,128)}, u32[]{:S(2)}, u32[]{:S(2)}) collective-permute-start(f32[128,1536]{1,0:T(8,128)S(1)} %get-tuple-element.502), channel_id=1, source_target_pairs={{0,2},{1,3},{2,0},{3,1},{4,6},{5,7},{6,4},{7,5},{8,10},{9,11},{10,... | collective-permute-start | bytes 2359304 | tf_op jit(solution)/shard_map/ppermute | solution.py:31
  410.7 17.3 %collective-permute-start.42 = (f32[128,768]{1,0:T(8,128)}, f32[128,768]{1,0:T(8,128)}, u32[]{:S(2)}, u32[]{:S(2)}) collective-permute-start(f32[128,768]{1,0:T(8,128)} %get-tuple-element.324), channel_id=1, source_target_pairs={{12,8},{13,9},{14,10},{15,11},{28,24},{29,25},{30,26},{31,27}} | collective-permute-start | bytes 1179656 | tf_op jit(solution)/shard_map/ppermute | solution.py:156
  428.0 24.4 %collective-permute-start.45 = (f32[1536,768]{1,0:T(8,128)}, f32[1536,768]{1,0:T(8,128)S(1)}, u32[]{:S(2)}, u32[]{:S(2)}) collective-permute-start(f32[1536,768]{1,0:T(8,128)} %copy-done.81), channel_id=1, source_target_pairs={{0,16},{16,0},{1,17},{17,1},{2,18},{18,2},{3,19},{19,3},{4,20},{20... | collective-permute-start | bytes 14155784 | tf_op jit(solution)/shard_map/ppermute | solution.py:31
  429.7 15.7 %collective-permute-start.41 = (f32[64,1536]{1,0:T(8,128)S(1)}, f32[64,1536]{1,0:T(8,128)S(1)}, u32[]{:S(2)}, u32[]{:S(2)}) collective-permute-start(f32[64,1536]{1,0:T(8,128)S(1)} %get-tuple-element.497), channel_id=1, source_target_pairs={{0,1},{1,0},{2,3},{3,2},{4,5},{5,4},{6,7},{7,6},{8,9},{9,8},{10,11... | collective-permute-start | bytes 1179656 | tf_op jit(solution)/shard_map/ppermute | solution.py:31
  432.7 12.8 %collective-permute-start.40 = (f32[64,1536]{1,0:T(8,128)S(1)}, f32[64,1536]{1,0:T(8,128)S(1)}, u32[]{:S(2)}, u32[]{:S(2)}) collective-permute-start(f32[64,1536]{1,0:T(8,128)S(1)} %get-tuple-element.499), channel_id=1, source_target_pairs={{0,2},{1,3},{2,0},{3,1},{4,6},{5,7},{6,4},{7,5},{8,10},{9,11},{10,... | collective-permute-start | bytes 1179656 | tf_op jit(solution)/shard_map/ppermute | solution.py:31
  434.5 14.6 %collective-permute-start.48 = (f32[128,768]{1,0:T(8,128)S(1)}, f32[128,768]{1,0:T(8,128)S(1)}, u32[]{:S(2)}, u32[]{:S(2)}) collective-permute-start(f32[128,768]{1,0:T(8,128)S(1)} %multiply_add_fusion.1), channel_id=1, source_target_pairs={{8,4},{9,5},{10,6},{11,7},{24,20},{25,21},{26,22},{27,23}} | collective-permute-start | bytes 1179656 | tf_op jit(solution)/shard_map/ppermute | solution.py:156
  451.1 14.6 %collective-permute-start.49 = (f32[128,768]{1,0:T(8,128)}, f32[128,768]{1,0:T(8,128)}, u32[]{:S(2)}, u32[]{:S(2)}) collective-permute-start(f32[128,768]{1,0:T(8,128)} %multiply_add_fusion), channel_id=1, source_target_pairs={{4,0},{5,1},{6,2},{7,3},{20,16},{21,17},{22,18},{23,19}} | collective-permute-start | bytes 1179656 | tf_op jit(solution)/shard_map/ppermute | solution.py:156
  460.6 19.0 %collective-permute-start.47 = (f32[128,1536]{1,0:T(8,128)}, f32[128,1536]{1,0:T(8,128)}, u32[]{:S(2)}, u32[]{:S(2)}) collective-permute-start(f32[128,1536]{1,0:T(8,128)} %pad_maximum_fusion.14), channel_id=1, source_target_pairs={{0,2},{1,3},{2,0},{3,1},{4,6},{5,7},{6,4},{7,5},{8,10},{9,11},{10,... | collective-permute-start | bytes 2359304 | tf_op jit(solution)/shard_map/ppermute | solution.py:31
  464.2 18.1 %collective-permute-start.46 = (f32[128,1536]{1,0:T(8,128)}, f32[128,1536]{1,0:T(8,128)}, u32[]{:S(2)}, u32[]{:S(2)}) collective-permute-start(f32[128,1536]{1,0:T(8,128)} %pad_maximum_fusion.13), channel_id=1, source_target_pairs={{0,1},{1,0},{2,3},{3,2},{4,5},{5,4},{6,7},{7,6},{8,9},{9,8},{10,11... | collective-permute-start | bytes 2359304 | tf_op jit(solution)/shard_map/ppermute | solution.py:31
  465.7 150.9 %reduce-scatter.11.cloned.1.call-start = ((), (), s32[]{:S(2)}) async-start(), calls=%async_computation.8 | async-start | bytes 3317760 | tf_op jit(solution)/shard_map/reduce_scatter | solution.py:785
  509.1 19.4 %collective-permute-start.52 = (f32[128,1536]{1,0:T(8,128)S(1)}, f32[128,1536]{1,0:T(8,128)S(1)}, u32[]{:S(2)}, u32[]{:S(2)}) collective-permute-start(f32[128,1536]{1,0:T(8,128)S(1)} %get-tuple-element.489), channel_id=1, source_target_pairs={{0,1},{1,0},{2,3},{3,2},{4,5},{5,4},{6,7},{7,6},{8,9},{9,8},{10,11... | collective-permute-start | bytes 2359304 | tf_op jit(solution)/shard_map/ppermute | solution.py:31
  509.8 18.7 %collective-permute-start.53 = (f32[128,1536]{1,0:T(8,128)S(1)}, f32[128,1536]{1,0:T(8,128)S(1)}, u32[]{:S(2)}, u32[]{:S(2)}) collective-permute-start(f32[128,1536]{1,0:T(8,128)S(1)} %get-tuple-element.488), channel_id=1, source_target_pairs={{0,2},{1,3},{2,0},{3,1},{4,6},{5,7},{6,4},{7,5},{8,10},{9,11},{10,... | collective-permute-start | bytes 2359304 | tf_op jit(solution)/shard_map/ppermute | solution.py:31
  537.8 17.4 %collective-permute-start.62 = (f32[4,432,384]{2,1,0:T(8,128)}, f32[4,432,384]{2,1,0:T(8,128)}, u32[]{:S(2)}, u32[]{:S(2)}) collective-permute-start(f32[4,432,384]{2,1,0:T(8,128)} %get-tuple-element.394), channel_id=1, source_target_pairs={{0,16},{16,0},{1,17},{17,1},{2,18},{18,2},{3,19},{19,3},{4,20},{20... | collective-permute-start | bytes 7962632 | tf_op jit(solution)/shard_map/ppermute | solution.py:31
  539.7 68.0 %collective-permute-start.64 = (f32[384,768]{1,0:T(8,128)}, f32[384,768]{1,0:T(8,128)}, u32[]{:S(2)}, u32[]{:S(2)}) collective-permute-start(f32[384,768]{1,0:T(8,128)} %reduce-scatter.5.cloned.1.call-done.refs_2_), channel_id=1, source_target_pairs={{0,16},{16,0},{1,17},{17,1},{2,18},{18,2},{3,19},{19,3},{4,20},{20... | collective-permute-start | bytes 3538952 | tf_op jit(solution)/shard_map/ppermute | solution.py:31
  547.5 12.0 %collective-permute-start.54 = (f32[64,1536]{1,0:T(8,128)}, f32[64,1536]{1,0:T(8,128)}, u32[]{:S(2)}, u32[]{:S(2)}) collective-permute-start(f32[64,1536]{1,0:T(8,128)} %dynamic-slice_add_fusion.1), channel_id=1, source_target_pairs={{0,2},{1,3},{2,0},{3,1},{4,6},{5,7},{6,4},{7,5},{8,10},{9,11},{10,... | collective-permute-start | bytes 1179656 | tf_op jit(solution)/shard_map/ppermute | solution.py:31
  550.8 11.2 %collective-permute-start.55 = (f32[64,1536]{1,0:T(8,128)}, f32[64,1536]{1,0:T(8,128)}, u32[]{:S(2)}, u32[]{:S(2)}) collective-permute-start(f32[64,1536]{1,0:T(8,128)} %dynamic-slice_add_fusion), channel_id=1, source_target_pairs={{0,1},{1,0},{2,3},{3,2},{4,5},{5,4},{6,7},{7,6},{8,9},{9,8},{10,11... | collective-permute-start | bytes 1179656 | tf_op jit(solution)/shard_map/ppermute | solution.py:31
  573.6 12.3 %collective-permute-start.65 = (f32[64,1536]{1,0:T(8,128)S(1)}, f32[64,1536]{1,0:T(8,128)S(1)}, u32[]{:S(2)}, u32[]{:S(2)}) collective-permute-start(f32[64,1536]{1,0:T(8,128)S(1)} %get-tuple-element.468), channel_id=1, source_target_pairs={{0,2},{1,3},{2,0},{3,1},{4,6},{5,7},{6,4},{7,5},{8,10},{9,11},{10,... | collective-permute-start | bytes 1179656 | tf_op jit(solution)/shard_map/ppermute | solution.py:31
  578.6 12.1 %collective-permute-start.67 = (f32[64,1536]{1,0:T(8,128)S(1)}, f32[64,1536]{1,0:T(8,128)S(1)}, u32[]{:S(2)}, u32[]{:S(2)}) collective-permute-start(f32[64,1536]{1,0:T(8,128)S(1)} %get-tuple-element.469), channel_id=1, source_target_pairs={{0,1},{1,0},{2,3},{3,2},{4,5},{5,4},{6,7},{7,6},{8,9},{9,8},{10,11... | collective-permute-start | bytes 1179656 | tf_op jit(solution)/shard_map/ppermute | solution.py:31
  583.5 12.2 %collective-permute-start.60 = (f32[132,128]{1,0:T(8,128)S(1)}, f32[132,128]{1,0:T(8,128)S(1)}, u32[]{:S(2)}, u32[]{:S(2)}) collective-permute-start(f32[132,128]{1,0:T(8,128)S(1)} %add.566), channel_id=1, source_target_pairs={{0,8},{4,12},{8,0},{12,4},{1,9},{5,13},{9,1},{13,5},{2,10},{6,14},... | collective-permute-start | bytes 202760 | tf_op jit(solution)/shard_map/ppermute | solution.py:31
  586.0 20.4 %collective-permute-start.66 = (f32[128,1536]{1,0:T(8,128)S(1)}, f32[128,1536]{1,0:T(8,128)S(1)}, u32[]{:S(2)}, u32[]{:S(2)}) collective-permute-start(f32[128,1536]{1,0:T(8,128)S(1)} %pad_maximum_fusion.15), channel_id=1, source_target_pairs={{0,1},{1,0},{2,3},{3,2},{4,5},{5,4},{6,7},{7,6},{8,9},{9,8},{10,11... | collective-permute-start | bytes 2359304 | tf_op jit(solution)/shard_map/ppermute | solution.py:31
  591.9 24.8 %collective-permute-start.68 = (f32[128,1536]{1,0:T(8,128)}, f32[128,1536]{1,0:T(8,128)}, u32[]{:S(2)}, u32[]{:S(2)}) collective-permute-start(f32[128,1536]{1,0:T(8,128)} %pad_maximum_fusion.16), channel_id=1, source_target_pairs={{0,2},{1,3},{2,0},{3,1},{4,6},{5,7},{6,4},{7,5},{8,10},{9,11},{10,... | collective-permute-start | bytes 2359304 | tf_op jit(solution)/shard_map/ppermute | solution.py:31
  593.4 14.3 %collective-permute-start.63 = (f32[384,768]{1,0:T(8,128)S(1)}, f32[384,768]{1,0:T(8,128)S(1)}, u32[]{:S(2)}, u32[]{:S(2)}) collective-permute-start(f32[384,768]{1,0:T(8,128)S(1)} %copy-done.38), channel_id=1, source_target_pairs={{0,16},{16,0},{1,17},{17,1},{2,18},{18,2},{3,19},{19,3},{4,20},{20... | collective-permute-start | bytes 3538952 | tf_op jit(solution)/shard_map/ppermute | solution.py:31
  (201 other events, 1695.2 us)
Sparse Core Ops, SparseCore 0:
  19.0 44.7 all-gather.1
  273.9 83.3 reduce-scatter.4
  364.6 52.2 reduce-scatter.6
  465.8 87.5 reduce-scatter.8
  559.6 56.9 reduce-scatter.10
